TPU v7x, 256 devices: a whole 4x4x8 slice. The times are simulated.
256 devices in a mesh: seq: 64 (over x, z, core), ch: 4 (over y).
Axes of the slice: x: 4, y: 4, z: 8, core: 2. Of those that a mesh axis runs over, the one named last changes fastest.
Arguments:
- queries: bfloat16 [8192, 2048], P('seq', 'ch'), may hold values from -6 to 6
- key_proj: bfloat16 [8192, 2048], P('seq', 'ch'), may hold values from -6 to 6
- value_proj: bfloat16 [8192, 2048], P('seq', 'ch'), may hold values from -6 to 6
- conv_out: bfloat16 [8192, 2048], P('seq', 'ch'), may hold values from -6 to 6
- filters: bfloat16 [8192, 2048], P('seq', 'ch'), may hold values from -0.0625 to 0.0625
- out_grad: bfloat16 [8192, 2048], P('seq', 'ch'), may hold values from -6 to 6
- out_weight: bfloat16 [2048, 2048], P('seq', 'ch'), may hold values from -0.125 to 0.125
Outputs:
- query_grad: bfloat16 [8192, 2048], P('seq', 'ch')
- key_grad: bfloat16 [8192, 2048], P('seq', 'ch')
- value_grad: bfloat16 [8192, 2048], P('seq', 'ch')
- weight_grad: float32 [2048, 2048], P('seq', 'ch')
All inputs are finite; a program needn't handle non-finite values.
Results may differ from a plain program's by a relative error of at most 0.008.
Values may be sent and summed in bfloat16 or wider, within the bound.
No kernel may reach another device: no remote copies, remote signals or barrier semaphores. Data moves between devices by JAX's collectives and lax.ppermute only.
A program may use at most 128 MiB of HBM per device.

v0:
```python
import math

import jax
import jax.numpy as jnp
from jax import lax
from jax.sharding import PartitionSpec as P


def make_tables(length):
    period = 2 * length
    bins_rows = lax.broadcasted_iota(jnp.int32, (length + 1, length), 0)
    time_cols = lax.broadcasted_iota(jnp.int32, (length + 1, length), 1)
    phase_angle = (bins_rows * time_cols % period).astype(jnp.float32) * (2.0 * math.pi / period)
    forward_cos = jnp.cos(phase_angle)
    forward_sin = jnp.sin(phase_angle)
    time_rows = lax.broadcasted_iota(jnp.int32, (period, length + 1), 0)
    bins_cols = lax.broadcasted_iota(jnp.int32, (period, length + 1), 1)
    back_angle = (time_rows * bins_cols % period).astype(jnp.float32) * (2.0 * math.pi / period)
    edge_bins = (bins_cols == 0) | (bins_cols == length)
    inv_weight = jnp.where(edge_bins, 1.0, 2.0).astype(jnp.float32) / period
    inverse_cos = inv_weight * jnp.cos(back_angle)
    inverse_sin = -inv_weight * jnp.sin(back_angle)
    return (forward_cos, forward_sin, inverse_cos, inverse_sin)


def transform(blocks, tables):
    flat = blocks.astype(jnp.float32)
    real_part = jnp.einsum("ft,ntc->nfc", tables[0], flat, precision=lax.Precision.HIGH)
    imag_part = -jnp.einsum("ft,ntc->nfc", tables[1], flat, precision=lax.Precision.HIGH)
    return (real_part, imag_part)


def back_transform(sums, tables, tok_rows):

    def apply(table, values):
        return jnp.dot(
            table, values, precision=lax.Precision.HIGH, preferred_element_type=jnp.float32
        )

    head = apply(tables[2][:tok_rows], sums[0]) + apply(tables[3][:tok_rows], sums[1])
    tail = apply(tables[2][tok_rows:], sums[2]) + apply(tables[3][tok_rows:], sums[3])
    return head + tail


def correlate(span_grads, span_filters, own_block, chan_count, tables):
    n_blocks = span_filters.shape[0]
    tok_rows = span_filters.shape[1]
    zeros = jnp.zeros((tok_rows + 1, chan_count), jnp.float32)
    first_block = lax.dynamic_slice(span_grads, (own_block, 0, 0), (1, tok_rows, chan_count))
    first_re, first_im = transform(first_block, tables)

    def lag_turn(lag_group, state):
        totals, carried = state
        fresh = lax.dynamic_slice(
            span_grads, (own_block + 8 * lag_group + 1, 0, 0), (8, tok_rows, chan_count)
        )
        filt_part = lax.dynamic_slice(
            span_filters, (8 * lag_group, 0, 0), (8, tok_rows, chan_count)
        )
        fresh_re, fresh_im = transform(fresh, tables)
        filt_re, filt_im = transform(filt_part, tables)
        grad_re = jnp.concatenate([carried[0], fresh_re], 0)
        grad_im = jnp.concatenate([carried[1], fresh_im], 0)
        head_re, head_im = (grad_re[:8], grad_im[:8])
        tail_re, tail_im = (grad_re[1:], grad_im[1:])
        new_totals = (
            totals[0] + jnp.sum(filt_re * head_re + filt_im * head_im, 0),
            totals[1] + jnp.sum(filt_re * head_im - filt_im * head_re, 0),
            totals[2] + jnp.sum(filt_re * tail_re + filt_im * tail_im, 0),
            totals[3] + jnp.sum(filt_re * tail_im - filt_im * tail_re, 0),
        )
        return (new_totals, (fresh_re[7:8], fresh_im[7:8]))

    turns = (n_blocks - own_block + 7) // 8
    sums, leftover = lax.fori_loop(
        0, turns, lag_turn, ((zeros, zeros, zeros, zeros), (first_re, first_im))
    )
    return back_transform(sums, tables, tok_rows)


def shards(queries, key_proj, value_proj, conv_out, filters, out_grad, out_weight):
    tok_rows, chan = queries.shape
    groups = lax.axis_size("seq")
    position = lax.axis_index("seq")
    tables = make_tables(tok_rows)
    wide = lax.all_gather(out_grad, "ch", axis=1, tiled=True)
    columns = wide
    grad_gate = jnp.dot(
        columns,
        lax.all_gather(out_weight, "seq", axis=0, tiled=True),
        preferred_element_type=jnp.float32,
    )
    gated = (queries.astype(jnp.float32) * conv_out.astype(jnp.float32)).astype(jnp.bfloat16)
    columns = wide
    weight_grad = lax.psum_scatter(
        lax.dot_general(
            columns, gated, (((0,), (0,)), ((), ())), preferred_element_type=jnp.float32
        ),
        "seq",
        scatter_dimension=0,
        tiled=True,
    ) * (tok_rows * groups) ** (-0.5)
    query_grad = (grad_gate * conv_out.astype(jnp.float32)).astype(jnp.bfloat16)
    conv_grad = (grad_gate * queries.astype(jnp.float32)).astype(jnp.bfloat16)
    grads_all, filters_all = (
        lax.all_gather(conv_grad, "seq", axis=0, tiled=True),
        lax.all_gather(filters, "seq", axis=0, tiled=True),
    )
    span_grads = jnp.concatenate(
        [grads_all.reshape(groups, tok_rows, chan), jnp.zeros((8, tok_rows, chan), jnp.bfloat16)], 0
    )
    span_filters = filters_all.reshape(groups, tok_rows, chan)
    inner = correlate(span_grads, span_filters, position, chan, tables)
    key_grad = (inner * value_proj.astype(jnp.float32)).astype(jnp.bfloat16)
    value_grad = (inner * key_proj.astype(jnp.float32)).astype(jnp.bfloat16)
    return (query_grad, key_grad, value_grad, weight_grad)


def solution(mesh):
    placed = (
        P("seq", "ch"),
        P("seq", "ch"),
        P("seq", "ch"),
        P("seq", "ch"),
        P("seq", "ch"),
        P("seq", "ch"),
        P("seq", "ch"),
    )
    return jax.shard_map(
        shards,
        mesh=mesh,
        in_specs=placed,
        out_specs=(P("seq", "ch"), P("seq", "ch"), P("seq", "ch"), P("seq", "ch")),
        check_vma=False,
    )
```

profile of v0, /device:TPU:1, one launch (start us, length us, event | category | flops | bytes accessed | tf_op | source)
XLA Modules:
  0.0 525.9 jit_solution(6694998513462512032)
XLA Ops:
  7.9 12.8 %all_gather.12 = bf16[128,2048]{1,0:T(8,128)(2,1)S(1)} all-gather(bf16[128,512]{1,0:T(8,128)(2,1)} %param.14), channel_id=1, replica_groups=mesh['seq'=64,'ch'=4] {'ch'}, dimensions={1}, use_global_device_ids=true | all-gather | bytes 655360 | tf_op jit(solution)/shard_map/all_gather | solution.py:86
  20.8 3.7 convolution_bitcast_fusion.1
  24.4 5.4 %copy.13 = f32[2048,512]{1,0:T(8,128)} copy(f32[2048,512]{0,1:T(8,128)} %convolution_bitcast_fusion.1) | data formatting | bytes 8388608
  29.9 62.3 %all-gather.4.cloned.1.call-done = bf16[2048,512]{1,0:T(8,128)(2,1)} async-done(((bf16[32,512]{1,0:T(8,128)(2,1)}), bf16[2048,512]{1,0:T(8,128)(2,1)}) %all-gather.4.cloned.1.call-update) | async-done | bytes 2097168 | tf_op jit(solution)/shard_map/all_gather | solution.py:90
  92.2 2.8 fusion.53
  99.0 133.5 %reduce-scatter.4.cloned.1.call-done = f32[32,512]{1,0:T(8,128)} async-done(((f32[2048,512]{1,0:T(8,128)}), f32[32,512]{1,0:T(8,128)}) %reduce-scatter.4.cloned.1.call-update) | async-done | bytes 65552
  234.2 88.9 %all-gather.6.cloned.1.call-done = bf16[8192,512]{1,0:T(8,128)(2,1)} async-done(((bf16[128,512]{1,0:T(8,128)(2,1)}), bf16[8192,512]{1,0:T(8,128)(2,1)}) %all-gather.6.cloned.1.call-update) | async-done | bytes 8388624 | tf_op jit(solution)/shard_map/all_gather | solution.py:106
  323.1 8.5 %concatenate.15 = bf16[72,128,512]{2,1,0:T(8,128)(2,1)} pad(bf16[64,128,512]{2,1,0:T(8,128)(2,1)} %bitcast.94, bf16[]{:T(256)} %constant.92.clone.1), padding=0_8x0_0x0_0 | pad | bytes 17825794 | tf_op jit(solution)/shard_map/concatenate | solution.py:109
  335.8 70.6 %all-gather.8.cloned.1.call-done = bf16[8192,512]{1,0:T(8,128)(2,1)} async-done(((bf16[128,512]{1,0:T(8,128)(2,1)}), bf16[8192,512]{1,0:T(8,128)(2,1)}) %all-gather.8.cloned.1.call-update) | async-done | bytes 8388624 | tf_op jit(solution)/shard_map/all_gather | solution.py:107
  406.5 108.2 %while.24 = (s32[]{:T(128)}, f32[129,512]{1,0:T(8,128)S(1)}, f32[129,512]{1,0:T(8,128)S(1)}, f32[129,512]{1,0:T(8,128)S(1)}, f32[129,512]{1,0:T(8,128)S(1)}, /*i...) while((s32[]{:T(128)}, f32[129,512]{1,0:T(8,128)S(1)}, ...), condition=%wide.region_5.6_spmd.clone.clone, body=%wide.region_0.0_spmd.clone.clone.sunk | while | flops 1635216384 | bytes 31142220 | solution.py:75
  408.9 2.3 fusion.114
  411.2 2.3 fusion.115
  414.6 3.6 fusion.116
  422.4 2.3 fusion.114
  424.8 2.3 fusion.115
  428.1 3.6 fusion.116
  435.9 2.3 fusion.114
  438.3 2.3 fusion.115
  441.7 3.6 fusion.116
  449.5 2.3 fusion.114
  451.8 2.3 fusion.115
  455.2 3.6 fusion.116
  463.0 2.3 fusion.114
  468.7 3.6 fusion.116
  476.5 2.3 fusion.114
  478.9 2.3 fusion.115
  482.2 3.6 fusion.116
  490.0 2.3 fusion.114
  495.8 3.6 fusion.116
  503.6 2.3 fusion.114
  505.9 2.3 fusion.115
  509.3 3.6 fusion.116
  (133 shorter events, 60.9 us)
Async XLA Ops:
  7.2 85.1 %all-gather.4.cloned.1.call-start = ((), (), s32[]{:S(2)}) async-start(), calls=%async_computation.1 | async-start | bytes 2129920 | tf_op jit(solution)/shard_map/all_gather | solution.py:90
  7.9 224.6 %reduce-scatter.4.cloned.1.call-start = ((), (), s32[]{:S(2)}) async-start(), calls=%async_computation.4 | async-start | bytes 4259840
  29.8 62.4 %copy-start.1 = (bf16[128,512]{1,0:T(8,128)(2,1)S(1)}, bf16[128,512]{1,0:T(8,128)(2,1)}, u32[]{:S(2)}) copy-start(bf16[128,512]{1,0:T(8,128)(2,1)} %param.9) | copy-start | bytes 393220
  29.8 62.4 %copy-start.2 = (bf16[128,512]{1,0:T(8,128)(2,1)S(1)}, bf16[128,512]{1,0:T(8,128)(2,1)}, u32[]{:S(2)}) copy-start(bf16[128,512]{1,0:T(8,128)(2,1)} %param.12) | copy-start | bytes 393220
  29.8 293.2 %all-gather.6.cloned.1.call-start = ((), (), s32[]{:S(2)}) async-start(), calls=%async_computation.2 | async-start | bytes 8519680 | tf_op jit(solution)/shard_map/all_gather | solution.py:106
  95.0 311.4 %all-gather.8.cloned.1.call-start = ((), (), s32[]{:S(2)}) async-start(), calls=%async_computation.3 | async-start | bytes 8519680 | tf_op jit(solution)/shard_map/all_gather | solution.py:107
  413.6 1.0 copy-start.3
  413.6 1.0 copy-start.4
  427.1 1.0 copy-start.3
  427.1 1.0 copy-start.4
  440.6 1.0 copy-start.3
  440.6 1.0 copy-start.4
  454.2 1.0 copy-start.3
  454.2 1.0 copy-start.4
  467.7 1.0 copy-start.3
  467.7 1.0 copy-start.4
  481.2 1.0 copy-start.3
  481.2 1.0 copy-start.4
  494.7 1.0 copy-start.3
  494.7 1.0 copy-start.4
  508.2 1.0 copy-start.3
  508.3 1.0 copy-start.4
  514.7 3.6 copy-start
  514.7 3.6 copy-start.5
  514.7 3.6 copy-start.6
Sparse Core Ops, SparseCore 0:
  10.8 81.4 all-gather.3
  96.4 136.0 reduce-scatter.3
  236.2 86.8 all-gather.5
  326.1 80.2 all-gather.7
where the time goes:
time: 528 us; the launch traced here: 526 us
  waiting for transfers between devices  357 us (68%)
  matrix products  100 us (19%)
  local copies, waits for them, and re-layouts  33.5 us (6%)
  between operations  13.9 us (3%)
  blocking collectives  12.8 us (2%)
  other arithmetic  7.96 us (2%)
    unnamed x5, waiting for transfers between devices  135 us
    all_gather x1, waiting for transfers between devices, shards(): lax.all_gather(conv_grad, 'seq', axis=0, tiled=True)  88.9 us
    all_gather x1, waiting for transfers between devices, shards(): lax.all_gather(filters, 'seq', axis=0, tiled=True)  70.6 us
    all_gather x1, waiting for transfers between devices, shards(): lax.all_gather(out_weight, 'seq', axis=0, tiled=True)  62.3 us
    dot_general x17, matrix products, transform(): jnp.einsum('ft,ntc->nfc', tables[0], flat, precision=lax.Precision.HIGH)  49.8 us
    dot_general x17, matrix products, transform(): jnp.einsum('ft,ntc->nfc', tables[1], flat, precision=lax.Precision.HIGH)  39.5 us
    all_gather x1, blocking collectives, shards(): wide = lax.all_gather(out_grad, 'ch', axis=1, tiled=True)  12.8 us
    slice x16, local copies, waits for them, and re-layouts, lag_turn(): return (new_totals, (fresh_re[7:8], fresh_im[7:8]))  11.8 us
  transfers between devices with their start and end apart: 4, of which 4 were waited for; matrix products, arithmetic and copies ran while one was open for 6% of the time, Pallas kernels for 0%

commit v1 on v0

v1 whole, which is shorter than its diff:
```python
import functools

import jax
import jax.numpy as jnp
import numpy as np
from jax import lax
from jax.experimental import pallas as pl
from jax.experimental.pallas import tpu as pltpu
from jax.sharding import PartitionSpec as P

BF16 = jnp.bfloat16
F32 = jnp.float32

CORES = 2


def core_pairs(groups):
    return [(i, i ^ 1) for i in range(groups)]


def same_core_groups(groups):
    return [list(range(core, groups, CORES)) for core in range(CORES)]


def dft_tables(blocks, rows, kept):
    period = 2 * blocks
    length = period * rows
    k1 = np.arange(kept)[:, None]
    used = k1 <= blocks
    angle = 2 * np.pi * ((k1 * np.arange(blocks)[None]) % period) / period
    first = np.concatenate([used * np.cos(angle), used * -np.sin(angle)], 0)
    weight = used * np.where((k1 == 0) | (k1 == blocks), 1.0, 2.0) / length
    last = np.concatenate([(weight * np.cos(angle)).T, -(weight * np.sin(angle)).T], 1)
    turn = 2 * np.pi * (k1 * np.arange(rows)[None]) / length
    twist = np.stack([np.cos(turn), -np.sin(turn)])
    angle = 2 * np.pi * ((np.arange(rows)[:, None] * np.arange(rows)[None]) % rows) / rows
    cos, sin = np.cos(angle), np.sin(angle)
    second = np.block([[cos, -sin], [sin, cos]])
    return first, twist, second, last


def halves(table):
    high = table.astype(BF16)
    low = (table - high.astype(np.float64)).astype(BF16)
    return high, low


def split(value):
    high = value.astype(BF16)
    return high, (value - high.astype(F32)).astype(BF16)


def dot(a, b):
    return jnp.dot(a, b, preferred_element_type=F32)


def dot3(a, b):
    return dot(a[0], b[0]) + (dot(a[0], b[1]) + dot(a[1], b[0]))


def spectrum(x_ref, first_ref, twist_ref, second_ref, plane, blocks, chans, rows, kept):
    plane[...] = x_ref[...].astype(F32)
    data = jnp.concatenate(
        [plane[pl.ds(c, blocks, stride=chans), :] for c in range(chans)], 1
    ).astype(BF16)
    bins = dot(first_ref[0], data) + dot(first_ref[1], data)
    cos, sin = twist_ref[0], twist_ref[1]
    parts = []
    for c in range(chans):
        re = bins[:kept, c * rows : (c + 1) * rows]
        im = bins[kept:, c * rows : (c + 1) * rows]
        parts.append(jnp.concatenate([re * cos - im * sin, re * sin + im * cos], 1))
    return dot3(split(jnp.concatenate(parts, 0)), (second_ref[0], second_ref[1]))


def filter_kernel(sizes, x_ref, first_ref, twist_ref, second_ref, out_ref, plane):
    out_ref[...] = spectrum(x_ref, first_ref, twist_ref, second_ref, plane, *sizes)


def correlate_kernel(
    sizes, x_ref, filt_ref, first_ref, twist_ref, second_ref, back_ref, last_ref, out_ref, plane
):
    blocks, chans, rows, kept = sizes
    grads = spectrum(x_ref, first_ref, twist_ref, second_ref, plane, *sizes)
    g_re, g_im = grads[:, :rows], grads[:, rows:]
    f_re, f_im = filt_ref[:, :rows], filt_ref[:, rows:]
    product = jnp.concatenate([g_re * f_re + g_im * f_im, g_im * f_re - g_re * f_im], 1)
    bins = dot3(split(product), (back_ref[0], back_ref[1]))
    cos, sin = twist_ref[0], twist_ref[1]
    parts = []
    for c in range(chans):
        re = bins[c * kept : (c + 1) * kept, :rows]
        im = bins[c * kept : (c + 1) * kept, rows:]
        parts.append(jnp.concatenate([re * cos + im * sin, im * cos - re * sin], 0))
    inner = dot3((last_ref[0], last_ref[1]), split(jnp.concatenate(parts, 1)))
    for c in range(chans):
        plane[pl.ds(c, blocks, stride=chans), :] = inner[:, c * rows : (c + 1) * rows]
    out_ref[...] = plane[...].astype(BF16)


def whole(count):
    return [pl.BlockSpec(memory_space=pltpu.VMEM)] * count


def shards(queries, key_proj, value_proj, conv_out, filters, out_grad, out_weight):
    rows, chan = queries.shape
    groups = lax.axis_size("seq")
    feats = out_weight.shape[0]
    chips = groups // CORES
    chans = chan // groups
    kept = -(-(groups + 1) // 8) * 8
    sizes = (groups, chans, rows, kept)
    odd = lax.axis_index("seq") % CORES == 1
    to_core = functools.partial(lax.ppermute, axis_name="seq", perm=core_pairs(groups))
    same_core = same_core_groups(groups)

    first, twist, second, last = dft_tables(groups, rows, kept)
    first, last = jnp.stack(halves(first)), jnp.stack(halves(last))
    second, back = jnp.stack(halves(second)), jnp.stack(halves(second.T))
    twist = jnp.asarray(twist, F32)

    def exchange(blocks):
        return lax.all_to_all(blocks.reshape(groups, chans, rows), "seq", 0, 0).reshape(chan, rows)

    copies = jnp.broadcast_to(out_weight[None], (chips, feats, chan))
    weight = lax.all_to_all(copies, "seq", 0, 0, axis_index_groups=same_core).reshape(-1, chan)

    wide = lax.all_gather(out_grad.T, "ch", axis=0).reshape(chips, CORES, feats, rows)
    own = jnp.where(odd, wide[:, 1], wide[:, 0]).reshape(chips * feats, rows)
    other = jnp.where(odd, wide[:, 0], wide[:, 1]).reshape(chips * feats, rows)
    grads = jnp.concatenate([own, to_core(other)], 1)

    filt = pl.pallas_call(
        functools.partial(filter_kernel, sizes),
        out_shape=jax.ShapeDtypeStruct((chans * kept, 2 * rows), F32),
        in_specs=whole(4),
        out_specs=pl.BlockSpec(memory_space=pltpu.VMEM),
        scratch_shapes=[pltpu.VMEM((chan, rows), F32)],
        compiler_params=pltpu.CompilerParams(vmem_limit_bytes=32 << 20),
    )(exchange(filters.T), first, twist, second)

    share = lax.dot_general(grads, weight, (((0,), (0,)), ((), ())), preferred_element_type=F32)
    grad_gate = share[:rows] + to_core(share[rows:])
    query_grad = (grad_gate * conv_out.astype(F32)).astype(BF16)
    conv_grad = (grad_gate * queries.astype(F32)).astype(BF16)

    inner = pl.pallas_call(
        functools.partial(correlate_kernel, sizes),
        out_shape=jax.ShapeDtypeStruct((chan, rows), BF16),
        in_specs=whole(7),
        out_specs=pl.BlockSpec(memory_space=pltpu.VMEM),
        scratch_shapes=[pltpu.VMEM((chan, rows), F32)],
        compiler_params=pltpu.CompilerParams(vmem_limit_bytes=32 << 20),
    )(exchange(conv_grad.T), filt, first, twist, second, back, last)
    inner = exchange(inner).T.astype(F32)
    key_grad = (inner * value_proj.astype(F32)).astype(BF16)
    value_grad = (inner * key_proj.astype(F32)).astype(BF16)

    gated = (queries.astype(F32) * conv_out.astype(F32)).astype(BF16)
    both = jnp.concatenate([gated, to_core(gated)], 0)
    part = dot(grads, both).astype(BF16).reshape(chips, feats, chan)
    parts = lax.all_to_all(part, "seq", 0, 0, axis_index_groups=same_core)
    weight_grad = jnp.sum(parts.astype(F32), 0) * (rows * groups) ** (-0.5)
    return (query_grad, key_grad, value_grad, weight_grad)


def solution(mesh):
    placed = (P("seq", "ch"),) * 7
    return jax.shard_map(
        shards,
        mesh=mesh,
        in_specs=placed,
        out_specs=(P("seq", "ch"),) * 4,
        check_vma=False,
    )
```

time: 528 us -> 128 us (0.24)
  the two profiles are of different devices: /device:TPU:1 before, /device:TPU:8 now
where the time goes in v1:
time: 128 us; the launch traced here: 127 us
  waiting for transfers between devices  68.7 us (54%)
  starting transfers between devices  31.9 us (25%)
  blocking collectives  13.7 us (11%)
  local copies, waits for them, and re-layouts  5.64 us (4%)
  Pallas kernels  2.89 us (2%)
  matrix products  1.87 us (1%)
  other arithmetic  1.64 us (1%)
    all_to_all x3, waiting for transfers between devices, exchange(): lax.all_to_all(blocks.reshape(groups, chans, rows), 'seq', 0, 0)  27.1 us
    all_to_all x1, waiting for transfers between devices, shards(): parts = lax.all_to_all(part, 'seq', 0, 0, axis_index_groups=same_core)  26.9 us
    all_to_all x3, starting transfers between devices, exchange(): lax.all_to_all(blocks.reshape(groups, chans, rows), 'seq', 0, 0)  15.7 us
    all_gather x1, blocking collectives, shards(): lax.all_gather(out_grad.T, 'ch', axis=0).reshape(chips, CORES, feats, rows)  13.7 us
    all_to_all x1, waiting for transfers between devices, shards(): lax.all_to_all(copies, 'seq', 0, 0, axis_index_groups=same_core)  13.1 us
    all_to_all x1, starting transfers between devices, shards(): lax.all_to_all(copies, 'seq', 0, 0, axis_index_groups=same_core)  11.4 us
    all_to_all x1, starting transfers between devices, shards(): parts = lax.all_to_all(part, 'seq', 0, 0, axis_index_groups=same_core)  4.45 us
    unnamed x28, local copies, waits for them, and re-layouts  2.99 us
  transfers between devices with their start and end apart: 8, of which 6 were waited for; matrix products, arithmetic and copies ran while one was open for 4% of the time, Pallas kernels for 2%

profile of v1, /device:TPU:8, one launch (start us, length us, event | category | flops | bytes accessed | tf_op | source)
XLA Modules:
  0.0 127.2 jit_solution(8606288392893056239)
XLA Ops:
  0.6 1.9 %broadcast_in_dim.2 = bf16[32,32,512]{2,1,0:T(8,128)(2,1)} broadcast(bf16[32,512]{1,0:T(8,128)(2,1)} %param.22), dimensions={1,2} | broadcast | bytes 1081344 | tf_op jit(solution)/shard_map/broadcast_in_dim | solution.py:125
  2.5 11.4 %all-to-all-start = ((bf16[32,32,512]{2,1,0:T(8,128)(2,1)}), bf16[32,32,512]{2,1,0:T(8,128)(2,1)S(1)}, u32[]{:S(2)}, u32[]{:S(2)}) async-start(bf16[32,32,512]{2,1,0:T(8,128)(2,1)} %broadcast_in_dim.2), calls=%async_computation | async-start | bytes 2097152 | tf_op jit(solution)/shard_map/all_to_all | solution.py:126
  14.0 0.1 copy.23
  14.1 13.7 %all-gather = bf16[2048,128]{1,0:T(8,128)(2,1)S(1)} all-gather(bf16[512,128]{1,0:T(8,128)(2,1)S(1)} %bitcast.34), channel_id=2, replica_groups=mesh['seq'=64,'ch'=4] {'ch'}, dimensions={0}, use_global_device_ids=true | all-gather | bytes 655360 | tf_op jit(solution)/shard_map/all_gather | solution.py:128
  27.8 0.1 collective-permute-start
  27.9 1.5 %collective-permute-done = bf16[1024,128]{1,0:T(8,128)(2,1)S(1)} collective-permute-done((bf16[1024,128]{1,0:T(8,128)(2,1)S(1)}, bf16[1024,128]{1,0:T(8,128)(2,1)S(1)}, u32[]{:S(2)}, u32[]{:S(2)}) %collective-permute-start) | collective-permute-done | bytes 262176 | tf_op jit(solution)/shard_map/ppermute | solution.py:131
  29.5 13.1 %all-to-all-done = bf16[32,32,512]{2,1,0:T(8,128)(2,1)S(1)} async-done(((bf16[32,32,512]{2,1,0:T(8,128)(2,1)}), bf16[32,32,512]{2,1,0:T(8,128)(2,1)S(1)}, u32[]{:S(2)}, u32[]{:S(2)}) %all-to-all-start) | async-done | bytes 1048608 | tf_op jit(solution)/shard_map/all_to_all | solution.py:126
  42.6 0.4 fusion
  43.1 0.1 collective-permute-start.1
  43.2 0.3 copy-done.8
  43.5 0.8 copy.25
  44.3 5.8 %all-to-all-start.2 = ((bf16[64,8,128]{2,1,0:T(8,128)(2,1)}), bf16[64,8,128]{2,1,0:T(8,128)(2,1)S(1)}, u32[]{:S(2)}, u32[]{:S(2)}) async-start(bf16[64,8,128]{2,1,0:T(8,128)(2,1)} %bitcast.9), calls=%async_computation.2 | async-start | bytes 262144 | tf_op jit(solution)/shard_map/all_to_all | solution.py:123
  50.1 0.7 fusion.11
  50.9 0.8 copy.24
  51.6 8.8 %all-to-all-done.2 = bf16[64,8,128]{2,1,0:T(8,128)(2,1)S(1)} async-done(((bf16[64,8,128]{2,1,0:T(8,128)(2,1)}), bf16[64,8,128]{2,1,0:T(8,128)(2,1)S(1)}, u32[]{:S(2)}, u32[]{:S(2)}) %all-to-all-start.2) | async-done | bytes 131104 | tf_op jit(solution)/shard_map/all_to_all | solution.py:123
  60.4 4.9 %all-to-all-start.1 = ((bf16[64,8,128]{2,1,0:T(8,128)(2,1)}), bf16[64,8,128]{2,1,0:T(8,128)(2,1)S(1)}, u32[]{:S(2)}, u32[]{:S(2)}) async-start(bf16[64,8,128]{2,1,0:T(8,128)(2,1)} %bitcast.6), calls=%async_computation.1 | async-start | bytes 262144 | tf_op jit(solution)/shard_map/all_to_all | solution.py:123
  65.3 0.1 collective-permute-start.2
  65.5 0.7 shard_map.183.filt_ref
  66.2 9.5 %all-to-all-done.1 = bf16[64,8,128]{2,1,0:T(8,128)(2,1)S(1)} async-done(((bf16[64,8,128]{2,1,0:T(8,128)(2,1)}), bf16[64,8,128]{2,1,0:T(8,128)(2,1)S(1)}, u32[]{:S(2)}, u32[]{:S(2)}) %all-to-all-start.1) | async-done | bytes 131104 | tf_op jit(solution)/shard_map/all_to_all | solution.py:123
  75.7 2.2 %shard_map.184 = bf16[512,128]{1,0:T(8,128)(2,1)} custom-call(bf16[512,128]{1,0:T(8,128)(2,1)S(1)} %bitcast.31, f32[576,256]{1,0:T(8,128)S(1)} %shard_map.183.filt_ref, bf16[2,144,64]{2,1,0:T(8,128)(2,1)S(1)} %copy-done.1, f32[2,72,128]{2,1,0:T(8,128)S(1)} %copy-done.2, bf16[2,256,256]{2,1,0:T(8,128)(2,1)S(1)} %copy-done, ...), custom_call_target="tpu_custom_call" | custom-call | tf_op jit(solution)/shard_map/pallas_call | solution.py:147
  77.9 4.9 %all-to-all-start.3 = ((bf16[64,8,128]{2,1,0:T(8,128)(2,1)}), bf16[64,8,128]{2,1,0:T(8,128)(2,1)S(1)}, u32[]{:S(2)}, u32[]{:S(2)}) async-start(bf16[64,8,128]{2,1,0:T(8,128)(2,1)} %bitcast.11), calls=%async_computation.3 | async-start | bytes 262144 | tf_op jit(solution)/shard_map/all_to_all | solution.py:123
  82.8 1.4 %convolution_convert_fusion = bf16[1024,512]{1,0:T(8,128)(2,1)} fusion(bf16[1024,128]{1,0:T(8,128)(2,1)S(1)} %collective-permute-done, bf16[1024,128]{1,0:T(8,128)(2,1)S(1)} %bitcast.36, bf16[128,512]{1,0:T(8,128)(2,1)S(1)} %collective-permute-done.2, bf16[128,512]{1,0:T(8,128)(2,1)S(1)} %get-tuple-element.12), kind=kOutput, calls=%fused_computation.1 | convolution fusion | flops 270532608 | bytes 1835008 | tf_op jit(solution)/shard_map/dot_general | solution.py:54
  84.3 8.9 %all-to-all-done.3 = bf16[64,8,128]{2,1,0:T(8,128)(2,1)S(1)} async-done(((bf16[64,8,128]{2,1,0:T(8,128)(2,1)}), bf16[64,8,128]{2,1,0:T(8,128)(2,1)S(1)}, u32[]{:S(2)}, u32[]{:S(2)}) %all-to-all-start.3) | async-done | bytes 131104 | tf_op jit(solution)/shard_map/all_to_all | solution.py:123
  93.1 4.5 %all-to-all-start.4 = ((bf16[32,32,512]{2,1,0:T(8,128)(2,1)}), bf16[32,32,512]{2,1,0:T(8,128)(2,1)S(1)}, u32[]{:S(2)}, u32[]{:S(2)}) async-start(bf16[32,32,512]{2,1,0:T(8,128)(2,1)} %bitcast.15), calls=%async_computation.4 | async-start | bytes 2097152 | tf_op jit(solution)/shard_map/all_to_all | solution.py:162
  97.6 0.1 copy.27
  97.7 0.1 copy.26
  97.9 0.1 fusion.10
  97.9 0.8 copy.28
  98.7 0.8 copy.29
  99.5 26.9 %all-to-all-done.4 = bf16[32,32,512]{2,1,0:T(8,128)(2,1)S(1)} async-done(((bf16[32,32,512]{2,1,0:T(8,128)(2,1)}), bf16[32,32,512]{2,1,0:T(8,128)(2,1)S(1)}, u32[]{:S(2)}, u32[]{:S(2)}) %all-to-all-start.4) | async-done | bytes 1048608 | tf_op jit(solution)/shard_map/all_to_all | solution.py:162
  126.4 0.2 convert_reduce_fusion
  126.5 0.6 broadcast_multiply_fusion
  (25 shorter events, 0.1 us)
Async XLA Ops:
  2.5 11.5 %copy-start.7 = (bf16[128,512]{1,0:T(8,128)(2,1)S(1)}, bf16[128,512]{1,0:T(8,128)(2,1)}, u32[]{:S(2)}) copy-start(bf16[128,512]{1,0:T(8,128)(2,1)} %param.21) | copy-start | bytes 393220
  2.5 40.1 %all-to-all-start = ((bf16[32,32,512]{2,1,0:T(8,128)(2,1)}), bf16[32,32,512]{2,1,0:T(8,128)(2,1)S(1)}, u32[]{:S(2)}, u32[]{:S(2)}) async-start(bf16[32,32,512]{2,1,0:T(8,128)(2,1)} %broadcast_in_dim.2), calls=%async_computation | async-start | bytes 2097152 | tf_op jit(solution)/shard_map/all_to_all | solution.py:126
  27.8 1.6 %collective-permute-start = (bf16[1024,128]{1,0:T(8,128)(2,1)S(1)}, bf16[1024,128]{1,0:T(8,128)(2,1)S(1)}, u32[]{:S(2)}, u32[]{:S(2)}) collective-permute-start(bf16[1024,128]{1,0:T(8,128)(2,1)S(1)} %bitcast.37), channel_id=1, source_target_pairs={{0,4},{4,0},{8,12},{12,8},{16,20},{20,16},{24,28},{28,24},{32,36},... | collective-permute-start | bytes 786440 | tf_op jit(solution)/shard_map/ppermute | solution.py:131
  42.6 0.9 copy-start.8
  43.1 7.1 %copy-start.5 = (bf16[128,512]{1,0:T(8,128)(2,1)S(1)}, bf16[128,512]{1,0:T(8,128)(2,1)}, u32[]{:S(2)}) copy-start(bf16[128,512]{1,0:T(8,128)(2,1)} %param.16) | copy-start | bytes 393220
  43.1 7.1 %copy-start.6 = (bf16[128,512]{1,0:T(8,128)(2,1)S(1)}, bf16[128,512]{1,0:T(8,128)(2,1)}, u32[]{:S(2)}) copy-start(bf16[128,512]{1,0:T(8,128)(2,1)} %param.19) | copy-start | bytes 393220
  43.1 7.0 %collective-permute-start.1 = (f32[128,512]{1,0:T(8,128)S(1)}, f32[128,512]{1,0:T(8,128)S(1)}, u32[]{:S(2)}, u32[]{:S(2)}) collective-permute-start(f32[128,512]{1,0:T(8,128)S(1)} %slice.21), channel_id=1, source_target_pairs={{0,4},{4,0},{8,12},{12,8},{16,20},{20,16},{24,28},{28,24},{32,36},... | collective-permute-start | bytes 786440 | tf_op jit(solution)/shard_map/ppermute | solution.py:143
  44.3 21.2 %copy-start = (bf16[2,256,256]{2,1,0:T(8,128)(2,1)S(1)}, bf16[2,256,256]{2,1,0:T(8,128)(2,1)}, u32[]{:S(2)}) copy-start(bf16[2,256,256]{2,1,0:T(8,128)(2,1)} %constant.57.second_ref) | copy-start | bytes 786436
  44.3 21.2 %copy-start.1 = (bf16[2,144,64]{2,1,0:T(8,128)(2,1)S(1)}, bf16[2,144,64]{2,1,0:T(8,128)(2,1)}, u32[]{:S(2)}) copy-start(bf16[2,144,64]{2,1,0:T(8,128)(2,1)} %constant.54.first_ref) | copy-start | bytes 110596
  44.3 21.2 %copy-start.2 = (f32[2,72,128]{2,1,0:T(8,128)S(1)}, f32[2,72,128]{2,1,0:T(8,128)}, u32[]{:S(2)}) copy-start(f32[2,72,128]{2,1,0:T(8,128)} %constant.50.clone.twist_ref) | copy-start | bytes 221188
  44.3 16.1 %all-to-all-start.2 = ((bf16[64,8,128]{2,1,0:T(8,128)(2,1)}), bf16[64,8,128]{2,1,0:T(8,128)(2,1)S(1)}, u32[]{:S(2)}, u32[]{:S(2)}) async-start(bf16[64,8,128]{2,1,0:T(8,128)(2,1)} %bitcast.9), calls=%async_computation.2 | async-start | bytes 262144 | tf_op jit(solution)/shard_map/all_to_all | solution.py:123
  50.9 24.8 %copy-start.3 = (bf16[2,256,256]{2,1,0:T(8,128)(2,1)S(1)}, bf16[2,256,256]{2,1,0:T(8,128)(2,1)}, u32[]{:S(2)}) copy-start(bf16[2,256,256]{2,1,0:T(8,128)(2,1)} %constant.60.back_ref) | copy-start | bytes 786436
  50.9 24.8 %copy-start.4 = (bf16[2,64,144]{2,1,0:T(8,128)(2,1)S(1)}, bf16[2,64,144]{2,1,0:T(8,128)(2,1)}, u32[]{:S(2)}) copy-start(bf16[2,64,144]{2,1,0:T(8,128)(2,1)} %constant.63.last_ref) | copy-start | bytes 110596
  60.4 15.2 %all-to-all-start.1 = ((bf16[64,8,128]{2,1,0:T(8,128)(2,1)}), bf16[64,8,128]{2,1,0:T(8,128)(2,1)S(1)}, u32[]{:S(2)}, u32[]{:S(2)}) async-start(bf16[64,8,128]{2,1,0:T(8,128)(2,1)} %bitcast.6), calls=%async_computation.1 | async-start | bytes 262144 | tf_op jit(solution)/shard_map/all_to_all | solution.py:123
  65.3 17.5 %collective-permute-start.2 = (bf16[128,512]{1,0:T(8,128)(2,1)S(1)}, bf16[128,512]{1,0:T(8,128)(2,1)S(1)}, u32[]{:S(2)}, u32[]{:S(2)}) collective-permute-start(bf16[128,512]{1,0:T(8,128)(2,1)S(1)} %get-tuple-element.12), channel_id=1, source_target_pairs={{0,4},{4,0},{8,12},{12,8},{16,20},{20,16},{24,28},{28,24},{32,36},... | collective-permute-start | bytes 393224 | tf_op jit(solution)/shard_map/ppermute | solution.py:160
  77.9 15.2 %all-to-all-start.3 = ((bf16[64,8,128]{2,1,0:T(8,128)(2,1)}), bf16[64,8,128]{2,1,0:T(8,128)(2,1)S(1)}, u32[]{:S(2)}, u32[]{:S(2)}) async-start(bf16[64,8,128]{2,1,0:T(8,128)(2,1)} %bitcast.11), calls=%async_computation.3 | async-start | bytes 262144 | tf_op jit(solution)/shard_map/all_to_all | solution.py:123
  93.1 4.5 %copy-start.9 = (bf16[128,512]{1,0:T(8,128)(2,1)S(1)}, bf16[128,512]{1,0:T(8,128)(2,1)}, u32[]{:S(2)}) copy-start(bf16[128,512]{1,0:T(8,128)(2,1)} %param.17) | copy-start | bytes 393220
  93.1 4.6 %copy-start.10 = (bf16[128,512]{1,0:T(8,128)(2,1)S(1)}, bf16[128,512]{1,0:T(8,128)(2,1)}, u32[]{:S(2)}) copy-start(bf16[128,512]{1,0:T(8,128)(2,1)} %param.18) | copy-start | bytes 393220
  93.1 33.2 %all-to-all-start.4 = ((bf16[32,32,512]{2,1,0:T(8,128)(2,1)}), bf16[32,32,512]{2,1,0:T(8,128)(2,1)S(1)}, u32[]{:S(2)}, u32[]{:S(2)}) async-start(bf16[32,32,512]{2,1,0:T(8,128)(2,1)} %bitcast.15), calls=%async_computation.4 | async-start | bytes 2097152 | tf_op jit(solution)/shard_map/all_to_all | solution.py:162

commit v2 on v1

--- a/solution.py
+++ b/solution.py
@@ -12,14 +12,11 @@
 F32 = jnp.float32
 
 CORES = 2
+ALONG_X = 4
 
 
 def core_pairs(groups):
     return [(i, i ^ 1) for i in range(groups)]
-
-
-def same_core_groups(groups):
-    return [list(range(core, groups, CORES)) for core in range(CORES)]
 
 
 def dft_tables(blocks, rows, kept):
@@ -98,6 +95,15 @@
     out_ref[...] = plane[...].astype(BF16)
 
 
+def gate_kernel(left_ref, arrived_ref, mine_ref, theirs_ref):
+    sources, feats = arrived_ref.shape[0], left_ref.shape[1] // arrived_ref.shape[0]
+    weight = arrived_ref[:, :feats, :].reshape(sources * feats, arrived_ref.shape[2])
+    share = dot(left_ref[...], weight)
+    rows = mine_ref.shape[0]
+    mine_ref[...] = share[:rows]
+    theirs_ref[...] = share[rows:]
+
+
 def whole(count):
     return [pl.BlockSpec(memory_space=pltpu.VMEM)] * count
 
@@ -107,12 +113,12 @@
     groups = lax.axis_size("seq")
     feats = out_weight.shape[0]
     chips = groups // CORES
+    half = chan // CORES
     chans = chan // groups
     kept = -(-(groups + 1) // 8) * 8
     sizes = (groups, chans, rows, kept)
     odd = lax.axis_index("seq") % CORES == 1
     to_core = functools.partial(lax.ppermute, axis_name="seq", perm=core_pairs(groups))
-    same_core = same_core_groups(groups)
 
     first, twist, second, last = dft_tables(groups, rows, kept)
     first, last = jnp.stack(halves(first)), jnp.stack(halves(last))
@@ -122,13 +128,20 @@
     def exchange(blocks):
         return lax.all_to_all(blocks.reshape(groups, chans, rows), "seq", 0, 0).reshape(chan, rows)
 
-    copies = jnp.broadcast_to(out_weight[None], (chips, feats, chan))
-    weight = lax.all_to_all(copies, "seq", 0, 0, axis_index_groups=same_core).reshape(-1, chan)
-
-    wide = lax.all_gather(out_grad.T, "ch", axis=0).reshape(chips, CORES, feats, rows)
-    own = jnp.where(odd, wide[:, 1], wide[:, 0]).reshape(chips * feats, rows)
-    other = jnp.where(odd, wide[:, 0], wide[:, 1]).reshape(chips * feats, rows)
-    grads = jnp.concatenate([own, to_core(other)], 1)
+    def other_half(value):
+        return jnp.where(odd, value[:, :half], value[:, half:])
+
+    def own_half(value):
+        return jnp.where(odd, value[:, half:], value[:, :half])
+
+    copies = jnp.broadcast_to(
+        out_weight.reshape(feats, CORES, half).transpose(1, 0, 2)[None], (chips, CORES, feats, half)
+    ).reshape(groups, feats, half)
+    sent = jnp.pad(filters.T.reshape(groups, chans, rows), ((0, 0), (0, 0), (0, half - rows)))
+    arrived = lax.all_to_all(jnp.concatenate([copies, sent], 1), "seq", 0, 0)
+
+    wide = lax.all_gather(out_grad.T, "ch", axis=0, tiled=True)
+    grads = jnp.concatenate([wide, to_core(wide)], 1)
 
     filt = pl.pallas_call(
         functools.partial(filter_kernel, sizes),
@@ -137,10 +150,19 @@
         out_specs=pl.BlockSpec(memory_space=pltpu.VMEM),
         scratch_shapes=[pltpu.VMEM((chan, rows), F32)],
         compiler_params=pltpu.CompilerParams(vmem_limit_bytes=32 << 20),
-    )(exchange(filters.T), first, twist, second)
-
-    share = lax.dot_general(grads, weight, (((0,), (0,)), ((), ())), preferred_element_type=F32)
-    grad_gate = share[:rows] + to_core(share[rows:])
+    )(arrived[:, feats:, :rows].reshape(chan, rows), first, twist, second)
+
+    mine, theirs = pl.pallas_call(
+        gate_kernel,
+        out_shape=[jax.ShapeDtypeStruct((rows, half), F32)] * 2,
+        in_specs=whole(2),
+        out_specs=whole(2),
+        compiler_params=pltpu.CompilerParams(vmem_limit_bytes=32 << 20),
+    )(grads.T, arrived)
+    theirs = to_core(theirs)
+    grad_gate = jnp.concatenate(
+        [jnp.where(odd, theirs, mine), jnp.where(odd, mine, theirs)], 1
+    )
     query_grad = (grad_gate * conv_out.astype(F32)).astype(BF16)
     conv_grad = (grad_gate * queries.astype(F32)).astype(BF16)
 
@@ -157,10 +179,31 @@
     value_grad = (inner * key_proj.astype(F32)).astype(BF16)
 
     gated = (queries.astype(F32) * conv_out.astype(F32)).astype(BF16)
-    both = jnp.concatenate([gated, to_core(gated)], 0)
-    part = dot(grads, both).astype(BF16).reshape(chips, feats, chan)
-    parts = lax.all_to_all(part, "seq", 0, 0, axis_index_groups=same_core)
-    weight_grad = jnp.sum(parts.astype(F32), 0) * (rows * groups) ** (-0.5)
+    both = jnp.concatenate([own_half(gated), to_core(other_half(gated))], 0)
+    along_z = chips // ALONG_X
+    by_z = grads.reshape(ALONG_X, along_z, CORES * feats, CORES * rows).swapaxes(0, 1)
+    part = dot(by_z.reshape(groups * feats, CORES * rows), both)
+    z_lines = [
+        [(x * along_z + z) * CORES + core for z in range(along_z)]
+        for x in range(ALONG_X)
+        for core in range(CORES)
+    ]
+    part = lax.psum_scatter(
+        part, "seq", scatter_dimension=0, tiled=True, axis_index_groups=z_lines
+    ).reshape(ALONG_X, CORES * feats, half)
+    x_place = lax.axis_index("seq") // (along_z * CORES)
+    total = lax.dynamic_index_in_dim(part, x_place, 0, keepdims=False)
+    step = along_z * CORES
+    for hop in range(1, ALONG_X):
+        block = lax.dynamic_index_in_dim(part, (x_place + hop) % ALONG_X, 0, keepdims=False)
+        total += lax.ppermute(
+            block, "seq", [(i, (i + hop * step) % groups) for i in range(groups)]
+        )
+    total = total.reshape(CORES, feats, half)
+    own = jnp.where(odd, total[1], total[0])
+    beside = to_core(jnp.where(odd, total[0], total[1]))
+    weight_grad = jnp.concatenate([jnp.where(odd, beside, own), jnp.where(odd, own, beside)], 1)
+    weight_grad = weight_grad * (rows * groups) ** (-0.5)
     return (query_grad, key_grad, value_grad, weight_grad)
 
 

time: 128 us -> 143 us (1.12)
  the two profiles are of different devices: /device:TPU:8 before, /device:TPU:1 now
where the time goes in v2:
time: 143 us; the launch traced here: 142 us
  waiting for transfers between devices  60.3 us (42%)
  starting transfers between devices  39 us (27%)
  between operations  14.4 us (10%)
  blocking collectives  11.6 us (8%)
  local copies, waits for them, and re-layouts  6.89 us (5%)
  other arithmetic  4.19 us (3%)
  Pallas kernels  3.33 us (2%)
  matrix products  2.62 us (2%)
    reduce_scatter x1, waiting for transfers between devices, shards(): lax.psum_scatter(part, 'seq', scatter_dimension=0, tiled=True, axis_index...  28.9 us
    all_to_all x2, starting transfers between devices, exchange(): lax.all_to_all(blocks.reshape(groups, chans, rows), 'seq', 0, 0)  18.8 us
    all_to_all x1, waiting for transfers between devices, shards(): arrived = lax.all_to_all(jnp.concatenate([copies, sent], 1), 'seq', 0, 0)  18.8 us
    all_to_all x1, starting transfers between devices, shards(): arrived = lax.all_to_all(jnp.concatenate([copies, sent], 1), 'seq', 0, 0)  13.1 us
    all_gather x1, blocking collectives, shards(): wide = lax.all_gather(out_grad.T, 'ch', axis=0, tiled=True)  11.6 us
    all_to_all x2, waiting for transfers between devices, exchange(): lax.all_to_all(blocks.reshape(groups, chans, rows), 'seq', 0, 0)  8.91 us
    ppermute x3, starting transfers between devices, shards(): lax.ppermute(block, 'seq', [(i, (i + hop * step) % groups) for i in range...  4.16 us
  transfers between devices with their start and end apart: 11, of which 6 were waited for; matrix products, arithmetic and copies ran while one was open for 4% of the time, Pallas kernels for 2%

profile of v2, /device:TPU:1, one launch (start us, length us, event | category | flops | bytes accessed | tf_op | source)
XLA Modules:
  0.0 142.4 jit_solution(9020862567046755368)
XLA Ops:
  7.2 1.0 copy.25
  8.2 0.8 reshape.47
  9.1 1.2 fusion.1
  10.3 13.1 %all-to-all-start = ((bf16[64,40,256]{2,1,0:T(8,128)(2,1)}), bf16[64,40,256]{2,1,0:T(8,128)(2,1)S(1)}, u32[]{:S(2)}, u32[]{:S(2)}) async-start(bf16[64,40,256]{2,1,0:T(8,128)(2,1)} %fusion.1), calls=%async_computation | async-start | bytes 2621440 | tf_op jit(solution)/shard_map/all_to_all | solution.py:141
  23.5 11.6 %all_gather.3 = bf16[2048,128]{0,1:T(8,128)(2,1)S(1)} all-gather(bf16[512,128]{0,1:T(8,128)(2,1)S(1)} %bitcast.53), channel_id=1, replica_groups=mesh['seq'=64,'ch'=4] {'ch'}, dimensions={0}, use_global_device_ids=true | all-gather | bytes 655360 | tf_op jit(solution)/shard_map/all_gather | solution.py:143
  35.1 2.2 %collective-permute-start = (bf16[2048,128]{0,1:T(8,128)(2,1)S(1)}, bf16[2048,128]{0,1:T(8,128)(2,1)S(1)}, u32[]{:S(2)}, u32[]{:S(2)}) collective-permute-start(bf16[2048,128]{0,1:T(8,128)(2,1)S(1)} %all_gather.3), channel_id=1, source_target_pairs={{0,4},{4,0},{8,12},{12,8},{16,20},{20,16},{24,28},{28,24},{32,36},... | collective-permute-start | bytes 1572872 | tf_op jit(solution)/shard_map/ppermute | solution.py:144
  37.3 1.5 %collective-permute-done = bf16[2048,128]{0,1:T(8,128)(2,1)S(1)} collective-permute-done((bf16[2048,128]{0,1:T(8,128)(2,1)S(1)}, bf16[2048,128]{0,1:T(8,128)(2,1)S(1)}, u32[]{:S(2)}, u32[]{:S(2)}) %collective-permute-start) | collective-permute-done | bytes 524320 | tf_op jit(solution)/shard_map/ppermute | solution.py:144
  38.8 18.8 %all-to-all-done.arrived_ref = bf16[64,40,256]{2,1,0:T(8,128)(2,1)S(1)} async-done(((bf16[64,40,256]{2,1,0:T(8,128)(2,1)}), bf16[64,40,256]{2,1,0:T(8,128)(2,1)S(1)}, u32[]{:S(2)}, u32[]{:S(2)}) %all-to-all-start) | async-done | bytes 1310752 | tf_op jit(solution)/shard_map/all_to_all | solution.py:141
  57.6 0.4 shard_map.183
  58.2 1.3 collective-permute-done.1
  59.5 0.7 fusion.9
  60.3 0.7 broadcast_select_fusion.1
  61.1 0.5 copy.29
  61.7 0.8 collective-permute-done.2
  62.5 2.6 %fusion.10 = f32[2048,256]{1,0:T(8,128)} fusion(bf16[2048,256]{1,0:T(8,128)(2,1)S(1)} %bitcast.47, bf16[128,256]{1,0:T(8,128)(2,1)} %collective-permute-done.2, bf16[128,256]{1,0:T(8,128)(2,1)S(1)} %copy-done.5), kind=kOutput, calls=%fused_computation.17 | convolution fusion | flops 268697600 | bytes 3276800 | tf_op jit(solution)/shard_map/dot_general | solution.py:51
  65.3 0.8 copy-done.9
  66.4 0.8 copy.26
  67.1 6.2 %all-to-all-start.1 = ((bf16[64,8,128]{2,1,0:T(8,128)(2,1)}), bf16[64,8,128]{2,1,0:T(8,128)(2,1)S(1)}, u32[]{:S(2)}, u32[]{:S(2)}) async-start(bf16[64,8,128]{2,1,0:T(8,128)(2,1)} %bitcast.7), calls=%async_computation.1 | async-start | bytes 262144 | tf_op jit(solution)/shard_map/all_to_all | solution.py:129
  73.3 28.9 %reduce-scatter.2.cloned.1.call-done = f32[256,256]{1,0:T(8,128)} async-done(((f32[2048,256]{1,0:T(8,128)}), f32[256,256]{1,0:T(8,128)}) %reduce-scatter.2.cloned.1.call-update) | async-done | bytes 262160 | tf_op jit(solution)/shard_map/reduce_scatter | solution.py:191
  102.2 0.9 dynamic-slice_bitcast_fusion.2
  103.1 3.1 %collective-permute-start.5 = (f32[64,256]{1,0:T(8,128)S(1)}, f32[64,256]{1,0:T(8,128)S(1)}, u32[]{:S(2)}, u32[]{:S(2)}) collective-permute-start(f32[64,256]{1,0:T(8,128)S(1)} %get-tuple-element.13), channel_id=1, source_target_pairs={{0,192},{4,196},{8,200},{12,204},{16,208},{20,212},{24,216},{28,22... | collective-permute-start | bytes 196616 | tf_op jit(solution)/shard_map/ppermute | solution.py:199
  106.2 0.3 collective-permute-start.4
  106.6 0.8 collective-permute-start.3
  107.4 0.7 shard_map.184.filt_ref
  108.1 2.2 %shard_map.185 = bf16[512,128]{1,0:T(8,128)(2,1)} custom-call(bf16[512,128]{1,0:T(8,128)(2,1)S(1)} %bitcast.46, f32[576,256]{1,0:T(8,128)S(1)} %shard_map.184.filt_ref, bf16[2,144,64]{2,1,0:T(8,128)(2,1)S(1)} %copy-done.1, f32[2,72,128]{2,1,0:T(8,128)S(1)} %copy-done.2, bf16[2,256,256]{2,1,0:T(8,128)(2,1)S(1)} %copy-done, ...), custom_call_target="tpu_custom_call" | custom-call | tf_op jit(solution)/shard_map/pallas_call | solution.py:169
  110.3 12.6 %all-to-all-start.2 = ((bf16[64,8,128]{2,1,0:T(8,128)(2,1)}), bf16[64,8,128]{2,1,0:T(8,128)(2,1)S(1)}, u32[]{:S(2)}, u32[]{:S(2)}) async-start(bf16[64,8,128]{2,1,0:T(8,128)(2,1)} %bitcast.10), calls=%async_computation.2 | async-start | bytes 262144 | tf_op jit(solution)/shard_map/all_to_all | solution.py:129
  123.0 0.9 fusion.15
  123.8 0.5 collective-permute-start.6
  124.4 8.9 %all-to-all-done.2 = bf16[64,8,128]{2,1,0:T(8,128)(2,1)S(1)} async-done(((bf16[64,8,128]{2,1,0:T(8,128)(2,1)}), bf16[64,8,128]{2,1,0:T(8,128)(2,1)S(1)}, u32[]{:S(2)}, u32[]{:S(2)}) %all-to-all-start.2) | async-done | bytes 131104 | tf_op jit(solution)/shard_map/all_to_all | solution.py:129
  133.4 0.8 copy.31
  134.1 0.8 copy.32
  134.9 0.6 maximum_multiply_fusion
  (42 shorter events, 1.0 us)
Async XLA Ops:
  10.3 13.2 %copy-start.6 = (bf16[128,512]{1,0:T(8,128)(2,1)S(1)}, bf16[128,512]{1,0:T(8,128)(2,1)}, u32[]{:S(2)}) copy-start(bf16[128,512]{1,0:T(8,128)(2,1)} %param.21) | copy-start | bytes 393220
  10.3 47.3 %all-to-all-start = ((bf16[64,40,256]{2,1,0:T(8,128)(2,1)}), bf16[64,40,256]{2,1,0:T(8,128)(2,1)S(1)}, u32[]{:S(2)}, u32[]{:S(2)}) async-start(bf16[64,40,256]{2,1,0:T(8,128)(2,1)} %fusion.1), calls=%async_computation | async-start | bytes 2621440 | tf_op jit(solution)/shard_map/all_to_all | solution.py:141
  23.4 78.8 %reduce-scatter.2.cloned.1.call-start = ((), (), s32[]{:S(2)}) async-start(), calls=%async_computation.4 | async-start | bytes 2359296 | tf_op jit(solution)/shard_map/reduce_scatter | solution.py:191
  35.1 3.7 %collective-permute-start = (bf16[2048,128]{0,1:T(8,128)(2,1)S(1)}, bf16[2048,128]{0,1:T(8,128)(2,1)S(1)}, u32[]{:S(2)}, u32[]{:S(2)}) collective-permute-start(bf16[2048,128]{0,1:T(8,128)(2,1)S(1)} %all_gather.3), channel_id=1, source_target_pairs={{0,4},{4,0},{8,12},{12,8},{16,20},{20,16},{24,28},{28,24},{32,36},... | collective-permute-start | bytes 1572872 | tf_op jit(solution)/shard_map/ppermute | solution.py:144
  57.6 1.9 %copy-start.7 = (bf16[128,512]{1,0:T(8,128)(2,1)S(1)}, bf16[128,512]{1,0:T(8,128)(2,1)}, u32[]{:S(2)}) copy-start(bf16[128,512]{1,0:T(8,128)(2,1)} %param.16) | copy-start | bytes 393220
  57.6 1.9 %copy-start.8 = (bf16[128,512]{1,0:T(8,128)(2,1)S(1)}, bf16[128,512]{1,0:T(8,128)(2,1)}, u32[]{:S(2)}) copy-start(bf16[128,512]{1,0:T(8,128)(2,1)} %param.19) | copy-start | bytes 393220
  58.1 1.4 %collective-permute-start.1 = (f32[128,256]{1,0:T(8,128)S(1)}, f32[128,256]{1,0:T(8,128)S(1)}, u32[]{:S(2)}, u32[]{:S(2)}) collective-permute-start(f32[128,256]{1,0:T(8,128)S(1)} %get-tuple-element.6), channel_id=1, source_target_pairs={{0,4},{4,0},{8,12},{12,8},{16,20},{20,16},{24,28},{28,24},{32,36},... | collective-permute-start | bytes 393224 | tf_op jit(solution)/shard_map/ppermute | solution.py:162
  60.9 1.6 %collective-permute-start.2 = (bf16[128,256]{1,0:T(8,128)(2,1)}, bf16[128,256]{1,0:T(8,128)(2,1)}, u32[]{:S(2)}, u32[]{:S(2)}) collective-permute-start(bf16[128,256]{1,0:T(8,128)(2,1)} %get-tuple-element.21), channel_id=1, source_target_pairs={{0,4},{4,0},{8,12},{12,8},{16,20},{20,16},{24,28},{28,24},{32,36},... | collective-permute-start | bytes 196616 | tf_op jit(solution)/shard_map/ppermute | solution.py:182
  61.6 0.9 copy-start.5
  65.2 0.9 copy-start.9
  65.2 1.0 copy-start.10
  65.2 42.1 %copy-start = (bf16[2,256,256]{2,1,0:T(8,128)(2,1)S(1)}, bf16[2,256,256]{2,1,0:T(8,128)(2,1)}, u32[]{:S(2)}) copy-start(bf16[2,256,256]{2,1,0:T(8,128)(2,1)} %constant.102.second_ref) | copy-start | bytes 786436
  65.2 42.1 %copy-start.1 = (bf16[2,144,64]{2,1,0:T(8,128)(2,1)S(1)}, bf16[2,144,64]{2,1,0:T(8,128)(2,1)}, u32[]{:S(2)}) copy-start(bf16[2,144,64]{2,1,0:T(8,128)(2,1)} %constant.99.first_ref) | copy-start | bytes 110596
  65.2 42.1 %copy-start.2 = (f32[2,72,128]{2,1,0:T(8,128)S(1)}, f32[2,72,128]{2,1,0:T(8,128)}, u32[]{:S(2)}) copy-start(f32[2,72,128]{2,1,0:T(8,128)} %constant.93.clone.twist_ref) | copy-start | bytes 221188
  66.2 41.9 %copy-start.3 = (bf16[2,256,256]{2,1,0:T(8,128)(2,1)S(1)}, bf16[2,256,256]{2,1,0:T(8,128)(2,1)}, u32[]{:S(2)}) copy-start(bf16[2,256,256]{2,1,0:T(8,128)(2,1)} %constant.105.back_ref) | copy-start | bytes 786436
  66.2 41.9 %copy-start.4 = (bf16[2,64,144]{2,1,0:T(8,128)(2,1)S(1)}, bf16[2,64,144]{2,1,0:T(8,128)(2,1)}, u32[]{:S(2)}) copy-start(bf16[2,64,144]{2,1,0:T(8,128)(2,1)} %constant.108.last_ref) | copy-start | bytes 110596
  67.1 40.9 %all-to-all-start.1 = ((bf16[64,8,128]{2,1,0:T(8,128)(2,1)}), bf16[64,8,128]{2,1,0:T(8,128)(2,1)S(1)}, u32[]{:S(2)}, u32[]{:S(2)}) async-start(bf16[64,8,128]{2,1,0:T(8,128)(2,1)} %bitcast.7), calls=%async_computation.1 | async-start | bytes 262144 | tf_op jit(solution)/shard_map/all_to_all | solution.py:129
  103.1 19.8 %collective-permute-start.5 = (f32[64,256]{1,0:T(8,128)S(1)}, f32[64,256]{1,0:T(8,128)S(1)}, u32[]{:S(2)}, u32[]{:S(2)}) collective-permute-start(f32[64,256]{1,0:T(8,128)S(1)} %get-tuple-element.13), channel_id=1, source_target_pairs={{0,192},{4,196},{8,200},{12,204},{16,208},{20,212},{24,216},{28,22... | collective-permute-start | bytes 196616 | tf_op jit(solution)/shard_map/ppermute | solution.py:199
  106.2 16.7 %collective-permute-start.4 = (f32[64,256]{1,0:T(8,128)S(1)}, f32[64,256]{1,0:T(8,128)S(1)}, u32[]{:S(2)}, u32[]{:S(2)}) collective-permute-start(f32[64,256]{1,0:T(8,128)S(1)} %get-tuple-element.14), channel_id=1, source_target_pairs={{0,128},{4,132},{8,136},{12,140},{16,144},{20,148},{24,152},{28,15... | collective-permute-start | bytes 196616 | tf_op jit(solution)/shard_map/ppermute | solution.py:199
  106.6 16.4 %collective-permute-start.3 = (f32[64,256]{1,0:T(8,128)S(1)}, f32[64,256]{1,0:T(8,128)S(1)}, u32[]{:S(2)}, u32[]{:S(2)}) collective-permute-start(f32[64,256]{1,0:T(8,128)S(1)} %get-tuple-element.12), channel_id=1, source_target_pairs={{0,64},{4,68},{8,72},{12,76},{16,80},{20,84},{24,88},{28,92},{32,9... | collective-permute-start | bytes 196616 | tf_op jit(solution)/shard_map/ppermute | solution.py:199
  110.3 23.0 %all-to-all-start.2 = ((bf16[64,8,128]{2,1,0:T(8,128)(2,1)}), bf16[64,8,128]{2,1,0:T(8,128)(2,1)S(1)}, u32[]{:S(2)}, u32[]{:S(2)}) async-start(bf16[64,8,128]{2,1,0:T(8,128)(2,1)} %bitcast.10), calls=%async_computation.2 | async-start | bytes 262144 | tf_op jit(solution)/shard_map/all_to_all | solution.py:129
  123.8 11.1 %collective-permute-start.6 = (f32[32,256]{1,0:T(8,128)S(1)}, f32[32,256]{1,0:T(8,128)S(1)}, u32[]{:S(2)}, u32[]{:S(2)}) collective-permute-start(f32[32,256]{1,0:T(8,128)S(1)} %slice_select_fusion.1), channel_id=1, source_target_pairs={{0,4},{4,0},{8,12},{12,8},{16,20},{20,16},{24,28},{28,24},{32,36},... | collective-permute-start | bytes 98312 | tf_op jit(solution)/shard_map/ppermute | solution.py:204
Sparse Core Ops, SparseCore 0:
  65.3 36.8 reduce-scatter.1

commit v3 on v1

--- a/solution.py
+++ b/solution.py
@@ -12,14 +12,7 @@
 F32 = jnp.float32
 
 CORES = 2
-
-
-def core_pairs(groups):
-    return [(i, i ^ 1) for i in range(groups)]
-
-
-def same_core_groups(groups):
-    return [list(range(core, groups, CORES)) for core in range(CORES)]
+ALONG_X = 4
 
 
 def dft_tables(blocks, rows, kept):
@@ -98,8 +91,83 @@
     out_ref[...] = plane[...].astype(BF16)
 
 
-def whole(count):
+def pack_kernel(filters_ref, weight_ref, out_ref):
+    groups, _, rows = out_ref.shape
+    chan = filters_ref.shape[1]
+    chans = chan // groups
+    feats = weight_ref.shape[0]
+    part = chan // (ALONG_X * CORES)
+    turned = filters_ref[...].astype(F32).T.astype(BF16)
+    out_ref[:, feats // 2 :, :] = turned.reshape(groups, chans, rows)
+    weight = weight_ref[...].astype(F32)
+    for x in range(ALONG_X):
+        for core in range(CORES):
+            start = (core * ALONG_X + x) * part
+            piece = weight[:, start : start + part]
+            folded = jnp.concatenate([piece[: feats // 2], piece[feats // 2 :]], 1).astype(BF16)
+            for dest in range(x * groups // ALONG_X + core, (x + 1) * groups // ALONG_X, CORES):
+                out_ref[dest, : feats // 2, :] = folded
+
+
+def gate_kernel(x_ref, left_ref, w0_ref, w1_ref, w2_ref, w3_ref, mine_ref, theirs_ref):
+    folded = jnp.concatenate([w0_ref[...], w1_ref[...], w2_ref[...], w3_ref[...]], 1)
+    depth = folded.shape[0]
+    low = dot(left_ref[:, :depth], folded)
+    high = dot(left_ref[:, depth:], folded)
+    rows, half = mine_ref.shape
+    part = half // ALONG_X
+    pieces = [
+        low[:, 2 * hop * part : (2 * hop + 1) * part]
+        + high[:, (2 * hop + 1) * part : (2 * hop + 2) * part]
+        for hop in range(ALONG_X)
+    ]
+    placed = []
+    for x in range(ALONG_X):
+        away = (x_ref[0] - x + ALONG_X) % ALONG_X
+        value = pieces[0]
+        for hop in range(1, ALONG_X):
+            value = jnp.where(away == hop, pieces[hop], value)
+        placed.append(value)
+    share = jnp.concatenate(placed, 1)
+    mine_ref[...] = share[:rows]
+    theirs_ref[...] = share[rows:]
+
+
+def grads_kernel(odd_ref, mine_ref, theirs_ref, queries_ref, conv_ref, query_grad_ref, turned_ref):
+    odd = odd_ref[0] == 1
+    mine, theirs = mine_ref[...], theirs_ref[...]
+    gate = jnp.concatenate([jnp.where(odd, theirs, mine), jnp.where(odd, mine, theirs)], 1)
+    query_grad_ref[...] = (gate * conv_ref[...].astype(F32)).astype(BF16)
+    conv_grad = (gate * queries_ref[...].astype(F32)).astype(BF16)
+    turned_ref[...] = conv_grad.astype(F32).T.astype(BF16)
+
+
+def outputs_kernel(inner_ref, key_ref, value_ref, key_grad_ref, value_grad_ref):
+    inner = inner_ref[...].astype(F32).T
+    key_grad_ref[...] = (inner * value_ref[...].astype(F32)).astype(BF16)
+    value_grad_ref[...] = (inner * key_ref[...].astype(F32)).astype(BF16)
+
+
+def weight_kernel(x_ref, grads_ref, both_ref, own_ref, *away_refs):
+    feats = own_ref.shape[0]
+    for hop, out_ref in enumerate((own_ref, *away_refs)):
+        start = pl.multiple_of(lax.rem(x_ref[0] + hop, ALONG_X) * feats, feats)
+        out_ref[...] = dot(grads_ref[pl.ds(start, feats), :], both_ref[...]).astype(out_ref.dtype)
+
+
+def in_vmem(count):
     return [pl.BlockSpec(memory_space=pltpu.VMEM)] * count
+
+
+def call(kernel, out, scalars, *operands, scratch=()):
+    return pl.pallas_call(
+        kernel,
+        out_shape=[jax.ShapeDtypeStruct(shape, dtype) for shape, dtype in out],
+        in_specs=[pl.BlockSpec(memory_space=pltpu.SMEM)] * len(scalars) + in_vmem(len(operands)),
+        out_specs=in_vmem(len(out)),
+        scratch_shapes=[pltpu.VMEM(shape, F32) for shape in scratch],
+        compiler_params=pltpu.CompilerParams(vmem_limit_bytes=32 << 20),
+    )(*scalars, *operands)
 
 
 def shards(queries, key_proj, value_proj, conv_out, filters, out_grad, out_weight):
@@ -107,12 +175,29 @@
     groups = lax.axis_size("seq")
     feats = out_weight.shape[0]
     chips = groups // CORES
+    along_z = chips // ALONG_X
+    half = chan // CORES
     chans = chan // groups
     kept = -(-(groups + 1) // 8) * 8
     sizes = (groups, chans, rows, kept)
-    odd = lax.axis_index("seq") % CORES == 1
-    to_core = functools.partial(lax.ppermute, axis_name="seq", perm=core_pairs(groups))
-    same_core = same_core_groups(groups)
+
+    place = lax.axis_index("seq")
+    odd = place % CORES == 1
+    x_place = place // (along_z * CORES)
+    z_place = place // CORES % along_z
+    x_scalar = x_place.reshape(1)
+    odd_scalar = odd.astype(jnp.int32).reshape(1)
+
+    def send(value, dx, dz, core):
+        pairs = []
+        for i in range(groups):
+            x, z, c = i // (along_z * CORES), i // CORES % along_z, i % CORES
+            x, z, c = (x + dx) % ALONG_X, (z + dz) % along_z, c ^ core
+            pairs.append((i, (x * along_z + z) * CORES + c))
+        return lax.ppermute(value, "seq", pairs)
+
+    def to_core(value):
+        return send(value, 0, 0, 1)
 
     first, twist, second, last = dft_tables(groups, rows, kept)
     first, last = jnp.stack(halves(first)), jnp.stack(halves(last))
@@ -122,45 +207,90 @@
     def exchange(blocks):
         return lax.all_to_all(blocks.reshape(groups, chans, rows), "seq", 0, 0).reshape(chan, rows)
 
-    copies = jnp.broadcast_to(out_weight[None], (chips, feats, chan))
-    weight = lax.all_to_all(copies, "seq", 0, 0, axis_index_groups=same_core).reshape(-1, chan)
-
-    wide = lax.all_gather(out_grad.T, "ch", axis=0).reshape(chips, CORES, feats, rows)
-    own = jnp.where(odd, wide[:, 1], wide[:, 0]).reshape(chips * feats, rows)
-    other = jnp.where(odd, wide[:, 0], wide[:, 1]).reshape(chips * feats, rows)
-    grads = jnp.concatenate([own, to_core(other)], 1)
-
-    filt = pl.pallas_call(
+    (packed,) = call(pack_kernel, [((groups, feats // 2 + chans, rows), BF16)], (), filters, out_weight)
+    arrived = lax.all_to_all(packed, "seq", 0, 0)
+    folded = arrived[:, : feats // 2].reshape(groups * feats // 2, rows)
+    weights = [folded] + [send(folded, hop, 0, 0) for hop in range(1, ALONG_X)]
+    (filt,) = call(
         functools.partial(filter_kernel, sizes),
-        out_shape=jax.ShapeDtypeStruct((chans * kept, 2 * rows), F32),
-        in_specs=whole(4),
-        out_specs=pl.BlockSpec(memory_space=pltpu.VMEM),
-        scratch_shapes=[pltpu.VMEM((chan, rows), F32)],
-        compiler_params=pltpu.CompilerParams(vmem_limit_bytes=32 << 20),
-    )(exchange(filters.T), first, twist, second)
-
-    share = lax.dot_general(grads, weight, (((0,), (0,)), ((), ())), preferred_element_type=F32)
-    grad_gate = share[:rows] + to_core(share[rows:])
-    query_grad = (grad_gate * conv_out.astype(F32)).astype(BF16)
-    conv_grad = (grad_gate * queries.astype(F32)).astype(BF16)
-
-    inner = pl.pallas_call(
+        [((chans * kept, 2 * rows), F32)],
+        (),
+        arrived[:, feats // 2 :].reshape(chan, rows),
+        first,
+        twist,
+        second,
+        scratch=[(chan, rows)],
+    )
+
+    wide = lax.all_gather(out_grad.T, "ch", axis=0, tiled=True)
+    grads = jnp.concatenate([wide, to_core(wide)], 1)
+    left = grads.reshape(groups, 2, feats // 2, CORES * rows).transpose(3, 1, 0, 2)
+
+    mine, theirs = call(
+        gate_kernel,
+        [((rows, half), F32)] * 2,
+        (x_scalar,),
+        left.reshape(CORES * rows, groups * feats),
+        *weights,
+    )
+    query_grad, turned = call(
+        grads_kernel,
+        [((rows, chan), BF16), ((chan, rows), BF16)],
+        (odd_scalar,),
+        mine,
+        to_core(theirs),
+        queries,
+        conv_out,
+    )
+    (inner,) = call(
         functools.partial(correlate_kernel, sizes),
-        out_shape=jax.ShapeDtypeStruct((chan, rows), BF16),
-        in_specs=whole(7),
-        out_specs=pl.BlockSpec(memory_space=pltpu.VMEM),
-        scratch_shapes=[pltpu.VMEM((chan, rows), F32)],
-        compiler_params=pltpu.CompilerParams(vmem_limit_bytes=32 << 20),
-    )(exchange(conv_grad.T), filt, first, twist, second, back, last)
-    inner = exchange(inner).T.astype(F32)
-    key_grad = (inner * value_proj.astype(F32)).astype(BF16)
-    value_grad = (inner * key_proj.astype(F32)).astype(BF16)
+        [((chan, rows), BF16)],
+        (),
+        exchange(turned),
+        filt,
+        first,
+        twist,
+        second,
+        back,
+        last,
+        scratch=[(chan, rows)],
+    )
+    key_grad, value_grad = call(
+        outputs_kernel, [((rows, chan), BF16)] * 2, (), exchange(inner), key_proj, value_proj
+    )
 
     gated = (queries.astype(F32) * conv_out.astype(F32)).astype(BF16)
-    both = jnp.concatenate([gated, to_core(gated)], 0)
-    part = dot(grads, both).astype(BF16).reshape(chips, feats, chan)
-    parts = lax.all_to_all(part, "seq", 0, 0, axis_index_groups=same_core)
-    weight_grad = jnp.sum(parts.astype(F32), 0) * (rows * groups) ** (-0.5)
+    own_half = jnp.where(odd, gated[:, half:], gated[:, :half])
+    other_half = jnp.where(odd, gated[:, :half], gated[:, half:])
+    both = jnp.concatenate([own_half, to_core(other_half)], 0)
+    block = groups * feats // ALONG_X
+    total, *away = call(
+        weight_kernel,
+        [((block, half), F32)] + [((block, half), BF16)] * (ALONG_X - 1),
+        (x_scalar,),
+        grads,
+        both,
+    )
+    for hop, value in enumerate(away, 1):
+        total += send(value, hop, 0, 0).astype(F32)
+    quads = along_z // 2
+    total = total.reshape(quads, 2 * CORES * feats, half)
+    quad = z_place // 2
+    part = lax.dynamic_index_in_dim(total, quad, 0, keepdims=False)
+    for hop in range(1, quads):
+        value = lax.dynamic_index_in_dim(total, (quad + hop) % quads, 0, keepdims=False)
+        part += send(value.astype(BF16), 0, 2 * hop, 0).astype(F32)
+    part = part.reshape(2, CORES * feats, half)
+    upper = z_place % 2 == 1
+    swap = [(i, i ^ CORES) for i in range(groups)]
+    part = jnp.where(upper, part[1], part[0]) + lax.ppermute(
+        jnp.where(upper, part[0], part[1]), "seq", swap
+    )
+    part = part.reshape(CORES, feats, half)
+    own = jnp.where(odd, part[1], part[0])
+    beside = to_core(jnp.where(odd, part[0], part[1]))
+    weight_grad = jnp.concatenate([jnp.where(odd, beside, own), jnp.where(odd, own, beside)], 1)
+    weight_grad = weight_grad * (rows * groups) ** (-0.5)
     return (query_grad, key_grad, value_grad, weight_grad)
 
 

time: 128 us -> 114 us (0.89)
  the two profiles are of different devices: /device:TPU:8 before, /device:TPU:1 now
where the time goes in v3:
time: 114 us; the launch traced here: 113 us
  starting transfers between devices  44.5 us (39%)
  waiting for transfers between devices  41.7 us (37%)
  blocking collectives  12.7 us (11%)
  Pallas kernels  6.74 us (6%)
  local copies, waits for them, and re-layouts  3.76 us (3%)
  other arithmetic  2.82 us (2%)
    ppermute x13, waiting for transfers between devices, send(): return lax.ppermute(value, 'seq', pairs)  23.9 us
    ppermute x13, starting transfers between devices, send(): return lax.ppermute(value, 'seq', pairs)  22.5 us
    all_to_all x2, waiting for transfers between devices, exchange(): lax.all_to_all(blocks.reshape(groups, chans, rows), 'seq', 0, 0)  17.8 us
    all_gather x1, blocking collectives, shards(): wide = lax.all_gather(out_grad.T, 'ch', axis=0, tiled=True)  12.7 us
    all_to_all x2, starting transfers between devices, exchange(): lax.all_to_all(blocks.reshape(groups, chans, rows), 'seq', 0, 0)  11.4 us
    all_to_all x1, starting transfers between devices, shards(): arrived = lax.all_to_all(packed, 'seq', 0, 0)  9.79 us
    pallas_call x7, Pallas kernels, call(): pl.pallas_call(kernel, out_shape=[jax.ShapeDtypeStruct(shape, dtype) for...  6.74 us
  transfers between devices with their start and end apart: 17, of which 9 were waited for; matrix products, arithmetic and copies ran while one was open for 4% of the time, Pallas kernels for 5%

profile of v3, /device:TPU:1, one launch (start us, length us, event | category | flops | bytes accessed | tf_op | source)
XLA Modules:
  0.0 113.3 jit_solution(4709298822576991240)
XLA Ops:
  0.6 1.0 copy.22
  1.7 12.7 %all_gather.3 = bf16[2048,128]{1,0:T(8,128)(2,1)S(1)} all-gather(bf16[512,128]{1,0:T(8,128)(2,1)S(1)} %bitcast.37), channel_id=1, replica_groups=mesh['seq'=64,'ch'=4] {'ch'}, dimensions={0}, use_global_device_ids=true | all-gather | bytes 655360 | tf_op jit(solution)/shard_map/all_gather | solution.py:225
  14.4 4.0 %collective-permute-start = (bf16[2048,128]{1,0:T(8,128)(2,1)S(1)}, bf16[2048,128]{1,0:T(8,128)(2,1)S(1)}, u32[]{:S(2)}, u32[]{:S(2)}) collective-permute-start(bf16[2048,128]{1,0:T(8,128)(2,1)S(1)} %all_gather.3), channel_id=1, source_target_pairs={{0,4},{4,0},{8,12},{12,8},{16,20},{20,16},{24,28},{28,24},{32,36},... | collective-permute-start | bytes 1572872 | tf_op jit(solution)/shard_map/ppermute | solution.py:197
  18.6 0.8 copy-done.6
  19.4 0.9 shard_map.183
  20.3 9.8 %all-to-all-start = ((bf16[64,24,128]{2,1,0:T(8,128)(2,1)}), bf16[64,24,128]{2,1,0:T(8,128)(2,1)S(1)}, u32[]{:S(2)}, u32[]{:S(2)}) async-start(bf16[64,24,128]{2,1,0:T(8,128)(2,1)} %shard_map.183), calls=%async_computation | async-start | bytes 786432 | tf_op jit(solution)/shard_map/all_to_all | solution.py:211
  30.8 1.5 %collective-permute-start.6 = (bf16[512,256]{1,0:T(8,128)(2,1)S(1)}, bf16[512,256]{1,0:T(8,128)(2,1)}, u32[]{:S(2)}, u32[]{:S(2)}) collective-permute-start(bf16[512,256]{1,0:T(8,128)(2,1)S(1)} %get-tuple-element.21), channel_id=1, source_target_pairs={{0,64},{4,68},{8,72},{12,76},{16,80},{20,84},{24,88},{28,92},{32,9... | collective-permute-start | bytes 786440 | tf_op jit(solution)/shard_map/ppermute | solution.py:197
  32.3 2.6 %collective-permute-start.7 = (bf16[512,256]{1,0:T(8,128)(2,1)S(1)}, bf16[512,256]{1,0:T(8,128)(2,1)}, u32[]{:S(2)}, u32[]{:S(2)}) collective-permute-start(bf16[512,256]{1,0:T(8,128)(2,1)S(1)} %get-tuple-element.22), channel_id=1, source_target_pairs={{0,128},{4,132},{8,136},{12,140},{16,144},{20,148},{24,152},{28,15... | collective-permute-start | bytes 786440 | tf_op jit(solution)/shard_map/ppermute | solution.py:197
  34.9 1.1 collective-permute-start.8
  35.9 7.3 %collective-permute-done.6 = bf16[512,256]{1,0:T(8,128)(2,1)} collective-permute-done((bf16[512,256]{1,0:T(8,128)(2,1)S(1)}, bf16[512,256]{1,0:T(8,128)(2,1)}, u32[]{:S(2)}, u32[]{:S(2)}) %collective-permute-start.6) | collective-permute-done | bytes 262176 | tf_op jit(solution)/shard_map/ppermute | solution.py:197
  43.3 7.2 %collective-permute-done.7 = bf16[512,256]{1,0:T(8,128)(2,1)} collective-permute-done((bf16[512,256]{1,0:T(8,128)(2,1)S(1)}, bf16[512,256]{1,0:T(8,128)(2,1)}, u32[]{:S(2)}, u32[]{:S(2)}) %collective-permute-start.7) | collective-permute-done | bytes 262176 | tf_op jit(solution)/shard_map/ppermute | solution.py:197
  50.5 1.2 %convert_add_fusion = f32[512,256]{1,0:T(8,128)S(1)} fusion(bf16[512,256]{1,0:T(8,128)(2,1)} %collective-permute-done.8, bf16[512,256]{1,0:T(8,128)(2,1)} %collective-permute-done.7, f32[512,256]{1,0:T(8,128)S(1)} %get-tuple-element.20, bf16[512,256]{1,0:T(8,128)(2,1)} %collective-permute-done.6), kind=kLoop, calls=%fused_computation | loop fusion | flops 786432 | bytes 1835008 | tf_op jit(solution)/shard_map/add | solution.py:275
  51.7 4.9 %collective-permute-start.10 = (bf16[128,256]{1,0:T(8,128)(2,1)S(1)}, bf16[128,256]{1,0:T(8,128)(2,1)S(1)}, u32[]{:S(2)}, u32[]{:S(2)}) collective-permute-start(bf16[128,256]{1,0:T(8,128)(2,1)S(1)} %get-tuple-element.26), channel_id=1, source_target_pairs={{0,32},{4,36},{8,40},{12,44},{16,48},{20,52},{24,56},{28,60},{32,0... | collective-permute-start | bytes 196616 | tf_op jit(solution)/shard_map/ppermute | solution.py:197
  56.9 2.1 %collective-permute-start.9 = (bf16[128,256]{1,0:T(8,128)(2,1)S(1)}, bf16[128,256]{1,0:T(8,128)(2,1)}, u32[]{:S(2)}, u32[]{:S(2)}) collective-permute-start(bf16[128,256]{1,0:T(8,128)(2,1)S(1)} %get-tuple-element.24), channel_id=1, source_target_pairs={{0,16},{4,20},{8,24},{12,28},{16,32},{20,36},{24,40},{28,44},{32,4... | collective-permute-start | bytes 196616 | tf_op jit(solution)/shard_map/ppermute | solution.py:197
  59.6 2.5 %collective-permute-start.2 = (bf16[1024,128]{1,0:T(8,128)(2,1)S(1)}, bf16[1024,128]{1,0:T(8,128)(2,1)S(1)}, u32[]{:S(2)}, u32[]{:S(2)}) collective-permute-start(bf16[1024,128]{1,0:T(8,128)(2,1)S(1)} %bitcast.29), channel_id=1, source_target_pairs={{0,128},{4,132},{8,136},{12,140},{16,144},{20,148},{24,152},{28,15... | collective-permute-start | bytes 786440 | tf_op jit(solution)/shard_map/ppermute | solution.py:197
  62.1 0.7 collective-permute-start.3
  63.4 0.9 fusion.1
  64.3 0.8 collective-permute-start.12
  65.9 0.8 collective-permute-done.1.w1_ref
  66.7 6.1 %collective-permute-done.2.w2_ref = bf16[1024,128]{1,0:T(8,128)(2,1)S(1)} collective-permute-done((bf16[1024,128]{1,0:T(8,128)(2,1)S(1)}, bf16[1024,128]{1,0:T(8,128)(2,1)S(1)}, u32[]{:S(2)}, u32[]{:S(2)}) %collective-permute-start.2) | collective-permute-done | bytes 262176 | tf_op jit(solution)/shard_map/ppermute | solution.py:197
  72.8 0.9 collective-permute-done.3.w3_ref
  73.7 0.9 shard_map.184
  74.7 1.7 %collective-permute-start.4 = (f32[128,256]{1,0:T(8,128)S(1)}, f32[128,256]{1,0:T(8,128)S(1)}, u32[]{:S(2)}, u32[]{:S(2)}) collective-permute-start(f32[128,256]{1,0:T(8,128)S(1)} %get-tuple-element.15), channel_id=1, source_target_pairs={{0,4},{4,0},{8,12},{12,8},{16,20},{20,16},{24,28},{28,24},{32,36},... | collective-permute-start | bytes 393224 | tf_op jit(solution)/shard_map/ppermute | solution.py:197
  76.3 1.0 collective-permute-done.4.theirs_ref
  77.3 0.8 shard_map.185
  78.1 6.5 %all-to-all-start.1 = ((bf16[64,8,128]{2,1,0:T(8,128)(2,1)}), bf16[64,8,128]{2,1,0:T(8,128)(2,1)S(1)}, u32[]{:S(2)}, u32[]{:S(2)}) async-start(bf16[64,8,128]{2,1,0:T(8,128)(2,1)} %bitcast.7), calls=%async_computation.1 | async-start | bytes 262144 | tf_op jit(solution)/shard_map/all_to_all | solution.py:208
  85.2 0.9 slice_bitcast_fusion.x_ref
  86.9 8.1 %all-to-all-done.1 = bf16[64,8,128]{2,1,0:T(8,128)(2,1)S(1)} async-done(((bf16[64,8,128]{2,1,0:T(8,128)(2,1)}), bf16[64,8,128]{2,1,0:T(8,128)(2,1)S(1)}, u32[]{:S(2)}, u32[]{:S(2)}) %all-to-all-start.1) | async-done | bytes 131104 | tf_op jit(solution)/shard_map/all_to_all | solution.py:208
  95.0 2.2 %shard_map.187 = bf16[512,128]{1,0:T(8,128)(2,1)} custom-call(bf16[512,128]{1,0:T(8,128)(2,1)S(1)} %bitcast.33, f32[576,256]{1,0:T(8,128)S(1)} %shard_map.186.filt_ref, bf16[2,144,64]{2,1,0:T(8,128)(2,1)S(1)} %copy-done.4, f32[2,72,128]{2,1,0:T(8,128)S(1)} %copy-done.3, bf16[2,256,256]{2,1,0:T(8,128)(2,1)S(1)} %copy-done, ...), custom_call_target="tpu_custom_call" | custom-call | tf_op jit(solution)/shard_map/pallas_call | solution.py:163
  97.2 4.9 %all-to-all-start.2 = ((bf16[64,8,128]{2,1,0:T(8,128)(2,1)}), bf16[64,8,128]{2,1,0:T(8,128)(2,1)S(1)}, u32[]{:S(2)}, u32[]{:S(2)}) async-start(bf16[64,8,128]{2,1,0:T(8,128)(2,1)} %bitcast.10), calls=%async_computation.2 | async-start | bytes 262144 | tf_op jit(solution)/shard_map/all_to_all | solution.py:208
  102.8 9.7 %all-to-all-done.2 = bf16[64,8,128]{2,1,0:T(8,128)(2,1)S(1)} async-done(((bf16[64,8,128]{2,1,0:T(8,128)(2,1)}), bf16[64,8,128]{2,1,0:T(8,128)(2,1)S(1)}, u32[]{:S(2)}, u32[]{:S(2)}) %all-to-all-start.2) | async-done | bytes 131104 | tf_op jit(solution)/shard_map/all_to_all | solution.py:208
  112.5 0.8 shard_map.188
  (56 shorter events, 4.9 us)
Async XLA Ops:
  1.7 16.8 %copy-start.1 = (bf16[128,512]{1,0:T(8,128)(2,1)S(1)}, bf16[128,512]{1,0:T(8,128)(2,1)}, u32[]{:S(2)}) copy-start(bf16[128,512]{1,0:T(8,128)(2,1)} %queries_ref.1) | copy-start | bytes 393220
  1.7 16.8 %copy-start.2 = (bf16[128,512]{1,0:T(8,128)(2,1)S(1)}, bf16[128,512]{1,0:T(8,128)(2,1)}, u32[]{:S(2)}) copy-start(bf16[128,512]{1,0:T(8,128)(2,1)} %conv_ref.1) | copy-start | bytes 393220
  14.4 15.8 %collective-permute-start = (bf16[2048,128]{1,0:T(8,128)(2,1)S(1)}, bf16[2048,128]{1,0:T(8,128)(2,1)S(1)}, u32[]{:S(2)}, u32[]{:S(2)}) collective-permute-start(bf16[2048,128]{1,0:T(8,128)(2,1)S(1)} %all_gather.3), channel_id=1, source_target_pairs={{0,4},{4,0},{8,12},{12,8},{16,20},{20,16},{24,28},{28,24},{32,36},... | collective-permute-start | bytes 1572872 | tf_op jit(solution)/shard_map/ppermute | solution.py:197
  18.5 0.9 copy-start.6
  18.5 0.9 copy-start.10
  18.5 11.7 %collective-permute-start.5 = (bf16[128,256]{1,0:T(8,128)(2,1)S(1)}, bf16[128,256]{1,0:T(8,128)(2,1)S(1)}, u32[]{:S(2)}, u32[]{:S(2)}) collective-permute-start(bf16[128,256]{1,0:T(8,128)(2,1)S(1)} %get-tuple-element.28), channel_id=1, source_target_pairs={{0,4},{4,0},{8,12},{12,8},{16,20},{20,16},{24,28},{28,24},{32,36},... | collective-permute-start | bytes 196616 | tf_op jit(solution)/shard_map/ppermute | solution.py:197
  20.3 38.8 %all-to-all-start = ((bf16[64,24,128]{2,1,0:T(8,128)(2,1)}), bf16[64,24,128]{2,1,0:T(8,128)(2,1)S(1)}, u32[]{:S(2)}, u32[]{:S(2)}) async-start(bf16[64,24,128]{2,1,0:T(8,128)(2,1)} %shard_map.183), calls=%async_computation | async-start | bytes 786432 | tf_op jit(solution)/shard_map/all_to_all | solution.py:211
  30.8 12.5 %collective-permute-start.6 = (bf16[512,256]{1,0:T(8,128)(2,1)S(1)}, bf16[512,256]{1,0:T(8,128)(2,1)}, u32[]{:S(2)}, u32[]{:S(2)}) collective-permute-start(bf16[512,256]{1,0:T(8,128)(2,1)S(1)} %get-tuple-element.21), channel_id=1, source_target_pairs={{0,64},{4,68},{8,72},{12,76},{16,80},{20,84},{24,88},{28,92},{32,9... | collective-permute-start | bytes 786440 | tf_op jit(solution)/shard_map/ppermute | solution.py:197
  32.3 18.2 %collective-permute-start.7 = (bf16[512,256]{1,0:T(8,128)(2,1)S(1)}, bf16[512,256]{1,0:T(8,128)(2,1)}, u32[]{:S(2)}, u32[]{:S(2)}) collective-permute-start(bf16[512,256]{1,0:T(8,128)(2,1)S(1)} %get-tuple-element.22), channel_id=1, source_target_pairs={{0,128},{4,132},{8,136},{12,140},{16,144},{20,148},{24,152},{28,15... | collective-permute-start | bytes 786440 | tf_op jit(solution)/shard_map/ppermute | solution.py:197
  34.9 15.6 %collective-permute-start.8 = (bf16[512,256]{1,0:T(8,128)(2,1)S(1)}, bf16[512,256]{1,0:T(8,128)(2,1)}, u32[]{:S(2)}, u32[]{:S(2)}) collective-permute-start(bf16[512,256]{1,0:T(8,128)(2,1)S(1)} %get-tuple-element.23), channel_id=1, source_target_pairs={{0,192},{4,196},{8,200},{12,204},{16,208},{20,212},{24,216},{28,22... | collective-permute-start | bytes 786440 | tf_op jit(solution)/shard_map/ppermute | solution.py:197
  51.7 10.4 %collective-permute-start.10 = (bf16[128,256]{1,0:T(8,128)(2,1)S(1)}, bf16[128,256]{1,0:T(8,128)(2,1)S(1)}, u32[]{:S(2)}, u32[]{:S(2)}) collective-permute-start(bf16[128,256]{1,0:T(8,128)(2,1)S(1)} %get-tuple-element.26), channel_id=1, source_target_pairs={{0,32},{4,36},{8,40},{12,44},{16,48},{20,52},{24,56},{28,60},{32,0... | collective-permute-start | bytes 196616 | tf_op jit(solution)/shard_map/ppermute | solution.py:197
  56.7 6.7 %collective-permute-start.11 = (bf16[128,256]{1,0:T(8,128)(2,1)S(1)}, bf16[128,256]{1,0:T(8,128)(2,1)S(1)}, u32[]{:S(2)}, u32[]{:S(2)}) collective-permute-start(bf16[128,256]{1,0:T(8,128)(2,1)S(1)} %get-tuple-element.25), channel_id=1, source_target_pairs={{0,48},{4,52},{8,56},{12,60},{16,0},{20,4},{24,8},{28,12},{32,16},... | collective-permute-start | bytes 196616 | tf_op jit(solution)/shard_map/ppermute | solution.py:197
  56.9 6.5 %collective-permute-start.9 = (bf16[128,256]{1,0:T(8,128)(2,1)S(1)}, bf16[128,256]{1,0:T(8,128)(2,1)}, u32[]{:S(2)}, u32[]{:S(2)}) collective-permute-start(bf16[128,256]{1,0:T(8,128)(2,1)S(1)} %get-tuple-element.24), channel_id=1, source_target_pairs={{0,16},{4,20},{8,24},{12,28},{16,32},{20,36},{24,40},{28,44},{32,4... | collective-permute-start | bytes 196616 | tf_op jit(solution)/shard_map/ppermute | solution.py:197
  59.0 5.2 %copy-start.11 = (bf16[64,24,128]{2,1,0:T(8,128)(2,1)}, bf16[64,24,128]{2,1,0:T(8,128)(2,1)S(1)}, u32[]{:S(2)}) copy-start(bf16[64,24,128]{2,1,0:T(8,128)(2,1)S(1)} %all-to-all-done) | copy-start | bytes 1179652
  59.1 7.6 %collective-permute-start.1 = (bf16[1024,128]{1,0:T(8,128)(2,1)S(1)}, bf16[1024,128]{1,0:T(8,128)(2,1)S(1)}, u32[]{:S(2)}, u32[]{:S(2)}) collective-permute-start(bf16[1024,128]{1,0:T(8,128)(2,1)S(1)} %bitcast.28), channel_id=1, source_target_pairs={{0,64},{4,68},{8,72},{12,76},{16,80},{20,84},{24,88},{28,92},{32,9... | collective-permute-start | bytes 786440 | tf_op jit(solution)/shard_map/ppermute | solution.py:197
  59.6 13.2 %collective-permute-start.2 = (bf16[1024,128]{1,0:T(8,128)(2,1)S(1)}, bf16[1024,128]{1,0:T(8,128)(2,1)S(1)}, u32[]{:S(2)}, u32[]{:S(2)}) collective-permute-start(bf16[1024,128]{1,0:T(8,128)(2,1)S(1)} %bitcast.29), channel_id=1, source_target_pairs={{0,128},{4,132},{8,136},{12,140},{16,144},{20,148},{24,152},{28,15... | collective-permute-start | bytes 786440 | tf_op jit(solution)/shard_map/ppermute | solution.py:197
  62.1 11.6 %collective-permute-start.3 = (bf16[1024,128]{1,0:T(8,128)(2,1)S(1)}, bf16[1024,128]{1,0:T(8,128)(2,1)S(1)}, u32[]{:S(2)}, u32[]{:S(2)}) collective-permute-start(bf16[1024,128]{1,0:T(8,128)(2,1)S(1)} %bitcast.30), channel_id=1, source_target_pairs={{0,192},{4,196},{8,200},{12,204},{16,208},{20,212},{24,216},{28,22... | collective-permute-start | bytes 786440 | tf_op jit(solution)/shard_map/ppermute | solution.py:197
  64.3 0.9 copy-start.12
  64.3 12.0 %collective-permute-start.12 = (f32[64,256]{1,0:T(8,128)S(1)}, f32[64,256]{1,0:T(8,128)S(1)}, u32[]{:S(2)}, u32[]{:S(2)}) collective-permute-start(f32[64,256]{1,0:T(8,128)S(1)} %slice_select_fusion), channel_id=1, source_target_pairs={{0,8},{4,12},{8,0},{12,4},{16,24},{20,28},{24,16},{28,20},{32,40},... | collective-permute-start | bytes 196616 | tf_op jit(solution)/shard_map/ppermute | solution.py:286
  65.9 10.4 %copy-start.13 = (f32[128,256]{1,0:T(8,128)S(1)}, f32[128,256]{1,0:T(8,128)}, u32[]{:S(2)}) copy-start(f32[128,256]{1,0:T(8,128)} %copy-done.12) | copy-start | bytes 393220
  74.7 2.7 %collective-permute-start.4 = (f32[128,256]{1,0:T(8,128)S(1)}, f32[128,256]{1,0:T(8,128)S(1)}, u32[]{:S(2)}, u32[]{:S(2)}) collective-permute-start(f32[128,256]{1,0:T(8,128)S(1)} %get-tuple-element.15), channel_id=1, source_target_pairs={{0,4},{4,0},{8,12},{12,8},{16,20},{20,16},{24,28},{28,24},{32,36},... | collective-permute-start | bytes 393224 | tf_op jit(solution)/shard_map/ppermute | solution.py:197
  78.1 8.0 %copy-start = (bf16[2,256,256]{2,1,0:T(8,128)(2,1)S(1)}, bf16[2,256,256]{2,1,0:T(8,128)(2,1)}, u32[]{:S(2)}) copy-start(bf16[2,256,256]{2,1,0:T(8,128)(2,1)} %constant.126.second_ref) | copy-start | bytes 786436
  78.1 16.9 %all-to-all-start.1 = ((bf16[64,8,128]{2,1,0:T(8,128)(2,1)}), bf16[64,8,128]{2,1,0:T(8,128)(2,1)S(1)}, u32[]{:S(2)}, u32[]{:S(2)}) async-start(bf16[64,8,128]{2,1,0:T(8,128)(2,1)} %bitcast.7), calls=%async_computation.1 | async-start | bytes 262144 | tf_op jit(solution)/shard_map/all_to_all | solution.py:208
  84.6 1.5 %copy-start.3 = (f32[2,72,128]{2,1,0:T(8,128)S(1)}, f32[2,72,128]{2,1,0:T(8,128)}, u32[]{:S(2)}) copy-start(f32[2,72,128]{2,1,0:T(8,128)} %constant.119.clone.twist_ref) | copy-start | bytes 221188
  84.7 1.5 %copy-start.4 = (bf16[2,144,64]{2,1,0:T(8,128)(2,1)S(1)}, bf16[2,144,64]{2,1,0:T(8,128)(2,1)}, u32[]{:S(2)}) copy-start(bf16[2,144,64]{2,1,0:T(8,128)(2,1)} %constant.123.first_ref) | copy-start | bytes 110596
  84.7 17.5 %collective-permute-start.13 = (f32[32,256]{1,0:T(8,128)S(1)}, f32[32,256]{1,0:T(8,128)S(1)}, u32[]{:S(2)}, u32[]{:S(2)}) collective-permute-start(f32[32,256]{1,0:T(8,128)S(1)} %slice_select_fusion.2), channel_id=1, source_target_pairs={{0,4},{4,0},{8,12},{12,8},{16,20},{20,16},{24,28},{28,24},{32,36},... | collective-permute-start | bytes 98312 | tf_op jit(solution)/shard_map/ppermute | solution.py:197
  86.2 8.8 %copy-start.5 = (bf16[2,256,256]{2,1,0:T(8,128)(2,1)S(1)}, bf16[2,256,256]{2,1,0:T(8,128)(2,1)}, u32[]{:S(2)}) copy-start(bf16[2,256,256]{2,1,0:T(8,128)(2,1)} %constant.129.back_ref) | copy-start | bytes 786436
  86.2 8.8 %copy-start.9 = (bf16[2,64,144]{2,1,0:T(8,128)(2,1)S(1)}, bf16[2,64,144]{2,1,0:T(8,128)(2,1)}, u32[]{:S(2)}) copy-start(bf16[2,64,144]{2,1,0:T(8,128)(2,1)} %constant.132.last_ref) | copy-start | bytes 110596
  97.2 15.2 %all-to-all-start.2 = ((bf16[64,8,128]{2,1,0:T(8,128)(2,1)}), bf16[64,8,128]{2,1,0:T(8,128)(2,1)S(1)}, u32[]{:S(2)}, u32[]{:S(2)}) async-start(bf16[64,8,128]{2,1,0:T(8,128)(2,1)} %bitcast.10), calls=%async_computation.2 | async-start | bytes 262144 | tf_op jit(solution)/shard_map/all_to_all | solution.py:208
  102.1 10.4 %copy-start.7 = (bf16[128,512]{1,0:T(8,128)(2,1)S(1)}, bf16[128,512]{1,0:T(8,128)(2,1)}, u32[]{:S(2)}) copy-start(bf16[128,512]{1,0:T(8,128)(2,1)} %key_ref.1) | copy-start | bytes 393220
  102.1 10.4 %copy-start.8 = (bf16[128,512]{1,0:T(8,128)(2,1)S(1)}, bf16[128,512]{1,0:T(8,128)(2,1)}, u32[]{:S(2)}) copy-start(bf16[128,512]{1,0:T(8,128)(2,1)} %value_ref.1) | copy-start | bytes 393220

commit v4 on v3

--- a/solution.py
+++ b/solution.py
@@ -148,26 +148,65 @@
     value_grad_ref[...] = (inner * key_ref[...].astype(F32)).astype(BF16)
 
 
-def weight_kernel(x_ref, grads_ref, both_ref, own_ref, *away_refs):
-    feats = own_ref.shape[0]
+def arrange_kernel(y_ref, *refs):
+    block = refs[0].shape[0]
+    for hop, ref in enumerate(refs[:-1]):
+        start = pl.multiple_of(lax.rem(y_ref[0] + hop, len(refs) - 1) * block, block)
+        refs[-1][pl.ds(start, block), :] = ref[...]
+
+
+def partial_kernel(quad_ref, after_ref, grads_ref, both_ref, own_ref, *away_refs):
+    quads = len(away_refs) + 1
+    size = grads_ref.shape[0] // (ALONG_X * quads)
     for hop, out_ref in enumerate((own_ref, *away_refs)):
-        start = pl.multiple_of(lax.rem(x_ref[0] + hop, ALONG_X) * feats, feats)
-        out_ref[...] = dot(grads_ref[pl.ds(start, feats), :], both_ref[...]).astype(out_ref.dtype)
+        quad = lax.rem(quad_ref[0] + hop, quads)
+        for x in range(ALONG_X):
+            start = pl.multiple_of((x * quads + quad) * size, size)
+            value = dot(grads_ref[pl.ds(start, size), :], both_ref[...])
+            out_ref[x * size : (x + 1) * size, :] = value.astype(out_ref.dtype)
+
+
+def pairs_kernel(upper_ref, after_ref, own_ref, a_ref, b_ref, c_ref, keep_ref, give_ref):
+    total = own_ref[...] + a_ref[...].astype(F32) + b_ref[...].astype(F32) + c_ref[...].astype(F32)
+    size = keep_ref.shape[0] // ALONG_X
+    upper = upper_ref[0] == 1
+    for x in range(ALONG_X):
+        low = total[2 * x * size : (2 * x + 1) * size]
+        high = total[(2 * x + 1) * size : (2 * x + 2) * size]
+        keep_ref[x * size : (x + 1) * size, :] = jnp.where(upper, high, low)
+        give_ref[x * size : (x + 1) * size, :] = jnp.where(upper, low, high)
+
+
+def lines_kernel(x_ref, after_ref, keep_ref, came_ref, *out_refs):
+    size = out_refs[0].shape[0]
+    for hop, out_ref in enumerate(out_refs):
+        place = pl.ds(pl.multiple_of(lax.rem(x_ref[0] + hop, ALONG_X) * size, size), size)
+        out_ref[...] = keep_ref[place, :] + came_ref[place, :]
+
+
+def cores_kernel(odd_ref, own_ref, a_ref, b_ref, c_ref, keep_ref, give_ref):
+    total = (own_ref[...] + a_ref[...]) + (b_ref[...] + c_ref[...])
+    size = keep_ref.shape[0]
+    odd = odd_ref[0] == 1
+    keep_ref[...] = jnp.where(odd, total[size:], total[:size])
+    give_ref[...] = jnp.where(odd, total[:size], total[size:])
 
 
 def in_vmem(count):
     return [pl.BlockSpec(memory_space=pltpu.VMEM)] * count
 
 
-def call(kernel, out, scalars, *operands, scratch=()):
+def call(kernel, out, scalars, *operands, scratch=(), after=()):
     return pl.pallas_call(
         kernel,
         out_shape=[jax.ShapeDtypeStruct(shape, dtype) for shape, dtype in out],
-        in_specs=[pl.BlockSpec(memory_space=pltpu.SMEM)] * len(scalars) + in_vmem(len(operands)),
+        in_specs=[pl.BlockSpec(memory_space=pltpu.SMEM)] * len(scalars)
+        + [pl.BlockSpec(memory_space=pl.ANY)] * len(after)
+        + in_vmem(len(operands)),
         out_specs=in_vmem(len(out)),
         scratch_shapes=[pltpu.VMEM(shape, F32) for shape in scratch],
         compiler_params=pltpu.CompilerParams(vmem_limit_bytes=32 << 20),
-    )(*scalars, *operands)
+    )(*scalars, *after, *operands)
 
 
 def shards(queries, key_proj, value_proj, conv_out, filters, out_grad, out_weight):
@@ -222,7 +261,18 @@
         scratch=[(chan, rows)],
     )
 
-    wide = lax.all_gather(out_grad.T, "ch", axis=0, tiled=True)
+    features = lax.axis_size("ch")
+    turned_grad = out_grad.T
+    around = [turned_grad] + [
+        lax.ppermute(turned_grad, "ch", [(i, (i - hop) % features) for i in range(features)])
+        for hop in range(1, features)
+    ]
+    (wide,) = call(
+        arrange_kernel,
+        [((groups * feats, rows), BF16)],
+        (lax.axis_index("ch").reshape(1),),
+        *around,
+    )
     grads = jnp.concatenate([wide, to_core(wide)], 1)
     left = grads.reshape(groups, 2, feats // 2, CORES * rows).transpose(3, 1, 0, 2)
 
@@ -263,33 +313,38 @@
     own_half = jnp.where(odd, gated[:, half:], gated[:, :half])
     other_half = jnp.where(odd, gated[:, :half], gated[:, half:])
     both = jnp.concatenate([own_half, to_core(other_half)], 0)
-    block = groups * feats // ALONG_X
-    total, *away = call(
-        weight_kernel,
-        [((block, half), F32)] + [((block, half), BF16)] * (ALONG_X - 1),
-        (x_scalar,),
+    quads = along_z // 2
+    size = groups * feats // quads
+    own, *away = call(
+        partial_kernel,
+        [((size, half), F32)] + [((size, half), BF16)] * (quads - 1),
+        ((z_place // 2).reshape(1),),
         grads,
         both,
-    )
-    for hop, value in enumerate(away, 1):
-        total += send(value, hop, 0, 0).astype(F32)
-    quads = along_z // 2
-    total = total.reshape(quads, 2 * CORES * feats, half)
-    quad = z_place // 2
-    part = lax.dynamic_index_in_dim(total, quad, 0, keepdims=False)
-    for hop in range(1, quads):
-        value = lax.dynamic_index_in_dim(total, (quad + hop) % quads, 0, keepdims=False)
-        part += send(value.astype(BF16), 0, 2 * hop, 0).astype(F32)
-    part = part.reshape(2, CORES * feats, half)
-    upper = z_place % 2 == 1
+        after=(arrived,),
+    )
+    away = [send(value, 0, 2 * hop, 0) for hop, value in enumerate(away, 1)]
+    keep, give = call(
+        pairs_kernel,
+        [((size // 2, half), F32)] * 2,
+        ((z_place % 2).reshape(1),),
+        own,
+        *away,
+        after=(turned,),
+    )
     swap = [(i, i ^ CORES) for i in range(groups)]
-    part = jnp.where(upper, part[1], part[0]) + lax.ppermute(
-        jnp.where(upper, part[0], part[1]), "seq", swap
-    )
-    part = part.reshape(CORES, feats, half)
-    own = jnp.where(odd, part[1], part[0])
-    beside = to_core(jnp.where(odd, part[0], part[1]))
-    weight_grad = jnp.concatenate([jnp.where(odd, beside, own), jnp.where(odd, own, beside)], 1)
+    own, *away = call(
+        lines_kernel,
+        [((CORES * feats, half), F32)] * ALONG_X,
+        (x_scalar,),
+        keep,
+        lax.ppermute(give, "seq", swap),
+        after=(inner,),
+    )
+    away = [send(value, hop, 0, 0) for hop, value in enumerate(away, 1)]
+    keep, give = call(cores_kernel, [((feats, half), F32)] * 2, (odd_scalar,), own, *away)
+    give = to_core(give)
+    weight_grad = jnp.concatenate([jnp.where(odd, give, keep), jnp.where(odd, keep, give)], 1)
     weight_grad = weight_grad * (rows * groups) ** (-0.5)
     return (query_grad, key_grad, value_grad, weight_grad)
 

time: 114 us -> 116 us (1.018)
  blocking collectives: 12.7 us -> 0 us
  starting transfers between devices: 44.5 us -> 52.4 us
  waiting for transfers between devices: 41.7 us -> 44.9 us
  Pallas kernels: 6.74 us -> 9.41 us
  local copies, waits for them, and re-layouts: 3.76 us -> 5.96 us
    all_gather x1 -> x0, blocking collectives: 12.7 us -> none  [shards(): wide = lax.all_gather(out_grad.T, 'ch', axis=0, tiled=True)]
    ppermute x1 -> x4, waiting for transfers between devices: 0.01 us -> 8.69 us  [the longest x3 8.69 us: shards(): lax.ppermute(turned_grad, 'ch', [(i, (i - hop) % features) for i in range...]
    ppermute x13, waiting for transfers between devices: 23.9 us -> 15.8 us  [send(): return lax.ppermute(value, 'seq', pairs)]
    all_to_all x1, starting transfers between devices: 9.79 us -> 13.1 us  [shards(): arrived = lax.all_to_all(packed, 'seq', 0, 0)]
    ppermute x1 -> x4, starting transfers between devices: 0.84 us -> 3.95 us  [the longest x3 3.85 us: shards(): lax.ppermute(turned_grad, 'ch', [(i, (i - hop) % features) for i in range...]
    all_to_all x2, starting transfers between devices: 11.4 us -> 14.3 us  [exchange(): lax.all_to_all(blocks.reshape(groups, chans, rows), 'seq', 0, 0)]
    pallas_call x7 -> x11, Pallas kernels: 6.74 us -> 9.41 us  [call(): pl.pallas_call(kernel, out_shape=[jax.ShapeDtypeStruct(shape, dtype) for...]
    add x3 -> x0, other arithmetic: 2.1 us -> none  [the longest x1 1.21 us: shards(): total += send(value, hop, 0, 0).astype(F32)]
  transfers between devices with their start and end apart: 17 -> 20, of which waited for: 9 -> 12; matrix products, arithmetic and copies ran while one was open for 4% -> 4% of each run, Pallas kernels for 5% -> 6%
where the time goes in v4:
time: 116 us; the launch traced here: 115 us
  starting transfers between devices  52.4 us (45%)
  waiting for transfers between devices  44.9 us (39%)
  Pallas kernels  9.41 us (8%)
  local copies, waits for them, and re-layouts  5.96 us (5%)
  other arithmetic  1.86 us (2%)
    ppermute x13, starting transfers between devices, send(): return lax.ppermute(value, 'seq', pairs)  21.1 us
    all_to_all x2, waiting for transfers between devices, exchange(): lax.all_to_all(blocks.reshape(groups, chans, rows), 'seq', 0, 0)  19.3 us
    ppermute x13, waiting for transfers between devices, send(): return lax.ppermute(value, 'seq', pairs)  15.8 us
    all_to_all x2, starting transfers between devices, exchange(): lax.all_to_all(blocks.reshape(groups, chans, rows), 'seq', 0, 0)  14.3 us
    all_to_all x1, starting transfers between devices, shards(): arrived = lax.all_to_all(packed, 'seq', 0, 0)  13.1 us
    pallas_call x11, Pallas kernels, call(): pl.pallas_call(kernel, out_shape=[jax.ShapeDtypeStruct(shape, dtype) for...  9.41 us
    ppermute x3, waiting for transfers between devices, shards(): lax.ppermute(turned_grad, 'ch', [(i, (i - hop) % features) for i in range...  8.69 us
    ppermute x3, starting transfers between devices, shards(): lax.ppermute(turned_grad, 'ch', [(i, (i - hop) % features) for i in range...  3.85 us
  transfers between devices with their start and end apart: 20, of which 12 were waited for; matrix products, arithmetic and copies ran while one was open for 4% of the time, Pallas kernels for 6%

profile of v4, /device:TPU:1, one launch (start us, length us, event | category | flops | bytes accessed | tf_op | source)
XLA Modules:
  0.0 115.5 jit_solution(4127811684016216389)
XLA Ops:
  2.3 0.9 shard_map.184
  3.2 13.1 %all-to-all-start = ((bf16[64,24,128]{2,1,0:T(8,128)(2,1)}), bf16[64,24,128]{2,1,0:T(8,128)(2,1)S(1)}, u32[]{:S(2)}, u32[]{:S(2)}) async-start(bf16[64,24,128]{2,1,0:T(8,128)(2,1)} %shard_map.184), calls=%async_computation | async-start | bytes 786432 | tf_op jit(solution)/shard_map/all_to_all | solution.py:250
  16.5 2.8 %collective-permute-start = (bf16[512,128]{1,0:T(8,128)(2,1)S(1)}, bf16[512,128]{1,0:T(8,128)(2,1)S(1)}, u32[]{:S(2)}, u32[]{:S(2)}) collective-permute-start(bf16[512,128]{1,0:T(8,128)(2,1)S(1)} %bitcast.24), channel_id=1, source_target_pairs={{0,3},{1,0},{2,1},{3,2},{4,7},{5,4},{6,5},{7,6},{8,11},{9,8},{10,9... | collective-permute-start | bytes 393224 | tf_op jit(solution)/shard_map/ppermute | solution.py:267
  20.3 4.1 %collective-permute-done.refs_1_ = bf16[512,128]{1,0:T(8,128)(2,1)S(1)} collective-permute-done((bf16[512,128]{1,0:T(8,128)(2,1)S(1)}, bf16[512,128]{1,0:T(8,128)(2,1)S(1)}, u32[]{:S(2)}, u32[]{:S(2)}) %collective-permute-start) | collective-permute-done | bytes 131104 | tf_op jit(solution)/shard_map/ppermute | solution.py:267
  25.1 3.9 %collective-permute-done.2.refs_3_ = bf16[512,128]{1,0:T(8,128)(2,1)S(1)} collective-permute-done((bf16[512,128]{1,0:T(8,128)(2,1)S(1)}, bf16[512,128]{1,0:T(8,128)(2,1)S(1)}, u32[]{:S(2)}, u32[]{:S(2)}) %collective-permute-start.2) | collective-permute-done | bytes 131104 | tf_op jit(solution)/shard_map/ppermute | solution.py:267
  29.9 1.1 all-to-all-done.after_ref
  31.0 1.2 %collective-permute-start.4 = (bf16[1024,128]{1,0:T(8,128)(2,1)S(1)}, bf16[1024,128]{1,0:T(8,128)(2,1)S(1)}, u32[]{:S(2)}, u32[]{:S(2)}) collective-permute-start(bf16[1024,128]{1,0:T(8,128)(2,1)S(1)} %bitcast.18), channel_id=1, source_target_pairs={{0,64},{4,68},{8,72},{12,76},{16,80},{20,84},{24,88},{28,92},{32,9... | collective-permute-start | bytes 786440 | tf_op jit(solution)/shard_map/ppermute | solution.py:236
  32.2 2.7 %collective-permute-start.5 = (bf16[1024,128]{1,0:T(8,128)(2,1)S(1)}, bf16[1024,128]{1,0:T(8,128)(2,1)S(1)}, u32[]{:S(2)}, u32[]{:S(2)}) collective-permute-start(bf16[1024,128]{1,0:T(8,128)(2,1)S(1)} %bitcast.19), channel_id=1, source_target_pairs={{0,128},{4,132},{8,136},{12,140},{16,144},{20,148},{24,152},{28,15... | collective-permute-start | bytes 786440 | tf_op jit(solution)/shard_map/ppermute | solution.py:236
  34.9 1.1 collective-permute-start.6
  36.0 1.2 %pad_maximum_fusion.grads_ref = bf16[2048,256]{1,0:T(8,128)(2,1)S(1)} fusion(bf16[2048,128]{1,0:T(8,128)(2,1)} %collective-permute-done.3, bf16[2048,128]{1,0:T(8,128)(2,1)S(1)} %shard_map.183), kind=kLoop, calls=%fused_computation | loop fusion | flops 2097152 | bytes 2097152 | tf_op jit(solution)/shard_map/concatenate | solution.py:276
  37.1 1.2 %shard_map.190 = (f32[512,256]{1,0:T(8,128)S(1)}, bf16[512,256]{1,0:T(8,128)(2,1)}, bf16[512,256]{1,0:T(8,128)(2,1)}, bf16[512,256]{1,0:T(8,128)(2,1)}) custom-call(s32[1]{0:T(128)} %bitcast.14.quad_ref, bf16[64,24,128]{2,1,0:T(8,128)(2,1)S(1)} %all-to-all-done.after_ref, bf16[2048,256]{1,0:T(8,128)(2,1)S(1)} %pad_maximum_fusion.grads_ref, ...), custom_call_target="tpu_custom_call" | custom-call | tf_op jit(solution)/shard_map/pallas_call | solution.py:200
  38.3 1.3 %collective-permute-start.9 = (bf16[512,256]{1,0:T(8,128)(2,1)}, bf16[512,256]{1,0:T(8,128)(2,1)S(1)}, u32[]{:S(2)}, u32[]{:S(2)}) collective-permute-start(bf16[512,256]{1,0:T(8,128)(2,1)} %get-tuple-element.29), channel_id=1, source_target_pairs={{0,16},{4,20},{8,24},{12,28},{16,32},{20,36},{24,40},{28,44},{32,4... | collective-permute-start | bytes 786440 | tf_op jit(solution)/shard_map/ppermute | solution.py:236
  39.6 3.4 %collective-permute-start.10 = (bf16[512,256]{1,0:T(8,128)(2,1)}, bf16[512,256]{1,0:T(8,128)(2,1)}, u32[]{:S(2)}, u32[]{:S(2)}) collective-permute-start(bf16[512,256]{1,0:T(8,128)(2,1)} %get-tuple-element.30), channel_id=1, source_target_pairs={{0,32},{4,36},{8,40},{12,44},{16,48},{20,52},{24,56},{28,60},{32,0... | collective-permute-start | bytes 786440 | tf_op jit(solution)/shard_map/ppermute | solution.py:236
  43.0 3.3 %collective-permute-start.11 = (bf16[512,256]{1,0:T(8,128)(2,1)}, bf16[512,256]{1,0:T(8,128)(2,1)}, u32[]{:S(2)}, u32[]{:S(2)}) collective-permute-start(bf16[512,256]{1,0:T(8,128)(2,1)} %get-tuple-element.31), channel_id=1, source_target_pairs={{0,48},{4,52},{8,56},{12,60},{16,0},{20,4},{24,8},{28,12},{32,16},... | collective-permute-start | bytes 786440 | tf_op jit(solution)/shard_map/ppermute | solution.py:236
  46.2 1.1 copy.23
  47.3 1.5 %copy.24.left_ref = bf16[256,2048]{1,0:T(8,128)(2,1)S(1)} copy(bf16[256,2048]{0,1:T(8,128)(2,1)} %bitcast.28) | data formatting | bytes 2097152 | tf_op jit(solution)/shard_map/reshape | solution.py:283
  48.8 1.6 %shard_map.185 = (f32[128,256]{1,0:T(8,128)S(1)}, f32[128,256]{1,0:T(8,128)}) custom-call(s32[1]{0:T(128)} %bitcast.1.x_ref, bf16[256,2048]{1,0:T(8,128)(2,1)S(1)} %copy.24.left_ref, bf16[1024,128]{1,0:T(8,128)(2,1)S(1)} %bitcast.21, bf16[1024,128]{1,0:T(8,128)(2,1)S(1)} %collective-permute-done.4.w1_ref, ...), custom_call_target="tpu_custom_call" | custom-call | tf_op jit(solution)/shard_map/pallas_call | solution.py:200
  51.1 2.1 %collective-permute-start.7 = (f32[128,256]{1,0:T(8,128)}, f32[128,256]{1,0:T(8,128)S(1)}, u32[]{:S(2)}, u32[]{:S(2)}) collective-permute-start(f32[128,256]{1,0:T(8,128)} %get-tuple-element.23), channel_id=1, source_target_pairs={{0,4},{4,0},{8,12},{12,8},{16,20},{20,16},{24,28},{28,24},{32,36},... | collective-permute-start | bytes 393224 | tf_op jit(solution)/shard_map/ppermute | solution.py:236
  53.2 1.2 %collective-permute-done.7.theirs_ref = f32[128,256]{1,0:T(8,128)S(1)} collective-permute-done((f32[128,256]{1,0:T(8,128)}, f32[128,256]{1,0:T(8,128)S(1)}, u32[]{:S(2)}, u32[]{:S(2)}) %collective-permute-start.7) | collective-permute-done | bytes 131104 | tf_op jit(solution)/shard_map/ppermute | solution.py:236
  54.4 0.9 copy-done.10
  56.1 3.6 %collective-permute-done.10.b_ref = bf16[512,256]{1,0:T(8,128)(2,1)} collective-permute-done((bf16[512,256]{1,0:T(8,128)(2,1)}, bf16[512,256]{1,0:T(8,128)(2,1)}, u32[]{:S(2)}, u32[]{:S(2)}) %collective-permute-start.10) | collective-permute-done | bytes 262176 | tf_op jit(solution)/shard_map/ppermute | solution.py:236
  59.7 8.5 %collective-permute-done.11.c_ref = bf16[512,256]{1,0:T(8,128)(2,1)} collective-permute-done((bf16[512,256]{1,0:T(8,128)(2,1)}, bf16[512,256]{1,0:T(8,128)(2,1)}, u32[]{:S(2)}, u32[]{:S(2)}) %collective-permute-start.11) | collective-permute-done | bytes 262176 | tf_op jit(solution)/shard_map/ppermute | solution.py:236
  68.2 1.2 shard_map.191
  69.5 8.4 %all-to-all-start.1 = ((bf16[64,8,128]{2,1,0:T(8,128)(2,1)}), bf16[64,8,128]{2,1,0:T(8,128)(2,1)S(1)}, u32[]{:S(2)}, u32[]{:S(2)}) async-start(bf16[64,8,128]{2,1,0:T(8,128)(2,1)} %bitcast.8), calls=%async_computation.1 | async-start | bytes 262144 | tf_op jit(solution)/shard_map/all_to_all | solution.py:247
  78.6 9.6 %all-to-all-done.1 = bf16[64,8,128]{2,1,0:T(8,128)(2,1)S(1)} async-done(((bf16[64,8,128]{2,1,0:T(8,128)(2,1)}), bf16[64,8,128]{2,1,0:T(8,128)(2,1)S(1)}, u32[]{:S(2)}, u32[]{:S(2)}) %all-to-all-start.1) | async-done | bytes 131104 | tf_op jit(solution)/shard_map/all_to_all | solution.py:247
  88.3 2.2 %shard_map.188.after_ref = bf16[512,128]{1,0:T(8,128)(2,1)} custom-call(bf16[512,128]{1,0:T(8,128)(2,1)S(1)} %bitcast.23, f32[576,256]{1,0:T(8,128)S(1)} %shard_map.187.filt_ref, bf16[2,144,64]{2,1,0:T(8,128)(2,1)S(1)} %copy-done.3, f32[2,72,128]{2,1,0:T(8,128)S(1)} %copy-done.4, bf16[2,256,256]{2,1,0:T(8,128)(2,1)S(1)} %copy-done, ...), custom_call_target="tpu_custom_call" | custom-call | tf_op jit(solution)/shard_map/pallas_call | solution.py:200
  91.0 2.1 %collective-permute-start.14 = (f32[64,256]{1,0:T(8,128)S(1)}, f32[64,256]{1,0:T(8,128)S(1)}, u32[]{:S(2)}, u32[]{:S(2)}) collective-permute-start(f32[64,256]{1,0:T(8,128)S(1)} %get-tuple-element.36), channel_id=1, source_target_pairs={{0,128},{4,132},{8,136},{12,140},{16,144},{20,148},{24,152},{28,15... | collective-permute-start | bytes 196616 | tf_op jit(solution)/shard_map/ppermute | solution.py:236
  93.1 1.2 %collective-permute-start.15 = (f32[64,256]{1,0:T(8,128)S(1)}, f32[64,256]{1,0:T(8,128)S(1)}, u32[]{:S(2)}, u32[]{:S(2)}) collective-permute-start(f32[64,256]{1,0:T(8,128)S(1)} %get-tuple-element.37), channel_id=1, source_target_pairs={{0,192},{4,196},{8,200},{12,204},{16,208},{20,212},{24,216},{28,22... | collective-permute-start | bytes 196616 | tf_op jit(solution)/shard_map/ppermute | solution.py:236
  94.9 1.7 %collective-permute-done.14.b_ref = f32[64,256]{1,0:T(8,128)S(1)} collective-permute-done((f32[64,256]{1,0:T(8,128)S(1)}, f32[64,256]{1,0:T(8,128)S(1)}, u32[]{:S(2)}, u32[]{:S(2)}) %collective-permute-start.14) | collective-permute-done | bytes 65568 | tf_op jit(solution)/shard_map/ppermute | solution.py:236
  96.8 1.6 %collective-permute-start.16 = (f32[32,256]{1,0:T(8,128)S(1)}, f32[32,256]{1,0:T(8,128)S(1)}, u32[]{:S(2)}, u32[]{:S(2)}) collective-permute-start(f32[32,256]{1,0:T(8,128)S(1)} %get-tuple-element.38), channel_id=1, source_target_pairs={{0,4},{4,0},{8,12},{12,8},{16,20},{20,16},{24,28},{28,24},{32,36},... | collective-permute-start | bytes 98312 | tf_op jit(solution)/shard_map/ppermute | solution.py:236
  98.4 5.8 %all-to-all-start.2 = ((bf16[64,8,128]{2,1,0:T(8,128)(2,1)}), bf16[64,8,128]{2,1,0:T(8,128)(2,1)S(1)}, u32[]{:S(2)}, u32[]{:S(2)}) async-start(bf16[64,8,128]{2,1,0:T(8,128)(2,1)} %bitcast.11), calls=%async_computation.2 | async-start | bytes 262144 | tf_op jit(solution)/shard_map/all_to_all | solution.py:247
  104.9 9.7 %all-to-all-done.2 = bf16[64,8,128]{2,1,0:T(8,128)(2,1)S(1)} async-done(((bf16[64,8,128]{2,1,0:T(8,128)(2,1)}), bf16[64,8,128]{2,1,0:T(8,128)(2,1)S(1)}, u32[]{:S(2)}, u32[]{:S(2)}) %all-to-all-start.2) | async-done | bytes 131104 | tf_op jit(solution)/shard_map/all_to_all | solution.py:247
  (58 shorter events, 9.4 us)
Async XLA Ops:
  0.6 0.9 copy-start.6
  2.3 14.0 %copy-start.13 = (bf16[128,512]{1,0:T(8,128)(2,1)S(1)}, bf16[128,512]{1,0:T(8,128)(2,1)}, u32[]{:S(2)}) copy-start(bf16[128,512]{1,0:T(8,128)(2,1)} %param.21) | copy-start | bytes 393220
  3.2 26.4 %copy-start.1 = (bf16[128,512]{1,0:T(8,128)(2,1)S(1)}, bf16[128,512]{1,0:T(8,128)(2,1)}, u32[]{:S(2)}) copy-start(bf16[128,512]{1,0:T(8,128)(2,1)} %queries_ref.1) | copy-start | bytes 393220
  3.2 26.4 %copy-start.2 = (bf16[128,512]{1,0:T(8,128)(2,1)S(1)}, bf16[128,512]{1,0:T(8,128)(2,1)}, u32[]{:S(2)}) copy-start(bf16[128,512]{1,0:T(8,128)(2,1)} %conv_ref.1) | copy-start | bytes 393220
  3.2 27.7 %all-to-all-start = ((bf16[64,24,128]{2,1,0:T(8,128)(2,1)}), bf16[64,24,128]{2,1,0:T(8,128)(2,1)S(1)}, u32[]{:S(2)}, u32[]{:S(2)}) async-start(bf16[64,24,128]{2,1,0:T(8,128)(2,1)} %shard_map.184), calls=%async_computation | async-start | bytes 786432 | tf_op jit(solution)/shard_map/all_to_all | solution.py:250
  16.5 7.9 %collective-permute-start = (bf16[512,128]{1,0:T(8,128)(2,1)S(1)}, bf16[512,128]{1,0:T(8,128)(2,1)S(1)}, u32[]{:S(2)}, u32[]{:S(2)}) collective-permute-start(bf16[512,128]{1,0:T(8,128)(2,1)S(1)} %bitcast.24), channel_id=1, source_target_pairs={{0,3},{1,0},{2,1},{3,2},{4,7},{5,4},{6,5},{7,6},{8,11},{9,8},{10,9... | collective-permute-start | bytes 393224 | tf_op jit(solution)/shard_map/ppermute | solution.py:267
  19.3 5.8 %collective-permute-start.1 = (bf16[512,128]{1,0:T(8,128)(2,1)S(1)}, bf16[512,128]{1,0:T(8,128)(2,1)S(1)}, u32[]{:S(2)}, u32[]{:S(2)}) collective-permute-start(bf16[512,128]{1,0:T(8,128)(2,1)S(1)} %bitcast.25), channel_id=1, source_target_pairs={{0,2},{1,3},{2,0},{3,1},{4,6},{5,7},{6,4},{7,5},{8,10},{9,11},{10,... | collective-permute-start | bytes 393224 | tf_op jit(solution)/shard_map/ppermute | solution.py:267
  19.6 9.4 %collective-permute-start.2 = (bf16[512,128]{1,0:T(8,128)(2,1)S(1)}, bf16[512,128]{1,0:T(8,128)(2,1)S(1)}, u32[]{:S(2)}, u32[]{:S(2)}) collective-permute-start(bf16[512,128]{1,0:T(8,128)(2,1)S(1)} %bitcast.26), channel_id=1, source_target_pairs={{0,1},{1,2},{2,3},{3,0},{4,5},{5,6},{6,7},{7,4},{8,9},{9,10},{10,1... | collective-permute-start | bytes 393224 | tf_op jit(solution)/shard_map/ppermute | solution.py:267
  29.1 6.9 %collective-permute-start.3 = (bf16[2048,128]{1,0:T(8,128)(2,1)S(1)}, bf16[2048,128]{1,0:T(8,128)(2,1)}, u32[]{:S(2)}, u32[]{:S(2)}) collective-permute-start(bf16[2048,128]{1,0:T(8,128)(2,1)S(1)} %shard_map.183), channel_id=1, source_target_pairs={{0,4},{4,0},{8,12},{12,8},{16,20},{20,16},{24,28},{28,24},{32,36},... | collective-permute-start | bytes 1572872 | tf_op jit(solution)/shard_map/ppermute | solution.py:236
  29.7 2.5 %collective-permute-start.8 = (bf16[128,256]{1,0:T(8,128)(2,1)S(1)}, bf16[128,256]{1,0:T(8,128)(2,1)S(1)}, u32[]{:S(2)}, u32[]{:S(2)}) collective-permute-start(bf16[128,256]{1,0:T(8,128)(2,1)S(1)} %get-tuple-element.41), channel_id=1, source_target_pairs={{0,4},{4,0},{8,12},{12,8},{16,20},{20,16},{24,28},{28,24},{32,36},... | collective-permute-start | bytes 196616 | tf_op jit(solution)/shard_map/ppermute | solution.py:236
  31.0 12.0 %collective-permute-start.4 = (bf16[1024,128]{1,0:T(8,128)(2,1)S(1)}, bf16[1024,128]{1,0:T(8,128)(2,1)S(1)}, u32[]{:S(2)}, u32[]{:S(2)}) collective-permute-start(bf16[1024,128]{1,0:T(8,128)(2,1)S(1)} %bitcast.18), channel_id=1, source_target_pairs={{0,64},{4,68},{8,72},{12,76},{16,80},{20,84},{24,88},{28,92},{32,9... | collective-permute-start | bytes 786440 | tf_op jit(solution)/shard_map/ppermute | solution.py:236
  32.2 16.6 %collective-permute-start.5 = (bf16[1024,128]{1,0:T(8,128)(2,1)S(1)}, bf16[1024,128]{1,0:T(8,128)(2,1)S(1)}, u32[]{:S(2)}, u32[]{:S(2)}) collective-permute-start(bf16[1024,128]{1,0:T(8,128)(2,1)S(1)} %bitcast.19), channel_id=1, source_target_pairs={{0,128},{4,132},{8,136},{12,140},{16,144},{20,148},{24,152},{28,15... | collective-permute-start | bytes 786440 | tf_op jit(solution)/shard_map/ppermute | solution.py:236
  34.9 13.9 %collective-permute-start.6 = (bf16[1024,128]{1,0:T(8,128)(2,1)S(1)}, bf16[1024,128]{1,0:T(8,128)(2,1)S(1)}, u32[]{:S(2)}, u32[]{:S(2)}) collective-permute-start(bf16[1024,128]{1,0:T(8,128)(2,1)S(1)} %bitcast.20), channel_id=1, source_target_pairs={{0,192},{4,196},{8,200},{12,204},{16,208},{20,212},{24,216},{28,22... | collective-permute-start | bytes 786440 | tf_op jit(solution)/shard_map/ppermute | solution.py:236
  38.3 17.7 %collective-permute-start.9 = (bf16[512,256]{1,0:T(8,128)(2,1)}, bf16[512,256]{1,0:T(8,128)(2,1)S(1)}, u32[]{:S(2)}, u32[]{:S(2)}) collective-permute-start(bf16[512,256]{1,0:T(8,128)(2,1)} %get-tuple-element.29), channel_id=1, source_target_pairs={{0,16},{4,20},{8,24},{12,28},{16,32},{20,36},{24,40},{28,44},{32,4... | collective-permute-start | bytes 786440 | tf_op jit(solution)/shard_map/ppermute | solution.py:236
  39.6 20.0 %collective-permute-start.10 = (bf16[512,256]{1,0:T(8,128)(2,1)}, bf16[512,256]{1,0:T(8,128)(2,1)}, u32[]{:S(2)}, u32[]{:S(2)}) collective-permute-start(bf16[512,256]{1,0:T(8,128)(2,1)} %get-tuple-element.30), channel_id=1, source_target_pairs={{0,32},{4,36},{8,40},{12,44},{16,48},{20,52},{24,56},{28,60},{32,0... | collective-permute-start | bytes 786440 | tf_op jit(solution)/shard_map/ppermute | solution.py:236
  43.0 25.2 %collective-permute-start.11 = (bf16[512,256]{1,0:T(8,128)(2,1)}, bf16[512,256]{1,0:T(8,128)(2,1)}, u32[]{:S(2)}, u32[]{:S(2)}) collective-permute-start(bf16[512,256]{1,0:T(8,128)(2,1)} %get-tuple-element.31), channel_id=1, source_target_pairs={{0,48},{4,52},{8,56},{12,60},{16,0},{20,4},{24,8},{28,12},{32,16},... | collective-permute-start | bytes 786440 | tf_op jit(solution)/shard_map/ppermute | solution.py:236
  51.1 3.3 %collective-permute-start.7 = (f32[128,256]{1,0:T(8,128)}, f32[128,256]{1,0:T(8,128)S(1)}, u32[]{:S(2)}, u32[]{:S(2)}) collective-permute-start(f32[128,256]{1,0:T(8,128)} %get-tuple-element.23), channel_id=1, source_target_pairs={{0,4},{4,0},{8,12},{12,8},{16,20},{20,16},{24,28},{28,24},{32,36},... | collective-permute-start | bytes 393224 | tf_op jit(solution)/shard_map/ppermute | solution.py:236
  54.4 0.9 copy-start.10
  56.1 21.9 %copy-start = (bf16[2,256,256]{2,1,0:T(8,128)(2,1)S(1)}, bf16[2,256,256]{2,1,0:T(8,128)(2,1)}, u32[]{:S(2)}) copy-start(bf16[2,256,256]{2,1,0:T(8,128)(2,1)} %constant.101.second_ref) | copy-start | bytes 786436
  56.1 21.9 %copy-start.3 = (bf16[2,144,64]{2,1,0:T(8,128)(2,1)S(1)}, bf16[2,144,64]{2,1,0:T(8,128)(2,1)}, u32[]{:S(2)}) copy-start(bf16[2,144,64]{2,1,0:T(8,128)(2,1)} %constant.98.first_ref) | copy-start | bytes 110596
  56.1 21.9 %copy-start.4 = (f32[2,72,128]{2,1,0:T(8,128)S(1)}, f32[2,72,128]{2,1,0:T(8,128)}, u32[]{:S(2)}) copy-start(f32[2,72,128]{2,1,0:T(8,128)} %constant.94.clone.twist_ref) | copy-start | bytes 221188
  69.3 18.9 %copy-start.5 = (bf16[2,256,256]{2,1,0:T(8,128)(2,1)S(1)}, bf16[2,256,256]{2,1,0:T(8,128)(2,1)}, u32[]{:S(2)}) copy-start(bf16[2,256,256]{2,1,0:T(8,128)(2,1)} %constant.104.back_ref) | copy-start | bytes 786436
  69.3 18.9 %copy-start.11 = (bf16[2,64,144]{2,1,0:T(8,128)(2,1)S(1)}, bf16[2,64,144]{2,1,0:T(8,128)(2,1)}, u32[]{:S(2)}) copy-start(bf16[2,64,144]{2,1,0:T(8,128)(2,1)} %constant.107.last_ref) | copy-start | bytes 110596
  69.4 21.1 %collective-permute-start.12 = (f32[256,256]{1,0:T(8,128)S(1)}, f32[256,256]{1,0:T(8,128)S(1)}, u32[]{:S(2)}, u32[]{:S(2)}) collective-permute-start(f32[256,256]{1,0:T(8,128)S(1)} %get-tuple-element.33), channel_id=1, source_target_pairs={{0,8},{4,12},{8,0},{12,4},{16,24},{20,28},{24,16},{28,20},{32,40},... | collective-permute-start | bytes 786440 | tf_op jit(solution)/shard_map/ppermute | solution.py:341
  69.5 18.8 %all-to-all-start.1 = ((bf16[64,8,128]{2,1,0:T(8,128)(2,1)}), bf16[64,8,128]{2,1,0:T(8,128)(2,1)S(1)}, u32[]{:S(2)}, u32[]{:S(2)}) async-start(bf16[64,8,128]{2,1,0:T(8,128)(2,1)} %bitcast.8), calls=%async_computation.1 | async-start | bytes 262144 | tf_op jit(solution)/shard_map/all_to_all | solution.py:247
  90.5 24.1 %copy-start.7 = (bf16[128,512]{1,0:T(8,128)(2,1)S(1)}, bf16[128,512]{1,0:T(8,128)(2,1)}, u32[]{:S(2)}) copy-start(bf16[128,512]{1,0:T(8,128)(2,1)} %key_ref.1) | copy-start | bytes 393220
  90.5 24.1 %copy-start.8 = (bf16[128,512]{1,0:T(8,128)(2,1)S(1)}, bf16[128,512]{1,0:T(8,128)(2,1)}, u32[]{:S(2)}) copy-start(bf16[128,512]{1,0:T(8,128)(2,1)} %value_ref.1) | copy-start | bytes 393220
  90.5 4.4 %collective-permute-start.13 = (f32[64,256]{1,0:T(8,128)S(1)}, f32[64,256]{1,0:T(8,128)S(1)}, u32[]{:S(2)}, u32[]{:S(2)}) collective-permute-start(f32[64,256]{1,0:T(8,128)S(1)} %get-tuple-element.35), channel_id=1, source_target_pairs={{0,64},{4,68},{8,72},{12,76},{16,80},{20,84},{24,88},{28,92},{32,9... | collective-permute-start | bytes 196616 | tf_op jit(solution)/shard_map/ppermute | solution.py:236
  91.0 5.6 %collective-permute-start.14 = (f32[64,256]{1,0:T(8,128)S(1)}, f32[64,256]{1,0:T(8,128)S(1)}, u32[]{:S(2)}, u32[]{:S(2)}) collective-permute-start(f32[64,256]{1,0:T(8,128)S(1)} %get-tuple-element.36), channel_id=1, source_target_pairs={{0,128},{4,132},{8,136},{12,140},{16,144},{20,148},{24,152},{28,15... | collective-permute-start | bytes 196616 | tf_op jit(solution)/shard_map/ppermute | solution.py:236
  93.1 3.7 %collective-permute-start.15 = (f32[64,256]{1,0:T(8,128)S(1)}, f32[64,256]{1,0:T(8,128)S(1)}, u32[]{:S(2)}, u32[]{:S(2)}) collective-permute-start(f32[64,256]{1,0:T(8,128)S(1)} %get-tuple-element.37), channel_id=1, source_target_pairs={{0,192},{4,196},{8,200},{12,204},{16,208},{20,212},{24,216},{28,22... | collective-permute-start | bytes 196616 | tf_op jit(solution)/shard_map/ppermute | solution.py:236
  96.8 7.5 %collective-permute-start.16 = (f32[32,256]{1,0:T(8,128)S(1)}, f32[32,256]{1,0:T(8,128)S(1)}, u32[]{:S(2)}, u32[]{:S(2)}) collective-permute-start(f32[32,256]{1,0:T(8,128)S(1)} %get-tuple-element.38), channel_id=1, source_target_pairs={{0,4},{4,0},{8,12},{12,8},{16,20},{20,16},{24,28},{28,24},{32,36},... | collective-permute-start | bytes 98312 | tf_op jit(solution)/shard_map/ppermute | solution.py:236
  98.4 16.2 %all-to-all-start.2 = ((bf16[64,8,128]{2,1,0:T(8,128)(2,1)}), bf16[64,8,128]{2,1,0:T(8,128)(2,1)S(1)}, u32[]{:S(2)}, u32[]{:S(2)}) async-start(bf16[64,8,128]{2,1,0:T(8,128)(2,1)} %bitcast.11), calls=%async_computation.2 | async-start | bytes 262144 | tf_op jit(solution)/shard_map/all_to_all | solution.py:247
  (2 other events, 1.4 us)

commit v5 on v3

v5 whole, which is shorter than its diff:
```python
import functools

import jax
import jax.numpy as jnp
import numpy as np
from jax import lax
from jax.experimental import pallas as pl
from jax.experimental.pallas import tpu as pltpu
from jax.sharding import PartitionSpec as P

BF16 = jnp.bfloat16
F32 = jnp.float32

CORES = 2
ALONG_X = 4
CHIPS = 32


def dft_tables(blocks, rows, kept):
    period = 2 * blocks
    length = period * rows
    k1 = np.arange(kept)[:, None]
    used = k1 <= blocks
    angle = 2 * np.pi * ((k1 * np.arange(blocks)[None]) % period) / period
    first = np.concatenate([used * np.cos(angle), used * -np.sin(angle)], 0)
    weight = used * np.where((k1 == 0) | (k1 == blocks), 1.0, 2.0) / length
    last = np.concatenate([(weight * np.cos(angle)).T, -(weight * np.sin(angle)).T], 1)
    turn = 2 * np.pi * (k1 * np.arange(rows)[None]) / length
    twist = np.stack([np.cos(turn), -np.sin(turn)])
    angle = 2 * np.pi * ((np.arange(rows)[:, None] * np.arange(rows)[None]) % rows) / rows
    cos, sin = np.cos(angle), np.sin(angle)
    second = np.block([[cos, -sin], [sin, cos]])
    return first, twist, second, last


def halves(table):
    high = table.astype(BF16)
    low = (table - high.astype(np.float64)).astype(BF16)
    return high, low


def split(value):
    high = value.astype(BF16)
    return high, (value - high.astype(F32)).astype(BF16)


def dot(a, b):
    return jnp.dot(a, b, preferred_element_type=F32)


def dot3(a, b):
    return dot(a[0], b[0]) + (dot(a[0], b[1]) + dot(a[1], b[0]))


def spectrum(data, first_ref, twist_ref, second_ref, chans, rows, kept):
    bins = dot(first_ref[0], data) + dot(first_ref[1], data)
    cos, sin = twist_ref[0], twist_ref[1]
    parts = []
    for c in range(chans):
        re = bins[:kept, c * rows : (c + 1) * rows]
        im = bins[kept:, c * rows : (c + 1) * rows]
        parts.append(jnp.concatenate([re * cos - im * sin, re * sin + im * cos], 1))
    return dot3(split(jnp.concatenate(parts, 0)), (second_ref[0], second_ref[1]))


def filter_kernel(sizes, x_ref, first_ref, twist_ref, second_ref, out_ref, plane):
    chips, chans, rows, kept = sizes
    plane[...] = x_ref[...].astype(F32)
    data = jnp.concatenate(
        [
            jnp.concatenate(
                [
                    plane[pl.ds(core * chans + c, chips, stride=CORES * chans), :]
                    for core in range(CORES)
                ],
                0,
            )
            for c in range(chans)
        ],
        1,
    ).astype(BF16)
    out_ref[...] = spectrum(data, first_ref, twist_ref, second_ref, chans, rows, kept)


def correlate_kernel(sizes, *refs):
    x_ref, filt_ref, first_ref, twist_ref, second_ref, back_ref, last_ref = refs[:7]
    kept_ref, *came_refs, out_ref, wide, plane = refs[7:]
    chips, chans, rows, kept = sizes
    for core in range(CORES):
        wide[core] = x_ref[:, core * rows : (core + 1) * rows].astype(F32)
    data = jnp.concatenate(
        [
            jnp.concatenate(
                [wide[core, pl.ds(c, chips, stride=chans), :] for core in range(CORES)], 0
            )
            for c in range(chans)
        ],
        1,
    ).astype(BF16)
    grads = spectrum(data, first_ref, twist_ref, second_ref, chans, rows, kept)
    g_re, g_im = grads[:, :rows], grads[:, rows:]
    f_re, f_im = filt_ref[:, :rows], filt_ref[:, rows:]
    product = jnp.concatenate([g_re * f_re + g_im * f_im, g_im * f_re - g_re * f_im], 1)
    bins = dot3(split(product), (back_ref[0], back_ref[1]))
    cos, sin = twist_ref[0], twist_ref[1]
    parts = []
    for c in range(chans):
        re = bins[c * kept : (c + 1) * kept, :rows]
        im = bins[c * kept : (c + 1) * kept, rows:]
        parts.append(jnp.concatenate([re * cos + im * sin, im * cos - re * sin], 0))
    inner = dot3((last_ref[0], last_ref[1]), split(jnp.concatenate(parts, 1)))
    for c in range(chans):
        for core in range(CORES):
            plane[pl.ds(core * chans + c, chips, stride=CORES * chans), :] = inner[
                core * chips : (core + 1) * chips, c * rows : (c + 1) * rows
            ]
    groups, depth, _ = out_ref.shape
    came = jnp.concatenate([ref[...] for ref in came_refs], 0)
    total = (kept_ref[...] + came.astype(F32)).astype(BF16)
    out_ref[:, : depth - chans, :] = total.reshape(groups, depth - chans, rows)
    out_ref[:, depth - chans :, :] = plane[...].astype(BF16).reshape(groups, chans, rows)


def pack_kernel(filters_ref, weight_ref, out_ref):
    groups, _, rows = out_ref.shape
    chan = filters_ref.shape[1]
    chans = chan // groups
    feats = weight_ref.shape[0]
    part = chan // (ALONG_X * CORES)
    turned = filters_ref[...].astype(F32).T.reshape(CORES, groups // CORES, chans, rows)
    turned = jnp.swapaxes(turned, 0, 1).reshape(groups, chans, rows)
    out_ref[:, feats // 2 :, :] = turned.astype(BF16)
    weight = weight_ref[...].astype(F32)
    for x in range(ALONG_X):
        for core in range(CORES):
            start = (core * ALONG_X + x) * part
            piece = weight[:, start : start + part]
            folded = jnp.concatenate([piece[: feats // 2], piece[feats // 2 :]], 1).astype(BF16)
            for dest in range(x * groups // ALONG_X + core, (x + 1) * groups // ALONG_X, CORES):
                out_ref[dest, : feats // 2, :] = folded


def left_kernel(mine_ref, theirs_ref, out_ref):
    rows = mine_ref.shape[1]
    depth = mine_ref.shape[0] // 2
    for i, ref in enumerate((mine_ref, theirs_ref)):
        turned = ref[...].reshape(2 * CHIPS, 2, depth // (2 * CHIPS), rows)
        for part in range(2):
            value = turned[:, part].reshape(depth, rows).astype(F32).T
            out_ref[i * rows : (i + 1) * rows, part * depth : (part + 1) * depth] = value.astype(BF16)


def halves_kernel(odd_ref, *refs):
    queries_ref, conv_ref, own_ref, other_ref = refs[-4:]
    odd = odd_ref[0] == 1
    rows, half = queries_ref.shape[0], own_ref.shape[1]
    for i, ref in enumerate((queries_ref, conv_ref)):
        left, right = ref[:, :half], ref[:, half:]
        own_ref[i * rows : (i + 1) * rows, :] = jnp.where(odd, right, left)
        other_ref[i * rows : (i + 1) * rows, :] = jnp.where(odd, left, right)


def both_cores(own_ref, came_ref):
    rows = own_ref.shape[0] // 2
    own, came = own_ref[...].astype(F32), came_ref[...].astype(F32)
    return (
        jnp.concatenate([own[:rows], came[:rows]], 0),
        jnp.concatenate([own[rows:], came[rows:]], 0),
    )


def gate_kernel(x_ref, odd_ref, *refs):
    own_ref, came_ref, left_ref, w0_ref, w1_ref, w2_ref, w3_ref, turned_ref, mine_ref, theirs_ref = refs[-10:]
    odd = odd_ref[0] == 1
    folded = jnp.concatenate([w0_ref[...], w1_ref[...], w2_ref[...], w3_ref[...]], 1)
    depth = folded.shape[0]
    low = dot(left_ref[:, :depth], folded)
    high = dot(left_ref[:, depth:], folded)
    rows, half = mine_ref.shape
    part = half // ALONG_X
    pieces = [
        low[:, 2 * hop * part : (2 * hop + 1) * part]
        + high[:, (2 * hop + 1) * part : (2 * hop + 2) * part]
        for hop in range(ALONG_X)
    ]
    placed = []
    for x in range(ALONG_X):
        away = (x_ref[0] - x + ALONG_X) % ALONG_X
        value = pieces[0]
        for hop in range(1, ALONG_X):
            value = jnp.where(away == hop, pieces[hop], value)
        placed.append(value)
    gate = jnp.concatenate(placed, 1)
    queries, conv = both_cores(own_ref, came_ref)
    turned = (gate * queries).astype(BF16).astype(F32).T
    swapped = jnp.concatenate([turned[:, rows:], turned[:, :rows]], 1)
    turned_ref[...] = jnp.where(odd, swapped, turned).astype(BF16)
    query_grad = (gate * conv).astype(BF16)
    mine_ref[...] = query_grad[:rows]
    theirs_ref[...] = query_grad[rows:]


def outputs_kernel(scale, came_ref, key_ref, value_ref, key_grad_ref, value_grad_ref, weight_grad_ref):
    rows, chan = key_ref.shape
    groups, depth, _ = came_ref.shape
    feats, chans = weight_grad_ref.shape[0], chan // groups
    folded = feats // 2
    inner = came_ref[:, folded:, :].astype(F32).reshape(CHIPS, CORES, chans, rows)
    inner = jnp.swapaxes(inner, 0, 1).reshape(chan, rows).T
    key_grad_ref[...] = (inner * value_ref[...].astype(F32)).astype(BF16)
    value_grad_ref[...] = (inner * key_ref[...].astype(F32)).astype(BF16)
    sums = came_ref[:, :folded, :].astype(F32)
    sums = sums.reshape(ALONG_X // 2, 2, CHIPS // ALONG_X // 2, 2, CORES, folded, rows)
    sums = jnp.sum(jnp.sum(sums, 2), 0) * scale
    part = rows // 2
    for high in range(2):
        value = jnp.concatenate(
            [
                sums[x, z, core, :, high * part : (high + 1) * part]
                for core in range(CORES)
                for z in range(2)
                for x in range(2)
            ],
            1,
        )
        weight_grad_ref[high * folded : (high + 1) * folded, :] = value


def arrange_kernel(y_ref, after_ref, *refs):
    block = refs[0].shape[0]
    for hop, ref in enumerate(refs[:-1]):
        start = pl.multiple_of(lax.rem(y_ref[0] + hop, len(refs) - 1) * block, block)
        refs[-1][pl.ds(start, block), :] = ref[...]


def partial_kernel(upper_ref, mine_ref, theirs_ref, own_ref, came_ref, keep_ref, *give_refs):
    queries, conv = both_cores(own_ref, came_ref)
    gated = (queries * conv).astype(BF16)
    part = gated.shape[1] // 2
    upper = upper_ref[0] == 1
    low, high = gated[:, :part], gated[:, part:]
    left = jnp.concatenate([mine_ref[...], theirs_ref[...]], 1)
    keep_ref[...] = dot(left, jnp.where(upper, high, low))
    give = dot(left, jnp.where(upper, low, high)).astype(BF16)
    size = give_refs[0].shape[0]
    for i, ref in enumerate(give_refs):
        ref[...] = give[i * size : (i + 1) * size]


def fold_kernel(upper_ref, after_ref, keep_ref, low_ref, high_ref, kept_ref, *give_refs):
    total = keep_ref[...] + jnp.concatenate([low_ref[...], high_ref[...]], 0).astype(F32)
    depth, width = total.shape
    total = total.reshape(CORES * CHIPS, 2, depth // (2 * CORES * CHIPS), width)
    first = total[:, 0].reshape(depth // 2, width)
    second = total[:, 1].reshape(depth // 2, width)
    part = width // 2
    low = jnp.concatenate([first[:, :part], second[:, :part]], 1)
    high = jnp.concatenate([first[:, part:], second[:, part:]], 1)
    upper = upper_ref[0] == 1
    kept_ref[...] = jnp.where(upper, high, low)
    give = jnp.where(upper, low, high).astype(BF16)
    size = give_refs[0].shape[0]
    for i, ref in enumerate(give_refs):
        ref[...] = give[i * size : (i + 1) * size]


def in_vmem(count):
    return [pl.BlockSpec(memory_space=pltpu.VMEM)] * count


def call(kernel, out, scalars, *operands, scratch=(), after=()):
    return pl.pallas_call(
        kernel,
        out_shape=[jax.ShapeDtypeStruct(shape, dtype) for shape, dtype in out],
        in_specs=[pl.BlockSpec(memory_space=pltpu.SMEM)] * len(scalars)
        + [pl.BlockSpec(memory_space=pl.ANY)] * len(after)
        + in_vmem(len(operands)),
        out_specs=in_vmem(len(out)),
        scratch_shapes=[pltpu.VMEM(shape, F32) for shape in scratch],
        compiler_params=pltpu.CompilerParams(vmem_limit_bytes=10 << 20),
    )(*scalars, *after, *operands)


def shards(queries, key_proj, value_proj, conv_out, filters, out_grad, out_weight):
    rows, chan = queries.shape
    groups = lax.axis_size("seq")
    feats = out_weight.shape[0]
    chips = groups // CORES
    along_z = chips // ALONG_X
    half = chan // CORES
    chans = chan // groups
    kept = -(-(groups + 1) // 8) * 8
    sizes = (chips, chans, rows, kept)

    place = lax.axis_index("seq")
    odd = place % CORES == 1
    x_place = place // (along_z * CORES)
    z_place = place // CORES % along_z
    x_scalar = x_place.reshape(1)
    odd_scalar = odd.astype(jnp.int32).reshape(1)

    def send(value, dx, dz, core):
        pairs = []
        for i in range(groups):
            x, z, c = i // (along_z * CORES), i // CORES % along_z, i % CORES
            x, z, c = (x + dx) % ALONG_X, (z + dz) % along_z, c ^ core
            pairs.append((i, (x * along_z + z) * CORES + c))
        return lax.ppermute(value, "seq", pairs)

    def to_core(value):
        return send(value, 0, 0, 1)

    order = np.arange(groups).reshape(chips, CORES).T.reshape(-1)
    first, twist, second, last = dft_tables(groups, rows, kept)
    first, last = first[:, order], last[order]
    first, last = jnp.stack(halves(first)), jnp.stack(halves(last))
    second, back = jnp.stack(halves(second)), jnp.stack(halves(second.T))
    twist = jnp.asarray(twist, F32)

    def by_core(own, other):
        return jnp.concatenate([jnp.where(odd, other, own), jnp.where(odd, own, other)], 1)

    (packed,) = call(pack_kernel, [((groups, feats // 2 + chans, rows), BF16)], (), filters, out_weight)
    arrived = lax.all_to_all(packed, "seq", 0, 0)
    folded = arrived[:, : feats // 2].reshape(groups * feats // 2, rows)
    weights = [folded] + [send(folded, hop, 0, 0) for hop in range(1, ALONG_X)]
    (filt,) = call(
        functools.partial(filter_kernel, sizes),
        [((chans * kept, 2 * rows), F32)],
        (),
        arrived[:, feats // 2 :].reshape(chan, rows),
        first,
        twist,
        second,
        scratch=[(chan, rows)],
    )

    features = lax.axis_size("ch")
    turned_grad = out_grad.T
    around = [turned_grad] + [
        lax.ppermute(turned_grad, "ch", [(i, (i - hop) % features) for i in range(features)])
        for hop in range(1, features)
    ]
    (wide,) = call(
        arrange_kernel,
        [((groups * feats, rows), BF16)],
        (lax.axis_index("ch").reshape(1),),
        *around,
        after=(arrived,),
    )
    wide_there = to_core(wide)
    (left,) = call(
        left_kernel, [((CORES * rows, groups * feats), BF16)], (), wide, wide_there
    )
    halves_own, halves_other = call(
        halves_kernel, [((CORES * rows, half), BF16)] * 2, (odd_scalar,), queries, conv_out
    )
    halves_came = to_core(halves_other)

    keep, *give = call(
        partial_kernel,
        [((groups * feats, half // 2), F32)] + [((groups * feats // 2, half // 2), BF16)] * 2,
        ((z_place % 2).reshape(1),),
        wide,
        wide_there,
        halves_own,
        halves_came,
    )
    turned, mine, theirs = call(
        gate_kernel,
        [((half, CORES * rows), BF16)] + [((rows, half), BF16)] * 2,
        (x_scalar, odd_scalar),
        halves_own,
        halves_came,
        left,
        *weights,
        after=(filt,),
    )
    keep, *give = call(
        fold_kernel,
        [((groups * feats // 2, half // 2), F32)]
        + [((groups * feats // 4, half // 2), BF16)] * 2,
        ((x_place % 2).reshape(1),),
        keep,
        *[lax.ppermute(value, "seq", [(i, i ^ CORES) for i in range(groups)]) for value in give],
        after=(turned,),
    )
    came = [
        lax.ppermute(value, "seq", [(i, i ^ (along_z * CORES)) for i in range(groups)])
        for value in give
    ]

    received = lax.all_to_all(
        turned.reshape(chips, chans, CORES * rows),
        "seq",
        0,
        0,
        axis_index_groups=[list(range(core, groups, CORES)) for core in range(CORES)],
    )
    query_grad = by_core(mine, to_core(theirs))
    (inner,) = call(
        functools.partial(correlate_kernel, sizes),
        [((groups, feats // 2 + chans, rows), BF16)],
        (),
        received.reshape(half, CORES * rows),
        filt,
        first,
        twist,
        second,
        back,
        last,
        keep,
        *came,
        scratch=[(CORES, half, rows), (chan, rows)],
    )
    key_grad, value_grad, weight_grad = call(
        functools.partial(outputs_kernel, (rows * groups) ** (-0.5)),
        [((rows, chan), BF16)] * 2 + [((feats, chan), F32)],
        (),
        lax.all_to_all(inner, "seq", 0, 0),
        key_proj,
        value_proj,
    )
    return (query_grad, key_grad, value_grad, weight_grad)


def solution(mesh):
    placed = (P("seq", "ch"),) * 7
    return jax.shard_map(
        shards,
        mesh=mesh,
        in_specs=placed,
        out_specs=(P("seq", "ch"),) * 4,
        check_vma=False,
    )
```

time: 114 us -> 97 us (0.85)
  blocking collectives: 12.7 us -> 0 us
  starting transfers between devices: 44.5 us -> 40.3 us
  Pallas kernels: 6.74 us -> 10.8 us
  other arithmetic: 2.82 us -> 0.68 us
  waiting for transfers between devices: 41.7 us -> 40.3 us
    ppermute x13 -> x6, starting transfers between devices: 22.5 us -> 4.93 us  [send(): return lax.ppermute(value, 'seq', pairs)]
    all_gather x1 -> x0, blocking collectives: 12.7 us -> none  [shards(): wide = lax.all_gather(out_grad.T, 'ch', axis=0, tiled=True)]
    ppermute x13 -> x6, waiting for transfers between devices: 23.9 us -> 11.3 us  [send(): return lax.ppermute(value, 'seq', pairs)]
    ppermute x1 -> x7, starting transfers between devices: 0.84 us -> 8.08 us  [the longest x3 5.06 us: shards(): lax.ppermute(turned_grad, 'ch', [(i, (i - hop) % features) for i in range...]
    ppermute x1 -> x7, waiting for transfers between devices: 0.01 us -> 5.91 us  [the longest x3 4.89 us: shards(): lax.ppermute(turned_grad, 'ch', [(i, (i - hop) % features) for i in range...]
    all_to_all x1, waiting for transfers between devices: 0.01 us -> 4.52 us  [shards(): arrived = lax.all_to_all(packed, 'seq', 0, 0)]
    pallas_call x7 -> x10, Pallas kernels: 6.74 us -> 10.8 us  [call(): pl.pallas_call(kernel, out_shape=[jax.ShapeDtypeStruct(shape, dtype) for...]
    all_to_all x1, starting transfers between devices: 9.79 us -> 13.1 us  [shards(): arrived = lax.all_to_all(packed, 'seq', 0, 0)]
  transfers between devices with their start and end apart: 17 -> 16, of which waited for: 9 -> 10; matrix products, arithmetic and copies ran while one was open for 4% -> 1% of each run, Pallas kernels for 5% -> 7%
where the time goes in v5:
time: 97 us; the launch traced here: 96.5 us
  starting transfers between devices  40.3 us (42%)
  waiting for transfers between devices  40.3 us (42%)
  Pallas kernels  10.8 us (11%)
  local copies, waits for them, and re-layouts  3.55 us (4%)
    all_to_all x1, starting transfers between devices, shards(): arrived = lax.all_to_all(packed, 'seq', 0, 0)  13.1 us
    all_to_all x1, waiting for transfers between devices, shards(): lax.all_to_all(inner, 'seq', 0, 0)  12.4 us
    ppermute x6, waiting for transfers between devices, send(): return lax.ppermute(value, 'seq', pairs)  11.3 us
    pallas_call x10, Pallas kernels, call(): pl.pallas_call(kernel, out_shape=[jax.ShapeDtypeStruct(shape, dtype) for...  10.8 us
    all_to_all x1, starting transfers between devices, shards(): lax.all_to_all(inner, 'seq', 0, 0)  10.3 us
    all_to_all x1, waiting for transfers between devices, shards(): lax.all_to_all(turned.reshape(chips, chans, CORES * rows), 'seq', 0, 0, a...  6.09 us
    ppermute x3, starting transfers between devices, shards(): lax.ppermute(turned_grad, 'ch', [(i, (i - hop) % features) for i in range...  5.06 us
    ppermute x6, starting transfers between devices, send(): return lax.ppermute(value, 'seq', pairs)  4.93 us
  transfers between devices with their start and end apart: 16, of which 10 were waited for; matrix products, arithmetic and copies ran while one was open for 1% of the time, Pallas kernels for 7%

profile of v5, /device:TPU:1, one launch (start us, length us, event | category | flops | bytes accessed | tf_op | source)
XLA Modules:
  0.0 96.5 jit_solution(5430446778048481541)
XLA Ops:
  0.6 0.9 copy-done.5
  1.5 0.8 copy-done.13
  2.3 0.9 shard_map.183
  3.2 13.1 %all-to-all-start = ((bf16[64,24,128]{2,1,0:T(8,128)(2,1)}), bf16[64,24,128]{2,1,0:T(8,128)(2,1)S(1)}, u32[]{:S(2)}, u32[]{:S(2)}) async-start(bf16[64,24,128]{2,1,0:T(8,128)(2,1)} %shard_map.183), calls=%async_computation | async-start | bytes 786432 | tf_op jit(solution)/shard_map/all_to_all | solution.py:324
  16.4 1.4 %collective-permute-start.3 = (bf16[512,128]{1,0:T(8,128)(2,1)S(1)}, bf16[512,128]{1,0:T(8,128)(2,1)S(1)}, u32[]{:S(2)}, u32[]{:S(2)}) collective-permute-start(bf16[512,128]{1,0:T(8,128)(2,1)S(1)} %bitcast.16), channel_id=1, source_target_pairs={{0,1},{1,2},{2,3},{3,0},{4,5},{5,6},{6,7},{7,4},{8,9},{9,10},{10,1... | collective-permute-start | bytes 393224 | tf_op jit(solution)/shard_map/ppermute | solution.py:341
  17.8 2.6 %collective-permute-start.2 = (bf16[512,128]{1,0:T(8,128)(2,1)S(1)}, bf16[512,128]{1,0:T(8,128)(2,1)S(1)}, u32[]{:S(2)}, u32[]{:S(2)}) collective-permute-start(bf16[512,128]{1,0:T(8,128)(2,1)S(1)} %bitcast.17), channel_id=1, source_target_pairs={{0,2},{1,3},{2,0},{3,1},{4,6},{5,7},{6,4},{7,5},{8,10},{9,11},{10,... | collective-permute-start | bytes 393224 | tf_op jit(solution)/shard_map/ppermute | solution.py:341
  20.4 1.1 %collective-permute-start.1 = (bf16[512,128]{1,0:T(8,128)(2,1)S(1)}, bf16[512,128]{1,0:T(8,128)(2,1)S(1)}, u32[]{:S(2)}, u32[]{:S(2)}) collective-permute-start(bf16[512,128]{1,0:T(8,128)(2,1)S(1)} %bitcast.18), channel_id=1, source_target_pairs={{0,3},{1,0},{2,1},{3,2},{4,7},{5,4},{6,5},{7,6},{8,11},{9,8},{10,9... | collective-permute-start | bytes 393224 | tf_op jit(solution)/shard_map/ppermute | solution.py:341
  21.5 1.0 %collective-permute-done.3.refs_3_ = bf16[512,128]{1,0:T(8,128)(2,1)S(1)} collective-permute-done((bf16[512,128]{1,0:T(8,128)(2,1)S(1)}, bf16[512,128]{1,0:T(8,128)(2,1)S(1)}, u32[]{:S(2)}, u32[]{:S(2)}) %collective-permute-start.3) | collective-permute-done | bytes 131104 | tf_op jit(solution)/shard_map/ppermute | solution.py:341
  22.5 3.9 %collective-permute-done.2.refs_2_ = bf16[512,128]{1,0:T(8,128)(2,1)S(1)} collective-permute-done((bf16[512,128]{1,0:T(8,128)(2,1)S(1)}, bf16[512,128]{1,0:T(8,128)(2,1)S(1)}, u32[]{:S(2)}, u32[]{:S(2)}) %collective-permute-start.2) | collective-permute-done | bytes 131104 | tf_op jit(solution)/shard_map/ppermute | solution.py:341
  26.4 4.5 %all-to-all-done.after_ref = bf16[64,24,128]{2,1,0:T(8,128)(2,1)S(1)} async-done(((bf16[64,24,128]{2,1,0:T(8,128)(2,1)}), bf16[64,24,128]{2,1,0:T(8,128)(2,1)S(1)}, u32[]{:S(2)}, u32[]{:S(2)}) %all-to-all-start) | async-done | bytes 393248 | tf_op jit(solution)/shard_map/all_to_all | solution.py:324
  32.4 2.4 %collective-permute-start.7 = (bf16[1024,128]{1,0:T(8,128)(2,1)S(1)}, bf16[1024,128]{1,0:T(8,128)(2,1)}, u32[]{:S(2)}, u32[]{:S(2)}) collective-permute-start(bf16[1024,128]{1,0:T(8,128)(2,1)S(1)} %bitcast.11), channel_id=1, source_target_pairs={{0,192},{4,196},{8,200},{12,204},{16,208},{20,212},{24,216},{28,22... | collective-permute-start | bytes 786440 | tf_op jit(solution)/shard_map/ppermute | solution.py:308
  35.1 0.7 collective-permute-start.5
  35.9 1.4 %shard_map.189 = (f32[2048,128]{1,0:T(8,128)S(1)}, bf16[1024,128]{1,0:T(8,128)(2,1)}, bf16[1024,128]{1,0:T(8,128)(2,1)}) custom-call(s32[1]{0:T(128)} %bitcast.9.upper_ref, bf16[2048,128]{1,0:T(8,128)(2,1)S(1)} %shard_map.186.mine_ref, bf16[2048,128]{1,0:T(8,128)(2,1)S(1)} %collective-permute-done.4.theirs_ref, ...), custom_call_target="tpu_custom_call" | custom-call | tf_op jit(solution)/shard_map/pallas_call | solution.py:272
  37.9 0.9 collective-permute-start.10
  38.8 0.7 shard_map.184.refs_0_.refs_1_
  39.8 0.7 collective-permute-done.7.refs_7_
  40.5 3.2 %collective-permute-done.6.refs_6_ = bf16[1024,128]{1,0:T(8,128)(2,1)} collective-permute-done((bf16[1024,128]{1,0:T(8,128)(2,1)S(1)}, bf16[1024,128]{1,0:T(8,128)(2,1)}, u32[]{:S(2)}, u32[]{:S(2)}) %collective-permute-start.6) | collective-permute-done | bytes 262176 | tf_op jit(solution)/shard_map/ppermute | solution.py:308
  43.7 6.6 %collective-permute-done.5.refs_5_ = bf16[1024,128]{1,0:T(8,128)(2,1)} collective-permute-done((bf16[1024,128]{1,0:T(8,128)(2,1)S(1)}, bf16[1024,128]{1,0:T(8,128)(2,1)}, u32[]{:S(2)}, u32[]{:S(2)}) %collective-permute-start.5) | collective-permute-done | bytes 262176 | tf_op jit(solution)/shard_map/ppermute | solution.py:308
  50.3 2.8 %shard_map.188 = (bf16[256,256]{1,0:T(8,128)(2,1)}, bf16[128,256]{1,0:T(8,128)(2,1)S(1)}, bf16[128,256]{1,0:T(8,128)(2,1)S(1)}) custom-call(s32[1]{0:T(128)} %bitcast.x_ref, s32[1]{0:T(128)} %bitcast.1.odd_ref, f32[576,256]{1,0:T(8,128)S(1)} %shard_map.184.refs_0_.refs_1_, bf16[256,256]{1,0:T(8,128)(2,1)S(1)} %get-tuple-element.18.refs_1_.own_ref, ...), custom_call_target="tpu_custom_call" | custom-call | tf_op jit(solution)/shard_map/pallas_call | solution.py:272
  53.0 0.6 copy-done.11
  53.6 0.6 copy-done.14
  54.3 3.9 %all-to-all-start.1 = ((bf16[32,8,256]{2,1,0:T(8,128)(2,1)}), bf16[32,8,256]{2,1,0:T(8,128)(2,1)S(1)}, u32[]{:S(2)}, u32[]{:S(2)}) async-start(bf16[32,8,256]{2,1,0:T(8,128)(2,1)} %bitcast.6), calls=%async_computation.1 | async-start | bytes 262144 | tf_op jit(solution)/shard_map/all_to_all | solution.py:393
  58.2 1.4 %shard_map.190 = (f32[1024,128]{1,0:T(8,128)S(1)}, bf16[512,128]{1,0:T(8,128)(2,1)S(1)}, bf16[512,128]{1,0:T(8,128)(2,1)S(1)}) custom-call(s32[1]{0:T(128)} %bitcast.8.upper_ref, bf16[256,256]{1,0:T(8,128)(2,1)} %get-tuple-element.22.after_ref, f32[2048,128]{1,0:T(8,128)S(1)} %get-tuple-element.23.keep_ref, ...), custom_call_target="tpu_custom_call" | custom-call | tf_op jit(solution)/shard_map/pallas_call | solution.py:272
  59.6 1.3 %collective-permute-start.11 = (bf16[512,128]{1,0:T(8,128)(2,1)S(1)}, bf16[512,128]{1,0:T(8,128)(2,1)S(1)}, u32[]{:S(2)}, u32[]{:S(2)}) collective-permute-start(bf16[512,128]{1,0:T(8,128)(2,1)S(1)} %get-tuple-element.27), channel_id=1, source_target_pairs={{0,64},{4,68},{8,72},{12,76},{16,80},{20,84},{24,88},{28,92},{32,9... | collective-permute-start | bytes 393224 | tf_op jit(solution)/shard_map/ppermute | solution.py:389
  61.2 6.1 %all-to-all-done.1 = bf16[32,8,256]{2,1,0:T(8,128)(2,1)S(1)} async-done(((bf16[32,8,256]{2,1,0:T(8,128)(2,1)}), bf16[32,8,256]{2,1,0:T(8,128)(2,1)S(1)}, u32[]{:S(2)}, u32[]{:S(2)}) %all-to-all-start.1) | async-done | bytes 131104 | tf_op jit(solution)/shard_map/all_to_all | solution.py:393
  67.3 1.0 %collective-permute-done.12.refs_9_ = bf16[512,128]{1,0:T(8,128)(2,1)S(1)} collective-permute-done((bf16[512,128]{1,0:T(8,128)(2,1)S(1)}, bf16[512,128]{1,0:T(8,128)(2,1)S(1)}, u32[]{:S(2)}, u32[]{:S(2)}) %collective-permute-start.12) | collective-permute-done | bytes 131104 | tf_op jit(solution)/shard_map/ppermute | solution.py:389
  68.3 2.4 %shard_map.191 = bf16[64,24,128]{2,1,0:T(8,128)(2,1)} custom-call(bf16[256,256]{1,0:T(8,128)(2,1)S(1)} %bitcast.15, f32[576,256]{1,0:T(8,128)S(1)} %shard_map.184.refs_0_.refs_1_, bf16[2,144,64]{2,1,0:T(8,128)(2,1)S(1)} %copy-done.1, f32[2,72,128]{2,1,0:T(8,128)S(1)} %copy-done.3, bf16[2,256,256]{2,1,0:T(8,128)(2,1)S(1)} %copy-done, ...), custom_call_target="tpu_custom_call" | custom-call | tf_op jit(solution)/shard_map/pallas_call | solution.py:272
  70.7 10.3 %all-to-all-start.2 = ((bf16[64,24,128]{2,1,0:T(8,128)(2,1)}), bf16[64,24,128]{2,1,0:T(8,128)(2,1)S(1)}, u32[]{:S(2)}, u32[]{:S(2)}) async-start(bf16[64,24,128]{2,1,0:T(8,128)(2,1)} %shard_map.191), calls=%async_computation.2 | async-start | bytes 786432 | tf_op jit(solution)/shard_map/all_to_all | solution.py:420
  81.6 0.9 collective-permute-done.8
  82.5 0.7 pad_maximum_fusion
  83.2 12.4 %all-to-all-done.2.came_ref = bf16[64,24,128]{2,1,0:T(8,128)(2,1)S(1)} async-done(((bf16[64,24,128]{2,1,0:T(8,128)(2,1)}), bf16[64,24,128]{2,1,0:T(8,128)(2,1)S(1)}, u32[]{:S(2)}, u32[]{:S(2)}) %all-to-all-start.2) | async-done | bytes 393248 | tf_op jit(solution)/shard_map/all_to_all | solution.py:420
  95.6 0.8 shard_map.192
  (49 shorter events, 3.8 us)
Async XLA Ops:
  0.6 0.9 copy-start.5
  1.5 0.8 copy-start.13
  3.2 13.1 %copy-start.16 = (bf16[128,512]{1,0:T(8,128)(2,1)S(1)}, bf16[128,512]{1,0:T(8,128)(2,1)}, u32[]{:S(2)}) copy-start(bf16[128,512]{1,0:T(8,128)(2,1)} %param.21) | copy-start | bytes 393220
  3.2 27.7 %all-to-all-start = ((bf16[64,24,128]{2,1,0:T(8,128)(2,1)}), bf16[64,24,128]{2,1,0:T(8,128)(2,1)S(1)}, u32[]{:S(2)}, u32[]{:S(2)}) async-start(bf16[64,24,128]{2,1,0:T(8,128)(2,1)} %shard_map.183), calls=%async_computation | async-start | bytes 786432 | tf_op jit(solution)/shard_map/all_to_all | solution.py:324
  16.4 6.0 %collective-permute-start.3 = (bf16[512,128]{1,0:T(8,128)(2,1)S(1)}, bf16[512,128]{1,0:T(8,128)(2,1)S(1)}, u32[]{:S(2)}, u32[]{:S(2)}) collective-permute-start(bf16[512,128]{1,0:T(8,128)(2,1)S(1)} %bitcast.16), channel_id=1, source_target_pairs={{0,1},{1,2},{2,3},{3,0},{4,5},{5,6},{6,7},{7,4},{8,9},{9,10},{10,1... | collective-permute-start | bytes 393224 | tf_op jit(solution)/shard_map/ppermute | solution.py:341
  17.8 8.6 %collective-permute-start.2 = (bf16[512,128]{1,0:T(8,128)(2,1)S(1)}, bf16[512,128]{1,0:T(8,128)(2,1)S(1)}, u32[]{:S(2)}, u32[]{:S(2)}) collective-permute-start(bf16[512,128]{1,0:T(8,128)(2,1)S(1)} %bitcast.17), channel_id=1, source_target_pairs={{0,2},{1,3},{2,0},{3,1},{4,6},{5,7},{6,4},{7,5},{8,10},{9,11},{10,... | collective-permute-start | bytes 393224 | tf_op jit(solution)/shard_map/ppermute | solution.py:341
  20.4 6.0 %collective-permute-start.1 = (bf16[512,128]{1,0:T(8,128)(2,1)S(1)}, bf16[512,128]{1,0:T(8,128)(2,1)S(1)}, u32[]{:S(2)}, u32[]{:S(2)}) collective-permute-start(bf16[512,128]{1,0:T(8,128)(2,1)S(1)} %bitcast.18), channel_id=1, source_target_pairs={{0,3},{1,0},{2,1},{3,2},{4,7},{5,4},{6,5},{7,6},{8,11},{9,8},{10,9... | collective-permute-start | bytes 393224 | tf_op jit(solution)/shard_map/ppermute | solution.py:341
  30.9 0.9 copy-start.8
  30.9 1.0 %copy-start.9 = (bf16[128,512]{1,0:T(8,128)(2,1)S(1)}, bf16[128,512]{1,0:T(8,128)(2,1)}, u32[]{:S(2)}) copy-start(bf16[128,512]{1,0:T(8,128)(2,1)} %refs_1_.1) | copy-start | bytes 393220
  31.0 4.9 %collective-permute-start.4 = (bf16[2048,128]{1,0:T(8,128)(2,1)S(1)}, bf16[2048,128]{1,0:T(8,128)(2,1)S(1)}, u32[]{:S(2)}, u32[]{:S(2)}) collective-permute-start(bf16[2048,128]{1,0:T(8,128)(2,1)S(1)} %shard_map.186.mine_ref), channel_id=1, source_target_pairs={{0,4},{4,0},{8,12},{12,8},{16,20},{20,16},{24,28},{28,24},{32,36},... | collective-permute-start | bytes 1572872 | tf_op jit(solution)/shard_map/ppermute | solution.py:308
  31.9 3.9 %collective-permute-start = (bf16[256,256]{1,0:T(8,128)(2,1)S(1)}, bf16[256,256]{1,0:T(8,128)(2,1)S(1)}, u32[]{:S(2)}, u32[]{:S(2)}) collective-permute-start(bf16[256,256]{1,0:T(8,128)(2,1)S(1)} %get-tuple-element.19), channel_id=1, source_target_pairs={{0,4},{4,0},{8,12},{12,8},{16,20},{20,16},{24,28},{28,24},{32,36},... | collective-permute-start | bytes 393224 | tf_op jit(solution)/shard_map/ppermute | solution.py:308
  32.4 8.1 %collective-permute-start.7 = (bf16[1024,128]{1,0:T(8,128)(2,1)S(1)}, bf16[1024,128]{1,0:T(8,128)(2,1)}, u32[]{:S(2)}, u32[]{:S(2)}) collective-permute-start(bf16[1024,128]{1,0:T(8,128)(2,1)S(1)} %bitcast.11), channel_id=1, source_target_pairs={{0,192},{4,196},{8,200},{12,204},{16,208},{20,212},{24,216},{28,22... | collective-permute-start | bytes 786440 | tf_op jit(solution)/shard_map/ppermute | solution.py:308
  34.8 8.9 %collective-permute-start.6 = (bf16[1024,128]{1,0:T(8,128)(2,1)S(1)}, bf16[1024,128]{1,0:T(8,128)(2,1)}, u32[]{:S(2)}, u32[]{:S(2)}) collective-permute-start(bf16[1024,128]{1,0:T(8,128)(2,1)S(1)} %bitcast.12), channel_id=1, source_target_pairs={{0,128},{4,132},{8,136},{12,140},{16,144},{20,148},{24,152},{28,15... | collective-permute-start | bytes 786440 | tf_op jit(solution)/shard_map/ppermute | solution.py:308
  35.1 15.1 %collective-permute-start.5 = (bf16[1024,128]{1,0:T(8,128)(2,1)S(1)}, bf16[1024,128]{1,0:T(8,128)(2,1)}, u32[]{:S(2)}, u32[]{:S(2)}) collective-permute-start(bf16[1024,128]{1,0:T(8,128)(2,1)S(1)} %bitcast.13), channel_id=1, source_target_pairs={{0,64},{4,68},{8,72},{12,76},{16,80},{20,84},{24,88},{28,92},{32,9... | collective-permute-start | bytes 786440 | tf_op jit(solution)/shard_map/ppermute | solution.py:308
  35.9 2.9 %copy-start.1 = (bf16[2,144,64]{2,1,0:T(8,128)(2,1)S(1)}, bf16[2,144,64]{2,1,0:T(8,128)(2,1)}, u32[]{:S(2)}) copy-start(bf16[2,144,64]{2,1,0:T(8,128)(2,1)} %constant.93.first_ref.refs_2_) | copy-start | bytes 110596
  35.9 2.9 %copy-start.2 = (f32[2,72,128]{2,1,0:T(8,128)S(1)}, f32[2,72,128]{2,1,0:T(8,128)}, u32[]{:S(2)}) copy-start(f32[2,72,128]{2,1,0:T(8,128)} %constant.89.clone.twist_ref.refs_3_) | copy-start | bytes 221188
  37.3 1.5 %copy-start = (bf16[2,256,256]{2,1,0:T(8,128)(2,1)S(1)}, bf16[2,256,256]{2,1,0:T(8,128)(2,1)}, u32[]{:S(2)}) copy-start(bf16[2,256,256]{2,1,0:T(8,128)(2,1)} %constant.96.second_ref.refs_4_) | copy-start | bytes 786436
  37.3 20.9 %collective-permute-start.9 = (bf16[1024,128]{1,0:T(8,128)(2,1)}, bf16[1024,128]{1,0:T(8,128)(2,1)}, u32[]{:S(2)}, u32[]{:S(2)}) collective-permute-start(bf16[1024,128]{1,0:T(8,128)(2,1)} %get-tuple-element.24), channel_id=1, source_target_pairs={{0,8},{4,12},{8,0},{12,4},{16,24},{20,28},{24,16},{28,20},{32,40},... | collective-permute-start | bytes 786440 | tf_op jit(solution)/shard_map/ppermute | solution.py:385
  37.9 20.3 %collective-permute-start.10 = (bf16[1024,128]{1,0:T(8,128)(2,1)}, bf16[1024,128]{1,0:T(8,128)(2,1)}, u32[]{:S(2)}, u32[]{:S(2)}) collective-permute-start(bf16[1024,128]{1,0:T(8,128)(2,1)} %get-tuple-element.25), channel_id=1, source_target_pairs={{0,8},{4,12},{8,0},{12,4},{16,24},{20,28},{24,16},{28,20},{32,40},... | collective-permute-start | bytes 786440 | tf_op jit(solution)/shard_map/ppermute | solution.py:385
  53.0 0.6 copy-start.11
  54.3 13.0 %all-to-all-start.1 = ((bf16[32,8,256]{2,1,0:T(8,128)(2,1)}), bf16[32,8,256]{2,1,0:T(8,128)(2,1)S(1)}, u32[]{:S(2)}, u32[]{:S(2)}) async-start(bf16[32,8,256]{2,1,0:T(8,128)(2,1)} %bitcast.6), calls=%async_computation.1 | async-start | bytes 262144 | tf_op jit(solution)/shard_map/all_to_all | solution.py:393
  58.2 10.1 %copy-start.3 = (f32[2,72,128]{2,1,0:T(8,128)S(1)}, f32[2,72,128]{2,1,0:T(8,128)}, u32[]{:S(2)}) copy-start(f32[2,72,128]{2,1,0:T(8,128)} %constant.89.clone.twist_ref.refs_3_) | copy-start | bytes 221188
  58.2 10.1 %copy-start.4 = (bf16[2,256,256]{2,1,0:T(8,128)(2,1)S(1)}, bf16[2,256,256]{2,1,0:T(8,128)(2,1)}, u32[]{:S(2)}) copy-start(bf16[2,256,256]{2,1,0:T(8,128)(2,1)} %constant.99.refs_5_) | copy-start | bytes 786436
  58.2 10.1 %copy-start.10 = (bf16[2,64,144]{2,1,0:T(8,128)(2,1)S(1)}, bf16[2,64,144]{2,1,0:T(8,128)(2,1)}, u32[]{:S(2)}) copy-start(bf16[2,64,144]{2,1,0:T(8,128)(2,1)} %constant.102.refs_6_) | copy-start | bytes 110596
  59.6 7.6 %collective-permute-start.11 = (bf16[512,128]{1,0:T(8,128)(2,1)S(1)}, bf16[512,128]{1,0:T(8,128)(2,1)S(1)}, u32[]{:S(2)}, u32[]{:S(2)}) collective-permute-start(bf16[512,128]{1,0:T(8,128)(2,1)S(1)} %get-tuple-element.27), channel_id=1, source_target_pairs={{0,64},{4,68},{8,72},{12,76},{16,80},{20,84},{24,88},{28,92},{32,9... | collective-permute-start | bytes 393224 | tf_op jit(solution)/shard_map/ppermute | solution.py:389
  60.9 7.4 %collective-permute-start.12 = (bf16[512,128]{1,0:T(8,128)(2,1)S(1)}, bf16[512,128]{1,0:T(8,128)(2,1)S(1)}, u32[]{:S(2)}, u32[]{:S(2)}) collective-permute-start(bf16[512,128]{1,0:T(8,128)(2,1)S(1)} %get-tuple-element.28), channel_id=1, source_target_pairs={{0,64},{4,68},{8,72},{12,76},{16,80},{20,84},{24,88},{28,92},{32,9... | collective-permute-start | bytes 393224 | tf_op jit(solution)/shard_map/ppermute | solution.py:389
  70.7 10.3 %copy-start.15 = (bf16[128,256]{1,0:T(8,128)(2,1)S(1)}, bf16[128,256]{1,0:T(8,128)(2,1)}, u32[]{:S(2)}) copy-start(bf16[128,256]{1,0:T(8,128)(2,1)} %copy-done.14) | copy-start | bytes 196612
  70.7 11.8 %copy-start.12 = (bf16[128,256]{1,0:T(8,128)(2,1)S(1)}, bf16[128,256]{1,0:T(8,128)(2,1)}, u32[]{:S(2)}) copy-start(bf16[128,256]{1,0:T(8,128)(2,1)} %copy-done.11) | copy-start | bytes 196612
  70.7 24.9 %all-to-all-start.2 = ((bf16[64,24,128]{2,1,0:T(8,128)(2,1)}), bf16[64,24,128]{2,1,0:T(8,128)(2,1)S(1)}, u32[]{:S(2)}, u32[]{:S(2)}) async-start(bf16[64,24,128]{2,1,0:T(8,128)(2,1)} %shard_map.191), calls=%async_computation.2 | async-start | bytes 786432 | tf_op jit(solution)/shard_map/all_to_all | solution.py:420
  81.0 1.4 %collective-permute-start.8 = (bf16[128,256]{1,0:T(8,128)(2,1)S(1)}, bf16[128,256]{1,0:T(8,128)(2,1)S(1)}, u32[]{:S(2)}, u32[]{:S(2)}) collective-permute-start(bf16[128,256]{1,0:T(8,128)(2,1)S(1)} %copy-done.15), channel_id=1, source_target_pairs={{0,4},{4,0},{8,12},{12,8},{16,20},{20,16},{24,28},{28,24},{32,36},... | collective-permute-start | bytes 196616 | tf_op jit(solution)/shard_map/ppermute | solution.py:308
  82.5 13.1 %copy-start.6 = (bf16[128,512]{1,0:T(8,128)(2,1)S(1)}, bf16[128,512]{1,0:T(8,128)(2,1)}, u32[]{:S(2)}) copy-start(bf16[128,512]{1,0:T(8,128)(2,1)} %key_ref.1) | copy-start | bytes 393220
  82.5 13.1 %copy-start.7 = (bf16[128,512]{1,0:T(8,128)(2,1)S(1)}, bf16[128,512]{1,0:T(8,128)(2,1)}, u32[]{:S(2)}) copy-start(bf16[128,512]{1,0:T(8,128)(2,1)} %value_ref.1) | copy-start | bytes 393220
  (1 other events, 0.6 us)

commit v6 on v5

--- a/solution.py
+++ b/solution.py
@@ -13,7 +13,14 @@
 
 CORES = 2
 ALONG_X = 4
+ALONG_Y = 4
 CHIPS = 32
+ALONG_Z = CHIPS // ALONG_X
+
+
+def own_place():
+    place = lax.axis_index("seq")
+    return place // (ALONG_Z * CORES), place // CORES % ALONG_Z, place % CORES
 
 
 def dft_tables(blocks, rows, kept):
@@ -63,40 +70,35 @@
     return dot3(split(jnp.concatenate(parts, 0)), (second_ref[0], second_ref[1]))
 
 
-def filter_kernel(sizes, x_ref, first_ref, twist_ref, second_ref, out_ref, plane):
-    chips, chans, rows, kept = sizes
-    plane[...] = x_ref[...].astype(F32)
-    data = jnp.concatenate(
+def by_channel(planes, chips, chans):
+    return jnp.concatenate(
         [
             jnp.concatenate(
-                [
-                    plane[pl.ds(core * chans + c, chips, stride=CORES * chans), :]
-                    for core in range(CORES)
-                ],
-                0,
+                [planes[core, pl.ds(c, chips, stride=chans), :] for core in range(CORES)], 0
             )
             for c in range(chans)
         ],
         1,
     ).astype(BF16)
+
+
+def filter_kernel(sizes, own_ref, came_ref, first_ref, twist_ref, second_ref, out_ref, planes):
+    chips, chans, rows, kept = sizes
+    odd = own_place()[2] == 1
+    own, came = own_ref[...].astype(F32), came_ref[...].astype(F32)
+    planes[0] = jnp.where(odd, came, own)
+    planes[1] = jnp.where(odd, own, came)
+    data = by_channel(planes, chips, chans)
     out_ref[...] = spectrum(data, first_ref, twist_ref, second_ref, chans, rows, kept)
 
 
 def correlate_kernel(sizes, *refs):
-    x_ref, filt_ref, first_ref, twist_ref, second_ref, back_ref, last_ref = refs[:7]
-    kept_ref, *came_refs, out_ref, wide, plane = refs[7:]
+    x_ref, filt_ref, first_ref, twist_ref, second_ref, back_ref, last_ref = refs[1:8]
+    kept_ref, *came_refs, out_ref, wide, plane = refs[8:]
     chips, chans, rows, kept = sizes
     for core in range(CORES):
         wide[core] = x_ref[:, core * rows : (core + 1) * rows].astype(F32)
-    data = jnp.concatenate(
-        [
-            jnp.concatenate(
-                [wide[core, pl.ds(c, chips, stride=chans), :] for core in range(CORES)], 0
-            )
-            for c in range(chans)
-        ],
-        1,
-    ).astype(BF16)
+    data = by_channel(wide, chips, chans)
     grads = spectrum(data, first_ref, twist_ref, second_ref, chans, rows, kept)
     g_re, g_im = grads[:, :rows], grads[:, rows:]
     f_re, f_im = filt_ref[:, :rows], filt_ref[:, rows:]
@@ -122,37 +124,53 @@
 
 
 def pack_kernel(filters_ref, weight_ref, out_ref):
-    groups, _, rows = out_ref.shape
+    chips, depth, rows = out_ref.shape
     chan = filters_ref.shape[1]
-    chans = chan // groups
     feats = weight_ref.shape[0]
-    part = chan // (ALONG_X * CORES)
-    turned = filters_ref[...].astype(F32).T.reshape(CORES, groups // CORES, chans, rows)
-    turned = jnp.swapaxes(turned, 0, 1).reshape(groups, chans, rows)
-    out_ref[:, feats // 2 :, :] = turned.astype(BF16)
-    weight = weight_ref[...].astype(F32)
-    for x in range(ALONG_X):
-        for core in range(CORES):
-            start = (core * ALONG_X + x) * part
-            piece = weight[:, start : start + part]
-            folded = jnp.concatenate([piece[: feats // 2], piece[feats // 2 :]], 1).astype(BF16)
-            for dest in range(x * groups // ALONG_X + core, (x + 1) * groups // ALONG_X, CORES):
-                out_ref[dest, : feats // 2, :] = folded
+    turned = filters_ref[...].astype(F32).T.reshape(CORES, chips, chan // (CORES * chips), rows)
+    turned = jnp.swapaxes(turned, 0, 1).reshape(chips, depth - CORES * feats, rows)
+    out_ref[:, CORES * feats :, :] = turned.astype(BF16)
+    for core in range(CORES):
+        for part in range(2):
+            start = (core * 2 + part) * rows
+            piece = weight_ref[:, start : start + rows]
+            for chip in range(chips):
+                if chip // ALONG_Z % 2 == part:
+                    out_ref[chip, core * feats : (core + 1) * feats, :] = piece
+
+
+def unpack_kernel(came_ref, own_ref, other_ref):
+    feats = own_ref.shape[0] // CHIPS
+    odd = own_place()[2] == 1
+    first, second = came_ref[:, :feats, :], came_ref[:, feats : 2 * feats, :]
+    own_ref[...] = jnp.where(odd, second, first).reshape(own_ref.shape)
+    other_ref[...] = jnp.where(odd, first, second).reshape(other_ref.shape)
+
+
+def unpack_filters_kernel(came_ref, own_ref, other_ref):
+    chans = own_ref.shape[0] // CHIPS
+    odd = own_place()[2] == 1
+    came = came_ref[:, -CORES * chans :, :].astype(F32)
+    came = came.reshape(CHIPS, CORES, chans, came.shape[2])
+    first, second = came[:, 0], came[:, 1]
+    own_ref[...] = jnp.where(odd, second, first).reshape(own_ref.shape).astype(BF16)
+    other_ref[...] = jnp.where(odd, first, second).reshape(other_ref.shape).astype(BF16)
 
 
 def left_kernel(mine_ref, theirs_ref, out_ref):
-    rows = mine_ref.shape[1]
-    depth = mine_ref.shape[0] // 2
+    depth, rows = mine_ref.shape[0] // CORES, mine_ref.shape[1]
+    odd = own_place()[2] == 1
     for i, ref in enumerate((mine_ref, theirs_ref)):
-        turned = ref[...].reshape(2 * CHIPS, 2, depth // (2 * CHIPS), rows)
-        for part in range(2):
-            value = turned[:, part].reshape(depth, rows).astype(F32).T
-            out_ref[i * rows : (i + 1) * rows, part * depth : (part + 1) * depth] = value.astype(BF16)
-
-
-def halves_kernel(odd_ref, *refs):
+        value = ref[...].reshape(CHIPS, CORES, depth // CHIPS, rows)
+        first, second = (value[:, core].reshape(depth, rows).astype(F32) for core in range(CORES))
+        place = slice(i * rows, (i + 1) * rows)
+        out_ref[place, :depth] = jnp.where(odd, second, first).T.astype(BF16)
+        out_ref[place, depth:] = jnp.where(odd, first, second).T.astype(BF16)
+
+
+def halves_kernel(*refs):
     queries_ref, conv_ref, own_ref, other_ref = refs[-4:]
-    odd = odd_ref[0] == 1
+    odd = own_place()[2] == 1
     rows, half = queries_ref.shape[0], own_ref.shape[1]
     for i, ref in enumerate((queries_ref, conv_ref)):
         left, right = ref[:, :half], ref[:, half:]
@@ -169,28 +187,16 @@
     )
 
 
-def gate_kernel(x_ref, odd_ref, *refs):
-    own_ref, came_ref, left_ref, w0_ref, w1_ref, w2_ref, w3_ref, turned_ref, mine_ref, theirs_ref = refs[-10:]
-    odd = odd_ref[0] == 1
-    folded = jnp.concatenate([w0_ref[...], w1_ref[...], w2_ref[...], w3_ref[...]], 1)
-    depth = folded.shape[0]
-    low = dot(left_ref[:, :depth], folded)
-    high = dot(left_ref[:, depth:], folded)
-    rows, half = mine_ref.shape
-    part = half // ALONG_X
-    pieces = [
-        low[:, 2 * hop * part : (2 * hop + 1) * part]
-        + high[:, (2 * hop + 1) * part : (2 * hop + 2) * part]
-        for hop in range(ALONG_X)
-    ]
-    placed = []
-    for x in range(ALONG_X):
-        away = (x_ref[0] - x + ALONG_X) % ALONG_X
-        value = pieces[0]
-        for hop in range(1, ALONG_X):
-            value = jnp.where(away == hop, pieces[hop], value)
-        placed.append(value)
-    gate = jnp.concatenate(placed, 1)
+def gate_kernel(*refs):
+    own_ref, came_ref, left_ref, a_ref, b_ref, c_ref, d_ref, turned_ref, mine_ref, theirs_ref = refs[-10:]
+    x, _, core = own_place()
+    odd = core == 1
+    rows = mine_ref.shape[0]
+    depth = a_ref.shape[0]
+    gate = dot(left_ref[:, :depth], jnp.concatenate([a_ref[...], b_ref[...]], 1))
+    gate += dot(left_ref[:, depth:], jnp.concatenate([c_ref[...], d_ref[...]], 1))
+    part = gate.shape[1] // 2
+    gate = jnp.where(x % 2 == 1, jnp.concatenate([gate[:, part:], gate[:, :part]], 1), gate)
     queries, conv = both_cores(own_ref, came_ref)
     turned = (gate * queries).astype(BF16).astype(F32).T
     swapped = jnp.concatenate([turned[:, rows:], turned[:, :rows]], 1)
@@ -198,6 +204,14 @@
     query_grad = (gate * conv).astype(BF16)
     mine_ref[...] = query_grad[:rows]
     theirs_ref[...] = query_grad[rows:]
+
+
+def join_kernel(mine_ref, theirs_ref, out_ref):
+    odd = own_place()[2] == 1
+    mine, theirs = mine_ref[...], theirs_ref[...]
+    half = mine.shape[1]
+    out_ref[:, :half] = jnp.where(odd, theirs, mine)
+    out_ref[:, half:] = jnp.where(odd, mine, theirs)
 
 
 def outputs_kernel(scale, came_ref, key_ref, value_ref, key_grad_ref, value_grad_ref, weight_grad_ref):
@@ -226,29 +240,30 @@
         weight_grad_ref[high * folded : (high + 1) * folded, :] = value
 
 
-def arrange_kernel(y_ref, after_ref, *refs):
-    block = refs[0].shape[0]
-    for hop, ref in enumerate(refs[:-1]):
-        start = pl.multiple_of(lax.rem(y_ref[0] + hop, len(refs) - 1) * block, block)
-        refs[-1][pl.ds(start, block), :] = ref[...]
-
-
-def partial_kernel(upper_ref, mine_ref, theirs_ref, own_ref, came_ref, keep_ref, *give_refs):
+def arrange_kernel(*refs):
+    *block_refs, out_ref = refs[-ALONG_Y - 1 :]
+    size = block_refs[0].shape[0]
+    for hop, ref in enumerate(block_refs):
+        start = pl.multiple_of(lax.rem(lax.axis_index("ch") + hop, ALONG_Y) * size, size)
+        out_ref[pl.ds(start, size), :] = ref[...]
+
+
+def partial_kernel(mine_ref, theirs_ref, own_ref, came_ref, keep_ref, *give_refs):
     queries, conv = both_cores(own_ref, came_ref)
     gated = (queries * conv).astype(BF16)
     part = gated.shape[1] // 2
-    upper = upper_ref[0] == 1
+    upper = own_place()[1] % 2 == 1
     low, high = gated[:, :part], gated[:, part:]
     left = jnp.concatenate([mine_ref[...], theirs_ref[...]], 1)
-    keep_ref[...] = dot(left, jnp.where(upper, high, low))
+    keep_ref[...] = dot(left, jnp.where(upper, high, low)).astype(BF16)
     give = dot(left, jnp.where(upper, low, high)).astype(BF16)
     size = give_refs[0].shape[0]
     for i, ref in enumerate(give_refs):
         ref[...] = give[i * size : (i + 1) * size]
 
 
-def fold_kernel(upper_ref, after_ref, keep_ref, low_ref, high_ref, kept_ref, *give_refs):
-    total = keep_ref[...] + jnp.concatenate([low_ref[...], high_ref[...]], 0).astype(F32)
+def fold_kernel(after_ref, keep_ref, low_ref, high_ref, kept_ref, *give_refs):
+    total = keep_ref[...].astype(F32) + jnp.concatenate([low_ref[...], high_ref[...]], 0).astype(F32)
     depth, width = total.shape
     total = total.reshape(CORES * CHIPS, 2, depth // (2 * CORES * CHIPS), width)
     first = total[:, 0].reshape(depth // 2, width)
@@ -256,7 +271,7 @@
     part = width // 2
     low = jnp.concatenate([first[:, :part], second[:, :part]], 1)
     high = jnp.concatenate([first[:, part:], second[:, part:]], 1)
-    upper = upper_ref[0] == 1
+    upper = own_place()[0] % 2 == 1
     kept_ref[...] = jnp.where(upper, high, low)
     give = jnp.where(upper, low, high).astype(BF16)
     size = give_refs[0].shape[0]
@@ -268,17 +283,15 @@
     return [pl.BlockSpec(memory_space=pltpu.VMEM)] * count
 
 
-def call(kernel, out, scalars, *operands, scratch=(), after=()):
+def call(kernel, out, *operands, scratch=(), after=()):
     return pl.pallas_call(
         kernel,
         out_shape=[jax.ShapeDtypeStruct(shape, dtype) for shape, dtype in out],
-        in_specs=[pl.BlockSpec(memory_space=pltpu.SMEM)] * len(scalars)
-        + [pl.BlockSpec(memory_space=pl.ANY)] * len(after)
-        + in_vmem(len(operands)),
+        in_specs=[pl.BlockSpec(memory_space=pl.ANY)] * len(after) + in_vmem(len(operands)),
         out_specs=in_vmem(len(out)),
         scratch_shapes=[pltpu.VMEM(shape, F32) for shape in scratch],
         compiler_params=pltpu.CompilerParams(vmem_limit_bytes=10 << 20),
-    )(*scalars, *after, *operands)
+    )(*after, *operands)
 
 
 def shards(queries, key_proj, value_proj, conv_out, filters, out_grad, out_weight):
@@ -292,13 +305,6 @@
     kept = -(-(groups + 1) // 8) * 8
     sizes = (chips, chans, rows, kept)
 
-    place = lax.axis_index("seq")
-    odd = place % CORES == 1
-    x_place = place // (along_z * CORES)
-    z_place = place // CORES % along_z
-    x_scalar = x_place.reshape(1)
-    odd_scalar = odd.astype(jnp.int32).reshape(1)
-
     def send(value, dx, dz, core):
         pairs = []
         for i in range(groups):
@@ -317,22 +323,32 @@
     second, back = jnp.stack(halves(second)), jnp.stack(halves(second.T))
     twist = jnp.asarray(twist, F32)
 
-    def by_core(own, other):
-        return jnp.concatenate([jnp.where(odd, other, own), jnp.where(odd, own, other)], 1)
-
-    (packed,) = call(pack_kernel, [((groups, feats // 2 + chans, rows), BF16)], (), filters, out_weight)
-    arrived = lax.all_to_all(packed, "seq", 0, 0)
-    folded = arrived[:, : feats // 2].reshape(groups * feats // 2, rows)
-    weights = [folded] + [send(folded, hop, 0, 0) for hop in range(1, ALONG_X)]
+    (packed,) = call(
+        pack_kernel, [((chips, CORES * (feats + chans), rows), BF16)], filters, out_weight
+    )
+    like_cores = [list(range(core, groups, CORES)) for core in range(CORES)]
+    arrived = lax.all_to_all(packed, "seq", 0, 0, axis_index_groups=like_cores)
+    weight_own, weight_other = call(unpack_kernel, [((chips * feats, rows), BF16)] * 2, arrived)
+    weight_came = to_core(weight_other)
+    weights = [
+        weight_own, send(weight_own, 1, 0, 0), weight_came, send(weight_came, -1, 0, 0)
+    ]
+    filters_own, filters_other = call(
+        unpack_filters_kernel, [((chips * chans, rows), BF16)] * 2, arrived
+    )
     (filt,) = call(
         functools.partial(filter_kernel, sizes),
         [((chans * kept, 2 * rows), F32)],
-        (),
-        arrived[:, feats // 2 :].reshape(chan, rows),
+        filters_own,
+        to_core(filters_other),
         first,
         twist,
         second,
-        scratch=[(chan, rows)],
+        scratch=[(CORES, half, rows)],
+    )
+
+    halves_own, halves_other = call(
+        halves_kernel, [((CORES * rows, half), BF16)] * 2, queries, conv_out
     )
 
     features = lax.axis_size("ch")
@@ -344,23 +360,18 @@
     (wide,) = call(
         arrange_kernel,
         [((groups * feats, rows), BF16)],
-        (lax.axis_index("ch").reshape(1),),
         *around,
-        after=(arrived,),
+        after=(arrived, halves_own),
     )
     wide_there = to_core(wide)
     (left,) = call(
-        left_kernel, [((CORES * rows, groups * feats), BF16)], (), wide, wide_there
-    )
-    halves_own, halves_other = call(
-        halves_kernel, [((CORES * rows, half), BF16)] * 2, (odd_scalar,), queries, conv_out
+        left_kernel, [((CORES * rows, groups * feats), BF16)], wide, wide_there
     )
     halves_came = to_core(halves_other)
 
     keep, *give = call(
         partial_kernel,
-        [((groups * feats, half // 2), F32)] + [((groups * feats // 2, half // 2), BF16)] * 2,
-        ((z_place % 2).reshape(1),),
+        [((groups * feats, half // 2), BF16)] + [((groups * feats // 2, half // 2), BF16)] * 2,
         wide,
         wide_there,
         halves_own,
@@ -369,7 +380,6 @@
     turned, mine, theirs = call(
         gate_kernel,
         [((half, CORES * rows), BF16)] + [((rows, half), BF16)] * 2,
-        (x_scalar, odd_scalar),
         halves_own,
         halves_came,
         left,
@@ -380,7 +390,6 @@
         fold_kernel,
         [((groups * feats // 2, half // 2), F32)]
         + [((groups * feats // 4, half // 2), BF16)] * 2,
-        ((x_place % 2).reshape(1),),
         keep,
         *[lax.ppermute(value, "seq", [(i, i ^ CORES) for i in range(groups)]) for value in give],
         after=(turned,),
@@ -395,13 +404,13 @@
         "seq",
         0,
         0,
-        axis_index_groups=[list(range(core, groups, CORES)) for core in range(CORES)],
-    )
-    query_grad = by_core(mine, to_core(theirs))
+        axis_index_groups=like_cores,
+    )
+    theirs = to_core(theirs)
+    (query_grad,) = call(join_kernel, [((rows, chan), BF16)], mine, theirs)
     (inner,) = call(
         functools.partial(correlate_kernel, sizes),
         [((groups, feats // 2 + chans, rows), BF16)],
-        (),
         received.reshape(half, CORES * rows),
         filt,
         first,
@@ -412,11 +421,11 @@
         keep,
         *came,
         scratch=[(CORES, half, rows), (chan, rows)],
+        after=(theirs,),
     )
     key_grad, value_grad, weight_grad = call(
         functools.partial(outputs_kernel, (rows * groups) ** (-0.5)),
         [((rows, chan), BF16)] * 2 + [((feats, chan), F32)],
-        (),
         lax.all_to_all(inner, "seq", 0, 0),
         key_proj,
         value_proj,

time: 97 us -> 91.7 us (0.945)
  waiting for transfers between devices: 40.3 us -> 33 us
  starting transfers between devices: 40.3 us -> 47.1 us
  Pallas kernels: 10.8 us -> 8.47 us
  local copies, waits for them, and re-layouts: 3.55 us -> 1.82 us
    ppermute x6 -> x7, waiting for transfers between devices: 11.3 us -> 3.72 us  [send(): return lax.ppermute(value, 'seq', pairs)]
    ppermute x6 -> x7, starting transfers between devices: 4.93 us -> 10.6 us  [send(): return lax.ppermute(value, 'seq', pairs)]
    pallas_call x10 -> x13, Pallas kernels: 10.8 us -> 8.47 us  [call(): pl.pallas_call(kernel, out_shape=[jax.ShapeDtypeStruct(shape, dtype) for...]
    all_to_all x1, waiting for transfers between devices: 4.52 us -> 6.79 us  [shards(): arrived = lax.all_to_all(packed, 'seq', 0, 0, axis_index_groups=like_cores)]
    all_to_all x1, waiting for transfers between devices: 6.09 us -> 3.99 us  [shards(): lax.all_to_all(turned.reshape(chips, chans, CORES * rows), 'seq', 0, 0, a...]
    all_to_all x1, starting transfers between devices: 3.86 us -> 5.77 us  [shards(): lax.all_to_all(turned.reshape(chips, chans, CORES * rows), 'seq', 0, 0, a...]
    unnamed x35 -> x25, local copies, waits for them, and re-layouts: 3.52 us -> 1.82 us
    all_to_all x1, waiting for transfers between devices: 12.4 us -> 13.9 us  [shards(): lax.all_to_all(inner, 'seq', 0, 0)]
  transfers between devices with their start and end apart: 16 -> 17, of which waited for: 10 -> 10; matrix products, arithmetic and copies ran while one was open for 1% -> 0% of each run, Pallas kernels for 7% -> 5%
where the time goes in v6:
time: 91.7 us; the launch traced here: 91.2 us
  starting transfers between devices  47.1 us (51%)
  waiting for transfers between devices  33 us (36%)
  Pallas kernels  8.47 us (9%)
  local copies, waits for them, and re-layouts  1.82 us (2%)
    all_to_all x1, waiting for transfers between devices, shards(): lax.all_to_all(inner, 'seq', 0, 0)  13.9 us
    all_to_all x1, starting transfers between devices, shards(): arrived = lax.all_to_all(packed, 'seq', 0, 0, axis_index_groups=like_cores)  12 us
    all_to_all x1, starting transfers between devices, shards(): lax.all_to_all(inner, 'seq', 0, 0)  10.6 us
    ppermute x7, starting transfers between devices, send(): return lax.ppermute(value, 'seq', pairs)  10.6 us
    pallas_call x13, Pallas kernels, call(): pl.pallas_call(kernel, out_shape=[jax.ShapeDtypeStruct(shape, dtype) for...  8.47 us
    all_to_all x1, waiting for transfers between devices, shards(): arrived = lax.all_to_all(packed, 'seq', 0, 0, axis_index_groups=like_cores)  6.79 us
    all_to_all x1, starting transfers between devices, shards(): lax.all_to_all(turned.reshape(chips, chans, CORES * rows), 'seq', 0, 0, a...  5.77 us
    ppermute x3, starting transfers between devices, shards(): lax.ppermute(turned_grad, 'ch', [(i, (i - hop) % features) for i in range...  5.06 us
  transfers between devices with their start and end apart: 17, of which 10 were waited for; matrix products, arithmetic and copies ran while one was open for 0% of the time, Pallas kernels for 5%

profile of v6, /device:TPU:1, one launch (start us, length us, event | category | flops | bytes accessed | tf_op | source)
XLA Modules:
  0.0 91.2 jit_solution(1830113847633938878)
XLA Ops:
  0.6 0.9 copy-done.4
  1.5 0.8 copy-done.10
  2.3 1.0 %shard_map.183 = bf16[32,80,128]{2,1,0:T(8,128)(2,1)} custom-call(bf16[128,512]{1,0:T(8,128)(2,1)S(1)} %copy-done.4, bf16[32,512]{1,0:T(8,128)(2,1)S(1)} %copy-done.10), custom_call_target="tpu_custom_call" | custom-call | tf_op jit(solution)/shard_map/pallas_call | solution.py:287
  3.3 12.0 %all-to-all-start = ((bf16[32,80,128]{2,1,0:T(8,128)(2,1)}), bf16[32,80,128]{2,1,0:T(8,128)(2,1)S(1)}, u32[]{:S(2)}, u32[]{:S(2)}) async-start(bf16[32,80,128]{2,1,0:T(8,128)(2,1)} %shard_map.183), calls=%async_computation | async-start | bytes 1310720 | tf_op jit(solution)/shard_map/all_to_all | solution.py:330
  15.4 1.4 %collective-permute-start.4 = (bf16[512,128]{1,0:T(8,128)(2,1)S(1)}, bf16[512,128]{1,0:T(8,128)(2,1)S(1)}, u32[]{:S(2)}, u32[]{:S(2)}) collective-permute-start(bf16[512,128]{1,0:T(8,128)(2,1)S(1)} %bitcast.3), channel_id=1, source_target_pairs={{0,1},{1,2},{2,3},{3,0},{4,5},{5,6},{6,7},{7,4},{8,9},{9,10},{10,1... | collective-permute-start | bytes 393224 | tf_op jit(solution)/shard_map/ppermute | solution.py:357
  16.8 2.6 %collective-permute-start.3 = (bf16[512,128]{1,0:T(8,128)(2,1)S(1)}, bf16[512,128]{1,0:T(8,128)(2,1)S(1)}, u32[]{:S(2)}, u32[]{:S(2)}) collective-permute-start(bf16[512,128]{1,0:T(8,128)(2,1)S(1)} %bitcast.4), channel_id=1, source_target_pairs={{0,2},{1,3},{2,0},{3,1},{4,6},{5,7},{6,4},{7,5},{8,10},{9,11},{10,... | collective-permute-start | bytes 393224 | tf_op jit(solution)/shard_map/ppermute | solution.py:357
  19.4 1.1 %collective-permute-start.2 = (bf16[512,128]{1,0:T(8,128)(2,1)S(1)}, bf16[512,128]{1,0:T(8,128)(2,1)S(1)}, u32[]{:S(2)}, u32[]{:S(2)}) collective-permute-start(bf16[512,128]{1,0:T(8,128)(2,1)S(1)} %bitcast.5), channel_id=1, source_target_pairs={{0,3},{1,0},{2,1},{3,2},{4,7},{5,4},{6,5},{7,6},{8,11},{9,8},{10,9... | collective-permute-start | bytes 393224 | tf_op jit(solution)/shard_map/ppermute | solution.py:357
  20.9 3.9 %collective-permute-done.3.refs_4_ = bf16[512,128]{1,0:T(8,128)(2,1)S(1)} collective-permute-done((bf16[512,128]{1,0:T(8,128)(2,1)S(1)}, bf16[512,128]{1,0:T(8,128)(2,1)S(1)}, u32[]{:S(2)}, u32[]{:S(2)}) %collective-permute-start.3) | collective-permute-done | bytes 131104 | tf_op jit(solution)/shard_map/ppermute | solution.py:357
  24.9 6.8 %all-to-all-done.came_ref.refs_0_ = bf16[32,80,128]{2,1,0:T(8,128)(2,1)S(1)} async-done(((bf16[32,80,128]{2,1,0:T(8,128)(2,1)}), bf16[32,80,128]{2,1,0:T(8,128)(2,1)S(1)}, u32[]{:S(2)}, u32[]{:S(2)}) %all-to-all-start) | async-done | bytes 655392 | tf_op jit(solution)/shard_map/all_to_all | solution.py:330
  31.7 5.1 %collective-permute-start.5 = (bf16[2048,128]{1,0:T(8,128)(2,1)S(1)}, bf16[2048,128]{1,0:T(8,128)(2,1)S(1)}, u32[]{:S(2)}, u32[]{:S(2)}) collective-permute-start(bf16[2048,128]{1,0:T(8,128)(2,1)S(1)} %shard_map.187.mine_ref), channel_id=1, source_target_pairs={{0,4},{4,0},{8,12},{12,8},{16,20},{20,16},{24,28},{28,24},{32,36},... | collective-permute-start | bytes 1572872 | tf_op jit(solution)/shard_map/ppermute | solution.py:314
  37.0 0.5 collective-permute-start.1
  37.5 1.2 %collective-permute-done.7.refs_6_ = bf16[1024,128]{1,0:T(8,128)(2,1)S(1)} collective-permute-done((bf16[1024,128]{1,0:T(8,128)(2,1)S(1)}, bf16[1024,128]{1,0:T(8,128)(2,1)S(1)}, u32[]{:S(2)}, u32[]{:S(2)}) %collective-permute-start.7) | collective-permute-done | bytes 262176 | tf_op jit(solution)/shard_map/ppermute | solution.py:314
  38.7 1.5 %collective-permute-start.8 = (bf16[1024,128]{1,0:T(8,128)(2,1)S(1)}, bf16[1024,128]{1,0:T(8,128)(2,1)S(1)}, u32[]{:S(2)}, u32[]{:S(2)}) collective-permute-start(bf16[1024,128]{1,0:T(8,128)(2,1)S(1)} %collective-permute-done.7.refs_6_), channel_id=1, source_target_pairs={{0,192},{4,196},{8,200},{12,204},{16,208},{20,212},{24,216},{28,22... | collective-permute-start | bytes 786440 | tf_op jit(solution)/shard_map/ppermute | solution.py:314
  40.2 0.7 shard_map.192
  41.0 1.4 %collective-permute-start.10 = (bf16[1024,128]{1,0:T(8,128)(2,1)S(1)}, bf16[1024,128]{1,0:T(8,128)(2,1)S(1)}, u32[]{:S(2)}, u32[]{:S(2)}) collective-permute-start(bf16[1024,128]{1,0:T(8,128)(2,1)S(1)} %get-tuple-element.32), channel_id=1, source_target_pairs={{0,8},{4,12},{8,0},{12,4},{16,24},{20,28},{24,16},{28,20},{32,40},... | collective-permute-start | bytes 786440 | tf_op jit(solution)/shard_map/ppermute | solution.py:394
  42.6 1.3 %collective-permute-start = (bf16[256,128]{1,0:T(8,128)(2,1)S(1)}, bf16[256,128]{1,0:T(8,128)(2,1)S(1)}, u32[]{:S(2)}, u32[]{:S(2)}) collective-permute-start(bf16[256,128]{1,0:T(8,128)(2,1)S(1)} %get-tuple-element.23), channel_id=1, source_target_pairs={{0,4},{4,0},{8,12},{12,8},{16,20},{20,16},{24,28},{28,24},{32,36},... | collective-permute-start | bytes 196616 | tf_op jit(solution)/shard_map/ppermute | solution.py:314
  43.8 0.9 collective-permute-done.came_ref
  44.8 0.7 shard_map.185.refs_0_.refs_2_
  45.4 0.4 shard_map.188.refs_3_
  45.9 0.7 collective-permute-done.6.refs_5_
  46.6 1.2 %shard_map.190 = (bf16[256,256]{1,0:T(8,128)(2,1)}, bf16[128,256]{1,0:T(8,128)(2,1)S(1)}, bf16[128,256]{1,0:T(8,128)(2,1)S(1)}) custom-call(f32[576,256]{1,0:T(8,128)S(1)} %shard_map.185.refs_0_.refs_2_, bf16[256,256]{1,0:T(8,128)(2,1)S(1)} %get-tuple-element.24.refs_1_.own_ref, bf16[256,256]{1,0:T(8,128)(2,1)S(1)} %collective-permute-done.1.refs_2_.came_ref, ...), custom_call_target="tpu_custom_call" | custom-call | tf_op jit(solution)/shard_map/pallas_call | solution.py:287
  47.8 5.8 %all-to-all-start.1 = ((bf16[32,8,256]{2,1,0:T(8,128)(2,1)}), bf16[32,8,256]{2,1,0:T(8,128)(2,1)S(1)}, u32[]{:S(2)}, u32[]{:S(2)}) async-start(bf16[32,8,256]{2,1,0:T(8,128)(2,1)} %bitcast.1), calls=%async_computation.1 | async-start | bytes 262144 | tf_op jit(solution)/shard_map/all_to_all | solution.py:402
  54.2 1.1 %collective-permute-start.12 = (bf16[512,128]{1,0:T(8,128)(2,1)S(1)}, bf16[512,128]{1,0:T(8,128)(2,1)S(1)}, u32[]{:S(2)}, u32[]{:S(2)}) collective-permute-start(bf16[512,128]{1,0:T(8,128)(2,1)S(1)} %get-tuple-element.35), channel_id=1, source_target_pairs={{0,64},{4,68},{8,72},{12,76},{16,80},{20,84},{24,88},{28,92},{32,9... | collective-permute-start | bytes 393224 | tf_op jit(solution)/shard_map/ppermute | solution.py:398
  55.3 0.5 collective-permute-start.13
  55.8 2.1 %collective-permute-start.9 = (bf16[128,256]{1,0:T(8,128)(2,1)S(1)}, bf16[128,256]{1,0:T(8,128)(2,1)S(1)}, u32[]{:S(2)}, u32[]{:S(2)}) collective-permute-start(bf16[128,256]{1,0:T(8,128)(2,1)S(1)} %get-tuple-element.29), channel_id=1, source_target_pairs={{0,4},{4,0},{8,12},{12,8},{16,20},{20,16},{24,28},{28,24},{32,36},... | collective-permute-start | bytes 196616 | tf_op jit(solution)/shard_map/ppermute | solution.py:314
  57.8 0.9 collective-permute-done.9.theirs_ref.refs_0_
  58.7 4.0 %all-to-all-done.1 = bf16[32,8,256]{2,1,0:T(8,128)(2,1)S(1)} async-done(((bf16[32,8,256]{2,1,0:T(8,128)(2,1)}), bf16[32,8,256]{2,1,0:T(8,128)(2,1)S(1)}, u32[]{:S(2)}, u32[]{:S(2)}) %all-to-all-start.1) | async-done | bytes 131104 | tf_op jit(solution)/shard_map/all_to_all | solution.py:402
  62.8 2.4 %shard_map.194 = bf16[64,24,128]{2,1,0:T(8,128)(2,1)} custom-call(bf16[128,256]{1,0:T(8,128)(2,1)S(1)} %collective-permute-done.9.theirs_ref.refs_0_, bf16[256,256]{1,0:T(8,128)(2,1)S(1)} %bitcast.7, f32[576,256]{1,0:T(8,128)S(1)} %shard_map.185.refs_0_.refs_2_, bf16[2,144,64]{2,1,0:T(8,128)(2,1)S(1)} %copy-done.1, f32[2,72,128]{2,1,0:T(8,128)S(1)} %copy-done.2, ...), custom_call_target="tpu_custom_call" | custom-call | tf_op jit(solution)/shard_map/pallas_call | solution.py:287
  65.2 10.6 %all-to-all-start.2 = ((bf16[64,24,128]{2,1,0:T(8,128)(2,1)}), bf16[64,24,128]{2,1,0:T(8,128)(2,1)S(1)}, u32[]{:S(2)}, u32[]{:S(2)}) async-start(bf16[64,24,128]{2,1,0:T(8,128)(2,1)} %shard_map.194), calls=%async_computation.2 | async-start | bytes 786432 | tf_op jit(solution)/shard_map/all_to_all | solution.py:429
  75.8 0.7 shard_map.191
  76.5 13.9 %all-to-all-done.2.came_ref = bf16[64,24,128]{2,1,0:T(8,128)(2,1)S(1)} async-done(((bf16[64,24,128]{2,1,0:T(8,128)(2,1)}), bf16[64,24,128]{2,1,0:T(8,128)(2,1)S(1)}, u32[]{:S(2)}, u32[]{:S(2)}) %all-to-all-start.2) | async-done | bytes 393248 | tf_op jit(solution)/shard_map/all_to_all | solution.py:429
  90.4 0.8 shard_map.195
  (40 shorter events, 1.7 us)
Async XLA Ops:
  0.6 0.9 copy-start.4
  1.5 0.8 copy-start.10
  3.3 12.0 %copy-start.11 = (bf16[128,512]{1,0:T(8,128)(2,1)S(1)}, bf16[128,512]{1,0:T(8,128)(2,1)}, u32[]{:S(2)}) copy-start(bf16[128,512]{1,0:T(8,128)(2,1)} %param.21) | copy-start | bytes 393220
  3.3 28.4 %all-to-all-start = ((bf16[32,80,128]{2,1,0:T(8,128)(2,1)}), bf16[32,80,128]{2,1,0:T(8,128)(2,1)S(1)}, u32[]{:S(2)}, u32[]{:S(2)}) async-start(bf16[32,80,128]{2,1,0:T(8,128)(2,1)} %shard_map.183), calls=%async_computation | async-start | bytes 1310720 | tf_op jit(solution)/shard_map/all_to_all | solution.py:330
  15.3 5.2 %copy-start.7 = (bf16[128,512]{1,0:T(8,128)(2,1)S(1)}, bf16[128,512]{1,0:T(8,128)(2,1)}, u32[]{:S(2)}) copy-start(bf16[128,512]{1,0:T(8,128)(2,1)} %refs_0_.1) | copy-start | bytes 393220
  15.3 5.2 %copy-start.8 = (bf16[128,512]{1,0:T(8,128)(2,1)S(1)}, bf16[128,512]{1,0:T(8,128)(2,1)}, u32[]{:S(2)}) copy-start(bf16[128,512]{1,0:T(8,128)(2,1)} %refs_1_.1) | copy-start | bytes 393220
  15.4 5.5 %collective-permute-start.4 = (bf16[512,128]{1,0:T(8,128)(2,1)S(1)}, bf16[512,128]{1,0:T(8,128)(2,1)S(1)}, u32[]{:S(2)}, u32[]{:S(2)}) collective-permute-start(bf16[512,128]{1,0:T(8,128)(2,1)S(1)} %bitcast.3), channel_id=1, source_target_pairs={{0,1},{1,2},{2,3},{3,0},{4,5},{5,6},{6,7},{7,4},{8,9},{9,10},{10,1... | collective-permute-start | bytes 393224 | tf_op jit(solution)/shard_map/ppermute | solution.py:357
  16.8 8.0 %collective-permute-start.3 = (bf16[512,128]{1,0:T(8,128)(2,1)S(1)}, bf16[512,128]{1,0:T(8,128)(2,1)S(1)}, u32[]{:S(2)}, u32[]{:S(2)}) collective-permute-start(bf16[512,128]{1,0:T(8,128)(2,1)S(1)} %bitcast.4), channel_id=1, source_target_pairs={{0,2},{1,3},{2,0},{3,1},{4,6},{5,7},{6,4},{7,5},{8,10},{9,11},{10,... | collective-permute-start | bytes 393224 | tf_op jit(solution)/shard_map/ppermute | solution.py:357
  19.4 5.4 %collective-permute-start.2 = (bf16[512,128]{1,0:T(8,128)(2,1)S(1)}, bf16[512,128]{1,0:T(8,128)(2,1)S(1)}, u32[]{:S(2)}, u32[]{:S(2)}) collective-permute-start(bf16[512,128]{1,0:T(8,128)(2,1)S(1)} %bitcast.5), channel_id=1, source_target_pairs={{0,3},{1,0},{2,1},{3,2},{4,7},{5,4},{6,5},{7,6},{8,11},{9,8},{10,9... | collective-permute-start | bytes 393224 | tf_op jit(solution)/shard_map/ppermute | solution.py:357
  31.7 8.5 %collective-permute-start.5 = (bf16[2048,128]{1,0:T(8,128)(2,1)S(1)}, bf16[2048,128]{1,0:T(8,128)(2,1)S(1)}, u32[]{:S(2)}, u32[]{:S(2)}) collective-permute-start(bf16[2048,128]{1,0:T(8,128)(2,1)S(1)} %shard_map.187.mine_ref), channel_id=1, source_target_pairs={{0,4},{4,0},{8,12},{12,8},{16,20},{20,16},{24,28},{28,24},{32,36},... | collective-permute-start | bytes 1572872 | tf_op jit(solution)/shard_map/ppermute | solution.py:314
  36.9 1.8 %collective-permute-start.7 = (bf16[1024,128]{1,0:T(8,128)(2,1)S(1)}, bf16[1024,128]{1,0:T(8,128)(2,1)S(1)}, u32[]{:S(2)}, u32[]{:S(2)}) collective-permute-start(bf16[1024,128]{1,0:T(8,128)(2,1)S(1)} %get-tuple-element.27), channel_id=1, source_target_pairs={{0,4},{4,0},{8,12},{12,8},{16,20},{20,16},{24,28},{28,24},{32,36},... | collective-permute-start | bytes 786440 | tf_op jit(solution)/shard_map/ppermute | solution.py:314
  37.0 3.2 %collective-permute-start.1 = (bf16[256,256]{1,0:T(8,128)(2,1)S(1)}, bf16[256,256]{1,0:T(8,128)(2,1)S(1)}, u32[]{:S(2)}, u32[]{:S(2)}) collective-permute-start(bf16[256,256]{1,0:T(8,128)(2,1)S(1)} %get-tuple-element.25), channel_id=1, source_target_pairs={{0,4},{4,0},{8,12},{12,8},{16,20},{20,16},{24,28},{28,24},{32,36},... | collective-permute-start | bytes 393224 | tf_op jit(solution)/shard_map/ppermute | solution.py:314
  37.5 9.1 %collective-permute-start.6 = (bf16[1024,128]{1,0:T(8,128)(2,1)S(1)}, bf16[1024,128]{1,0:T(8,128)(2,1)S(1)}, u32[]{:S(2)}, u32[]{:S(2)}) collective-permute-start(bf16[1024,128]{1,0:T(8,128)(2,1)S(1)} %get-tuple-element.26.refs_4_), channel_id=1, source_target_pairs={{0,64},{4,68},{8,72},{12,76},{16,80},{20,84},{24,88},{28,92},{32,9... | collective-permute-start | bytes 786440 | tf_op jit(solution)/shard_map/ppermute | solution.py:314
  38.7 7.9 %collective-permute-start.8 = (bf16[1024,128]{1,0:T(8,128)(2,1)S(1)}, bf16[1024,128]{1,0:T(8,128)(2,1)S(1)}, u32[]{:S(2)}, u32[]{:S(2)}) collective-permute-start(bf16[1024,128]{1,0:T(8,128)(2,1)S(1)} %collective-permute-done.7.refs_6_), channel_id=1, source_target_pairs={{0,192},{4,196},{8,200},{12,204},{16,208},{20,212},{24,216},{28,22... | collective-permute-start | bytes 786440 | tf_op jit(solution)/shard_map/ppermute | solution.py:314
  41.0 12.6 %collective-permute-start.10 = (bf16[1024,128]{1,0:T(8,128)(2,1)S(1)}, bf16[1024,128]{1,0:T(8,128)(2,1)S(1)}, u32[]{:S(2)}, u32[]{:S(2)}) collective-permute-start(bf16[1024,128]{1,0:T(8,128)(2,1)S(1)} %get-tuple-element.32), channel_id=1, source_target_pairs={{0,8},{4,12},{8,0},{12,4},{16,24},{20,28},{24,16},{28,20},{32,40},... | collective-permute-start | bytes 786440 | tf_op jit(solution)/shard_map/ppermute | solution.py:394
  42.4 2.4 %copy-start = (bf16[2,256,256]{2,1,0:T(8,128)(2,1)S(1)}, bf16[2,256,256]{2,1,0:T(8,128)(2,1)}, u32[]{:S(2)}) copy-start(bf16[2,256,256]{2,1,0:T(8,128)(2,1)} %constant.33.second_ref.refs_5_) | copy-start | bytes 786436
  42.4 2.4 %copy-start.1 = (bf16[2,144,64]{2,1,0:T(8,128)(2,1)S(1)}, bf16[2,144,64]{2,1,0:T(8,128)(2,1)}, u32[]{:S(2)}) copy-start(bf16[2,144,64]{2,1,0:T(8,128)(2,1)} %constant.30.first_ref.refs_3_) | copy-start | bytes 110596
  42.4 2.4 %copy-start.2 = (f32[2,72,128]{2,1,0:T(8,128)S(1)}, f32[2,72,128]{2,1,0:T(8,128)}, u32[]{:S(2)}) copy-start(f32[2,72,128]{2,1,0:T(8,128)} %constant.26.clone.twist_ref.refs_4_) | copy-start | bytes 221188
  42.4 11.5 %collective-permute-start.11 = (bf16[1024,128]{1,0:T(8,128)(2,1)S(1)}, bf16[1024,128]{1,0:T(8,128)(2,1)S(1)}, u32[]{:S(2)}, u32[]{:S(2)}) collective-permute-start(bf16[1024,128]{1,0:T(8,128)(2,1)S(1)} %get-tuple-element.33), channel_id=1, source_target_pairs={{0,8},{4,12},{8,0},{12,4},{16,24},{20,28},{24,16},{28,20},{32,40},... | collective-permute-start | bytes 786440 | tf_op jit(solution)/shard_map/ppermute | solution.py:394
  42.6 2.2 %collective-permute-start = (bf16[256,128]{1,0:T(8,128)(2,1)S(1)}, bf16[256,128]{1,0:T(8,128)(2,1)S(1)}, u32[]{:S(2)}, u32[]{:S(2)}) collective-permute-start(bf16[256,128]{1,0:T(8,128)(2,1)S(1)} %get-tuple-element.23), channel_id=1, source_target_pairs={{0,4},{4,0},{8,12},{12,8},{16,20},{20,16},{24,28},{28,24},{32,36},... | collective-permute-start | bytes 196616 | tf_op jit(solution)/shard_map/ppermute | solution.py:314
  47.8 15.0 %all-to-all-start.1 = ((bf16[32,8,256]{2,1,0:T(8,128)(2,1)}), bf16[32,8,256]{2,1,0:T(8,128)(2,1)S(1)}, u32[]{:S(2)}, u32[]{:S(2)}) async-start(bf16[32,8,256]{2,1,0:T(8,128)(2,1)} %bitcast.1), calls=%async_computation.1 | async-start | bytes 262144 | tf_op jit(solution)/shard_map/all_to_all | solution.py:402
  53.9 8.9 %copy-start.3 = (bf16[2,256,256]{2,1,0:T(8,128)(2,1)S(1)}, bf16[2,256,256]{2,1,0:T(8,128)(2,1)}, u32[]{:S(2)}) copy-start(bf16[2,256,256]{2,1,0:T(8,128)(2,1)} %constant.36.refs_6_) | copy-start | bytes 786436
  53.9 8.9 %copy-start.9 = (bf16[2,64,144]{2,1,0:T(8,128)(2,1)S(1)}, bf16[2,64,144]{2,1,0:T(8,128)(2,1)}, u32[]{:S(2)}) copy-start(bf16[2,64,144]{2,1,0:T(8,128)(2,1)} %constant.39.refs_7_) | copy-start | bytes 110596
  54.2 8.5 %collective-permute-start.12 = (bf16[512,128]{1,0:T(8,128)(2,1)S(1)}, bf16[512,128]{1,0:T(8,128)(2,1)S(1)}, u32[]{:S(2)}, u32[]{:S(2)}) collective-permute-start(bf16[512,128]{1,0:T(8,128)(2,1)S(1)} %get-tuple-element.35), channel_id=1, source_target_pairs={{0,64},{4,68},{8,72},{12,76},{16,80},{20,84},{24,88},{28,92},{32,9... | collective-permute-start | bytes 393224 | tf_op jit(solution)/shard_map/ppermute | solution.py:398
  55.3 7.5 %collective-permute-start.13 = (bf16[512,128]{1,0:T(8,128)(2,1)S(1)}, bf16[512,128]{1,0:T(8,128)(2,1)S(1)}, u32[]{:S(2)}, u32[]{:S(2)}) collective-permute-start(bf16[512,128]{1,0:T(8,128)(2,1)S(1)} %get-tuple-element.36), channel_id=1, source_target_pairs={{0,64},{4,68},{8,72},{12,76},{16,80},{20,84},{24,88},{28,92},{32,9... | collective-permute-start | bytes 393224 | tf_op jit(solution)/shard_map/ppermute | solution.py:398
  55.8 3.0 %collective-permute-start.9 = (bf16[128,256]{1,0:T(8,128)(2,1)S(1)}, bf16[128,256]{1,0:T(8,128)(2,1)S(1)}, u32[]{:S(2)}, u32[]{:S(2)}) collective-permute-start(bf16[128,256]{1,0:T(8,128)(2,1)S(1)} %get-tuple-element.29), channel_id=1, source_target_pairs={{0,4},{4,0},{8,12},{12,8},{16,20},{20,16},{24,28},{28,24},{32,36},... | collective-permute-start | bytes 196616 | tf_op jit(solution)/shard_map/ppermute | solution.py:314
  65.2 25.2 %all-to-all-start.2 = ((bf16[64,24,128]{2,1,0:T(8,128)(2,1)}), bf16[64,24,128]{2,1,0:T(8,128)(2,1)S(1)}, u32[]{:S(2)}, u32[]{:S(2)}) async-start(bf16[64,24,128]{2,1,0:T(8,128)(2,1)} %shard_map.194), calls=%async_computation.2 | async-start | bytes 786432 | tf_op jit(solution)/shard_map/all_to_all | solution.py:429
  75.8 14.6 %copy-start.5 = (bf16[128,512]{1,0:T(8,128)(2,1)S(1)}, bf16[128,512]{1,0:T(8,128)(2,1)}, u32[]{:S(2)}) copy-start(bf16[128,512]{1,0:T(8,128)(2,1)} %key_ref.1) | copy-start | bytes 393220
  75.8 14.6 %copy-start.6 = (bf16[128,512]{1,0:T(8,128)(2,1)S(1)}, bf16[128,512]{1,0:T(8,128)(2,1)}, u32[]{:S(2)}) copy-start(bf16[128,512]{1,0:T(8,128)(2,1)} %value_ref.1) | copy-start | bytes 393220

commit v7 on v6

--- a/solution.py
+++ b/solution.py
@@ -94,10 +94,11 @@
 
 def correlate_kernel(sizes, *refs):
     x_ref, filt_ref, first_ref, twist_ref, second_ref, back_ref, last_ref = refs[1:8]
-    kept_ref, *came_refs, out_ref, wide, plane = refs[8:]
+    kept_ref, *came_refs, out_ref, wide = refs[8:]
     chips, chans, rows, kept = sizes
+    came = x_ref[...].astype(F32)
     for core in range(CORES):
-        wide[core] = x_ref[:, core * rows : (core + 1) * rows].astype(F32)
+        wide[core] = came[:, core * chans : (core + 1) * chans].reshape(chips * chans, rows)
     data = by_channel(wide, chips, chans)
     grads = spectrum(data, first_ref, twist_ref, second_ref, chans, rows, kept)
     g_re, g_im = grads[:, :rows], grads[:, rows:]
@@ -113,14 +114,15 @@
     inner = dot3((last_ref[0], last_ref[1]), split(jnp.concatenate(parts, 1)))
     for c in range(chans):
         for core in range(CORES):
-            plane[pl.ds(core * chans + c, chips, stride=CORES * chans), :] = inner[
+            wide[core, pl.ds(c, chips, stride=chans), :] = inner[
                 core * chips : (core + 1) * chips, c * rows : (c + 1) * rows
             ]
-    groups, depth, _ = out_ref.shape
+    depth = out_ref.shape[1] - CORES * chans
     came = jnp.concatenate([ref[...] for ref in came_refs], 0)
     total = (kept_ref[...] + came.astype(F32)).astype(BF16)
-    out_ref[:, : depth - chans, :] = total.reshape(groups, depth - chans, rows)
-    out_ref[:, depth - chans :, :] = plane[...].astype(BF16).reshape(groups, chans, rows)
+    out_ref[:, :depth, :] = total.reshape(chips, depth, rows)
+    blocks = [wide[core].reshape(chips, chans, rows) for core in range(CORES)]
+    out_ref[:, depth:, :] = jnp.concatenate(blocks, 1).astype(BF16)
 
 
 def pack_kernel(filters_ref, weight_ref, out_ref):
@@ -139,12 +141,16 @@
                     out_ref[chip, core * feats : (core + 1) * feats, :] = piece
 
 
-def unpack_kernel(came_ref, own_ref, other_ref):
-    feats = own_ref.shape[0] // CHIPS
-    odd = own_place()[2] == 1
-    first, second = came_ref[:, :feats, :], came_ref[:, feats : 2 * feats, :]
-    own_ref[...] = jnp.where(odd, second, first).reshape(own_ref.shape)
-    other_ref[...] = jnp.where(odd, first, second).reshape(other_ref.shape)
+def unpack_kernel(after_ref, came_ref, *out_refs):
+    size = out_refs[0].shape[0]
+    chips = came_ref.shape[0]
+    feats = 2 * size // chips
+    odd = own_place()[2] == 1
+    for i in range(2):
+        place = slice(i * chips // 2, (i + 1) * chips // 2)
+        first, second = came_ref[place, :feats, :], came_ref[place, feats : 2 * feats, :]
+        out_refs[i][...] = jnp.where(odd, second, first).reshape(size, -1)
+        out_refs[2 + i][...] = jnp.where(odd, first, second).reshape(size, -1)
 
 
 def unpack_filters_kernel(came_ref, own_ref, other_ref):
@@ -188,25 +194,32 @@
 
 
 def gate_kernel(*refs):
-    own_ref, came_ref, left_ref, a_ref, b_ref, c_ref, d_ref, turned_ref, mine_ref, theirs_ref = refs[-10:]
+    own_ref, came_ref, left_ref, *weight_refs, turned_ref, mine_ref, theirs_ref = refs[-14:]
     x, _, core = own_place()
     odd = core == 1
     rows = mine_ref.shape[0]
-    depth = a_ref.shape[0]
-    gate = dot(left_ref[:, :depth], jnp.concatenate([a_ref[...], b_ref[...]], 1))
-    gate += dot(left_ref[:, depth:], jnp.concatenate([c_ref[...], d_ref[...]], 1))
+    weight = jnp.concatenate(
+        [jnp.concatenate([ref[...] for ref in weight_refs[i : i + 4]], 0) for i in (0, 4)], 1
+    )
+    gate = dot(left_ref[...], weight)
     part = gate.shape[1] // 2
     gate = jnp.where(x % 2 == 1, jnp.concatenate([gate[:, part:], gate[:, :part]], 1), gate)
     queries, conv = both_cores(own_ref, came_ref)
     turned = (gate * queries).astype(BF16).astype(F32).T
-    swapped = jnp.concatenate([turned[:, rows:], turned[:, :rows]], 1)
-    turned_ref[...] = jnp.where(odd, swapped, turned).astype(BF16)
+    chips, blocks, _ = turned_ref.shape
+    own, other = (
+        turned[:, i * rows : (i + 1) * rows].reshape(chips, blocks // CORES, rows) for i in range(2)
+    )
+    turned_ref[...] = jnp.concatenate(
+        [jnp.where(odd, other, own), jnp.where(odd, own, other)], 1
+    ).astype(BF16)
     query_grad = (gate * conv).astype(BF16)
     mine_ref[...] = query_grad[:rows]
     theirs_ref[...] = query_grad[rows:]
 
 
-def join_kernel(mine_ref, theirs_ref, out_ref):
+def join_kernel(mine_ref, theirs_ref, out_ref, token_ref):
+    token_ref[...] = jnp.zeros_like(token_ref)
     odd = own_place()[2] == 1
     mine, theirs = mine_ref[...], theirs_ref[...]
     half = mine.shape[1]
@@ -214,30 +227,53 @@
     out_ref[:, half:] = jnp.where(odd, mine, theirs)
 
 
-def outputs_kernel(scale, came_ref, key_ref, value_ref, key_grad_ref, value_grad_ref, weight_grad_ref):
-    rows, chan = key_ref.shape
-    groups, depth, _ = came_ref.shape
-    feats, chans = weight_grad_ref.shape[0], chan // groups
-    folded = feats // 2
-    inner = came_ref[:, folded:, :].astype(F32).reshape(CHIPS, CORES, chans, rows)
-    inner = jnp.swapaxes(inner, 0, 1).reshape(chan, rows).T
-    key_grad_ref[...] = (inner * value_ref[...].astype(F32)).astype(BF16)
-    value_grad_ref[...] = (inner * key_ref[...].astype(F32)).astype(BF16)
-    sums = came_ref[:, :folded, :].astype(F32)
-    sums = sums.reshape(ALONG_X // 2, 2, CHIPS // ALONG_X // 2, 2, CORES, folded, rows)
-    sums = jnp.sum(jnp.sum(sums, 2), 0) * scale
+def parts_kernel(came_ref, inner_ref, inner_other_ref, weight_ref, weight_other_ref):
+    odd = own_place()[2] == 1
+    chips, depth, rows = came_ref.shape
+    feats = weight_ref.shape[0]
+    chans = inner_ref.shape[0] // chips
+    inner = came_ref[:, feats:, :].astype(F32).reshape(chips, CORES, chans, rows)
+    first, second = (inner[:, core].reshape(chips * chans, rows) for core in range(CORES))
+    inner_ref[...] = jnp.where(odd, second, first).astype(BF16)
+    inner_other_ref[...] = jnp.where(odd, first, second).astype(BF16)
+    sums = came_ref[:, :feats, :].astype(F32)
+    sums = sums.reshape(ALONG_X // 2, 2, ALONG_Z // 2, 2, CORES, feats // 2, rows)
+    sums = jnp.sum(jnp.sum(sums, 2), 0)
     part = rows // 2
-    for high in range(2):
-        value = jnp.concatenate(
+    first, second = (
+        jnp.concatenate(
             [
-                sums[x, z, core, :, high * part : (high + 1) * part]
-                for core in range(CORES)
-                for z in range(2)
-                for x in range(2)
+                jnp.concatenate(
+                    [
+                        sums[x, z, core, :, high * part : (high + 1) * part]
+                        for z in range(2)
+                        for x in range(2)
+                    ],
+                    1,
+                )
+                for high in range(2)
             ],
-            1,
+            0,
         )
-        weight_grad_ref[high * folded : (high + 1) * folded, :] = value
+        for core in range(CORES)
+    )
+    weight_ref[...] = jnp.where(odd, second, first)
+    weight_other_ref[...] = jnp.where(odd, first, second)
+
+
+def outputs_kernel(
+    scale, own_ref, came_ref, weight_ref, beside_ref, key_ref, value_ref, key_grad_ref, value_grad_ref, weight_grad_ref
+):
+    odd = own_place()[2] == 1
+    half = own_ref.shape[0]
+    own, came = own_ref[...].astype(F32).T, came_ref[...].astype(F32).T
+    for i, inner in enumerate((jnp.where(odd, came, own), jnp.where(odd, own, came))):
+        place = slice(i * half, (i + 1) * half)
+        key_grad_ref[:, place] = (inner * value_ref[:, place].astype(F32)).astype(BF16)
+        value_grad_ref[:, place] = (inner * key_ref[:, place].astype(F32)).astype(BF16)
+    own, came = weight_ref[...] * scale, beside_ref[...] * scale
+    weight_grad_ref[:, :half] = jnp.where(odd, came, own)
+    weight_grad_ref[:, half:] = jnp.where(odd, own, came)
 
 
 def arrange_kernel(*refs):
@@ -262,8 +298,9 @@
         ref[...] = give[i * size : (i + 1) * size]
 
 
-def fold_kernel(after_ref, keep_ref, low_ref, high_ref, kept_ref, *give_refs):
-    total = keep_ref[...].astype(F32) + jnp.concatenate([low_ref[...], high_ref[...]], 0).astype(F32)
+def fold_kernel(after_ref, keep_ref, *refs):
+    came_refs, (kept_ref, *give_refs) = refs[:1], refs[1:]
+    total = keep_ref[...].astype(F32) + jnp.concatenate([ref[...] for ref in came_refs], 0).astype(F32)
     depth, width = total.shape
     total = total.reshape(CORES * CHIPS, 2, depth // (2 * CORES * CHIPS), width)
     first = total[:, 0].reshape(depth // 2, width)
@@ -328,25 +365,6 @@
     )
     like_cores = [list(range(core, groups, CORES)) for core in range(CORES)]
     arrived = lax.all_to_all(packed, "seq", 0, 0, axis_index_groups=like_cores)
-    weight_own, weight_other = call(unpack_kernel, [((chips * feats, rows), BF16)] * 2, arrived)
-    weight_came = to_core(weight_other)
-    weights = [
-        weight_own, send(weight_own, 1, 0, 0), weight_came, send(weight_came, -1, 0, 0)
-    ]
-    filters_own, filters_other = call(
-        unpack_filters_kernel, [((chips * chans, rows), BF16)] * 2, arrived
-    )
-    (filt,) = call(
-        functools.partial(filter_kernel, sizes),
-        [((chans * kept, 2 * rows), F32)],
-        filters_own,
-        to_core(filters_other),
-        first,
-        twist,
-        second,
-        scratch=[(CORES, half, rows)],
-    )
-
     halves_own, halves_other = call(
         halves_kernel, [((CORES * rows, half), BF16)] * 2, queries, conv_out
     )
@@ -361,7 +379,7 @@
         arrange_kernel,
         [((groups * feats, rows), BF16)],
         *around,
-        after=(arrived, halves_own),
+        after=(halves_own,),
     )
     wide_there = to_core(wide)
     (left,) = call(
@@ -371,20 +389,36 @@
 
     keep, *give = call(
         partial_kernel,
-        [((groups * feats, half // 2), BF16)] + [((groups * feats // 2, half // 2), BF16)] * 2,
+        [((groups * feats, half // 2), BF16)] + [((groups * feats // 1, half // 2), BF16)] * 1,
         wide,
         wide_there,
         halves_own,
         halves_came,
     )
+    pieces = call(unpack_kernel, [((chips * feats // 2, rows), BF16)] * 4, arrived, after=(keep,))
+    pieces = [*pieces[:2]] + [to_core(piece) for piece in pieces[2:]]
+    weights = pieces + [send(piece, 1 - 2 * (i % 2), 0, 0) for i, piece in enumerate(pieces)]
+    filters_own, filters_other = call(
+        unpack_filters_kernel, [((chips * chans, rows), BF16)] * 2, arrived
+    )
+    (filt,) = call(
+        functools.partial(filter_kernel, sizes),
+        [((chans * kept, 2 * rows), F32)],
+        filters_own,
+        to_core(filters_other),
+        first,
+        twist,
+        second,
+        scratch=[(CORES, half, rows)],
+    )
+
     turned, mine, theirs = call(
         gate_kernel,
-        [((half, CORES * rows), BF16)] + [((rows, half), BF16)] * 2,
+        [((chips, CORES * chans, rows), BF16)] + [((rows, half), BF16)] * 2,
         halves_own,
         halves_came,
         left,
         *weights,
-        after=(filt,),
     )
     keep, *give = call(
         fold_kernel,
@@ -400,18 +434,20 @@
     ]
 
     received = lax.all_to_all(
-        turned.reshape(chips, chans, CORES * rows),
+        turned,
         "seq",
         0,
         0,
         axis_index_groups=like_cores,
     )
     theirs = to_core(theirs)
-    (query_grad,) = call(join_kernel, [((rows, chan), BF16)], mine, theirs)
+    query_grad, joined = call(
+        join_kernel, [((rows, chan), BF16), ((8, rows), F32)], mine, theirs
+    )
     (inner,) = call(
         functools.partial(correlate_kernel, sizes),
-        [((groups, feats // 2 + chans, rows), BF16)],
-        received.reshape(half, CORES * rows),
+        [((chips, CORES * (feats // 2 + chans), rows), BF16)],
+        received,
         filt,
         first,
         twist,
@@ -420,13 +456,21 @@
         last,
         keep,
         *came,
-        scratch=[(CORES, half, rows), (chan, rows)],
-        after=(theirs,),
+        scratch=[(CORES, half, rows)],
+        after=(joined,),
+    )
+    inner, inner_other, weight_sum, weight_sum_other = call(
+        parts_kernel,
+        [((half, rows), BF16)] * 2 + [((feats, half), F32)] * 2,
+        lax.all_to_all(inner, "seq", 0, 0, axis_index_groups=like_cores),
     )
     key_grad, value_grad, weight_grad = call(
         functools.partial(outputs_kernel, (rows * groups) ** (-0.5)),
         [((rows, chan), BF16)] * 2 + [((feats, chan), F32)],
-        lax.all_to_all(inner, "seq", 0, 0),
+        inner,
+        to_core(inner_other),
+        weight_sum,
+        to_core(weight_sum_other),
         key_proj,
         value_proj,
     )

time: 91.7 us -> 88.8 us (0.968)
  blocking collectives: 0 us -> 18 us
  waiting for transfers between devices: 33 us -> 15.7 us
  starting transfers between devices: 47.1 us -> 43.5 us
    all_to_all x0 -> x1, blocking collectives: none -> 18 us  [shards(): lax.all_to_all(inner, 'seq', 0, 0, axis_index_groups=like_cores)]
    all_to_all x2 -> x1, waiting for transfers between devices: 17.9 us -> 1.58 us  [shards(): received = lax.all_to_all(turned, 'seq', 0, 0, axis_index_groups=like_cores)]
    all_to_all x2 -> x1, starting transfers between devices: 16.4 us -> 5.76 us  [shards(): received = lax.all_to_all(turned, 'seq', 0, 0, axis_index_groups=like_cores)]
    ppermute x7 -> x12, starting transfers between devices: 10.6 us -> 19 us  [send(): return lax.ppermute(value, 'seq', pairs)]
    all_to_all x1, waiting for transfers between devices: 6.79 us -> 0.01 us  [shards(): arrived = lax.all_to_all(packed, 'seq', 0, 0, axis_index_groups=like_cores)]
    ppermute x3, waiting for transfers between devices: 4.32 us -> 8.19 us  [shards(): lax.ppermute(turned_grad, 'ch', [(i, (i - hop) % features) for i in range...]
    ppermute x7 -> x12, waiting for transfers between devices: 3.72 us -> 5.92 us  [send(): return lax.ppermute(value, 'seq', pairs)]
    ppermute x3, starting transfers between devices: 5.06 us -> 3.85 us  [shards(): lax.ppermute(turned_grad, 'ch', [(i, (i - hop) % features) for i in range...]
  transfers between devices with their start and end apart: 17 -> 20, of which waited for: 10 -> 9; matrix products, arithmetic and copies ran while one was open for 0% -> 0% of each run, Pallas kernels for 5% -> 6%
where the time goes in v7:
time: 88.8 us; the launch traced here: 88.4 us
  starting transfers between devices  43.5 us (49%)
  blocking collectives  18 us (20%)
  waiting for transfers between devices  15.7 us (18%)
  Pallas kernels  8.61 us (10%)
  local copies, waits for them, and re-layouts  1.82 us (2%)
    ppermute x12, starting transfers between devices, send(): return lax.ppermute(value, 'seq', pairs)  19 us
    all_to_all x1, blocking collectives, shards(): lax.all_to_all(inner, 'seq', 0, 0, axis_index_groups=like_cores)  18 us
    all_to_all x1, starting transfers between devices, shards(): arrived = lax.all_to_all(packed, 'seq', 0, 0, axis_index_groups=like_cores)  12 us
    pallas_call x14, Pallas kernels, call(): pl.pallas_call(kernel, out_shape=[jax.ShapeDtypeStruct(shape, dtype) for...  8.61 us
    ppermute x3, waiting for transfers between devices, shards(): lax.ppermute(turned_grad, 'ch', [(i, (i - hop) % features) for i in range...  8.19 us
    ppermute x12, waiting for transfers between devices, send(): return lax.ppermute(value, 'seq', pairs)  5.92 us
    all_to_all x1, starting transfers between devices, shards(): received = lax.all_to_all(turned, 'seq', 0, 0, axis_index_groups=like_cores)  5.76 us
    ppermute x3, starting transfers between devices, shards(): lax.ppermute(turned_grad, 'ch', [(i, (i - hop) % features) for i in range...  3.85 us
  transfers between devices with their start and end apart: 20, of which 9 were waited for; matrix products, arithmetic and copies ran while one was open for 0% of the time, Pallas kernels for 6%

profile of v7, /device:TPU:1, one launch (start us, length us, event | category | flops | bytes accessed | tf_op | source)
XLA Modules:
  0.0 88.4 jit_solution(6533765228794543997)
XLA Ops:
  0.6 0.9 %copy-done.4 = bf16[128,512]{1,0:T(8,128)(2,1)S(1)} copy-done((bf16[128,512]{1,0:T(8,128)(2,1)S(1)}, bf16[128,512]{1,0:T(8,128)(2,1)}, u32[]{:S(2)}) %copy-start.4) | copy-done | bytes 131096
  1.5 0.8 copy-done.10
  2.3 1.0 %shard_map.187 = bf16[32,80,128]{2,1,0:T(8,128)(2,1)} custom-call(bf16[128,512]{1,0:T(8,128)(2,1)S(1)} %copy-done.4, bf16[32,512]{1,0:T(8,128)(2,1)S(1)} %copy-done.10), custom_call_target="tpu_custom_call" | custom-call | tf_op jit(solution)/shard_map/pallas_call | solution.py:324
  3.3 12.0 %all-to-all-start = ((bf16[32,80,128]{2,1,0:T(8,128)(2,1)}), bf16[32,80,128]{2,1,0:T(8,128)(2,1)S(1)}, u32[]{:S(2)}, u32[]{:S(2)}) async-start(bf16[32,80,128]{2,1,0:T(8,128)(2,1)} %shard_map.187), calls=%async_computation | async-start | bytes 1310720 | tf_op jit(solution)/shard_map/all_to_all | solution.py:367
  15.4 2.8 %collective-permute-start.1 = (bf16[512,128]{1,0:T(8,128)(2,1)S(1)}, bf16[512,128]{1,0:T(8,128)(2,1)S(1)}, u32[]{:S(2)}, u32[]{:S(2)}) collective-permute-start(bf16[512,128]{1,0:T(8,128)(2,1)S(1)} %bitcast.1), channel_id=1, source_target_pairs={{0,3},{1,0},{2,1},{3,2},{4,7},{5,4},{6,5},{7,6},{8,11},{9,8},{10,9... | collective-permute-start | bytes 393224 | tf_op jit(solution)/shard_map/ppermute | solution.py:375
  18.6 0.7 collective-permute-start.3
  19.3 1.9 %collective-permute-done.1.refs_2_ = bf16[512,128]{1,0:T(8,128)(2,1)S(1)} collective-permute-done((bf16[512,128]{1,0:T(8,128)(2,1)S(1)}, bf16[512,128]{1,0:T(8,128)(2,1)S(1)}, u32[]{:S(2)}, u32[]{:S(2)}) %collective-permute-start.1) | collective-permute-done | bytes 131104 | tf_op jit(solution)/shard_map/ppermute | solution.py:375
  21.2 2.4 %collective-permute-done.2.refs_3_ = bf16[512,128]{1,0:T(8,128)(2,1)S(1)} collective-permute-done((bf16[512,128]{1,0:T(8,128)(2,1)S(1)}, bf16[512,128]{1,0:T(8,128)(2,1)S(1)}, u32[]{:S(2)}, u32[]{:S(2)}) %collective-permute-start.2) | collective-permute-done | bytes 131104 | tf_op jit(solution)/shard_map/ppermute | solution.py:375
  23.7 3.8 %collective-permute-done.3.refs_4_ = bf16[512,128]{1,0:T(8,128)(2,1)S(1)} collective-permute-done((bf16[512,128]{1,0:T(8,128)(2,1)S(1)}, bf16[512,128]{1,0:T(8,128)(2,1)S(1)}, u32[]{:S(2)}, u32[]{:S(2)}) %collective-permute-start.3) | collective-permute-done | bytes 131104 | tf_op jit(solution)/shard_map/ppermute | solution.py:375
  27.5 1.0 %collective-permute-start.4 = (bf16[2048,128]{1,0:T(8,128)(2,1)S(1)}, bf16[2048,128]{1,0:T(8,128)(2,1)S(1)}, u32[]{:S(2)}, u32[]{:S(2)}) collective-permute-start(bf16[2048,128]{1,0:T(8,128)(2,1)S(1)} %shard_map.184.mine_ref), channel_id=1, source_target_pairs={{0,4},{4,0},{8,12},{12,8},{16,20},{20,16},{24,28},{28,24},{32,36},... | collective-permute-start | bytes 1572872 | tf_op jit(solution)/shard_map/ppermute | solution.py:351
  28.7 1.6 %collective-permute-done.came_ref.refs_1_ = bf16[256,256]{1,0:T(8,128)(2,1)S(1)} collective-permute-done((bf16[256,256]{1,0:T(8,128)(2,1)S(1)}, bf16[256,256]{1,0:T(8,128)(2,1)S(1)}, u32[]{:S(2)}, u32[]{:S(2)}) %collective-permute-start) | collective-permute-done | bytes 131104 | tf_op jit(solution)/shard_map/ppermute | solution.py:351
  30.3 1.5 %shard_map.186 = (bf16[2048,128]{1,0:T(8,128)(2,1)S(1)}, bf16[2048,128]{1,0:T(8,128)(2,1)}) custom-call(bf16[2048,128]{1,0:T(8,128)(2,1)S(1)} %shard_map.184.mine_ref, bf16[2048,128]{1,0:T(8,128)(2,1)S(1)} %collective-permute-done.4.theirs_ref, bf16[256,256]{1,0:T(8,128)(2,1)S(1)} %get-tuple-element.29.refs_0_.own_ref, ...), custom_call_target="tpu_custom_call" | custom-call | tf_op jit(solution)/shard_map/pallas_call | solution.py:324
  31.9 1.2 %collective-permute-start.13 = (bf16[2048,128]{1,0:T(8,128)(2,1)}, bf16[2048,128]{1,0:T(8,128)(2,1)S(1)}, u32[]{:S(2)}, u32[]{:S(2)}) collective-permute-start(bf16[2048,128]{1,0:T(8,128)(2,1)} %get-tuple-element.43), channel_id=1, source_target_pairs={{0,8},{4,12},{8,0},{12,4},{16,24},{20,28},{24,16},{28,20},{32,40},... | collective-permute-start | bytes 1572872 | tf_op jit(solution)/shard_map/ppermute | solution.py:428
  33.2 3.6 %collective-permute-start.5 = (bf16[512,128]{1,0:T(8,128)(2,1)S(1)}, bf16[512,128]{1,0:T(8,128)(2,1)S(1)}, u32[]{:S(2)}, u32[]{:S(2)}) collective-permute-start(bf16[512,128]{1,0:T(8,128)(2,1)S(1)} %get-tuple-element.34), channel_id=1, source_target_pairs={{0,4},{4,0},{8,12},{12,8},{16,20},{20,16},{24,28},{28,24},{32,36},... | collective-permute-start | bytes 393224 | tf_op jit(solution)/shard_map/ppermute | solution.py:351
  37.0 2.7 %collective-permute-start.8 = (bf16[512,128]{1,0:T(8,128)(2,1)S(1)}, bf16[512,128]{1,0:T(8,128)(2,1)S(1)}, u32[]{:S(2)}, u32[]{:S(2)}) collective-permute-start(bf16[512,128]{1,0:T(8,128)(2,1)S(1)} %get-tuple-element.33.refs_4_), channel_id=1, source_target_pairs={{0,192},{4,196},{8,200},{12,204},{16,208},{20,212},{24,216},{28,22... | collective-permute-start | bytes 393224 | tf_op jit(solution)/shard_map/ppermute | solution.py:351
  39.7 2.7 %collective-permute-start.10 = (bf16[512,128]{1,0:T(8,128)(2,1)S(1)}, bf16[512,128]{1,0:T(8,128)(2,1)S(1)}, u32[]{:S(2)}, u32[]{:S(2)}) collective-permute-start(bf16[512,128]{1,0:T(8,128)(2,1)S(1)} %collective-permute-done.6.refs_6_), channel_id=1, source_target_pairs={{0,192},{4,196},{8,200},{12,204},{16,208},{20,212},{24,216},{28,22... | collective-permute-start | bytes 393224 | tf_op jit(solution)/shard_map/ppermute | solution.py:351
  42.3 0.4 shard_map.185.refs_2_
  42.8 2.3 %collective-permute-done.9.refs_9_ = bf16[512,128]{1,0:T(8,128)(2,1)S(1)} collective-permute-done((bf16[512,128]{1,0:T(8,128)(2,1)S(1)}, bf16[512,128]{1,0:T(8,128)(2,1)S(1)}, u32[]{:S(2)}, u32[]{:S(2)}) %collective-permute-start.9) | collective-permute-done | bytes 131104 | tf_op jit(solution)/shard_map/ppermute | solution.py:351
  45.1 1.2 %shard_map.189 = (bf16[32,16,128]{2,1,0:T(8,128)(2,1)}, bf16[128,256]{1,0:T(8,128)(2,1)S(1)}, bf16[128,256]{1,0:T(8,128)(2,1)S(1)}) custom-call(bf16[256,256]{1,0:T(8,128)(2,1)S(1)} %get-tuple-element.29.refs_0_.own_ref, bf16[256,256]{1,0:T(8,128)(2,1)S(1)} %collective-permute-done.came_ref.refs_1_, bf16[256,2048]{1,0:T(8,128)(2,1)S(1)} %shard_map.185.refs_2_, ...), custom_call_target="tpu_custom_call" | custom-call | tf_op jit(solution)/shard_map/pallas_call | solution.py:324
  46.3 5.8 %all-to-all-start.1 = ((bf16[32,16,128]{2,1,0:T(8,128)(2,1)}), bf16[32,16,128]{2,1,0:T(8,128)(2,1)S(1)}, u32[]{:S(2)}, u32[]{:S(2)}) async-start(bf16[32,16,128]{2,1,0:T(8,128)(2,1)} %get-tuple-element.40.after_ref), calls=%async_computation.1 | async-start | bytes 262144 | tf_op jit(solution)/shard_map/all_to_all | solution.py:436
  52.4 1.3 %collective-permute-start.14 = (bf16[512,128]{1,0:T(8,128)(2,1)S(1)}, bf16[512,128]{1,0:T(8,128)(2,1)S(1)}, u32[]{:S(2)}, u32[]{:S(2)}) collective-permute-start(bf16[512,128]{1,0:T(8,128)(2,1)S(1)} %get-tuple-element.45), channel_id=1, source_target_pairs={{0,64},{4,68},{8,72},{12,76},{16,80},{20,84},{24,88},{28,92},{32,9... | collective-permute-start | bytes 393224 | tf_op jit(solution)/shard_map/ppermute | solution.py:432
  53.8 0.4 collective-permute-start.15
  54.2 3.2 %collective-permute-start.12 = (bf16[256,128]{1,0:T(8,128)(2,1)S(1)}, bf16[256,128]{1,0:T(8,128)(2,1)S(1)}, u32[]{:S(2)}, u32[]{:S(2)}) collective-permute-start(bf16[256,128]{1,0:T(8,128)(2,1)S(1)} %get-tuple-element.42), channel_id=1, source_target_pairs={{0,4},{4,0},{8,12},{12,8},{16,20},{20,16},{24,28},{28,24},{32,36},... | collective-permute-start | bytes 196616 | tf_op jit(solution)/shard_map/ppermute | solution.py:351
  57.5 0.8 collective-permute-done.12.came_ref
  58.3 0.7 shard_map.192.refs_2_
  59.0 0.7 shard_map.190
  59.7 1.6 %all-to-all-done.1.refs_1_ = bf16[32,16,128]{2,1,0:T(8,128)(2,1)S(1)} async-done(((bf16[32,16,128]{2,1,0:T(8,128)(2,1)}), bf16[32,16,128]{2,1,0:T(8,128)(2,1)S(1)}, u32[]{:S(2)}, u32[]{:S(2)}) %all-to-all-start.1) | async-done | bytes 131104 | tf_op jit(solution)/shard_map/all_to_all | solution.py:436
  61.3 1.6 %shard_map.194 = bf16[32,48,128]{2,1,0:T(8,128)(2,1)S(1)} custom-call(f32[8,128]{1,0:T(8,128)S(1)} %get-tuple-element.39.refs_0_, bf16[32,16,128]{2,1,0:T(8,128)(2,1)S(1)} %all-to-all-done.1.refs_1_, f32[576,256]{1,0:T(8,128)S(1)} %shard_map.192.refs_2_, bf16[2,144,64]{2,1,0:T(8,128)(2,1)S(1)} %copy-done.1, f32[2,72,128]{2,1,0:T(8,128)S(1)} %copy-done.2, ...), custom_call_target="tpu_custom_call" | custom-call | tf_op jit(solution)/shard_map/pallas_call | solution.py:324
  62.9 18.0 %all_to_all.15.came_ref = bf16[32,48,128]{2,1,0:T(8,128)(2,1)S(1)} all-to-all(bf16[32,48,128]{2,1,0:T(8,128)(2,1)S(1)} %shard_map.194), channel_id=1, replica_groups={{0,8,16,24,32,40,48,56,64,72,80,88,96,104,112,120,128,136,144,152,160,1..., dimensions={0} | all-to-all | bytes 786432 | tf_op jit(solution)/shard_map/all_to_all | solution.py:465
  81.0 5.3 %collective-permute-start.16 = (bf16[256,128]{1,0:T(8,128)(2,1)S(1)}, bf16[256,128]{1,0:T(8,128)(2,1)S(1)}, u32[]{:S(2)}, u32[]{:S(2)}) collective-permute-start(bf16[256,128]{1,0:T(8,128)(2,1)S(1)} %get-tuple-element.48), channel_id=1, source_target_pairs={{0,4},{4,0},{8,12},{12,8},{16,20},{20,16},{24,28},{28,24},{32,36},... | collective-permute-start | bytes 196616 | tf_op jit(solution)/shard_map/ppermute | solution.py:351
  86.4 1.1 %collective-permute-done.17.beside_ref = f32[32,256]{1,0:T(8,128)S(1)} collective-permute-done((f32[32,256]{1,0:T(8,128)S(1)}, f32[32,256]{1,0:T(8,128)S(1)}, u32[]{:S(2)}, u32[]{:S(2)}) %collective-permute-start.17) | collective-permute-done | bytes 32800 | tf_op jit(solution)/shard_map/ppermute | solution.py:351
  87.5 0.8 shard_map.196
  (48 shorter events, 1.7 us)
Async XLA Ops:
  0.6 0.9 %copy-start.4 = (bf16[128,512]{1,0:T(8,128)(2,1)S(1)}, bf16[128,512]{1,0:T(8,128)(2,1)}, u32[]{:S(2)}) copy-start(bf16[128,512]{1,0:T(8,128)(2,1)} %filters_ref.1) | copy-start | bytes 393220
  1.5 0.8 copy-start.10
  3.2 12.0 %copy-start.11 = (bf16[128,512]{1,0:T(8,128)(2,1)S(1)}, bf16[128,512]{1,0:T(8,128)(2,1)}, u32[]{:S(2)}) copy-start(bf16[128,512]{1,0:T(8,128)(2,1)} %param.21) | copy-start | bytes 393220
  3.3 29.8 %all-to-all-start = ((bf16[32,80,128]{2,1,0:T(8,128)(2,1)}), bf16[32,80,128]{2,1,0:T(8,128)(2,1)S(1)}, u32[]{:S(2)}, u32[]{:S(2)}) async-start(bf16[32,80,128]{2,1,0:T(8,128)(2,1)} %shard_map.187), calls=%async_computation | async-start | bytes 1310720 | tf_op jit(solution)/shard_map/all_to_all | solution.py:367
  15.3 4.0 %copy-start.7 = (bf16[128,512]{1,0:T(8,128)(2,1)S(1)}, bf16[128,512]{1,0:T(8,128)(2,1)}, u32[]{:S(2)}) copy-start(bf16[128,512]{1,0:T(8,128)(2,1)} %refs_0_.1) | copy-start | bytes 393220
  15.3 4.0 %copy-start.8 = (bf16[128,512]{1,0:T(8,128)(2,1)S(1)}, bf16[128,512]{1,0:T(8,128)(2,1)}, u32[]{:S(2)}) copy-start(bf16[128,512]{1,0:T(8,128)(2,1)} %refs_1_.1) | copy-start | bytes 393220
  15.4 5.8 %collective-permute-start.1 = (bf16[512,128]{1,0:T(8,128)(2,1)S(1)}, bf16[512,128]{1,0:T(8,128)(2,1)S(1)}, u32[]{:S(2)}, u32[]{:S(2)}) collective-permute-start(bf16[512,128]{1,0:T(8,128)(2,1)S(1)} %bitcast.1), channel_id=1, source_target_pairs={{0,3},{1,0},{2,1},{3,2},{4,7},{5,4},{6,5},{7,6},{8,11},{9,8},{10,9... | collective-permute-start | bytes 393224 | tf_op jit(solution)/shard_map/ppermute | solution.py:375
  18.2 5.4 %collective-permute-start.2 = (bf16[512,128]{1,0:T(8,128)(2,1)S(1)}, bf16[512,128]{1,0:T(8,128)(2,1)S(1)}, u32[]{:S(2)}, u32[]{:S(2)}) collective-permute-start(bf16[512,128]{1,0:T(8,128)(2,1)S(1)} %bitcast.2), channel_id=1, source_target_pairs={{0,2},{1,3},{2,0},{3,1},{4,6},{5,7},{6,4},{7,5},{8,10},{9,11},{10,... | collective-permute-start | bytes 393224 | tf_op jit(solution)/shard_map/ppermute | solution.py:375
  18.6 8.9 %collective-permute-start.3 = (bf16[512,128]{1,0:T(8,128)(2,1)S(1)}, bf16[512,128]{1,0:T(8,128)(2,1)S(1)}, u32[]{:S(2)}, u32[]{:S(2)}) collective-permute-start(bf16[512,128]{1,0:T(8,128)(2,1)S(1)} %bitcast.3), channel_id=1, source_target_pairs={{0,1},{1,2},{2,3},{3,0},{4,5},{5,6},{6,7},{7,4},{8,9},{9,10},{10,1... | collective-permute-start | bytes 393224 | tf_op jit(solution)/shard_map/ppermute | solution.py:375
  27.5 2.8 %collective-permute-start.4 = (bf16[2048,128]{1,0:T(8,128)(2,1)S(1)}, bf16[2048,128]{1,0:T(8,128)(2,1)S(1)}, u32[]{:S(2)}, u32[]{:S(2)}) collective-permute-start(bf16[2048,128]{1,0:T(8,128)(2,1)S(1)} %shard_map.184.mine_ref), channel_id=1, source_target_pairs={{0,4},{4,0},{8,12},{12,8},{16,20},{20,16},{24,28},{28,24},{32,36},... | collective-permute-start | bytes 1572872 | tf_op jit(solution)/shard_map/ppermute | solution.py:351
  28.6 1.7 %collective-permute-start = (bf16[256,256]{1,0:T(8,128)(2,1)S(1)}, bf16[256,256]{1,0:T(8,128)(2,1)S(1)}, u32[]{:S(2)}, u32[]{:S(2)}) collective-permute-start(bf16[256,256]{1,0:T(8,128)(2,1)S(1)} %get-tuple-element.30), channel_id=1, source_target_pairs={{0,4},{4,0},{8,12},{12,8},{16,20},{20,16},{24,28},{28,24},{32,36},... | collective-permute-start | bytes 393224 | tf_op jit(solution)/shard_map/ppermute | solution.py:351
  31.9 20.2 %collective-permute-start.13 = (bf16[2048,128]{1,0:T(8,128)(2,1)}, bf16[2048,128]{1,0:T(8,128)(2,1)S(1)}, u32[]{:S(2)}, u32[]{:S(2)}) collective-permute-start(bf16[2048,128]{1,0:T(8,128)(2,1)} %get-tuple-element.43), channel_id=1, source_target_pairs={{0,8},{4,12},{8,0},{12,4},{16,24},{20,28},{24,16},{28,20},{32,40},... | collective-permute-start | bytes 1572872 | tf_op jit(solution)/shard_map/ppermute | solution.py:428
  33.2 6.4 %collective-permute-start.5 = (bf16[512,128]{1,0:T(8,128)(2,1)S(1)}, bf16[512,128]{1,0:T(8,128)(2,1)S(1)}, u32[]{:S(2)}, u32[]{:S(2)}) collective-permute-start(bf16[512,128]{1,0:T(8,128)(2,1)S(1)} %get-tuple-element.34), channel_id=1, source_target_pairs={{0,4},{4,0},{8,12},{12,8},{16,20},{20,16},{24,28},{28,24},{32,36},... | collective-permute-start | bytes 393224 | tf_op jit(solution)/shard_map/ppermute | solution.py:351
  36.9 2.8 %collective-permute-start.6 = (bf16[512,128]{1,0:T(8,128)(2,1)S(1)}, bf16[512,128]{1,0:T(8,128)(2,1)S(1)}, u32[]{:S(2)}, u32[]{:S(2)}) collective-permute-start(bf16[512,128]{1,0:T(8,128)(2,1)S(1)} %get-tuple-element.35), channel_id=1, source_target_pairs={{0,4},{4,0},{8,12},{12,8},{16,20},{20,16},{24,28},{28,24},{32,36},... | collective-permute-start | bytes 393224 | tf_op jit(solution)/shard_map/ppermute | solution.py:351
  37.0 5.9 %collective-permute-start.7 = (bf16[512,128]{1,0:T(8,128)(2,1)S(1)}, bf16[512,128]{1,0:T(8,128)(2,1)S(1)}, u32[]{:S(2)}, u32[]{:S(2)}) collective-permute-start(bf16[512,128]{1,0:T(8,128)(2,1)S(1)} %get-tuple-element.32.refs_3_), channel_id=1, source_target_pairs={{0,64},{4,68},{8,72},{12,76},{16,80},{20,84},{24,88},{28,92},{32,9... | collective-permute-start | bytes 393224 | tf_op jit(solution)/shard_map/ppermute | solution.py:351
  37.0 5.9 %collective-permute-start.8 = (bf16[512,128]{1,0:T(8,128)(2,1)S(1)}, bf16[512,128]{1,0:T(8,128)(2,1)S(1)}, u32[]{:S(2)}, u32[]{:S(2)}) collective-permute-start(bf16[512,128]{1,0:T(8,128)(2,1)S(1)} %get-tuple-element.33.refs_4_), channel_id=1, source_target_pairs={{0,192},{4,196},{8,200},{12,204},{16,208},{20,212},{24,216},{28,22... | collective-permute-start | bytes 393224 | tf_op jit(solution)/shard_map/ppermute | solution.py:351
  39.6 5.5 %collective-permute-start.9 = (bf16[512,128]{1,0:T(8,128)(2,1)S(1)}, bf16[512,128]{1,0:T(8,128)(2,1)S(1)}, u32[]{:S(2)}, u32[]{:S(2)}) collective-permute-start(bf16[512,128]{1,0:T(8,128)(2,1)S(1)} %collective-permute-done.5.refs_5_), channel_id=1, source_target_pairs={{0,64},{4,68},{8,72},{12,76},{16,80},{20,84},{24,88},{28,92},{32,9... | collective-permute-start | bytes 393224 | tf_op jit(solution)/shard_map/ppermute | solution.py:351
  39.7 5.5 %collective-permute-start.10 = (bf16[512,128]{1,0:T(8,128)(2,1)S(1)}, bf16[512,128]{1,0:T(8,128)(2,1)S(1)}, u32[]{:S(2)}, u32[]{:S(2)}) collective-permute-start(bf16[512,128]{1,0:T(8,128)(2,1)S(1)} %collective-permute-done.6.refs_6_), channel_id=1, source_target_pairs={{0,192},{4,196},{8,200},{12,204},{16,208},{20,212},{24,216},{28,22... | collective-permute-start | bytes 393224 | tf_op jit(solution)/shard_map/ppermute | solution.py:351
  46.3 14.9 %all-to-all-start.1 = ((bf16[32,16,128]{2,1,0:T(8,128)(2,1)}), bf16[32,16,128]{2,1,0:T(8,128)(2,1)S(1)}, u32[]{:S(2)}, u32[]{:S(2)}) async-start(bf16[32,16,128]{2,1,0:T(8,128)(2,1)} %get-tuple-element.40.after_ref), calls=%async_computation.1 | async-start | bytes 262144 | tf_op jit(solution)/shard_map/all_to_all | solution.py:436
  52.4 7.2 %collective-permute-start.14 = (bf16[512,128]{1,0:T(8,128)(2,1)S(1)}, bf16[512,128]{1,0:T(8,128)(2,1)S(1)}, u32[]{:S(2)}, u32[]{:S(2)}) collective-permute-start(bf16[512,128]{1,0:T(8,128)(2,1)S(1)} %get-tuple-element.45), channel_id=1, source_target_pairs={{0,64},{4,68},{8,72},{12,76},{16,80},{20,84},{24,88},{28,92},{32,9... | collective-permute-start | bytes 393224 | tf_op jit(solution)/shard_map/ppermute | solution.py:432
  53.8 4.5 %copy-start = (bf16[2,256,256]{2,1,0:T(8,128)(2,1)S(1)}, bf16[2,256,256]{2,1,0:T(8,128)(2,1)}, u32[]{:S(2)}) copy-start(bf16[2,256,256]{2,1,0:T(8,128)(2,1)} %constant.33.second_ref.refs_5_) | copy-start | bytes 786436
  53.8 4.5 %copy-start.1 = (bf16[2,144,64]{2,1,0:T(8,128)(2,1)S(1)}, bf16[2,144,64]{2,1,0:T(8,128)(2,1)}, u32[]{:S(2)}) copy-start(bf16[2,144,64]{2,1,0:T(8,128)(2,1)} %constant.30.first_ref.refs_3_) | copy-start | bytes 110596
  53.8 4.5 %copy-start.2 = (f32[2,72,128]{2,1,0:T(8,128)S(1)}, f32[2,72,128]{2,1,0:T(8,128)}, u32[]{:S(2)}) copy-start(f32[2,72,128]{2,1,0:T(8,128)} %constant.26.clone.twist_ref.refs_4_) | copy-start | bytes 221188
  53.8 5.9 %collective-permute-start.15 = (bf16[512,128]{1,0:T(8,128)(2,1)S(1)}, bf16[512,128]{1,0:T(8,128)(2,1)S(1)}, u32[]{:S(2)}, u32[]{:S(2)}) collective-permute-start(bf16[512,128]{1,0:T(8,128)(2,1)S(1)} %get-tuple-element.46), channel_id=1, source_target_pairs={{0,64},{4,68},{8,72},{12,76},{16,80},{20,84},{24,88},{28,92},{32,9... | collective-permute-start | bytes 393224 | tf_op jit(solution)/shard_map/ppermute | solution.py:432
  54.2 4.1 %collective-permute-start.12 = (bf16[256,128]{1,0:T(8,128)(2,1)S(1)}, bf16[256,128]{1,0:T(8,128)(2,1)S(1)}, u32[]{:S(2)}, u32[]{:S(2)}) collective-permute-start(bf16[256,128]{1,0:T(8,128)(2,1)S(1)} %get-tuple-element.42), channel_id=1, source_target_pairs={{0,4},{4,0},{8,12},{12,8},{16,20},{20,16},{24,28},{28,24},{32,36},... | collective-permute-start | bytes 196616 | tf_op jit(solution)/shard_map/ppermute | solution.py:351
  57.4 1.6 %collective-permute-start.11 = (bf16[128,256]{1,0:T(8,128)(2,1)S(1)}, bf16[128,256]{1,0:T(8,128)(2,1)S(1)}, u32[]{:S(2)}, u32[]{:S(2)}) collective-permute-start(bf16[128,256]{1,0:T(8,128)(2,1)S(1)} %get-tuple-element.37), channel_id=1, source_target_pairs={{0,4},{4,0},{8,12},{12,8},{16,20},{20,16},{24,28},{28,24},{32,36},... | collective-permute-start | bytes 196616 | tf_op jit(solution)/shard_map/ppermute | solution.py:351
  58.3 3.0 %copy-start.3 = (bf16[2,256,256]{2,1,0:T(8,128)(2,1)S(1)}, bf16[2,256,256]{2,1,0:T(8,128)(2,1)}, u32[]{:S(2)}) copy-start(bf16[2,256,256]{2,1,0:T(8,128)(2,1)} %constant.36.refs_6_) | copy-start | bytes 786436
  59.0 2.3 %copy-start.9 = (bf16[2,64,144]{2,1,0:T(8,128)(2,1)S(1)}, bf16[2,64,144]{2,1,0:T(8,128)(2,1)}, u32[]{:S(2)}) copy-start(bf16[2,64,144]{2,1,0:T(8,128)(2,1)} %constant.39.refs_7_) | copy-start | bytes 110596
  80.9 6.7 %copy-start.5 = (bf16[128,512]{1,0:T(8,128)(2,1)S(1)}, bf16[128,512]{1,0:T(8,128)(2,1)}, u32[]{:S(2)}) copy-start(bf16[128,512]{1,0:T(8,128)(2,1)} %key_ref.1) | copy-start | bytes 393220
  80.9 6.7 %copy-start.6 = (bf16[128,512]{1,0:T(8,128)(2,1)S(1)}, bf16[128,512]{1,0:T(8,128)(2,1)}, u32[]{:S(2)}) copy-start(bf16[128,512]{1,0:T(8,128)(2,1)} %value_ref.1) | copy-start | bytes 393220
  81.0 6.6 %collective-permute-start.16 = (bf16[256,128]{1,0:T(8,128)(2,1)S(1)}, bf16[256,128]{1,0:T(8,128)(2,1)S(1)}, u32[]{:S(2)}, u32[]{:S(2)}) collective-permute-start(bf16[256,128]{1,0:T(8,128)(2,1)S(1)} %get-tuple-element.48), channel_id=1, source_target_pairs={{0,4},{4,0},{8,12},{12,8},{16,20},{20,16},{24,28},{28,24},{32,36},... | collective-permute-start | bytes 196616 | tf_op jit(solution)/shard_map/ppermute | solution.py:351
  86.3 1.2 %collective-permute-start.17 = (f32[32,256]{1,0:T(8,128)S(1)}, f32[32,256]{1,0:T(8,128)S(1)}, u32[]{:S(2)}, u32[]{:S(2)}) collective-permute-start(f32[32,256]{1,0:T(8,128)S(1)} %get-tuple-element.50), channel_id=1, source_target_pairs={{0,4},{4,0},{8,12},{12,8},{16,20},{20,16},{24,28},{28,24},{32,36},... | collective-permute-start | bytes 98312 | tf_op jit(solution)/shard_map/ppermute | solution.py:351

commit v8 on v7

--- a/solution.py
+++ b/solution.py
@@ -218,15 +218,6 @@
     theirs_ref[...] = query_grad[rows:]
 
 
-def join_kernel(mine_ref, theirs_ref, out_ref, token_ref):
-    token_ref[...] = jnp.zeros_like(token_ref)
-    odd = own_place()[2] == 1
-    mine, theirs = mine_ref[...], theirs_ref[...]
-    half = mine.shape[1]
-    out_ref[:, :half] = jnp.where(odd, theirs, mine)
-    out_ref[:, half:] = jnp.where(odd, mine, theirs)
-
-
 def parts_kernel(came_ref, inner_ref, inner_other_ref, weight_ref, weight_other_ref):
     odd = own_place()[2] == 1
     chips, depth, rows = came_ref.shape
@@ -261,10 +252,10 @@
     weight_other_ref[...] = jnp.where(odd, first, second)
 
 
-def outputs_kernel(
-    scale, own_ref, came_ref, weight_ref, beside_ref, key_ref, value_ref, key_grad_ref, value_grad_ref, weight_grad_ref
-):
-    odd = own_place()[2] == 1
+def outputs_kernel(scale, *refs):
+    odd = own_place()[2] == 1
+    own_ref, came_ref, weight_ref, beside_ref, mine_ref, theirs_ref, key_ref, value_ref = refs[:8]
+    query_grad_ref, key_grad_ref, value_grad_ref, weight_grad_ref = refs[8:]
     half = own_ref.shape[0]
     own, came = own_ref[...].astype(F32).T, came_ref[...].astype(F32).T
     for i, inner in enumerate((jnp.where(odd, came, own), jnp.where(odd, own, came))):
@@ -274,6 +265,9 @@
     own, came = weight_ref[...] * scale, beside_ref[...] * scale
     weight_grad_ref[:, :half] = jnp.where(odd, came, own)
     weight_grad_ref[:, half:] = jnp.where(odd, own, came)
+    own, came = mine_ref[...], theirs_ref[...]
+    query_grad_ref[:, :half] = jnp.where(odd, came, own)
+    query_grad_ref[:, half:] = jnp.where(odd, own, came)
 
 
 def arrange_kernel(*refs):
@@ -428,10 +422,7 @@
         *[lax.ppermute(value, "seq", [(i, i ^ CORES) for i in range(groups)]) for value in give],
         after=(turned,),
     )
-    came = [
-        lax.ppermute(value, "seq", [(i, i ^ (along_z * CORES)) for i in range(groups)])
-        for value in give
-    ]
+    came = [send(value, dx, 0, 0) for value, dx in zip(give, (1, -1), strict=True)]
 
     received = lax.all_to_all(
         turned,
@@ -441,9 +432,6 @@
         axis_index_groups=like_cores,
     )
     theirs = to_core(theirs)
-    query_grad, joined = call(
-        join_kernel, [((rows, chan), BF16), ((8, rows), F32)], mine, theirs
-    )
     (inner,) = call(
         functools.partial(correlate_kernel, sizes),
         [((chips, CORES * (feats // 2 + chans), rows), BF16)],
@@ -457,24 +445,25 @@
         keep,
         *came,
         scratch=[(CORES, half, rows)],
-        after=(joined,),
+        after=(theirs,),
     )
     inner, inner_other, weight_sum, weight_sum_other = call(
         parts_kernel,
         [((half, rows), BF16)] * 2 + [((feats, half), F32)] * 2,
         lax.all_to_all(inner, "seq", 0, 0, axis_index_groups=like_cores),
     )
-    key_grad, value_grad, weight_grad = call(
+    return call(
         functools.partial(outputs_kernel, (rows * groups) ** (-0.5)),
-        [((rows, chan), BF16)] * 2 + [((feats, chan), F32)],
+        [((rows, chan), BF16)] * 3 + [((feats, chan), F32)],
         inner,
         to_core(inner_other),
         weight_sum,
         to_core(weight_sum_other),
+        mine,
+        theirs,
         key_proj,
         value_proj,
     )
-    return (query_grad, key_grad, value_grad, weight_grad)
 
 
 def solution(mesh):

time: 88.8 us -> 88.1 us (level)
  starting transfers between devices: 43.5 us -> 44.7 us
    ppermute x12 -> x14, starting transfers between devices: 19 us -> 21.9 us  [send(): return lax.ppermute(value, 'seq', pairs)]
    ppermute x2 -> x0, starting transfers between devices: 1.67 us -> none  [shards(): lax.ppermute(value, 'seq', [(i, i ^ along_z * CORES) for i in range(group...]
    pallas_call x14 -> x13, Pallas kernels: 8.61 us -> 7.91 us  [call(): pl.pallas_call(kernel, out_shape=[jax.ShapeDtypeStruct(shape, dtype) for...]
    ppermute x12 -> x14, waiting for transfers between devices: 5.92 us -> 5.92 us  [send(): return lax.ppermute(value, 'seq', pairs)]
  transfers between devices with their start and end apart: 20 -> 20, of which waited for: 9 -> 9; matrix products, arithmetic and copies ran while one was open for 0% -> 0% of each run, Pallas kernels for 6% -> 5%
where the time goes in v8:
time: 88.1 us; the launch traced here: 87.8 us
  starting transfers between devices  44.7 us (51%)
  blocking collectives  17.4 us (20%)
  waiting for transfers between devices  15.1 us (17%)
  Pallas kernels  7.91 us (9%)
  local copies, waits for them, and re-layouts  1.82 us (2%)
    ppermute x14, starting transfers between devices, send(): return lax.ppermute(value, 'seq', pairs)  21.9 us
    all_to_all x1, blocking collectives, shards(): lax.all_to_all(inner, 'seq', 0, 0, axis_index_groups=like_cores)  17.4 us
    all_to_all x1, starting transfers between devices, shards(): arrived = lax.all_to_all(packed, 'seq', 0, 0, axis_index_groups=like_cores)  12 us
    ppermute x3, waiting for transfers between devices, shards(): lax.ppermute(turned_grad, 'ch', [(i, (i - hop) % features) for i in range...  8.19 us
    pallas_call x13, Pallas kernels, call(): pl.pallas_call(kernel, out_shape=[jax.ShapeDtypeStruct(shape, dtype) for...  7.91 us
    ppermute x14, waiting for transfers between devices, send(): return lax.ppermute(value, 'seq', pairs)  5.92 us
    all_to_all x1, starting transfers between devices, shards(): received = lax.all_to_all(turned, 'seq', 0, 0, axis_index_groups=like_cores)  5.75 us
    ppermute x3, starting transfers between devices, shards(): lax.ppermute(turned_grad, 'ch', [(i, (i - hop) % features) for i in range...  3.85 us
  transfers between devices with their start and end apart: 20, of which 9 were waited for; matrix products, arithmetic and copies ran while one was open for 0% of the time, Pallas kernels for 5%

profile of v8, /device:TPU:1, one launch (start us, length us, event | category | flops | bytes accessed | tf_op | source)
XLA Modules:
  0.0 87.8 jit_solution(17258654431842183613)
XLA Ops:
  0.6 0.9 %copy-done.4 = bf16[128,512]{1,0:T(8,128)(2,1)S(1)} copy-done((bf16[128,512]{1,0:T(8,128)(2,1)S(1)}, bf16[128,512]{1,0:T(8,128)(2,1)}, u32[]{:S(2)}) %copy-start.4) | copy-done | bytes 131096
  1.5 0.8 copy-done.10
  2.3 1.0 %shard_map.187 = bf16[32,80,128]{2,1,0:T(8,128)(2,1)} custom-call(bf16[128,512]{1,0:T(8,128)(2,1)S(1)} %copy-done.4, bf16[32,512]{1,0:T(8,128)(2,1)S(1)} %copy-done.10), custom_call_target="tpu_custom_call" | custom-call | tf_op jit(solution)/shard_map/pallas_call | solution.py:318
  3.3 12.0 %all-to-all-start = ((bf16[32,80,128]{2,1,0:T(8,128)(2,1)}), bf16[32,80,128]{2,1,0:T(8,128)(2,1)S(1)}, u32[]{:S(2)}, u32[]{:S(2)}) async-start(bf16[32,80,128]{2,1,0:T(8,128)(2,1)} %shard_map.187), calls=%async_computation | async-start | bytes 1310720 | tf_op jit(solution)/shard_map/all_to_all | solution.py:361
  15.4 2.8 %collective-permute-start.1 = (bf16[512,128]{1,0:T(8,128)(2,1)S(1)}, bf16[512,128]{1,0:T(8,128)(2,1)S(1)}, u32[]{:S(2)}, u32[]{:S(2)}) collective-permute-start(bf16[512,128]{1,0:T(8,128)(2,1)S(1)} %bitcast.1), channel_id=1, source_target_pairs={{0,3},{1,0},{2,1},{3,2},{4,7},{5,4},{6,5},{7,6},{8,11},{9,8},{10,9... | collective-permute-start | bytes 393224 | tf_op jit(solution)/shard_map/ppermute | solution.py:369
  18.2 0.3 collective-permute-start.2
  18.6 0.7 collective-permute-start.3
  19.3 1.9 %collective-permute-done.1.refs_2_ = bf16[512,128]{1,0:T(8,128)(2,1)S(1)} collective-permute-done((bf16[512,128]{1,0:T(8,128)(2,1)S(1)}, bf16[512,128]{1,0:T(8,128)(2,1)S(1)}, u32[]{:S(2)}, u32[]{:S(2)}) %collective-permute-start.1) | collective-permute-done | bytes 131104 | tf_op jit(solution)/shard_map/ppermute | solution.py:369
  21.2 2.4 %collective-permute-done.2.refs_3_ = bf16[512,128]{1,0:T(8,128)(2,1)S(1)} collective-permute-done((bf16[512,128]{1,0:T(8,128)(2,1)S(1)}, bf16[512,128]{1,0:T(8,128)(2,1)S(1)}, u32[]{:S(2)}, u32[]{:S(2)}) %collective-permute-start.2) | collective-permute-done | bytes 131104 | tf_op jit(solution)/shard_map/ppermute | solution.py:369
  23.7 3.8 %collective-permute-done.3.refs_4_ = bf16[512,128]{1,0:T(8,128)(2,1)S(1)} collective-permute-done((bf16[512,128]{1,0:T(8,128)(2,1)S(1)}, bf16[512,128]{1,0:T(8,128)(2,1)S(1)}, u32[]{:S(2)}, u32[]{:S(2)}) %collective-permute-start.3) | collective-permute-done | bytes 131104 | tf_op jit(solution)/shard_map/ppermute | solution.py:369
  27.5 1.0 %collective-permute-start.4 = (bf16[2048,128]{1,0:T(8,128)(2,1)S(1)}, bf16[2048,128]{1,0:T(8,128)(2,1)S(1)}, u32[]{:S(2)}, u32[]{:S(2)}) collective-permute-start(bf16[2048,128]{1,0:T(8,128)(2,1)S(1)} %shard_map.184.mine_ref), channel_id=1, source_target_pairs={{0,4},{4,0},{8,12},{12,8},{16,20},{20,16},{24,28},{28,24},{32,36},... | collective-permute-start | bytes 1572872 | tf_op jit(solution)/shard_map/ppermute | solution.py:345
  28.7 1.6 %collective-permute-done.came_ref.refs_1_ = bf16[256,256]{1,0:T(8,128)(2,1)S(1)} collective-permute-done((bf16[256,256]{1,0:T(8,128)(2,1)S(1)}, bf16[256,256]{1,0:T(8,128)(2,1)S(1)}, u32[]{:S(2)}, u32[]{:S(2)}) %collective-permute-start) | collective-permute-done | bytes 131104 | tf_op jit(solution)/shard_map/ppermute | solution.py:345
  30.3 1.5 %shard_map.186 = (bf16[2048,128]{1,0:T(8,128)(2,1)S(1)}, bf16[2048,128]{1,0:T(8,128)(2,1)}) custom-call(bf16[2048,128]{1,0:T(8,128)(2,1)S(1)} %shard_map.184.mine_ref, bf16[2048,128]{1,0:T(8,128)(2,1)S(1)} %collective-permute-done.4.theirs_ref, bf16[256,256]{1,0:T(8,128)(2,1)S(1)} %get-tuple-element.24.refs_0_.own_ref, ...), custom_call_target="tpu_custom_call" | custom-call | tf_op jit(solution)/shard_map/pallas_call | solution.py:318
  31.9 1.2 %collective-permute-start.13 = (bf16[2048,128]{1,0:T(8,128)(2,1)}, bf16[2048,128]{1,0:T(8,128)(2,1)S(1)}, u32[]{:S(2)}, u32[]{:S(2)}) collective-permute-start(bf16[2048,128]{1,0:T(8,128)(2,1)} %get-tuple-element.35), channel_id=1, source_target_pairs={{0,8},{4,12},{8,0},{12,4},{16,24},{20,28},{24,16},{28,20},{32,40},... | collective-permute-start | bytes 1572872 | tf_op jit(solution)/shard_map/ppermute | solution.py:422
  33.2 3.6 %collective-permute-start.5 = (bf16[512,128]{1,0:T(8,128)(2,1)S(1)}, bf16[512,128]{1,0:T(8,128)(2,1)S(1)}, u32[]{:S(2)}, u32[]{:S(2)}) collective-permute-start(bf16[512,128]{1,0:T(8,128)(2,1)S(1)} %get-tuple-element.29), channel_id=1, source_target_pairs={{0,4},{4,0},{8,12},{12,8},{16,20},{20,16},{24,28},{28,24},{32,36},... | collective-permute-start | bytes 393224 | tf_op jit(solution)/shard_map/ppermute | solution.py:345
  37.0 2.7 %collective-permute-start.8 = (bf16[512,128]{1,0:T(8,128)(2,1)S(1)}, bf16[512,128]{1,0:T(8,128)(2,1)S(1)}, u32[]{:S(2)}, u32[]{:S(2)}) collective-permute-start(bf16[512,128]{1,0:T(8,128)(2,1)S(1)} %get-tuple-element.28.refs_4_), channel_id=1, source_target_pairs={{0,192},{4,196},{8,200},{12,204},{16,208},{20,212},{24,216},{28,22... | collective-permute-start | bytes 393224 | tf_op jit(solution)/shard_map/ppermute | solution.py:345
  39.7 2.7 %collective-permute-start.10 = (bf16[512,128]{1,0:T(8,128)(2,1)S(1)}, bf16[512,128]{1,0:T(8,128)(2,1)S(1)}, u32[]{:S(2)}, u32[]{:S(2)}) collective-permute-start(bf16[512,128]{1,0:T(8,128)(2,1)S(1)} %collective-permute-done.6.refs_6_), channel_id=1, source_target_pairs={{0,192},{4,196},{8,200},{12,204},{16,208},{20,212},{24,216},{28,22... | collective-permute-start | bytes 393224 | tf_op jit(solution)/shard_map/ppermute | solution.py:345
  42.3 0.4 shard_map.185.refs_2_
  42.9 2.3 %collective-permute-done.9.refs_9_ = bf16[512,128]{1,0:T(8,128)(2,1)S(1)} collective-permute-done((bf16[512,128]{1,0:T(8,128)(2,1)S(1)}, bf16[512,128]{1,0:T(8,128)(2,1)S(1)}, u32[]{:S(2)}, u32[]{:S(2)}) %collective-permute-start.9) | collective-permute-done | bytes 131104 | tf_op jit(solution)/shard_map/ppermute | solution.py:345
  45.1 1.2 %shard_map.189 = (bf16[32,16,128]{2,1,0:T(8,128)(2,1)}, bf16[128,256]{1,0:T(8,128)(2,1)S(1)}, bf16[128,256]{1,0:T(8,128)(2,1)S(1)}) custom-call(bf16[256,256]{1,0:T(8,128)(2,1)S(1)} %get-tuple-element.24.refs_0_.own_ref, bf16[256,256]{1,0:T(8,128)(2,1)S(1)} %collective-permute-done.came_ref.refs_1_, bf16[256,2048]{1,0:T(8,128)(2,1)S(1)} %shard_map.185.refs_2_, ...), custom_call_target="tpu_custom_call" | custom-call | tf_op jit(solution)/shard_map/pallas_call | solution.py:318
  46.3 5.8 %all-to-all-start.1 = ((bf16[32,16,128]{2,1,0:T(8,128)(2,1)}), bf16[32,16,128]{2,1,0:T(8,128)(2,1)S(1)}, u32[]{:S(2)}, u32[]{:S(2)}) async-start(bf16[32,16,128]{2,1,0:T(8,128)(2,1)} %get-tuple-element.32.after_ref), calls=%async_computation.1 | async-start | bytes 262144 | tf_op jit(solution)/shard_map/all_to_all | solution.py:427
  52.4 1.3 %collective-permute-start.14 = (bf16[512,128]{1,0:T(8,128)(2,1)S(1)}, bf16[512,128]{1,0:T(8,128)(2,1)S(1)}, u32[]{:S(2)}, u32[]{:S(2)}) collective-permute-start(bf16[512,128]{1,0:T(8,128)(2,1)S(1)} %get-tuple-element.37), channel_id=1, source_target_pairs={{0,64},{4,68},{8,72},{12,76},{16,80},{20,84},{24,88},{28,92},{32,9... | collective-permute-start | bytes 393224 | tf_op jit(solution)/shard_map/ppermute | solution.py:345
  53.8 1.6 %collective-permute-start.15 = (bf16[512,128]{1,0:T(8,128)(2,1)S(1)}, bf16[512,128]{1,0:T(8,128)(2,1)S(1)}, u32[]{:S(2)}, u32[]{:S(2)}) collective-permute-start(bf16[512,128]{1,0:T(8,128)(2,1)S(1)} %get-tuple-element.38), channel_id=1, source_target_pairs={{0,192},{4,196},{8,200},{12,204},{16,208},{20,212},{24,216},{28,22... | collective-permute-start | bytes 393224 | tf_op jit(solution)/shard_map/ppermute | solution.py:345
  55.4 3.2 %collective-permute-start.12 = (bf16[256,128]{1,0:T(8,128)(2,1)S(1)}, bf16[256,128]{1,0:T(8,128)(2,1)S(1)}, u32[]{:S(2)}, u32[]{:S(2)}) collective-permute-start(bf16[256,128]{1,0:T(8,128)(2,1)S(1)} %get-tuple-element.34), channel_id=1, source_target_pairs={{0,4},{4,0},{8,12},{12,8},{16,20},{20,16},{24,28},{28,24},{32,36},... | collective-permute-start | bytes 196616 | tf_op jit(solution)/shard_map/ppermute | solution.py:345
  58.7 0.8 collective-permute-done.12.came_ref
  59.5 0.7 shard_map.191.refs_2_
  60.2 1.0 %all-to-all-done.1.refs_1_ = bf16[32,16,128]{2,1,0:T(8,128)(2,1)S(1)} async-done(((bf16[32,16,128]{2,1,0:T(8,128)(2,1)}), bf16[32,16,128]{2,1,0:T(8,128)(2,1)S(1)}, u32[]{:S(2)}, u32[]{:S(2)}) %all-to-all-start.1) | async-done | bytes 131104 | tf_op jit(solution)/shard_map/all_to_all | solution.py:427
  61.3 1.6 %shard_map.193 = bf16[32,48,128]{2,1,0:T(8,128)(2,1)S(1)} custom-call(bf16[128,256]{1,0:T(8,128)(2,1)S(1)} %collective-permute-done.11.refs_0_.refs_5_, bf16[32,16,128]{2,1,0:T(8,128)(2,1)S(1)} %all-to-all-done.1.refs_1_, f32[576,256]{1,0:T(8,128)S(1)} %shard_map.191.refs_2_, bf16[2,144,64]{2,1,0:T(8,128)(2,1)S(1)} %copy-done.1, ...), custom_call_target="tpu_custom_call" | custom-call | tf_op jit(solution)/shard_map/pallas_call | solution.py:318
  62.9 17.4 %all_to_all.15.came_ref = bf16[32,48,128]{2,1,0:T(8,128)(2,1)S(1)} all-to-all(bf16[32,48,128]{2,1,0:T(8,128)(2,1)S(1)} %shard_map.193), channel_id=1, replica_groups={{0,8,16,24,32,40,48,56,64,72,80,88,96,104,112,120,128,136,144,152,160,1..., dimensions={0} | all-to-all | bytes 786432 | tf_op jit(solution)/shard_map/all_to_all | solution.py:453
  80.4 5.3 %collective-permute-start.16 = (bf16[256,128]{1,0:T(8,128)(2,1)S(1)}, bf16[256,128]{1,0:T(8,128)(2,1)S(1)}, u32[]{:S(2)}, u32[]{:S(2)}) collective-permute-start(bf16[256,128]{1,0:T(8,128)(2,1)S(1)} %get-tuple-element.40), channel_id=1, source_target_pairs={{0,4},{4,0},{8,12},{12,8},{16,20},{20,16},{24,28},{28,24},{32,36},... | collective-permute-start | bytes 196616 | tf_op jit(solution)/shard_map/ppermute | solution.py:345
  85.8 1.1 %collective-permute-done.17.refs_3_ = f32[32,256]{1,0:T(8,128)S(1)} collective-permute-done((f32[32,256]{1,0:T(8,128)S(1)}, f32[32,256]{1,0:T(8,128)S(1)}, u32[]{:S(2)}, u32[]{:S(2)}) %collective-permute-start.17) | collective-permute-done | bytes 32800 | tf_op jit(solution)/shard_map/ppermute | solution.py:345
  86.9 0.8 shard_map.195
  (47 shorter events, 1.4 us)
Async XLA Ops:
  0.6 0.9 %copy-start.4 = (bf16[128,512]{1,0:T(8,128)(2,1)S(1)}, bf16[128,512]{1,0:T(8,128)(2,1)}, u32[]{:S(2)}) copy-start(bf16[128,512]{1,0:T(8,128)(2,1)} %filters_ref.1) | copy-start | bytes 393220
  1.5 0.8 copy-start.10
  3.3 12.0 %copy-start.11 = (bf16[128,512]{1,0:T(8,128)(2,1)S(1)}, bf16[128,512]{1,0:T(8,128)(2,1)}, u32[]{:S(2)}) copy-start(bf16[128,512]{1,0:T(8,128)(2,1)} %param.21) | copy-start | bytes 393220
  3.3 29.9 %all-to-all-start = ((bf16[32,80,128]{2,1,0:T(8,128)(2,1)}), bf16[32,80,128]{2,1,0:T(8,128)(2,1)S(1)}, u32[]{:S(2)}, u32[]{:S(2)}) async-start(bf16[32,80,128]{2,1,0:T(8,128)(2,1)} %shard_map.187), calls=%async_computation | async-start | bytes 1310720 | tf_op jit(solution)/shard_map/all_to_all | solution.py:361
  15.3 4.0 %copy-start.5 = (bf16[128,512]{1,0:T(8,128)(2,1)S(1)}, bf16[128,512]{1,0:T(8,128)(2,1)}, u32[]{:S(2)}) copy-start(bf16[128,512]{1,0:T(8,128)(2,1)} %refs_0_.1) | copy-start | bytes 393220
  15.3 4.0 %copy-start.6 = (bf16[128,512]{1,0:T(8,128)(2,1)S(1)}, bf16[128,512]{1,0:T(8,128)(2,1)}, u32[]{:S(2)}) copy-start(bf16[128,512]{1,0:T(8,128)(2,1)} %refs_1_.1) | copy-start | bytes 393220
  15.4 5.8 %collective-permute-start.1 = (bf16[512,128]{1,0:T(8,128)(2,1)S(1)}, bf16[512,128]{1,0:T(8,128)(2,1)S(1)}, u32[]{:S(2)}, u32[]{:S(2)}) collective-permute-start(bf16[512,128]{1,0:T(8,128)(2,1)S(1)} %bitcast.1), channel_id=1, source_target_pairs={{0,3},{1,0},{2,1},{3,2},{4,7},{5,4},{6,5},{7,6},{8,11},{9,8},{10,9... | collective-permute-start | bytes 393224 | tf_op jit(solution)/shard_map/ppermute | solution.py:369
  18.2 5.4 %collective-permute-start.2 = (bf16[512,128]{1,0:T(8,128)(2,1)S(1)}, bf16[512,128]{1,0:T(8,128)(2,1)S(1)}, u32[]{:S(2)}, u32[]{:S(2)}) collective-permute-start(bf16[512,128]{1,0:T(8,128)(2,1)S(1)} %bitcast.2), channel_id=1, source_target_pairs={{0,2},{1,3},{2,0},{3,1},{4,6},{5,7},{6,4},{7,5},{8,10},{9,11},{10,... | collective-permute-start | bytes 393224 | tf_op jit(solution)/shard_map/ppermute | solution.py:369
  18.6 8.9 %collective-permute-start.3 = (bf16[512,128]{1,0:T(8,128)(2,1)S(1)}, bf16[512,128]{1,0:T(8,128)(2,1)S(1)}, u32[]{:S(2)}, u32[]{:S(2)}) collective-permute-start(bf16[512,128]{1,0:T(8,128)(2,1)S(1)} %bitcast.3), channel_id=1, source_target_pairs={{0,1},{1,2},{2,3},{3,0},{4,5},{5,6},{6,7},{7,4},{8,9},{9,10},{10,1... | collective-permute-start | bytes 393224 | tf_op jit(solution)/shard_map/ppermute | solution.py:369
  27.5 2.8 %collective-permute-start.4 = (bf16[2048,128]{1,0:T(8,128)(2,1)S(1)}, bf16[2048,128]{1,0:T(8,128)(2,1)S(1)}, u32[]{:S(2)}, u32[]{:S(2)}) collective-permute-start(bf16[2048,128]{1,0:T(8,128)(2,1)S(1)} %shard_map.184.mine_ref), channel_id=1, source_target_pairs={{0,4},{4,0},{8,12},{12,8},{16,20},{20,16},{24,28},{28,24},{32,36},... | collective-permute-start | bytes 1572872 | tf_op jit(solution)/shard_map/ppermute | solution.py:345
  28.6 1.7 %collective-permute-start = (bf16[256,256]{1,0:T(8,128)(2,1)S(1)}, bf16[256,256]{1,0:T(8,128)(2,1)S(1)}, u32[]{:S(2)}, u32[]{:S(2)}) collective-permute-start(bf16[256,256]{1,0:T(8,128)(2,1)S(1)} %get-tuple-element.25), channel_id=1, source_target_pairs={{0,4},{4,0},{8,12},{12,8},{16,20},{20,16},{24,28},{28,24},{32,36},... | collective-permute-start | bytes 393224 | tf_op jit(solution)/shard_map/ppermute | solution.py:345
  31.9 20.2 %collective-permute-start.13 = (bf16[2048,128]{1,0:T(8,128)(2,1)}, bf16[2048,128]{1,0:T(8,128)(2,1)S(1)}, u32[]{:S(2)}, u32[]{:S(2)}) collective-permute-start(bf16[2048,128]{1,0:T(8,128)(2,1)} %get-tuple-element.35), channel_id=1, source_target_pairs={{0,8},{4,12},{8,0},{12,4},{16,24},{20,28},{24,16},{28,20},{32,40},... | collective-permute-start | bytes 1572872 | tf_op jit(solution)/shard_map/ppermute | solution.py:422
  33.2 6.4 %collective-permute-start.5 = (bf16[512,128]{1,0:T(8,128)(2,1)S(1)}, bf16[512,128]{1,0:T(8,128)(2,1)S(1)}, u32[]{:S(2)}, u32[]{:S(2)}) collective-permute-start(bf16[512,128]{1,0:T(8,128)(2,1)S(1)} %get-tuple-element.29), channel_id=1, source_target_pairs={{0,4},{4,0},{8,12},{12,8},{16,20},{20,16},{24,28},{28,24},{32,36},... | collective-permute-start | bytes 393224 | tf_op jit(solution)/shard_map/ppermute | solution.py:345
  36.9 2.8 %collective-permute-start.6 = (bf16[512,128]{1,0:T(8,128)(2,1)S(1)}, bf16[512,128]{1,0:T(8,128)(2,1)S(1)}, u32[]{:S(2)}, u32[]{:S(2)}) collective-permute-start(bf16[512,128]{1,0:T(8,128)(2,1)S(1)} %get-tuple-element.30), channel_id=1, source_target_pairs={{0,4},{4,0},{8,12},{12,8},{16,20},{20,16},{24,28},{28,24},{32,36},... | collective-permute-start | bytes 393224 | tf_op jit(solution)/shard_map/ppermute | solution.py:345
  37.0 5.9 %collective-permute-start.7 = (bf16[512,128]{1,0:T(8,128)(2,1)S(1)}, bf16[512,128]{1,0:T(8,128)(2,1)S(1)}, u32[]{:S(2)}, u32[]{:S(2)}) collective-permute-start(bf16[512,128]{1,0:T(8,128)(2,1)S(1)} %get-tuple-element.27.refs_3_), channel_id=1, source_target_pairs={{0,64},{4,68},{8,72},{12,76},{16,80},{20,84},{24,88},{28,92},{32,9... | collective-permute-start | bytes 393224 | tf_op jit(solution)/shard_map/ppermute | solution.py:345
  37.0 5.9 %collective-permute-start.8 = (bf16[512,128]{1,0:T(8,128)(2,1)S(1)}, bf16[512,128]{1,0:T(8,128)(2,1)S(1)}, u32[]{:S(2)}, u32[]{:S(2)}) collective-permute-start(bf16[512,128]{1,0:T(8,128)(2,1)S(1)} %get-tuple-element.28.refs_4_), channel_id=1, source_target_pairs={{0,192},{4,196},{8,200},{12,204},{16,208},{20,212},{24,216},{28,22... | collective-permute-start | bytes 393224 | tf_op jit(solution)/shard_map/ppermute | solution.py:345
  39.7 5.5 %collective-permute-start.9 = (bf16[512,128]{1,0:T(8,128)(2,1)S(1)}, bf16[512,128]{1,0:T(8,128)(2,1)S(1)}, u32[]{:S(2)}, u32[]{:S(2)}) collective-permute-start(bf16[512,128]{1,0:T(8,128)(2,1)S(1)} %collective-permute-done.5.refs_5_), channel_id=1, source_target_pairs={{0,64},{4,68},{8,72},{12,76},{16,80},{20,84},{24,88},{28,92},{32,9... | collective-permute-start | bytes 393224 | tf_op jit(solution)/shard_map/ppermute | solution.py:345
  39.7 5.5 %collective-permute-start.10 = (bf16[512,128]{1,0:T(8,128)(2,1)S(1)}, bf16[512,128]{1,0:T(8,128)(2,1)S(1)}, u32[]{:S(2)}, u32[]{:S(2)}) collective-permute-start(bf16[512,128]{1,0:T(8,128)(2,1)S(1)} %collective-permute-done.6.refs_6_), channel_id=1, source_target_pairs={{0,192},{4,196},{8,200},{12,204},{16,208},{20,212},{24,216},{28,22... | collective-permute-start | bytes 393224 | tf_op jit(solution)/shard_map/ppermute | solution.py:345
  46.3 14.9 %all-to-all-start.1 = ((bf16[32,16,128]{2,1,0:T(8,128)(2,1)}), bf16[32,16,128]{2,1,0:T(8,128)(2,1)S(1)}, u32[]{:S(2)}, u32[]{:S(2)}) async-start(bf16[32,16,128]{2,1,0:T(8,128)(2,1)} %get-tuple-element.32.after_ref), calls=%async_computation.1 | async-start | bytes 262144 | tf_op jit(solution)/shard_map/all_to_all | solution.py:427
  52.4 7.8 %collective-permute-start.14 = (bf16[512,128]{1,0:T(8,128)(2,1)S(1)}, bf16[512,128]{1,0:T(8,128)(2,1)S(1)}, u32[]{:S(2)}, u32[]{:S(2)}) collective-permute-start(bf16[512,128]{1,0:T(8,128)(2,1)S(1)} %get-tuple-element.37), channel_id=1, source_target_pairs={{0,64},{4,68},{8,72},{12,76},{16,80},{20,84},{24,88},{28,92},{32,9... | collective-permute-start | bytes 393224 | tf_op jit(solution)/shard_map/ppermute | solution.py:345
  53.8 5.7 %copy-start = (bf16[2,256,256]{2,1,0:T(8,128)(2,1)S(1)}, bf16[2,256,256]{2,1,0:T(8,128)(2,1)}, u32[]{:S(2)}) copy-start(bf16[2,256,256]{2,1,0:T(8,128)(2,1)} %constant.33.second_ref.refs_5_) | copy-start | bytes 786436
  53.8 5.7 %copy-start.1 = (bf16[2,144,64]{2,1,0:T(8,128)(2,1)S(1)}, bf16[2,144,64]{2,1,0:T(8,128)(2,1)}, u32[]{:S(2)}) copy-start(bf16[2,144,64]{2,1,0:T(8,128)(2,1)} %constant.30.first_ref.refs_3_) | copy-start | bytes 110596
  53.8 5.7 %copy-start.2 = (f32[2,72,128]{2,1,0:T(8,128)S(1)}, f32[2,72,128]{2,1,0:T(8,128)}, u32[]{:S(2)}) copy-start(f32[2,72,128]{2,1,0:T(8,128)} %constant.26.clone.twist_ref.refs_4_) | copy-start | bytes 221188
  53.8 6.5 %collective-permute-start.15 = (bf16[512,128]{1,0:T(8,128)(2,1)S(1)}, bf16[512,128]{1,0:T(8,128)(2,1)S(1)}, u32[]{:S(2)}, u32[]{:S(2)}) collective-permute-start(bf16[512,128]{1,0:T(8,128)(2,1)S(1)} %get-tuple-element.38), channel_id=1, source_target_pairs={{0,192},{4,196},{8,200},{12,204},{16,208},{20,212},{24,216},{28,22... | collective-permute-start | bytes 393224 | tf_op jit(solution)/shard_map/ppermute | solution.py:345
  55.4 4.1 %collective-permute-start.12 = (bf16[256,128]{1,0:T(8,128)(2,1)S(1)}, bf16[256,128]{1,0:T(8,128)(2,1)S(1)}, u32[]{:S(2)}, u32[]{:S(2)}) collective-permute-start(bf16[256,128]{1,0:T(8,128)(2,1)S(1)} %get-tuple-element.34), channel_id=1, source_target_pairs={{0,4},{4,0},{8,12},{12,8},{16,20},{20,16},{24,28},{28,24},{32,36},... | collective-permute-start | bytes 196616 | tf_op jit(solution)/shard_map/ppermute | solution.py:345
  58.6 1.6 %collective-permute-start.11 = (bf16[128,256]{1,0:T(8,128)(2,1)S(1)}, bf16[128,256]{1,0:T(8,128)(2,1)S(1)}, u32[]{:S(2)}, u32[]{:S(2)}) collective-permute-start(bf16[128,256]{1,0:T(8,128)(2,1)S(1)} %get-tuple-element.31), channel_id=1, source_target_pairs={{0,4},{4,0},{8,12},{12,8},{16,20},{20,16},{24,28},{28,24},{32,36},... | collective-permute-start | bytes 196616 | tf_op jit(solution)/shard_map/ppermute | solution.py:345
  59.5 1.8 %copy-start.3 = (bf16[2,256,256]{2,1,0:T(8,128)(2,1)S(1)}, bf16[2,256,256]{2,1,0:T(8,128)(2,1)}, u32[]{:S(2)}) copy-start(bf16[2,256,256]{2,1,0:T(8,128)(2,1)} %constant.36.refs_6_) | copy-start | bytes 786436
  59.5 1.8 %copy-start.9 = (bf16[2,64,144]{2,1,0:T(8,128)(2,1)S(1)}, bf16[2,64,144]{2,1,0:T(8,128)(2,1)}, u32[]{:S(2)}) copy-start(bf16[2,64,144]{2,1,0:T(8,128)(2,1)} %constant.39.refs_7_) | copy-start | bytes 110596
  80.3 6.7 %copy-start.7 = (bf16[128,512]{1,0:T(8,128)(2,1)S(1)}, bf16[128,512]{1,0:T(8,128)(2,1)}, u32[]{:S(2)}) copy-start(bf16[128,512]{1,0:T(8,128)(2,1)} %refs_6_.1) | copy-start | bytes 393220
  80.3 6.7 %copy-start.8 = (bf16[128,512]{1,0:T(8,128)(2,1)S(1)}, bf16[128,512]{1,0:T(8,128)(2,1)}, u32[]{:S(2)}) copy-start(bf16[128,512]{1,0:T(8,128)(2,1)} %refs_7_.1) | copy-start | bytes 393220
  80.4 6.6 %collective-permute-start.16 = (bf16[256,128]{1,0:T(8,128)(2,1)S(1)}, bf16[256,128]{1,0:T(8,128)(2,1)S(1)}, u32[]{:S(2)}, u32[]{:S(2)}) collective-permute-start(bf16[256,128]{1,0:T(8,128)(2,1)S(1)} %get-tuple-element.40), channel_id=1, source_target_pairs={{0,4},{4,0},{8,12},{12,8},{16,20},{20,16},{24,28},{28,24},{32,36},... | collective-permute-start | bytes 196616 | tf_op jit(solution)/shard_map/ppermute | solution.py:345
  85.7 1.2 %collective-permute-start.17 = (f32[32,256]{1,0:T(8,128)S(1)}, f32[32,256]{1,0:T(8,128)S(1)}, u32[]{:S(2)}, u32[]{:S(2)}) collective-permute-start(f32[32,256]{1,0:T(8,128)S(1)} %get-tuple-element.42), channel_id=1, source_target_pairs={{0,4},{4,0},{8,12},{12,8},{16,20},{20,16},{24,28},{28,24},{32,36},... | collective-permute-start | bytes 98312 | tf_op jit(solution)/shard_map/ppermute | solution.py:345

commit v9 on v8

--- a/solution.py
+++ b/solution.py
@@ -128,14 +128,13 @@
 def pack_kernel(filters_ref, weight_ref, out_ref):
     chips, depth, rows = out_ref.shape
     chan = filters_ref.shape[1]
-    feats = weight_ref.shape[0]
+    feats = weight_ref.shape[1]
     turned = filters_ref[...].astype(F32).T.reshape(CORES, chips, chan // (CORES * chips), rows)
     turned = jnp.swapaxes(turned, 0, 1).reshape(chips, depth - CORES * feats, rows)
     out_ref[:, CORES * feats :, :] = turned.astype(BF16)
     for core in range(CORES):
         for part in range(2):
-            start = (core * 2 + part) * rows
-            piece = weight_ref[:, start : start + rows]
+            piece = weight_ref[core * 2 + part]
             for chip in range(chips):
                 if chip // ALONG_Z % 2 == part:
                     out_ref[chip, core * feats : (core + 1) * feats, :] = piece
@@ -355,7 +354,10 @@
     twist = jnp.asarray(twist, F32)
 
     (packed,) = call(
-        pack_kernel, [((chips, CORES * (feats + chans), rows), BF16)], filters, out_weight
+        pack_kernel,
+        [((chips, CORES * (feats + chans), rows), BF16)],
+        filters,
+        out_weight.reshape(feats, CORES * 2, rows).swapaxes(0, 1),
     )
     like_cores = [list(range(core, groups, CORES)) for core in range(CORES)]
     arrived = lax.all_to_all(packed, "seq", 0, 0, axis_index_groups=like_cores)

time: 88.1 us -> 88.2 us (level)
  no operation moved by 1% of the time
where the time goes in v9:
time: 88.2 us; the launch traced here: 87.8 us
  starting transfers between devices  44.7 us (51%)
  blocking collectives  17.4 us (20%)
  waiting for transfers between devices  15.1 us (17%)
  Pallas kernels  7.92 us (9%)
  local copies, waits for them, and re-layouts  1.83 us (2%)
    ppermute x14, starting transfers between devices, send(): return lax.ppermute(value, 'seq', pairs)  21.9 us
    all_to_all x1, blocking collectives, shards(): lax.all_to_all(inner, 'seq', 0, 0, axis_index_groups=like_cores)  17.4 us
    all_to_all x1, starting transfers between devices, shards(): arrived = lax.all_to_all(packed, 'seq', 0, 0, axis_index_groups=like_cores)  12 us
    ppermute x3, waiting for transfers between devices, shards(): lax.ppermute(turned_grad, 'ch', [(i, (i - hop) % features) for i in range...  8.19 us
    pallas_call x13, Pallas kernels, call(): pl.pallas_call(kernel, out_shape=[jax.ShapeDtypeStruct(shape, dtype) for...  7.92 us
    ppermute x14, waiting for transfers between devices, send(): return lax.ppermute(value, 'seq', pairs)  5.92 us
    all_to_all x1, starting transfers between devices, shards(): received = lax.all_to_all(turned, 'seq', 0, 0, axis_index_groups=like_cores)  5.76 us
    ppermute x3, starting transfers between devices, shards(): lax.ppermute(turned_grad, 'ch', [(i, (i - hop) % features) for i in range...  3.85 us
  transfers between devices with their start and end apart: 20, of which 9 were waited for; matrix products, arithmetic and copies ran while one was open for 0% of the time, Pallas kernels for 5%

profile of v9, /device:TPU:1, one launch (start us, length us, event | category | flops | bytes accessed | tf_op | source)
XLA Modules:
  0.0 87.8 jit_solution(13834040341590164030)
XLA Ops:
  0.6 0.7 copy-done
  1.4 0.9 %copy-done.5 = bf16[128,512]{1,0:T(8,128)(2,1)S(1)} copy-done((bf16[128,512]{1,0:T(8,128)(2,1)S(1)}, bf16[128,512]{1,0:T(8,128)(2,1)}, u32[]{:S(2)}) %copy-start.5) | copy-done | bytes 131096
  2.3 1.0 %shard_map.187 = bf16[32,80,128]{2,1,0:T(8,128)(2,1)} custom-call(bf16[128,512]{1,0:T(8,128)(2,1)S(1)} %copy-done.5, bf16[4,32,128]{2,1,0:T(8,128)(2,1)S(1)} %bitcast_bitcast_fusion.weight_ref), custom_call_target="tpu_custom_call" | custom-call | tf_op jit(solution)/shard_map/pallas_call | solution.py:317
  3.3 12.0 %all-to-all-start = ((bf16[32,80,128]{2,1,0:T(8,128)(2,1)}), bf16[32,80,128]{2,1,0:T(8,128)(2,1)S(1)}, u32[]{:S(2)}, u32[]{:S(2)}) async-start(bf16[32,80,128]{2,1,0:T(8,128)(2,1)} %shard_map.187), calls=%async_computation | async-start | bytes 1310720 | tf_op jit(solution)/shard_map/all_to_all | solution.py:363
  15.4 2.8 %collective-permute-start.1 = (bf16[512,128]{1,0:T(8,128)(2,1)S(1)}, bf16[512,128]{1,0:T(8,128)(2,1)S(1)}, u32[]{:S(2)}, u32[]{:S(2)}) collective-permute-start(bf16[512,128]{1,0:T(8,128)(2,1)S(1)} %bitcast.8), channel_id=1, source_target_pairs={{0,3},{1,0},{2,1},{3,2},{4,7},{5,4},{6,5},{7,6},{8,11},{9,8},{10,9... | collective-permute-start | bytes 393224 | tf_op jit(solution)/shard_map/ppermute | solution.py:371
  18.2 0.3 collective-permute-start.2
  18.6 0.7 collective-permute-start.3
  19.3 1.9 %collective-permute-done.1.refs_2_ = bf16[512,128]{1,0:T(8,128)(2,1)S(1)} collective-permute-done((bf16[512,128]{1,0:T(8,128)(2,1)S(1)}, bf16[512,128]{1,0:T(8,128)(2,1)S(1)}, u32[]{:S(2)}, u32[]{:S(2)}) %collective-permute-start.1) | collective-permute-done | bytes 131104 | tf_op jit(solution)/shard_map/ppermute | solution.py:371
  21.3 2.4 %collective-permute-done.2.refs_3_ = bf16[512,128]{1,0:T(8,128)(2,1)S(1)} collective-permute-done((bf16[512,128]{1,0:T(8,128)(2,1)S(1)}, bf16[512,128]{1,0:T(8,128)(2,1)S(1)}, u32[]{:S(2)}, u32[]{:S(2)}) %collective-permute-start.2) | collective-permute-done | bytes 131104 | tf_op jit(solution)/shard_map/ppermute | solution.py:371
  23.7 3.8 %collective-permute-done.3.refs_4_ = bf16[512,128]{1,0:T(8,128)(2,1)S(1)} collective-permute-done((bf16[512,128]{1,0:T(8,128)(2,1)S(1)}, bf16[512,128]{1,0:T(8,128)(2,1)S(1)}, u32[]{:S(2)}, u32[]{:S(2)}) %collective-permute-start.3) | collective-permute-done | bytes 131104 | tf_op jit(solution)/shard_map/ppermute | solution.py:371
  27.6 1.0 %collective-permute-start.4 = (bf16[2048,128]{1,0:T(8,128)(2,1)S(1)}, bf16[2048,128]{1,0:T(8,128)(2,1)S(1)}, u32[]{:S(2)}, u32[]{:S(2)}) collective-permute-start(bf16[2048,128]{1,0:T(8,128)(2,1)S(1)} %shard_map.184.mine_ref), channel_id=1, source_target_pairs={{0,4},{4,0},{8,12},{12,8},{16,20},{20,16},{24,28},{28,24},{32,36},... | collective-permute-start | bytes 1572872 | tf_op jit(solution)/shard_map/ppermute | solution.py:344
  28.7 1.6 %collective-permute-done.came_ref.refs_1_ = bf16[256,256]{1,0:T(8,128)(2,1)S(1)} collective-permute-done((bf16[256,256]{1,0:T(8,128)(2,1)S(1)}, bf16[256,256]{1,0:T(8,128)(2,1)S(1)}, u32[]{:S(2)}, u32[]{:S(2)}) %collective-permute-start) | collective-permute-done | bytes 131104 | tf_op jit(solution)/shard_map/ppermute | solution.py:344
  30.3 1.6 %shard_map.186 = (bf16[2048,128]{1,0:T(8,128)(2,1)S(1)}, bf16[2048,128]{1,0:T(8,128)(2,1)}) custom-call(bf16[2048,128]{1,0:T(8,128)(2,1)S(1)} %shard_map.184.mine_ref, bf16[2048,128]{1,0:T(8,128)(2,1)S(1)} %collective-permute-done.4.theirs_ref, bf16[256,256]{1,0:T(8,128)(2,1)S(1)} %get-tuple-element.24.refs_0_.own_ref, ...), custom_call_target="tpu_custom_call" | custom-call | tf_op jit(solution)/shard_map/pallas_call | solution.py:317
  31.9 1.2 %collective-permute-start.13 = (bf16[2048,128]{1,0:T(8,128)(2,1)}, bf16[2048,128]{1,0:T(8,128)(2,1)S(1)}, u32[]{:S(2)}, u32[]{:S(2)}) collective-permute-start(bf16[2048,128]{1,0:T(8,128)(2,1)} %get-tuple-element.35), channel_id=1, source_target_pairs={{0,8},{4,12},{8,0},{12,4},{16,24},{20,28},{24,16},{28,20},{32,40},... | collective-permute-start | bytes 1572872 | tf_op jit(solution)/shard_map/ppermute | solution.py:424
  33.2 3.6 %collective-permute-start.5 = (bf16[512,128]{1,0:T(8,128)(2,1)S(1)}, bf16[512,128]{1,0:T(8,128)(2,1)S(1)}, u32[]{:S(2)}, u32[]{:S(2)}) collective-permute-start(bf16[512,128]{1,0:T(8,128)(2,1)S(1)} %get-tuple-element.29), channel_id=1, source_target_pairs={{0,4},{4,0},{8,12},{12,8},{16,20},{20,16},{24,28},{28,24},{32,36},... | collective-permute-start | bytes 393224 | tf_op jit(solution)/shard_map/ppermute | solution.py:344
  37.0 2.7 %collective-permute-start.8 = (bf16[512,128]{1,0:T(8,128)(2,1)S(1)}, bf16[512,128]{1,0:T(8,128)(2,1)S(1)}, u32[]{:S(2)}, u32[]{:S(2)}) collective-permute-start(bf16[512,128]{1,0:T(8,128)(2,1)S(1)} %get-tuple-element.28.refs_4_), channel_id=1, source_target_pairs={{0,192},{4,196},{8,200},{12,204},{16,208},{20,212},{24,216},{28,22... | collective-permute-start | bytes 393224 | tf_op jit(solution)/shard_map/ppermute | solution.py:344
  39.7 2.7 %collective-permute-start.10 = (bf16[512,128]{1,0:T(8,128)(2,1)S(1)}, bf16[512,128]{1,0:T(8,128)(2,1)S(1)}, u32[]{:S(2)}, u32[]{:S(2)}) collective-permute-start(bf16[512,128]{1,0:T(8,128)(2,1)S(1)} %collective-permute-done.6.refs_6_), channel_id=1, source_target_pairs={{0,192},{4,196},{8,200},{12,204},{16,208},{20,212},{24,216},{28,22... | collective-permute-start | bytes 393224 | tf_op jit(solution)/shard_map/ppermute | solution.py:344
  42.3 0.4 shard_map.185.refs_2_
  42.9 2.3 %collective-permute-done.9.refs_9_ = bf16[512,128]{1,0:T(8,128)(2,1)S(1)} collective-permute-done((bf16[512,128]{1,0:T(8,128)(2,1)S(1)}, bf16[512,128]{1,0:T(8,128)(2,1)S(1)}, u32[]{:S(2)}, u32[]{:S(2)}) %collective-permute-start.9) | collective-permute-done | bytes 131104 | tf_op jit(solution)/shard_map/ppermute | solution.py:344
  45.2 1.2 %shard_map.189 = (bf16[32,16,128]{2,1,0:T(8,128)(2,1)}, bf16[128,256]{1,0:T(8,128)(2,1)S(1)}, bf16[128,256]{1,0:T(8,128)(2,1)S(1)}) custom-call(bf16[256,256]{1,0:T(8,128)(2,1)S(1)} %get-tuple-element.24.refs_0_.own_ref, bf16[256,256]{1,0:T(8,128)(2,1)S(1)} %collective-permute-done.came_ref.refs_1_, bf16[256,2048]{1,0:T(8,128)(2,1)S(1)} %shard_map.185.refs_2_, ...), custom_call_target="tpu_custom_call" | custom-call | tf_op jit(solution)/shard_map/pallas_call | solution.py:317
  46.3 5.8 %all-to-all-start.1 = ((bf16[32,16,128]{2,1,0:T(8,128)(2,1)}), bf16[32,16,128]{2,1,0:T(8,128)(2,1)S(1)}, u32[]{:S(2)}, u32[]{:S(2)}) async-start(bf16[32,16,128]{2,1,0:T(8,128)(2,1)} %get-tuple-element.32.after_ref), calls=%async_computation.1 | async-start | bytes 262144 | tf_op jit(solution)/shard_map/all_to_all | solution.py:429
  52.5 1.3 %collective-permute-start.14 = (bf16[512,128]{1,0:T(8,128)(2,1)S(1)}, bf16[512,128]{1,0:T(8,128)(2,1)S(1)}, u32[]{:S(2)}, u32[]{:S(2)}) collective-permute-start(bf16[512,128]{1,0:T(8,128)(2,1)S(1)} %get-tuple-element.37), channel_id=1, source_target_pairs={{0,64},{4,68},{8,72},{12,76},{16,80},{20,84},{24,88},{28,92},{32,9... | collective-permute-start | bytes 393224 | tf_op jit(solution)/shard_map/ppermute | solution.py:344
  53.8 1.6 %collective-permute-start.15 = (bf16[512,128]{1,0:T(8,128)(2,1)S(1)}, bf16[512,128]{1,0:T(8,128)(2,1)S(1)}, u32[]{:S(2)}, u32[]{:S(2)}) collective-permute-start(bf16[512,128]{1,0:T(8,128)(2,1)S(1)} %get-tuple-element.38), channel_id=1, source_target_pairs={{0,192},{4,196},{8,200},{12,204},{16,208},{20,212},{24,216},{28,22... | collective-permute-start | bytes 393224 | tf_op jit(solution)/shard_map/ppermute | solution.py:344
  55.4 3.2 %collective-permute-start.12 = (bf16[256,128]{1,0:T(8,128)(2,1)S(1)}, bf16[256,128]{1,0:T(8,128)(2,1)S(1)}, u32[]{:S(2)}, u32[]{:S(2)}) collective-permute-start(bf16[256,128]{1,0:T(8,128)(2,1)S(1)} %get-tuple-element.34), channel_id=1, source_target_pairs={{0,4},{4,0},{8,12},{12,8},{16,20},{20,16},{24,28},{28,24},{32,36},... | collective-permute-start | bytes 196616 | tf_op jit(solution)/shard_map/ppermute | solution.py:344
  58.7 0.8 collective-permute-done.12.came_ref
  59.5 0.7 shard_map.191.refs_2_
  60.3 1.0 %all-to-all-done.1.refs_1_ = bf16[32,16,128]{2,1,0:T(8,128)(2,1)S(1)} async-done(((bf16[32,16,128]{2,1,0:T(8,128)(2,1)}), bf16[32,16,128]{2,1,0:T(8,128)(2,1)S(1)}, u32[]{:S(2)}, u32[]{:S(2)}) %all-to-all-start.1) | async-done | bytes 131104 | tf_op jit(solution)/shard_map/all_to_all | solution.py:429
  61.3 1.6 %shard_map.193 = bf16[32,48,128]{2,1,0:T(8,128)(2,1)S(1)} custom-call(bf16[128,256]{1,0:T(8,128)(2,1)S(1)} %collective-permute-done.11.refs_0_.refs_5_, bf16[32,16,128]{2,1,0:T(8,128)(2,1)S(1)} %all-to-all-done.1.refs_1_, f32[576,256]{1,0:T(8,128)S(1)} %shard_map.191.refs_2_, bf16[2,144,64]{2,1,0:T(8,128)(2,1)S(1)} %copy-done.2, ...), custom_call_target="tpu_custom_call" | custom-call | tf_op jit(solution)/shard_map/pallas_call | solution.py:317
  62.9 17.4 %all_to_all.15.came_ref = bf16[32,48,128]{2,1,0:T(8,128)(2,1)S(1)} all-to-all(bf16[32,48,128]{2,1,0:T(8,128)(2,1)S(1)} %shard_map.193), channel_id=1, replica_groups={{0,8,16,24,32,40,48,56,64,72,80,88,96,104,112,120,128,136,144,152,160,1..., dimensions={0} | all-to-all | bytes 786432 | tf_op jit(solution)/shard_map/all_to_all | solution.py:455
  80.4 5.3 %collective-permute-start.16 = (bf16[256,128]{1,0:T(8,128)(2,1)S(1)}, bf16[256,128]{1,0:T(8,128)(2,1)S(1)}, u32[]{:S(2)}, u32[]{:S(2)}) collective-permute-start(bf16[256,128]{1,0:T(8,128)(2,1)S(1)} %get-tuple-element.40), channel_id=1, source_target_pairs={{0,4},{4,0},{8,12},{12,8},{16,20},{20,16},{24,28},{28,24},{32,36},... | collective-permute-start | bytes 196616 | tf_op jit(solution)/shard_map/ppermute | solution.py:344
  85.8 1.1 %collective-permute-done.17.refs_3_ = f32[32,256]{1,0:T(8,128)S(1)} collective-permute-done((f32[32,256]{1,0:T(8,128)S(1)}, f32[32,256]{1,0:T(8,128)S(1)}, u32[]{:S(2)}, u32[]{:S(2)}) %collective-permute-start.17) | collective-permute-done | bytes 32800 | tf_op jit(solution)/shard_map/ppermute | solution.py:344
  86.9 0.8 shard_map.195
  (48 shorter events, 1.4 us)
Async XLA Ops:
  0.6 0.8 copy-start
  1.4 0.9 %copy-start.5 = (bf16[128,512]{1,0:T(8,128)(2,1)S(1)}, bf16[128,512]{1,0:T(8,128)(2,1)}, u32[]{:S(2)}) copy-start(bf16[128,512]{1,0:T(8,128)(2,1)} %filters_ref.1) | copy-start | bytes 393220
  3.3 12.0 %copy-start.11 = (bf16[128,512]{1,0:T(8,128)(2,1)S(1)}, bf16[128,512]{1,0:T(8,128)(2,1)}, u32[]{:S(2)}) copy-start(bf16[128,512]{1,0:T(8,128)(2,1)} %param.21) | copy-start | bytes 393220
  3.3 29.9 %all-to-all-start = ((bf16[32,80,128]{2,1,0:T(8,128)(2,1)}), bf16[32,80,128]{2,1,0:T(8,128)(2,1)S(1)}, u32[]{:S(2)}, u32[]{:S(2)}) async-start(bf16[32,80,128]{2,1,0:T(8,128)(2,1)} %shard_map.187), calls=%async_computation | async-start | bytes 1310720 | tf_op jit(solution)/shard_map/all_to_all | solution.py:363
  15.3 4.0 %copy-start.6 = (bf16[128,512]{1,0:T(8,128)(2,1)S(1)}, bf16[128,512]{1,0:T(8,128)(2,1)}, u32[]{:S(2)}) copy-start(bf16[128,512]{1,0:T(8,128)(2,1)} %refs_0_.1) | copy-start | bytes 393220
  15.3 4.0 %copy-start.7 = (bf16[128,512]{1,0:T(8,128)(2,1)S(1)}, bf16[128,512]{1,0:T(8,128)(2,1)}, u32[]{:S(2)}) copy-start(bf16[128,512]{1,0:T(8,128)(2,1)} %refs_1_.1) | copy-start | bytes 393220
  15.4 5.8 %collective-permute-start.1 = (bf16[512,128]{1,0:T(8,128)(2,1)S(1)}, bf16[512,128]{1,0:T(8,128)(2,1)S(1)}, u32[]{:S(2)}, u32[]{:S(2)}) collective-permute-start(bf16[512,128]{1,0:T(8,128)(2,1)S(1)} %bitcast.8), channel_id=1, source_target_pairs={{0,3},{1,0},{2,1},{3,2},{4,7},{5,4},{6,5},{7,6},{8,11},{9,8},{10,9... | collective-permute-start | bytes 393224 | tf_op jit(solution)/shard_map/ppermute | solution.py:371
  18.2 5.4 %collective-permute-start.2 = (bf16[512,128]{1,0:T(8,128)(2,1)S(1)}, bf16[512,128]{1,0:T(8,128)(2,1)S(1)}, u32[]{:S(2)}, u32[]{:S(2)}) collective-permute-start(bf16[512,128]{1,0:T(8,128)(2,1)S(1)} %bitcast.9), channel_id=1, source_target_pairs={{0,2},{1,3},{2,0},{3,1},{4,6},{5,7},{6,4},{7,5},{8,10},{9,11},{10,... | collective-permute-start | bytes 393224 | tf_op jit(solution)/shard_map/ppermute | solution.py:371
  18.6 8.9 %collective-permute-start.3 = (bf16[512,128]{1,0:T(8,128)(2,1)S(1)}, bf16[512,128]{1,0:T(8,128)(2,1)S(1)}, u32[]{:S(2)}, u32[]{:S(2)}) collective-permute-start(bf16[512,128]{1,0:T(8,128)(2,1)S(1)} %bitcast.10), channel_id=1, source_target_pairs={{0,1},{1,2},{2,3},{3,0},{4,5},{5,6},{6,7},{7,4},{8,9},{9,10},{10,1... | collective-permute-start | bytes 393224 | tf_op jit(solution)/shard_map/ppermute | solution.py:371
  27.6 2.8 %collective-permute-start.4 = (bf16[2048,128]{1,0:T(8,128)(2,1)S(1)}, bf16[2048,128]{1,0:T(8,128)(2,1)S(1)}, u32[]{:S(2)}, u32[]{:S(2)}) collective-permute-start(bf16[2048,128]{1,0:T(8,128)(2,1)S(1)} %shard_map.184.mine_ref), channel_id=1, source_target_pairs={{0,4},{4,0},{8,12},{12,8},{16,20},{20,16},{24,28},{28,24},{32,36},... | collective-permute-start | bytes 1572872 | tf_op jit(solution)/shard_map/ppermute | solution.py:344
  28.6 1.7 %collective-permute-start = (bf16[256,256]{1,0:T(8,128)(2,1)S(1)}, bf16[256,256]{1,0:T(8,128)(2,1)S(1)}, u32[]{:S(2)}, u32[]{:S(2)}) collective-permute-start(bf16[256,256]{1,0:T(8,128)(2,1)S(1)} %get-tuple-element.25), channel_id=1, source_target_pairs={{0,4},{4,0},{8,12},{12,8},{16,20},{20,16},{24,28},{28,24},{32,36},... | collective-permute-start | bytes 393224 | tf_op jit(solution)/shard_map/ppermute | solution.py:344
  31.9 20.2 %collective-permute-start.13 = (bf16[2048,128]{1,0:T(8,128)(2,1)}, bf16[2048,128]{1,0:T(8,128)(2,1)S(1)}, u32[]{:S(2)}, u32[]{:S(2)}) collective-permute-start(bf16[2048,128]{1,0:T(8,128)(2,1)} %get-tuple-element.35), channel_id=1, source_target_pairs={{0,8},{4,12},{8,0},{12,4},{16,24},{20,28},{24,16},{28,20},{32,40},... | collective-permute-start | bytes 1572872 | tf_op jit(solution)/shard_map/ppermute | solution.py:424
  33.2 6.4 %collective-permute-start.5 = (bf16[512,128]{1,0:T(8,128)(2,1)S(1)}, bf16[512,128]{1,0:T(8,128)(2,1)S(1)}, u32[]{:S(2)}, u32[]{:S(2)}) collective-permute-start(bf16[512,128]{1,0:T(8,128)(2,1)S(1)} %get-tuple-element.29), channel_id=1, source_target_pairs={{0,4},{4,0},{8,12},{12,8},{16,20},{20,16},{24,28},{28,24},{32,36},... | collective-permute-start | bytes 393224 | tf_op jit(solution)/shard_map/ppermute | solution.py:344
  36.9 2.8 %collective-permute-start.6 = (bf16[512,128]{1,0:T(8,128)(2,1)S(1)}, bf16[512,128]{1,0:T(8,128)(2,1)S(1)}, u32[]{:S(2)}, u32[]{:S(2)}) collective-permute-start(bf16[512,128]{1,0:T(8,128)(2,1)S(1)} %get-tuple-element.30), channel_id=1, source_target_pairs={{0,4},{4,0},{8,12},{12,8},{16,20},{20,16},{24,28},{28,24},{32,36},... | collective-permute-start | bytes 393224 | tf_op jit(solution)/shard_map/ppermute | solution.py:344
  37.0 5.9 %collective-permute-start.7 = (bf16[512,128]{1,0:T(8,128)(2,1)S(1)}, bf16[512,128]{1,0:T(8,128)(2,1)S(1)}, u32[]{:S(2)}, u32[]{:S(2)}) collective-permute-start(bf16[512,128]{1,0:T(8,128)(2,1)S(1)} %get-tuple-element.27.refs_3_), channel_id=1, source_target_pairs={{0,64},{4,68},{8,72},{12,76},{16,80},{20,84},{24,88},{28,92},{32,9... | collective-permute-start | bytes 393224 | tf_op jit(solution)/shard_map/ppermute | solution.py:344
  37.0 5.9 %collective-permute-start.8 = (bf16[512,128]{1,0:T(8,128)(2,1)S(1)}, bf16[512,128]{1,0:T(8,128)(2,1)S(1)}, u32[]{:S(2)}, u32[]{:S(2)}) collective-permute-start(bf16[512,128]{1,0:T(8,128)(2,1)S(1)} %get-tuple-element.28.refs_4_), channel_id=1, source_target_pairs={{0,192},{4,196},{8,200},{12,204},{16,208},{20,212},{24,216},{28,22... | collective-permute-start | bytes 393224 | tf_op jit(solution)/shard_map/ppermute | solution.py:344
  39.7 5.5 %collective-permute-start.9 = (bf16[512,128]{1,0:T(8,128)(2,1)S(1)}, bf16[512,128]{1,0:T(8,128)(2,1)S(1)}, u32[]{:S(2)}, u32[]{:S(2)}) collective-permute-start(bf16[512,128]{1,0:T(8,128)(2,1)S(1)} %collective-permute-done.5.refs_5_), channel_id=1, source_target_pairs={{0,64},{4,68},{8,72},{12,76},{16,80},{20,84},{24,88},{28,92},{32,9... | collective-permute-start | bytes 393224 | tf_op jit(solution)/shard_map/ppermute | solution.py:344
  39.7 5.5 %collective-permute-start.10 = (bf16[512,128]{1,0:T(8,128)(2,1)S(1)}, bf16[512,128]{1,0:T(8,128)(2,1)S(1)}, u32[]{:S(2)}, u32[]{:S(2)}) collective-permute-start(bf16[512,128]{1,0:T(8,128)(2,1)S(1)} %collective-permute-done.6.refs_6_), channel_id=1, source_target_pairs={{0,192},{4,196},{8,200},{12,204},{16,208},{20,212},{24,216},{28,22... | collective-permute-start | bytes 393224 | tf_op jit(solution)/shard_map/ppermute | solution.py:344
  46.3 14.9 %all-to-all-start.1 = ((bf16[32,16,128]{2,1,0:T(8,128)(2,1)}), bf16[32,16,128]{2,1,0:T(8,128)(2,1)S(1)}, u32[]{:S(2)}, u32[]{:S(2)}) async-start(bf16[32,16,128]{2,1,0:T(8,128)(2,1)} %get-tuple-element.32.after_ref), calls=%async_computation.1 | async-start | bytes 262144 | tf_op jit(solution)/shard_map/all_to_all | solution.py:429
  52.5 7.8 %collective-permute-start.14 = (bf16[512,128]{1,0:T(8,128)(2,1)S(1)}, bf16[512,128]{1,0:T(8,128)(2,1)S(1)}, u32[]{:S(2)}, u32[]{:S(2)}) collective-permute-start(bf16[512,128]{1,0:T(8,128)(2,1)S(1)} %get-tuple-element.37), channel_id=1, source_target_pairs={{0,64},{4,68},{8,72},{12,76},{16,80},{20,84},{24,88},{28,92},{32,9... | collective-permute-start | bytes 393224 | tf_op jit(solution)/shard_map/ppermute | solution.py:344
  53.8 5.7 %copy-start.1 = (bf16[2,256,256]{2,1,0:T(8,128)(2,1)S(1)}, bf16[2,256,256]{2,1,0:T(8,128)(2,1)}, u32[]{:S(2)}) copy-start(bf16[2,256,256]{2,1,0:T(8,128)(2,1)} %constant.33.second_ref.refs_5_) | copy-start | bytes 786436
  53.8 5.7 %copy-start.2 = (bf16[2,144,64]{2,1,0:T(8,128)(2,1)S(1)}, bf16[2,144,64]{2,1,0:T(8,128)(2,1)}, u32[]{:S(2)}) copy-start(bf16[2,144,64]{2,1,0:T(8,128)(2,1)} %constant.30.first_ref.refs_3_) | copy-start | bytes 110596
  53.8 5.7 %copy-start.3 = (f32[2,72,128]{2,1,0:T(8,128)S(1)}, f32[2,72,128]{2,1,0:T(8,128)}, u32[]{:S(2)}) copy-start(f32[2,72,128]{2,1,0:T(8,128)} %constant.26.clone.twist_ref.refs_4_) | copy-start | bytes 221188
  53.8 6.5 %collective-permute-start.15 = (bf16[512,128]{1,0:T(8,128)(2,1)S(1)}, bf16[512,128]{1,0:T(8,128)(2,1)S(1)}, u32[]{:S(2)}, u32[]{:S(2)}) collective-permute-start(bf16[512,128]{1,0:T(8,128)(2,1)S(1)} %get-tuple-element.38), channel_id=1, source_target_pairs={{0,192},{4,196},{8,200},{12,204},{16,208},{20,212},{24,216},{28,22... | collective-permute-start | bytes 393224 | tf_op jit(solution)/shard_map/ppermute | solution.py:344
  55.4 4.1 %collective-permute-start.12 = (bf16[256,128]{1,0:T(8,128)(2,1)S(1)}, bf16[256,128]{1,0:T(8,128)(2,1)S(1)}, u32[]{:S(2)}, u32[]{:S(2)}) collective-permute-start(bf16[256,128]{1,0:T(8,128)(2,1)S(1)} %get-tuple-element.34), channel_id=1, source_target_pairs={{0,4},{4,0},{8,12},{12,8},{16,20},{20,16},{24,28},{28,24},{32,36},... | collective-permute-start | bytes 196616 | tf_op jit(solution)/shard_map/ppermute | solution.py:344
  58.6 1.6 %collective-permute-start.11 = (bf16[128,256]{1,0:T(8,128)(2,1)S(1)}, bf16[128,256]{1,0:T(8,128)(2,1)S(1)}, u32[]{:S(2)}, u32[]{:S(2)}) collective-permute-start(bf16[128,256]{1,0:T(8,128)(2,1)S(1)} %get-tuple-element.31), channel_id=1, source_target_pairs={{0,4},{4,0},{8,12},{12,8},{16,20},{20,16},{24,28},{28,24},{32,36},... | collective-permute-start | bytes 196616 | tf_op jit(solution)/shard_map/ppermute | solution.py:344
  59.5 1.8 %copy-start.4 = (bf16[2,256,256]{2,1,0:T(8,128)(2,1)S(1)}, bf16[2,256,256]{2,1,0:T(8,128)(2,1)}, u32[]{:S(2)}) copy-start(bf16[2,256,256]{2,1,0:T(8,128)(2,1)} %constant.36.refs_6_) | copy-start | bytes 786436
  59.5 1.8 %copy-start.10 = (bf16[2,64,144]{2,1,0:T(8,128)(2,1)S(1)}, bf16[2,64,144]{2,1,0:T(8,128)(2,1)}, u32[]{:S(2)}) copy-start(bf16[2,64,144]{2,1,0:T(8,128)(2,1)} %constant.39.refs_7_) | copy-start | bytes 110596
  80.3 6.7 %copy-start.8 = (bf16[128,512]{1,0:T(8,128)(2,1)S(1)}, bf16[128,512]{1,0:T(8,128)(2,1)}, u32[]{:S(2)}) copy-start(bf16[128,512]{1,0:T(8,128)(2,1)} %refs_6_.1) | copy-start | bytes 393220
  80.3 6.7 %copy-start.9 = (bf16[128,512]{1,0:T(8,128)(2,1)S(1)}, bf16[128,512]{1,0:T(8,128)(2,1)}, u32[]{:S(2)}) copy-start(bf16[128,512]{1,0:T(8,128)(2,1)} %refs_7_.1) | copy-start | bytes 393220
  80.4 6.6 %collective-permute-start.16 = (bf16[256,128]{1,0:T(8,128)(2,1)S(1)}, bf16[256,128]{1,0:T(8,128)(2,1)S(1)}, u32[]{:S(2)}, u32[]{:S(2)}) collective-permute-start(bf16[256,128]{1,0:T(8,128)(2,1)S(1)} %get-tuple-element.40), channel_id=1, source_target_pairs={{0,4},{4,0},{8,12},{12,8},{16,20},{20,16},{24,28},{28,24},{32,36},... | collective-permute-start | bytes 196616 | tf_op jit(solution)/shard_map/ppermute | solution.py:344
  85.7 1.2 %collective-permute-start.17 = (f32[32,256]{1,0:T(8,128)S(1)}, f32[32,256]{1,0:T(8,128)S(1)}, u32[]{:S(2)}, u32[]{:S(2)}) collective-permute-start(f32[32,256]{1,0:T(8,128)S(1)} %get-tuple-element.42), channel_id=1, source_target_pairs={{0,4},{4,0},{8,12},{12,8},{16,20},{20,16},{24,28},{28,24},{32,36},... | collective-permute-start | bytes 98312 | tf_op jit(solution)/shard_map/ppermute | solution.py:344

commit v10 on v9

--- a/solution.py
+++ b/solution.py
@@ -60,7 +60,7 @@
 
 
 def spectrum(data, first_ref, twist_ref, second_ref, chans, rows, kept):
-    bins = dot(first_ref[0], data) + dot(first_ref[1], data)
+    bins = dot(first_ref[...], jnp.concatenate([data, data], 0))
     cos, sin = twist_ref[0], twist_ref[1]
     parts = []
     for c in range(chans):
@@ -111,7 +111,8 @@
         re = bins[c * kept : (c + 1) * kept, :rows]
         im = bins[c * kept : (c + 1) * kept, rows:]
         parts.append(jnp.concatenate([re * cos + im * sin, im * cos - re * sin], 0))
-    inner = dot3((last_ref[0], last_ref[1]), split(jnp.concatenate(parts, 1)))
+    high, low = split(jnp.concatenate(parts, 1))
+    inner = dot(last_ref[...], jnp.concatenate([high, high, low], 0))
     for c in range(chans):
         for core in range(CORES):
             wide[core, pl.ds(c, chips, stride=chans), :] = inner[
@@ -349,7 +350,9 @@
     order = np.arange(groups).reshape(chips, CORES).T.reshape(-1)
     first, twist, second, last = dft_tables(groups, rows, kept)
     first, last = first[:, order], last[order]
-    first, last = jnp.stack(halves(first)), jnp.stack(halves(last))
+    first = jnp.concatenate(halves(first), 1)
+    high, low = halves(last)
+    last = jnp.concatenate([high, low, high], 1)
     second, back = jnp.stack(halves(second)), jnp.stack(halves(second.T))
     twist = jnp.asarray(twist, F32)
 

time: 88.2 us -> 88 us (level)
  no operation moved by 1% of the time
where the time goes in v10:
time: 88 us; the launch traced here: 87.7 us
  starting transfers between devices  44.7 us (51%)
  blocking collectives  17.4 us (20%)
  waiting for transfers between devices  15.2 us (17%)
  Pallas kernels  7.72 us (9%)
  local copies, waits for them, and re-layouts  1.83 us (2%)
    ppermute x14, starting transfers between devices, send(): return lax.ppermute(value, 'seq', pairs)  21.9 us
    all_to_all x1, blocking collectives, shards(): lax.all_to_all(inner, 'seq', 0, 0, axis_index_groups=like_cores)  17.4 us
    all_to_all x1, starting transfers between devices, shards(): arrived = lax.all_to_all(packed, 'seq', 0, 0, axis_index_groups=like_cores)  12 us
    ppermute x3, waiting for transfers between devices, shards(): lax.ppermute(turned_grad, 'ch', [(i, (i - hop) % features) for i in range...  8.19 us
    pallas_call x13, Pallas kernels, call(): pl.pallas_call(kernel, out_shape=[jax.ShapeDtypeStruct(shape, dtype) for...  7.72 us
    ppermute x14, waiting for transfers between devices, send(): return lax.ppermute(value, 'seq', pairs)  5.92 us
    all_to_all x1, starting transfers between devices, shards(): received = lax.all_to_all(turned, 'seq', 0, 0, axis_index_groups=like_cores)  5.76 us
    ppermute x3, starting transfers between devices, shards(): lax.ppermute(turned_grad, 'ch', [(i, (i - hop) % features) for i in range...  3.85 us
  transfers between devices with their start and end apart: 20, of which 9 were waited for; matrix products, arithmetic and copies ran while one was open for 0% of the time, Pallas kernels for 5%

profile of v10, /device:TPU:1, one launch (start us, length us, event | category | flops | bytes accessed | tf_op | source)
XLA Modules:
  0.0 87.7 jit_solution(13626868987642735879)
XLA Ops:
  0.6 0.7 copy-done
  1.4 0.9 %copy-done.5 = bf16[128,512]{1,0:T(8,128)(2,1)S(1)} copy-done((bf16[128,512]{1,0:T(8,128)(2,1)S(1)}, bf16[128,512]{1,0:T(8,128)(2,1)}, u32[]{:S(2)}) %copy-start.5) | copy-done | bytes 131096
  2.3 1.0 %shard_map.196 = bf16[32,80,128]{2,1,0:T(8,128)(2,1)} custom-call(bf16[128,512]{1,0:T(8,128)(2,1)S(1)} %copy-done.5, bf16[4,32,128]{2,1,0:T(8,128)(2,1)S(1)} %bitcast_bitcast_fusion.weight_ref), custom_call_target="tpu_custom_call" | custom-call | tf_op jit(solution)/shard_map/pallas_call | solution.py:318
  3.3 12.0 %all-to-all-start = ((bf16[32,80,128]{2,1,0:T(8,128)(2,1)}), bf16[32,80,128]{2,1,0:T(8,128)(2,1)S(1)}, u32[]{:S(2)}, u32[]{:S(2)}) async-start(bf16[32,80,128]{2,1,0:T(8,128)(2,1)} %shard_map.196), calls=%async_computation | async-start | bytes 1310720 | tf_op jit(solution)/shard_map/all_to_all | solution.py:366
  15.4 2.8 %collective-permute-start.1 = (bf16[512,128]{1,0:T(8,128)(2,1)S(1)}, bf16[512,128]{1,0:T(8,128)(2,1)S(1)}, u32[]{:S(2)}, u32[]{:S(2)}) collective-permute-start(bf16[512,128]{1,0:T(8,128)(2,1)S(1)} %bitcast.8), channel_id=1, source_target_pairs={{0,3},{1,0},{2,1},{3,2},{4,7},{5,4},{6,5},{7,6},{8,11},{9,8},{10,9... | collective-permute-start | bytes 393224 | tf_op jit(solution)/shard_map/ppermute | solution.py:374
  18.2 0.3 collective-permute-start.2
  18.6 0.7 collective-permute-start.3
  19.3 1.9 %collective-permute-done.1.refs_2_ = bf16[512,128]{1,0:T(8,128)(2,1)S(1)} collective-permute-done((bf16[512,128]{1,0:T(8,128)(2,1)S(1)}, bf16[512,128]{1,0:T(8,128)(2,1)S(1)}, u32[]{:S(2)}, u32[]{:S(2)}) %collective-permute-start.1) | collective-permute-done | bytes 131104 | tf_op jit(solution)/shard_map/ppermute | solution.py:374
  21.3 2.4 %collective-permute-done.2.refs_3_ = bf16[512,128]{1,0:T(8,128)(2,1)S(1)} collective-permute-done((bf16[512,128]{1,0:T(8,128)(2,1)S(1)}, bf16[512,128]{1,0:T(8,128)(2,1)S(1)}, u32[]{:S(2)}, u32[]{:S(2)}) %collective-permute-start.2) | collective-permute-done | bytes 131104 | tf_op jit(solution)/shard_map/ppermute | solution.py:374
  23.7 3.8 %collective-permute-done.3.refs_4_ = bf16[512,128]{1,0:T(8,128)(2,1)S(1)} collective-permute-done((bf16[512,128]{1,0:T(8,128)(2,1)S(1)}, bf16[512,128]{1,0:T(8,128)(2,1)S(1)}, u32[]{:S(2)}, u32[]{:S(2)}) %collective-permute-start.3) | collective-permute-done | bytes 131104 | tf_op jit(solution)/shard_map/ppermute | solution.py:374
  27.6 1.0 %collective-permute-start.4 = (bf16[2048,128]{1,0:T(8,128)(2,1)S(1)}, bf16[2048,128]{1,0:T(8,128)(2,1)S(1)}, u32[]{:S(2)}, u32[]{:S(2)}) collective-permute-start(bf16[2048,128]{1,0:T(8,128)(2,1)S(1)} %shard_map.193.mine_ref), channel_id=1, source_target_pairs={{0,4},{4,0},{8,12},{12,8},{16,20},{20,16},{24,28},{28,24},{32,36},... | collective-permute-start | bytes 1572872 | tf_op jit(solution)/shard_map/ppermute | solution.py:345
  28.7 1.6 %collective-permute-done.came_ref.refs_1_ = bf16[256,256]{1,0:T(8,128)(2,1)S(1)} collective-permute-done((bf16[256,256]{1,0:T(8,128)(2,1)S(1)}, bf16[256,256]{1,0:T(8,128)(2,1)S(1)}, u32[]{:S(2)}, u32[]{:S(2)}) %collective-permute-start) | collective-permute-done | bytes 131104 | tf_op jit(solution)/shard_map/ppermute | solution.py:345
  30.3 1.6 %shard_map.195 = (bf16[2048,128]{1,0:T(8,128)(2,1)S(1)}, bf16[2048,128]{1,0:T(8,128)(2,1)}) custom-call(bf16[2048,128]{1,0:T(8,128)(2,1)S(1)} %shard_map.193.mine_ref, bf16[2048,128]{1,0:T(8,128)(2,1)S(1)} %collective-permute-done.4.theirs_ref, bf16[256,256]{1,0:T(8,128)(2,1)S(1)} %get-tuple-element.24.refs_0_.own_ref, ...), custom_call_target="tpu_custom_call" | custom-call | tf_op jit(solution)/shard_map/pallas_call | solution.py:318
  31.9 1.2 %collective-permute-start.13 = (bf16[2048,128]{1,0:T(8,128)(2,1)}, bf16[2048,128]{1,0:T(8,128)(2,1)S(1)}, u32[]{:S(2)}, u32[]{:S(2)}) collective-permute-start(bf16[2048,128]{1,0:T(8,128)(2,1)} %get-tuple-element.35), channel_id=1, source_target_pairs={{0,8},{4,12},{8,0},{12,4},{16,24},{20,28},{24,16},{28,20},{32,40},... | collective-permute-start | bytes 1572872 | tf_op jit(solution)/shard_map/ppermute | solution.py:427
  33.2 3.6 %collective-permute-start.5 = (bf16[512,128]{1,0:T(8,128)(2,1)S(1)}, bf16[512,128]{1,0:T(8,128)(2,1)S(1)}, u32[]{:S(2)}, u32[]{:S(2)}) collective-permute-start(bf16[512,128]{1,0:T(8,128)(2,1)S(1)} %get-tuple-element.29), channel_id=1, source_target_pairs={{0,4},{4,0},{8,12},{12,8},{16,20},{20,16},{24,28},{28,24},{32,36},... | collective-permute-start | bytes 393224 | tf_op jit(solution)/shard_map/ppermute | solution.py:345
  37.0 2.7 %collective-permute-start.8 = (bf16[512,128]{1,0:T(8,128)(2,1)S(1)}, bf16[512,128]{1,0:T(8,128)(2,1)S(1)}, u32[]{:S(2)}, u32[]{:S(2)}) collective-permute-start(bf16[512,128]{1,0:T(8,128)(2,1)S(1)} %get-tuple-element.28.refs_4_), channel_id=1, source_target_pairs={{0,192},{4,196},{8,200},{12,204},{16,208},{20,212},{24,216},{28,22... | collective-permute-start | bytes 393224 | tf_op jit(solution)/shard_map/ppermute | solution.py:345
  39.7 2.7 %collective-permute-start.10 = (bf16[512,128]{1,0:T(8,128)(2,1)S(1)}, bf16[512,128]{1,0:T(8,128)(2,1)S(1)}, u32[]{:S(2)}, u32[]{:S(2)}) collective-permute-start(bf16[512,128]{1,0:T(8,128)(2,1)S(1)} %collective-permute-done.6.refs_6_), channel_id=1, source_target_pairs={{0,192},{4,196},{8,200},{12,204},{16,208},{20,212},{24,216},{28,22... | collective-permute-start | bytes 393224 | tf_op jit(solution)/shard_map/ppermute | solution.py:345
  42.3 0.4 shard_map.194.refs_2_
  42.9 2.3 %collective-permute-done.9.refs_9_ = bf16[512,128]{1,0:T(8,128)(2,1)S(1)} collective-permute-done((bf16[512,128]{1,0:T(8,128)(2,1)S(1)}, bf16[512,128]{1,0:T(8,128)(2,1)S(1)}, u32[]{:S(2)}, u32[]{:S(2)}) %collective-permute-start.9) | collective-permute-done | bytes 131104 | tf_op jit(solution)/shard_map/ppermute | solution.py:345
  45.2 1.2 %shard_map.198 = (bf16[32,16,128]{2,1,0:T(8,128)(2,1)}, bf16[128,256]{1,0:T(8,128)(2,1)S(1)}, bf16[128,256]{1,0:T(8,128)(2,1)S(1)}) custom-call(bf16[256,256]{1,0:T(8,128)(2,1)S(1)} %get-tuple-element.24.refs_0_.own_ref, bf16[256,256]{1,0:T(8,128)(2,1)S(1)} %collective-permute-done.came_ref.refs_1_, bf16[256,2048]{1,0:T(8,128)(2,1)S(1)} %shard_map.194.refs_2_, ...), custom_call_target="tpu_custom_call" | custom-call | tf_op jit(solution)/shard_map/pallas_call | solution.py:318
  46.3 5.8 %all-to-all-start.1 = ((bf16[32,16,128]{2,1,0:T(8,128)(2,1)}), bf16[32,16,128]{2,1,0:T(8,128)(2,1)S(1)}, u32[]{:S(2)}, u32[]{:S(2)}) async-start(bf16[32,16,128]{2,1,0:T(8,128)(2,1)} %get-tuple-element.32.after_ref), calls=%async_computation.1 | async-start | bytes 262144 | tf_op jit(solution)/shard_map/all_to_all | solution.py:432
  52.5 1.3 %collective-permute-start.14 = (bf16[512,128]{1,0:T(8,128)(2,1)S(1)}, bf16[512,128]{1,0:T(8,128)(2,1)S(1)}, u32[]{:S(2)}, u32[]{:S(2)}) collective-permute-start(bf16[512,128]{1,0:T(8,128)(2,1)S(1)} %get-tuple-element.37), channel_id=1, source_target_pairs={{0,64},{4,68},{8,72},{12,76},{16,80},{20,84},{24,88},{28,92},{32,9... | collective-permute-start | bytes 393224 | tf_op jit(solution)/shard_map/ppermute | solution.py:345
  53.8 1.6 %collective-permute-start.15 = (bf16[512,128]{1,0:T(8,128)(2,1)S(1)}, bf16[512,128]{1,0:T(8,128)(2,1)S(1)}, u32[]{:S(2)}, u32[]{:S(2)}) collective-permute-start(bf16[512,128]{1,0:T(8,128)(2,1)S(1)} %get-tuple-element.38), channel_id=1, source_target_pairs={{0,192},{4,196},{8,200},{12,204},{16,208},{20,212},{24,216},{28,22... | collective-permute-start | bytes 393224 | tf_op jit(solution)/shard_map/ppermute | solution.py:345
  55.4 3.2 %collective-permute-start.12 = (bf16[256,128]{1,0:T(8,128)(2,1)S(1)}, bf16[256,128]{1,0:T(8,128)(2,1)S(1)}, u32[]{:S(2)}, u32[]{:S(2)}) collective-permute-start(bf16[256,128]{1,0:T(8,128)(2,1)S(1)} %get-tuple-element.34), channel_id=1, source_target_pairs={{0,4},{4,0},{8,12},{12,8},{16,20},{20,16},{24,28},{28,24},{32,36},... | collective-permute-start | bytes 196616 | tf_op jit(solution)/shard_map/ppermute | solution.py:345
  58.7 0.8 collective-permute-done.12.came_ref
  59.5 0.6 shard_map.200.refs_2_
  60.2 1.1 %all-to-all-done.1.refs_1_ = bf16[32,16,128]{2,1,0:T(8,128)(2,1)S(1)} async-done(((bf16[32,16,128]{2,1,0:T(8,128)(2,1)}), bf16[32,16,128]{2,1,0:T(8,128)(2,1)S(1)}, u32[]{:S(2)}, u32[]{:S(2)}) %all-to-all-start.1) | async-done | bytes 131104 | tf_op jit(solution)/shard_map/all_to_all | solution.py:432
  61.3 1.5 %shard_map.202 = bf16[32,48,128]{2,1,0:T(8,128)(2,1)S(1)} custom-call(bf16[128,256]{1,0:T(8,128)(2,1)S(1)} %collective-permute-done.11.refs_0_.refs_5_, bf16[32,16,128]{2,1,0:T(8,128)(2,1)S(1)} %all-to-all-done.1.refs_1_, f32[576,256]{1,0:T(8,128)S(1)} %shard_map.200.refs_2_, bf16[144,128]{1,0:T(8,128)(2,1)S(1)} %copy-done.4, f32[2,72,128]{2,1,0:T(8,128)S(1)} %copy-done.2, ...), custom_call_target="tpu_custom_call" | custom-call | tf_op jit(solution)/shard_map/pallas_call | solution.py:318
  62.8 17.4 %all_to_all.15.came_ref = bf16[32,48,128]{2,1,0:T(8,128)(2,1)S(1)} all-to-all(bf16[32,48,128]{2,1,0:T(8,128)(2,1)S(1)} %shard_map.202), channel_id=1, replica_groups={{0,8,16,24,32,40,48,56,64,72,80,88,96,104,112,120,128,136,144,152,160,1..., dimensions={0} | all-to-all | bytes 786432 | tf_op jit(solution)/shard_map/all_to_all | solution.py:458
  80.3 5.3 %collective-permute-start.16 = (bf16[256,128]{1,0:T(8,128)(2,1)S(1)}, bf16[256,128]{1,0:T(8,128)(2,1)S(1)}, u32[]{:S(2)}, u32[]{:S(2)}) collective-permute-start(bf16[256,128]{1,0:T(8,128)(2,1)S(1)} %get-tuple-element.40), channel_id=1, source_target_pairs={{0,4},{4,0},{8,12},{12,8},{16,20},{20,16},{24,28},{28,24},{32,36},... | collective-permute-start | bytes 196616 | tf_op jit(solution)/shard_map/ppermute | solution.py:345
  85.7 1.1 %collective-permute-done.17.refs_3_ = f32[32,256]{1,0:T(8,128)S(1)} collective-permute-done((f32[32,256]{1,0:T(8,128)S(1)}, f32[32,256]{1,0:T(8,128)S(1)}, u32[]{:S(2)}, u32[]{:S(2)}) %collective-permute-start.17) | collective-permute-done | bytes 32800 | tf_op jit(solution)/shard_map/ppermute | solution.py:345
  86.8 0.8 shard_map.204
  (48 shorter events, 1.4 us)
Async XLA Ops:
  0.6 0.8 copy-start
  1.4 0.9 %copy-start.5 = (bf16[128,512]{1,0:T(8,128)(2,1)S(1)}, bf16[128,512]{1,0:T(8,128)(2,1)}, u32[]{:S(2)}) copy-start(bf16[128,512]{1,0:T(8,128)(2,1)} %filters_ref.1) | copy-start | bytes 393220
  3.3 12.0 %copy-start.11 = (bf16[128,512]{1,0:T(8,128)(2,1)S(1)}, bf16[128,512]{1,0:T(8,128)(2,1)}, u32[]{:S(2)}) copy-start(bf16[128,512]{1,0:T(8,128)(2,1)} %param.22) | copy-start | bytes 393220
  3.3 29.9 %all-to-all-start = ((bf16[32,80,128]{2,1,0:T(8,128)(2,1)}), bf16[32,80,128]{2,1,0:T(8,128)(2,1)S(1)}, u32[]{:S(2)}, u32[]{:S(2)}) async-start(bf16[32,80,128]{2,1,0:T(8,128)(2,1)} %shard_map.196), calls=%async_computation | async-start | bytes 1310720 | tf_op jit(solution)/shard_map/all_to_all | solution.py:366
  15.3 4.0 %copy-start.6 = (bf16[128,512]{1,0:T(8,128)(2,1)S(1)}, bf16[128,512]{1,0:T(8,128)(2,1)}, u32[]{:S(2)}) copy-start(bf16[128,512]{1,0:T(8,128)(2,1)} %refs_0_.1) | copy-start | bytes 393220
  15.3 4.0 %copy-start.7 = (bf16[128,512]{1,0:T(8,128)(2,1)S(1)}, bf16[128,512]{1,0:T(8,128)(2,1)}, u32[]{:S(2)}) copy-start(bf16[128,512]{1,0:T(8,128)(2,1)} %refs_1_.1) | copy-start | bytes 393220
  15.4 5.8 %collective-permute-start.1 = (bf16[512,128]{1,0:T(8,128)(2,1)S(1)}, bf16[512,128]{1,0:T(8,128)(2,1)S(1)}, u32[]{:S(2)}, u32[]{:S(2)}) collective-permute-start(bf16[512,128]{1,0:T(8,128)(2,1)S(1)} %bitcast.8), channel_id=1, source_target_pairs={{0,3},{1,0},{2,1},{3,2},{4,7},{5,4},{6,5},{7,6},{8,11},{9,8},{10,9... | collective-permute-start | bytes 393224 | tf_op jit(solution)/shard_map/ppermute | solution.py:374
  18.2 5.4 %collective-permute-start.2 = (bf16[512,128]{1,0:T(8,128)(2,1)S(1)}, bf16[512,128]{1,0:T(8,128)(2,1)S(1)}, u32[]{:S(2)}, u32[]{:S(2)}) collective-permute-start(bf16[512,128]{1,0:T(8,128)(2,1)S(1)} %bitcast.9), channel_id=1, source_target_pairs={{0,2},{1,3},{2,0},{3,1},{4,6},{5,7},{6,4},{7,5},{8,10},{9,11},{10,... | collective-permute-start | bytes 393224 | tf_op jit(solution)/shard_map/ppermute | solution.py:374
  18.6 8.9 %collective-permute-start.3 = (bf16[512,128]{1,0:T(8,128)(2,1)S(1)}, bf16[512,128]{1,0:T(8,128)(2,1)S(1)}, u32[]{:S(2)}, u32[]{:S(2)}) collective-permute-start(bf16[512,128]{1,0:T(8,128)(2,1)S(1)} %bitcast.10), channel_id=1, source_target_pairs={{0,1},{1,2},{2,3},{3,0},{4,5},{5,6},{6,7},{7,4},{8,9},{9,10},{10,1... | collective-permute-start | bytes 393224 | tf_op jit(solution)/shard_map/ppermute | solution.py:374
  27.6 2.8 %collective-permute-start.4 = (bf16[2048,128]{1,0:T(8,128)(2,1)S(1)}, bf16[2048,128]{1,0:T(8,128)(2,1)S(1)}, u32[]{:S(2)}, u32[]{:S(2)}) collective-permute-start(bf16[2048,128]{1,0:T(8,128)(2,1)S(1)} %shard_map.193.mine_ref), channel_id=1, source_target_pairs={{0,4},{4,0},{8,12},{12,8},{16,20},{20,16},{24,28},{28,24},{32,36},... | collective-permute-start | bytes 1572872 | tf_op jit(solution)/shard_map/ppermute | solution.py:345
  28.6 1.7 %collective-permute-start = (bf16[256,256]{1,0:T(8,128)(2,1)S(1)}, bf16[256,256]{1,0:T(8,128)(2,1)S(1)}, u32[]{:S(2)}, u32[]{:S(2)}) collective-permute-start(bf16[256,256]{1,0:T(8,128)(2,1)S(1)} %get-tuple-element.25), channel_id=1, source_target_pairs={{0,4},{4,0},{8,12},{12,8},{16,20},{20,16},{24,28},{28,24},{32,36},... | collective-permute-start | bytes 393224 | tf_op jit(solution)/shard_map/ppermute | solution.py:345
  31.9 20.2 %collective-permute-start.13 = (bf16[2048,128]{1,0:T(8,128)(2,1)}, bf16[2048,128]{1,0:T(8,128)(2,1)S(1)}, u32[]{:S(2)}, u32[]{:S(2)}) collective-permute-start(bf16[2048,128]{1,0:T(8,128)(2,1)} %get-tuple-element.35), channel_id=1, source_target_pairs={{0,8},{4,12},{8,0},{12,4},{16,24},{20,28},{24,16},{28,20},{32,40},... | collective-permute-start | bytes 1572872 | tf_op jit(solution)/shard_map/ppermute | solution.py:427
  33.2 6.4 %collective-permute-start.5 = (bf16[512,128]{1,0:T(8,128)(2,1)S(1)}, bf16[512,128]{1,0:T(8,128)(2,1)S(1)}, u32[]{:S(2)}, u32[]{:S(2)}) collective-permute-start(bf16[512,128]{1,0:T(8,128)(2,1)S(1)} %get-tuple-element.29), channel_id=1, source_target_pairs={{0,4},{4,0},{8,12},{12,8},{16,20},{20,16},{24,28},{28,24},{32,36},... | collective-permute-start | bytes 393224 | tf_op jit(solution)/shard_map/ppermute | solution.py:345
  36.9 2.8 %collective-permute-start.6 = (bf16[512,128]{1,0:T(8,128)(2,1)S(1)}, bf16[512,128]{1,0:T(8,128)(2,1)S(1)}, u32[]{:S(2)}, u32[]{:S(2)}) collective-permute-start(bf16[512,128]{1,0:T(8,128)(2,1)S(1)} %get-tuple-element.30), channel_id=1, source_target_pairs={{0,4},{4,0},{8,12},{12,8},{16,20},{20,16},{24,28},{28,24},{32,36},... | collective-permute-start | bytes 393224 | tf_op jit(solution)/shard_map/ppermute | solution.py:345
  37.0 5.9 %collective-permute-start.7 = (bf16[512,128]{1,0:T(8,128)(2,1)S(1)}, bf16[512,128]{1,0:T(8,128)(2,1)S(1)}, u32[]{:S(2)}, u32[]{:S(2)}) collective-permute-start(bf16[512,128]{1,0:T(8,128)(2,1)S(1)} %get-tuple-element.27.refs_3_), channel_id=1, source_target_pairs={{0,64},{4,68},{8,72},{12,76},{16,80},{20,84},{24,88},{28,92},{32,9... | collective-permute-start | bytes 393224 | tf_op jit(solution)/shard_map/ppermute | solution.py:345
  37.0 5.9 %collective-permute-start.8 = (bf16[512,128]{1,0:T(8,128)(2,1)S(1)}, bf16[512,128]{1,0:T(8,128)(2,1)S(1)}, u32[]{:S(2)}, u32[]{:S(2)}) collective-permute-start(bf16[512,128]{1,0:T(8,128)(2,1)S(1)} %get-tuple-element.28.refs_4_), channel_id=1, source_target_pairs={{0,192},{4,196},{8,200},{12,204},{16,208},{20,212},{24,216},{28,22... | collective-permute-start | bytes 393224 | tf_op jit(solution)/shard_map/ppermute | solution.py:345
  39.7 5.5 %collective-permute-start.9 = (bf16[512,128]{1,0:T(8,128)(2,1)S(1)}, bf16[512,128]{1,0:T(8,128)(2,1)S(1)}, u32[]{:S(2)}, u32[]{:S(2)}) collective-permute-start(bf16[512,128]{1,0:T(8,128)(2,1)S(1)} %collective-permute-done.5.refs_5_), channel_id=1, source_target_pairs={{0,64},{4,68},{8,72},{12,76},{16,80},{20,84},{24,88},{28,92},{32,9... | collective-permute-start | bytes 393224 | tf_op jit(solution)/shard_map/ppermute | solution.py:345
  39.7 5.5 %collective-permute-start.10 = (bf16[512,128]{1,0:T(8,128)(2,1)S(1)}, bf16[512,128]{1,0:T(8,128)(2,1)S(1)}, u32[]{:S(2)}, u32[]{:S(2)}) collective-permute-start(bf16[512,128]{1,0:T(8,128)(2,1)S(1)} %collective-permute-done.6.refs_6_), channel_id=1, source_target_pairs={{0,192},{4,196},{8,200},{12,204},{16,208},{20,212},{24,216},{28,22... | collective-permute-start | bytes 393224 | tf_op jit(solution)/shard_map/ppermute | solution.py:345
  46.3 14.9 %all-to-all-start.1 = ((bf16[32,16,128]{2,1,0:T(8,128)(2,1)}), bf16[32,16,128]{2,1,0:T(8,128)(2,1)S(1)}, u32[]{:S(2)}, u32[]{:S(2)}) async-start(bf16[32,16,128]{2,1,0:T(8,128)(2,1)} %get-tuple-element.32.after_ref), calls=%async_computation.1 | async-start | bytes 262144 | tf_op jit(solution)/shard_map/all_to_all | solution.py:432
  52.5 7.7 %collective-permute-start.14 = (bf16[512,128]{1,0:T(8,128)(2,1)S(1)}, bf16[512,128]{1,0:T(8,128)(2,1)S(1)}, u32[]{:S(2)}, u32[]{:S(2)}) collective-permute-start(bf16[512,128]{1,0:T(8,128)(2,1)S(1)} %get-tuple-element.37), channel_id=1, source_target_pairs={{0,64},{4,68},{8,72},{12,76},{16,80},{20,84},{24,88},{28,92},{32,9... | collective-permute-start | bytes 393224 | tf_op jit(solution)/shard_map/ppermute | solution.py:345
  53.8 5.7 %copy-start.1 = (bf16[2,256,256]{2,1,0:T(8,128)(2,1)S(1)}, bf16[2,256,256]{2,1,0:T(8,128)(2,1)}, u32[]{:S(2)}) copy-start(bf16[2,256,256]{2,1,0:T(8,128)(2,1)} %constant.31.second_ref.refs_5_) | copy-start | bytes 786436
  53.8 5.7 %copy-start.2 = (f32[2,72,128]{2,1,0:T(8,128)S(1)}, f32[2,72,128]{2,1,0:T(8,128)}, u32[]{:S(2)}) copy-start(f32[2,72,128]{2,1,0:T(8,128)} %constant.26.clone.twist_ref.refs_4_) | copy-start | bytes 221188
  53.8 5.7 %copy-start.4 = (bf16[144,128]{1,0:T(8,128)(2,1)S(1)}, bf16[144,128]{1,0:T(8,128)(2,1)}, u32[]{:S(2)}) copy-start(bf16[144,128]{1,0:T(8,128)(2,1)} %constant.28.first_ref.refs_3_) | copy-start | bytes 110596
  53.8 6.4 %collective-permute-start.15 = (bf16[512,128]{1,0:T(8,128)(2,1)S(1)}, bf16[512,128]{1,0:T(8,128)(2,1)S(1)}, u32[]{:S(2)}, u32[]{:S(2)}) collective-permute-start(bf16[512,128]{1,0:T(8,128)(2,1)S(1)} %get-tuple-element.38), channel_id=1, source_target_pairs={{0,192},{4,196},{8,200},{12,204},{16,208},{20,212},{24,216},{28,22... | collective-permute-start | bytes 393224 | tf_op jit(solution)/shard_map/ppermute | solution.py:345
  55.4 4.1 %collective-permute-start.12 = (bf16[256,128]{1,0:T(8,128)(2,1)S(1)}, bf16[256,128]{1,0:T(8,128)(2,1)S(1)}, u32[]{:S(2)}, u32[]{:S(2)}) collective-permute-start(bf16[256,128]{1,0:T(8,128)(2,1)S(1)} %get-tuple-element.34), channel_id=1, source_target_pairs={{0,4},{4,0},{8,12},{12,8},{16,20},{20,16},{24,28},{28,24},{32,36},... | collective-permute-start | bytes 196616 | tf_op jit(solution)/shard_map/ppermute | solution.py:345
  58.6 1.5 %collective-permute-start.11 = (bf16[128,256]{1,0:T(8,128)(2,1)S(1)}, bf16[128,256]{1,0:T(8,128)(2,1)S(1)}, u32[]{:S(2)}, u32[]{:S(2)}) collective-permute-start(bf16[128,256]{1,0:T(8,128)(2,1)S(1)} %get-tuple-element.31), channel_id=1, source_target_pairs={{0,4},{4,0},{8,12},{12,8},{16,20},{20,16},{24,28},{28,24},{32,36},... | collective-permute-start | bytes 196616 | tf_op jit(solution)/shard_map/ppermute | solution.py:345
  59.5 1.8 %copy-start.3 = (bf16[2,256,256]{2,1,0:T(8,128)(2,1)S(1)}, bf16[2,256,256]{2,1,0:T(8,128)(2,1)}, u32[]{:S(2)}) copy-start(bf16[2,256,256]{2,1,0:T(8,128)(2,1)} %constant.34.refs_6_) | copy-start | bytes 786436
  59.5 1.8 %copy-start.10 = (bf16[64,432]{1,0:T(8,128)(2,1)S(1)}, bf16[64,432]{1,0:T(8,128)(2,1)}, u32[]{:S(2)}) copy-start(bf16[64,432]{1,0:T(8,128)(2,1)} %constant.35.refs_7_) | copy-start | bytes 165892
  80.1 6.7 %copy-start.8 = (bf16[128,512]{1,0:T(8,128)(2,1)S(1)}, bf16[128,512]{1,0:T(8,128)(2,1)}, u32[]{:S(2)}) copy-start(bf16[128,512]{1,0:T(8,128)(2,1)} %refs_6_.1) | copy-start | bytes 393220
  80.2 6.7 %copy-start.9 = (bf16[128,512]{1,0:T(8,128)(2,1)S(1)}, bf16[128,512]{1,0:T(8,128)(2,1)}, u32[]{:S(2)}) copy-start(bf16[128,512]{1,0:T(8,128)(2,1)} %refs_7_.1) | copy-start | bytes 393220
  80.3 6.6 %collective-permute-start.16 = (bf16[256,128]{1,0:T(8,128)(2,1)S(1)}, bf16[256,128]{1,0:T(8,128)(2,1)S(1)}, u32[]{:S(2)}, u32[]{:S(2)}) collective-permute-start(bf16[256,128]{1,0:T(8,128)(2,1)S(1)} %get-tuple-element.40), channel_id=1, source_target_pairs={{0,4},{4,0},{8,12},{12,8},{16,20},{20,16},{24,28},{28,24},{32,36},... | collective-permute-start | bytes 196616 | tf_op jit(solution)/shard_map/ppermute | solution.py:345
  85.6 1.2 %collective-permute-start.17 = (f32[32,256]{1,0:T(8,128)S(1)}, f32[32,256]{1,0:T(8,128)S(1)}, u32[]{:S(2)}, u32[]{:S(2)}) collective-permute-start(f32[32,256]{1,0:T(8,128)S(1)} %get-tuple-element.42), channel_id=1, source_target_pairs={{0,4},{4,0},{8,12},{12,8},{16,20},{20,16},{24,28},{28,24},{32,36},... | collective-permute-start | bytes 98312 | tf_op jit(solution)/shard_map/ppermute | solution.py:345

commit v11 on v10

--- a/solution.py
+++ b/solution.py
@@ -252,22 +252,35 @@
     weight_other_ref[...] = jnp.where(odd, first, second)
 
 
+def own_outputs_kernel(own_ref, mine_ref, theirs_ref, key_ref, value_ref, query_grad_ref, key_own_ref, value_own_ref):
+    odd = own_place()[2] == 1
+    half = own_ref.shape[0]
+    inner = own_ref[...].astype(F32).T
+    for ref, out_ref in ((value_ref, key_own_ref), (key_ref, value_own_ref)):
+        factor = jnp.where(odd, ref[:, half:], ref[:, :half])
+        out_ref[...] = (inner * factor.astype(F32)).astype(BF16)
+    own, came = mine_ref[...], theirs_ref[...]
+    query_grad_ref[:, :half] = jnp.where(odd, came, own)
+    query_grad_ref[:, half:] = jnp.where(odd, own, came)
+
+
 def outputs_kernel(scale, *refs):
     odd = own_place()[2] == 1
-    own_ref, came_ref, weight_ref, beside_ref, mine_ref, theirs_ref, key_ref, value_ref = refs[:8]
-    query_grad_ref, key_grad_ref, value_grad_ref, weight_grad_ref = refs[8:]
-    half = own_ref.shape[0]
-    own, came = own_ref[...].astype(F32).T, came_ref[...].astype(F32).T
-    for i, inner in enumerate((jnp.where(odd, came, own), jnp.where(odd, own, came))):
-        place = slice(i * half, (i + 1) * half)
-        key_grad_ref[:, place] = (inner * value_ref[:, place].astype(F32)).astype(BF16)
-        value_grad_ref[:, place] = (inner * key_ref[:, place].astype(F32)).astype(BF16)
+    key_own_ref, value_own_ref, came_ref, weight_ref, beside_ref, key_ref, value_ref = refs[:7]
+    key_grad_ref, value_grad_ref, weight_grad_ref = refs[7:]
+    half = came_ref.shape[0]
+    inner = came_ref[...].astype(F32).T
+    for ref, own_ref, out_ref in (
+        (value_ref, key_own_ref, key_grad_ref),
+        (key_ref, value_own_ref, value_grad_ref),
+    ):
+        factor = jnp.where(odd, ref[:, :half], ref[:, half:])
+        came, own = (inner * factor.astype(F32)).astype(BF16), own_ref[...]
+        out_ref[:, :half] = jnp.where(odd, came, own)
+        out_ref[:, half:] = jnp.where(odd, own, came)
     own, came = weight_ref[...] * scale, beside_ref[...] * scale
     weight_grad_ref[:, :half] = jnp.where(odd, came, own)
     weight_grad_ref[:, half:] = jnp.where(odd, own, came)
-    own, came = mine_ref[...], theirs_ref[...]
-    query_grad_ref[:, :half] = jnp.where(odd, came, own)
-    query_grad_ref[:, half:] = jnp.where(odd, own, came)
 
 
 def arrange_kernel(*refs):
@@ -457,18 +470,27 @@
         [((half, rows), BF16)] * 2 + [((feats, half), F32)] * 2,
         lax.all_to_all(inner, "seq", 0, 0, axis_index_groups=like_cores),
     )
-    return call(
-        functools.partial(outputs_kernel, (rows * groups) ** (-0.5)),
-        [((rows, chan), BF16)] * 3 + [((feats, chan), F32)],
+    query_grad, key_own, value_own = call(
+        own_outputs_kernel,
+        [((rows, chan), BF16)] + [((rows, half), BF16)] * 2,
         inner,
-        to_core(inner_other),
-        weight_sum,
-        to_core(weight_sum_other),
         mine,
         theirs,
         key_proj,
         value_proj,
     )
+    key_grad, value_grad, weight_grad = call(
+        functools.partial(outputs_kernel, (rows * groups) ** (-0.5)),
+        [((rows, chan), BF16)] * 2 + [((feats, chan), F32)],
+        key_own,
+        value_own,
+        to_core(inner_other),
+        weight_sum,
+        to_core(weight_sum_other),
+        key_proj,
+        value_proj,
+    )
+    return query_grad, key_grad, value_grad, weight_grad
 
 
 def solution(mesh):

time: 88 us -> 88 us (level)
    pallas_call x13 -> x14, Pallas kernels: 7.72 us -> 8.4 us  [call(): pl.pallas_call(kernel, out_shape=[jax.ShapeDtypeStruct(shape, dtype) for...]
  transfers between devices with their start and end apart: 20 -> 20, of which waited for: 9 -> 9; matrix products, arithmetic and copies ran while one was open for 0% -> 0% of each run, Pallas kernels for 5% -> 6%
where the time goes in v11:
time: 88 us; the launch traced here: 87.6 us
  starting transfers between devices  44.7 us (51%)
  blocking collectives  17.4 us (20%)
  waiting for transfers between devices  14.5 us (16%)
  Pallas kernels  8.4 us (10%)
  local copies, waits for them, and re-layouts  1.83 us (2%)
    ppermute x14, starting transfers between devices, send(): return lax.ppermute(value, 'seq', pairs)  21.9 us
    all_to_all x1, blocking collectives, shards(): lax.all_to_all(inner, 'seq', 0, 0, axis_index_groups=like_cores)  17.4 us
    all_to_all x1, starting transfers between devices, shards(): arrived = lax.all_to_all(packed, 'seq', 0, 0, axis_index_groups=like_cores)  12 us
    pallas_call x14, Pallas kernels, call(): pl.pallas_call(kernel, out_shape=[jax.ShapeDtypeStruct(shape, dtype) for...  8.4 us
    ppermute x3, waiting for transfers between devices, shards(): lax.ppermute(turned_grad, 'ch', [(i, (i - hop) % features) for i in range...  8.19 us
    all_to_all x1, starting transfers between devices, shards(): received = lax.all_to_all(turned, 'seq', 0, 0, axis_index_groups=like_cores)  5.76 us
    ppermute x14, waiting for transfers between devices, send(): return lax.ppermute(value, 'seq', pairs)  5.23 us
    ppermute x3, starting transfers between devices, shards(): lax.ppermute(turned_grad, 'ch', [(i, (i - hop) % features) for i in range...  3.85 us
  transfers between devices with their start and end apart: 20, of which 9 were waited for; matrix products, arithmetic and copies ran while one was open for 0% of the time, Pallas kernels for 6%

profile of v11, /device:TPU:1, one launch (start us, length us, event | category | flops | bytes accessed | tf_op | source)
XLA Modules:
  0.0 87.6 jit_solution(14412833808128538567)
XLA Ops:
  0.6 0.7 copy-done
  1.4 0.9 %copy-done.7 = bf16[128,512]{1,0:T(8,128)(2,1)S(1)} copy-done((bf16[128,512]{1,0:T(8,128)(2,1)S(1)}, bf16[128,512]{1,0:T(8,128)(2,1)}, u32[]{:S(2)}) %copy-start.7) | copy-done | bytes 131096
  2.3 1.0 %shard_map.196 = bf16[32,80,128]{2,1,0:T(8,128)(2,1)} custom-call(bf16[128,512]{1,0:T(8,128)(2,1)S(1)} %copy-done.7, bf16[4,32,128]{2,1,0:T(8,128)(2,1)S(1)} %bitcast_bitcast_fusion.weight_ref), custom_call_target="tpu_custom_call" | custom-call | tf_op jit(solution)/shard_map/pallas_call | solution.py:331
  3.3 12.0 %all-to-all-start = ((bf16[32,80,128]{2,1,0:T(8,128)(2,1)}), bf16[32,80,128]{2,1,0:T(8,128)(2,1)S(1)}, u32[]{:S(2)}, u32[]{:S(2)}) async-start(bf16[32,80,128]{2,1,0:T(8,128)(2,1)} %shard_map.196), calls=%async_computation | async-start | bytes 1310720 | tf_op jit(solution)/shard_map/all_to_all | solution.py:379
  15.4 2.8 %collective-permute-start.1 = (bf16[512,128]{1,0:T(8,128)(2,1)S(1)}, bf16[512,128]{1,0:T(8,128)(2,1)S(1)}, u32[]{:S(2)}, u32[]{:S(2)}) collective-permute-start(bf16[512,128]{1,0:T(8,128)(2,1)S(1)} %bitcast.8), channel_id=1, source_target_pairs={{0,3},{1,0},{2,1},{3,2},{4,7},{5,4},{6,5},{7,6},{8,11},{9,8},{10,9... | collective-permute-start | bytes 393224 | tf_op jit(solution)/shard_map/ppermute | solution.py:387
  18.6 0.7 collective-permute-start.3
  19.3 1.9 %collective-permute-done.1.refs_2_ = bf16[512,128]{1,0:T(8,128)(2,1)S(1)} collective-permute-done((bf16[512,128]{1,0:T(8,128)(2,1)S(1)}, bf16[512,128]{1,0:T(8,128)(2,1)S(1)}, u32[]{:S(2)}, u32[]{:S(2)}) %collective-permute-start.1) | collective-permute-done | bytes 131104 | tf_op jit(solution)/shard_map/ppermute | solution.py:387
  21.2 2.4 %collective-permute-done.2.refs_3_ = bf16[512,128]{1,0:T(8,128)(2,1)S(1)} collective-permute-done((bf16[512,128]{1,0:T(8,128)(2,1)S(1)}, bf16[512,128]{1,0:T(8,128)(2,1)S(1)}, u32[]{:S(2)}, u32[]{:S(2)}) %collective-permute-start.2) | collective-permute-done | bytes 131104 | tf_op jit(solution)/shard_map/ppermute | solution.py:387
  23.7 3.8 %collective-permute-done.3.refs_4_ = bf16[512,128]{1,0:T(8,128)(2,1)S(1)} collective-permute-done((bf16[512,128]{1,0:T(8,128)(2,1)S(1)}, bf16[512,128]{1,0:T(8,128)(2,1)S(1)}, u32[]{:S(2)}, u32[]{:S(2)}) %collective-permute-start.3) | collective-permute-done | bytes 131104 | tf_op jit(solution)/shard_map/ppermute | solution.py:387
  27.6 1.0 %collective-permute-start.4 = (bf16[2048,128]{1,0:T(8,128)(2,1)S(1)}, bf16[2048,128]{1,0:T(8,128)(2,1)S(1)}, u32[]{:S(2)}, u32[]{:S(2)}) collective-permute-start(bf16[2048,128]{1,0:T(8,128)(2,1)S(1)} %shard_map.193.mine_ref), channel_id=1, source_target_pairs={{0,4},{4,0},{8,12},{12,8},{16,20},{20,16},{24,28},{28,24},{32,36},... | collective-permute-start | bytes 1572872 | tf_op jit(solution)/shard_map/ppermute | solution.py:358
  28.7 1.6 %collective-permute-done.came_ref.refs_1_ = bf16[256,256]{1,0:T(8,128)(2,1)S(1)} collective-permute-done((bf16[256,256]{1,0:T(8,128)(2,1)S(1)}, bf16[256,256]{1,0:T(8,128)(2,1)S(1)}, u32[]{:S(2)}, u32[]{:S(2)}) %collective-permute-start) | collective-permute-done | bytes 131104 | tf_op jit(solution)/shard_map/ppermute | solution.py:358
  30.3 1.6 %shard_map.195 = (bf16[2048,128]{1,0:T(8,128)(2,1)S(1)}, bf16[2048,128]{1,0:T(8,128)(2,1)}) custom-call(bf16[2048,128]{1,0:T(8,128)(2,1)S(1)} %shard_map.193.mine_ref, bf16[2048,128]{1,0:T(8,128)(2,1)S(1)} %collective-permute-done.4.theirs_ref, bf16[256,256]{1,0:T(8,128)(2,1)S(1)} %get-tuple-element.30.refs_0_.own_ref, ...), custom_call_target="tpu_custom_call" | custom-call | tf_op jit(solution)/shard_map/pallas_call | solution.py:331
  31.9 1.2 %collective-permute-start.13 = (bf16[2048,128]{1,0:T(8,128)(2,1)}, bf16[2048,128]{1,0:T(8,128)(2,1)S(1)}, u32[]{:S(2)}, u32[]{:S(2)}) collective-permute-start(bf16[2048,128]{1,0:T(8,128)(2,1)} %get-tuple-element.41), channel_id=1, source_target_pairs={{0,8},{4,12},{8,0},{12,4},{16,24},{20,28},{24,16},{28,20},{32,40},... | collective-permute-start | bytes 1572872 | tf_op jit(solution)/shard_map/ppermute | solution.py:440
  33.2 3.6 %collective-permute-start.5 = (bf16[512,128]{1,0:T(8,128)(2,1)S(1)}, bf16[512,128]{1,0:T(8,128)(2,1)S(1)}, u32[]{:S(2)}, u32[]{:S(2)}) collective-permute-start(bf16[512,128]{1,0:T(8,128)(2,1)S(1)} %get-tuple-element.35), channel_id=1, source_target_pairs={{0,4},{4,0},{8,12},{12,8},{16,20},{20,16},{24,28},{28,24},{32,36},... | collective-permute-start | bytes 393224 | tf_op jit(solution)/shard_map/ppermute | solution.py:358
  37.0 2.7 %collective-permute-start.8 = (bf16[512,128]{1,0:T(8,128)(2,1)S(1)}, bf16[512,128]{1,0:T(8,128)(2,1)S(1)}, u32[]{:S(2)}, u32[]{:S(2)}) collective-permute-start(bf16[512,128]{1,0:T(8,128)(2,1)S(1)} %get-tuple-element.34.refs_4_), channel_id=1, source_target_pairs={{0,192},{4,196},{8,200},{12,204},{16,208},{20,212},{24,216},{28,22... | collective-permute-start | bytes 393224 | tf_op jit(solution)/shard_map/ppermute | solution.py:358
  39.7 2.7 %collective-permute-start.10 = (bf16[512,128]{1,0:T(8,128)(2,1)S(1)}, bf16[512,128]{1,0:T(8,128)(2,1)S(1)}, u32[]{:S(2)}, u32[]{:S(2)}) collective-permute-start(bf16[512,128]{1,0:T(8,128)(2,1)S(1)} %collective-permute-done.6.refs_6_), channel_id=1, source_target_pairs={{0,192},{4,196},{8,200},{12,204},{16,208},{20,212},{24,216},{28,22... | collective-permute-start | bytes 393224 | tf_op jit(solution)/shard_map/ppermute | solution.py:358
  42.3 0.4 shard_map.194.refs_2_
  42.9 2.3 %collective-permute-done.9.refs_9_ = bf16[512,128]{1,0:T(8,128)(2,1)S(1)} collective-permute-done((bf16[512,128]{1,0:T(8,128)(2,1)S(1)}, bf16[512,128]{1,0:T(8,128)(2,1)S(1)}, u32[]{:S(2)}, u32[]{:S(2)}) %collective-permute-start.9) | collective-permute-done | bytes 131104 | tf_op jit(solution)/shard_map/ppermute | solution.py:358
  45.2 1.2 %shard_map.198 = (bf16[32,16,128]{2,1,0:T(8,128)(2,1)}, bf16[128,256]{1,0:T(8,128)(2,1)S(1)}, bf16[128,256]{1,0:T(8,128)(2,1)S(1)}) custom-call(bf16[256,256]{1,0:T(8,128)(2,1)S(1)} %get-tuple-element.30.refs_0_.own_ref, bf16[256,256]{1,0:T(8,128)(2,1)S(1)} %collective-permute-done.came_ref.refs_1_, bf16[256,2048]{1,0:T(8,128)(2,1)S(1)} %shard_map.194.refs_2_, ...), custom_call_target="tpu_custom_call" | custom-call | tf_op jit(solution)/shard_map/pallas_call | solution.py:331
  46.3 5.8 %all-to-all-start.1 = ((bf16[32,16,128]{2,1,0:T(8,128)(2,1)}), bf16[32,16,128]{2,1,0:T(8,128)(2,1)S(1)}, u32[]{:S(2)}, u32[]{:S(2)}) async-start(bf16[32,16,128]{2,1,0:T(8,128)(2,1)} %get-tuple-element.38.after_ref), calls=%async_computation.1 | async-start | bytes 262144 | tf_op jit(solution)/shard_map/all_to_all | solution.py:445
  52.4 1.3 %collective-permute-start.14 = (bf16[512,128]{1,0:T(8,128)(2,1)S(1)}, bf16[512,128]{1,0:T(8,128)(2,1)S(1)}, u32[]{:S(2)}, u32[]{:S(2)}) collective-permute-start(bf16[512,128]{1,0:T(8,128)(2,1)S(1)} %get-tuple-element.43), channel_id=1, source_target_pairs={{0,64},{4,68},{8,72},{12,76},{16,80},{20,84},{24,88},{28,92},{32,9... | collective-permute-start | bytes 393224 | tf_op jit(solution)/shard_map/ppermute | solution.py:358
  53.8 1.6 %collective-permute-start.15 = (bf16[512,128]{1,0:T(8,128)(2,1)S(1)}, bf16[512,128]{1,0:T(8,128)(2,1)S(1)}, u32[]{:S(2)}, u32[]{:S(2)}) collective-permute-start(bf16[512,128]{1,0:T(8,128)(2,1)S(1)} %get-tuple-element.44), channel_id=1, source_target_pairs={{0,192},{4,196},{8,200},{12,204},{16,208},{20,212},{24,216},{28,22... | collective-permute-start | bytes 393224 | tf_op jit(solution)/shard_map/ppermute | solution.py:358
  55.4 3.2 %collective-permute-start.12 = (bf16[256,128]{1,0:T(8,128)(2,1)S(1)}, bf16[256,128]{1,0:T(8,128)(2,1)S(1)}, u32[]{:S(2)}, u32[]{:S(2)}) collective-permute-start(bf16[256,128]{1,0:T(8,128)(2,1)S(1)} %get-tuple-element.40), channel_id=1, source_target_pairs={{0,4},{4,0},{8,12},{12,8},{16,20},{20,16},{24,28},{28,24},{32,36},... | collective-permute-start | bytes 196616 | tf_op jit(solution)/shard_map/ppermute | solution.py:358
  58.7 0.8 collective-permute-done.12.came_ref
  59.5 0.6 shard_map.200.refs_2_
  60.2 1.1 %all-to-all-done.1.refs_1_ = bf16[32,16,128]{2,1,0:T(8,128)(2,1)S(1)} async-done(((bf16[32,16,128]{2,1,0:T(8,128)(2,1)}), bf16[32,16,128]{2,1,0:T(8,128)(2,1)S(1)}, u32[]{:S(2)}, u32[]{:S(2)}) %all-to-all-start.1) | async-done | bytes 131104 | tf_op jit(solution)/shard_map/all_to_all | solution.py:445
  61.3 1.5 %shard_map.202 = bf16[32,48,128]{2,1,0:T(8,128)(2,1)S(1)} custom-call(bf16[128,256]{1,0:T(8,128)(2,1)S(1)} %collective-permute-done.11.refs_0_.theirs_ref, bf16[32,16,128]{2,1,0:T(8,128)(2,1)S(1)} %all-to-all-done.1.refs_1_, f32[576,256]{1,0:T(8,128)S(1)} %shard_map.200.refs_2_, bf16[144,128]{1,0:T(8,128)(2,1)S(1)} %copy-done.6, ...), custom_call_target="tpu_custom_call" | custom-call | tf_op jit(solution)/shard_map/pallas_call | solution.py:331
  62.8 17.4 %all_to_all.15.came_ref = bf16[32,48,128]{2,1,0:T(8,128)(2,1)S(1)} all-to-all(bf16[32,48,128]{2,1,0:T(8,128)(2,1)S(1)} %shard_map.202), channel_id=1, replica_groups={{0,8,16,24,32,40,48,56,64,72,80,88,96,104,112,120,128,136,144,152,160,1..., dimensions={0} | all-to-all | bytes 786432 | tf_op jit(solution)/shard_map/all_to_all | solution.py:471
  80.3 5.3 %collective-permute-start.16 = (bf16[256,128]{1,0:T(8,128)(2,1)S(1)}, bf16[256,128]{1,0:T(8,128)(2,1)S(1)}, u32[]{:S(2)}, u32[]{:S(2)}) collective-permute-start(bf16[256,128]{1,0:T(8,128)(2,1)S(1)} %get-tuple-element.50), channel_id=1, source_target_pairs={{0,4},{4,0},{8,12},{12,8},{16,20},{20,16},{24,28},{28,24},{32,36},... | collective-permute-start | bytes 196616 | tf_op jit(solution)/shard_map/ppermute | solution.py:358
  85.7 0.7 shard_map.204
  86.4 0.4 collective-permute-done.17.refs_4_
  86.8 0.8 shard_map.205
  (49 shorter events, 1.7 us)
Async XLA Ops:
  0.6 0.8 copy-start
  1.4 0.9 %copy-start.7 = (bf16[128,512]{1,0:T(8,128)(2,1)S(1)}, bf16[128,512]{1,0:T(8,128)(2,1)}, u32[]{:S(2)}) copy-start(bf16[128,512]{1,0:T(8,128)(2,1)} %filters_ref.1) | copy-start | bytes 393220
  3.3 12.0 %copy-start.11 = (bf16[128,512]{1,0:T(8,128)(2,1)S(1)}, bf16[128,512]{1,0:T(8,128)(2,1)}, u32[]{:S(2)}) copy-start(bf16[128,512]{1,0:T(8,128)(2,1)} %param.22) | copy-start | bytes 393220
  3.3 29.9 %all-to-all-start = ((bf16[32,80,128]{2,1,0:T(8,128)(2,1)}), bf16[32,80,128]{2,1,0:T(8,128)(2,1)S(1)}, u32[]{:S(2)}, u32[]{:S(2)}) async-start(bf16[32,80,128]{2,1,0:T(8,128)(2,1)} %shard_map.196), calls=%async_computation | async-start | bytes 1310720 | tf_op jit(solution)/shard_map/all_to_all | solution.py:379
  15.3 4.0 %copy-start.8 = (bf16[128,512]{1,0:T(8,128)(2,1)S(1)}, bf16[128,512]{1,0:T(8,128)(2,1)}, u32[]{:S(2)}) copy-start(bf16[128,512]{1,0:T(8,128)(2,1)} %refs_0_.1) | copy-start | bytes 393220
  15.3 4.0 %copy-start.9 = (bf16[128,512]{1,0:T(8,128)(2,1)S(1)}, bf16[128,512]{1,0:T(8,128)(2,1)}, u32[]{:S(2)}) copy-start(bf16[128,512]{1,0:T(8,128)(2,1)} %refs_1_.1) | copy-start | bytes 393220
  15.4 5.8 %collective-permute-start.1 = (bf16[512,128]{1,0:T(8,128)(2,1)S(1)}, bf16[512,128]{1,0:T(8,128)(2,1)S(1)}, u32[]{:S(2)}, u32[]{:S(2)}) collective-permute-start(bf16[512,128]{1,0:T(8,128)(2,1)S(1)} %bitcast.8), channel_id=1, source_target_pairs={{0,3},{1,0},{2,1},{3,2},{4,7},{5,4},{6,5},{7,6},{8,11},{9,8},{10,9... | collective-permute-start | bytes 393224 | tf_op jit(solution)/shard_map/ppermute | solution.py:387
  18.2 5.4 %collective-permute-start.2 = (bf16[512,128]{1,0:T(8,128)(2,1)S(1)}, bf16[512,128]{1,0:T(8,128)(2,1)S(1)}, u32[]{:S(2)}, u32[]{:S(2)}) collective-permute-start(bf16[512,128]{1,0:T(8,128)(2,1)S(1)} %bitcast.9), channel_id=1, source_target_pairs={{0,2},{1,3},{2,0},{3,1},{4,6},{5,7},{6,4},{7,5},{8,10},{9,11},{10,... | collective-permute-start | bytes 393224 | tf_op jit(solution)/shard_map/ppermute | solution.py:387
  18.6 8.9 %collective-permute-start.3 = (bf16[512,128]{1,0:T(8,128)(2,1)S(1)}, bf16[512,128]{1,0:T(8,128)(2,1)S(1)}, u32[]{:S(2)}, u32[]{:S(2)}) collective-permute-start(bf16[512,128]{1,0:T(8,128)(2,1)S(1)} %bitcast.10), channel_id=1, source_target_pairs={{0,1},{1,2},{2,3},{3,0},{4,5},{5,6},{6,7},{7,4},{8,9},{9,10},{10,1... | collective-permute-start | bytes 393224 | tf_op jit(solution)/shard_map/ppermute | solution.py:387
  27.6 2.8 %collective-permute-start.4 = (bf16[2048,128]{1,0:T(8,128)(2,1)S(1)}, bf16[2048,128]{1,0:T(8,128)(2,1)S(1)}, u32[]{:S(2)}, u32[]{:S(2)}) collective-permute-start(bf16[2048,128]{1,0:T(8,128)(2,1)S(1)} %shard_map.193.mine_ref), channel_id=1, source_target_pairs={{0,4},{4,0},{8,12},{12,8},{16,20},{20,16},{24,28},{28,24},{32,36},... | collective-permute-start | bytes 1572872 | tf_op jit(solution)/shard_map/ppermute | solution.py:358
  28.6 1.7 %collective-permute-start = (bf16[256,256]{1,0:T(8,128)(2,1)S(1)}, bf16[256,256]{1,0:T(8,128)(2,1)S(1)}, u32[]{:S(2)}, u32[]{:S(2)}) collective-permute-start(bf16[256,256]{1,0:T(8,128)(2,1)S(1)} %get-tuple-element.31), channel_id=1, source_target_pairs={{0,4},{4,0},{8,12},{12,8},{16,20},{20,16},{24,28},{28,24},{32,36},... | collective-permute-start | bytes 393224 | tf_op jit(solution)/shard_map/ppermute | solution.py:358
  31.9 20.2 %collective-permute-start.13 = (bf16[2048,128]{1,0:T(8,128)(2,1)}, bf16[2048,128]{1,0:T(8,128)(2,1)S(1)}, u32[]{:S(2)}, u32[]{:S(2)}) collective-permute-start(bf16[2048,128]{1,0:T(8,128)(2,1)} %get-tuple-element.41), channel_id=1, source_target_pairs={{0,8},{4,12},{8,0},{12,4},{16,24},{20,28},{24,16},{28,20},{32,40},... | collective-permute-start | bytes 1572872 | tf_op jit(solution)/shard_map/ppermute | solution.py:440
  33.2 6.4 %collective-permute-start.5 = (bf16[512,128]{1,0:T(8,128)(2,1)S(1)}, bf16[512,128]{1,0:T(8,128)(2,1)S(1)}, u32[]{:S(2)}, u32[]{:S(2)}) collective-permute-start(bf16[512,128]{1,0:T(8,128)(2,1)S(1)} %get-tuple-element.35), channel_id=1, source_target_pairs={{0,4},{4,0},{8,12},{12,8},{16,20},{20,16},{24,28},{28,24},{32,36},... | collective-permute-start | bytes 393224 | tf_op jit(solution)/shard_map/ppermute | solution.py:358
  36.9 2.8 %collective-permute-start.6 = (bf16[512,128]{1,0:T(8,128)(2,1)S(1)}, bf16[512,128]{1,0:T(8,128)(2,1)S(1)}, u32[]{:S(2)}, u32[]{:S(2)}) collective-permute-start(bf16[512,128]{1,0:T(8,128)(2,1)S(1)} %get-tuple-element.36), channel_id=1, source_target_pairs={{0,4},{4,0},{8,12},{12,8},{16,20},{20,16},{24,28},{28,24},{32,36},... | collective-permute-start | bytes 393224 | tf_op jit(solution)/shard_map/ppermute | solution.py:358
  37.0 5.9 %collective-permute-start.7 = (bf16[512,128]{1,0:T(8,128)(2,1)S(1)}, bf16[512,128]{1,0:T(8,128)(2,1)S(1)}, u32[]{:S(2)}, u32[]{:S(2)}) collective-permute-start(bf16[512,128]{1,0:T(8,128)(2,1)S(1)} %get-tuple-element.33.refs_3_), channel_id=1, source_target_pairs={{0,64},{4,68},{8,72},{12,76},{16,80},{20,84},{24,88},{28,92},{32,9... | collective-permute-start | bytes 393224 | tf_op jit(solution)/shard_map/ppermute | solution.py:358
  37.0 5.9 %collective-permute-start.8 = (bf16[512,128]{1,0:T(8,128)(2,1)S(1)}, bf16[512,128]{1,0:T(8,128)(2,1)S(1)}, u32[]{:S(2)}, u32[]{:S(2)}) collective-permute-start(bf16[512,128]{1,0:T(8,128)(2,1)S(1)} %get-tuple-element.34.refs_4_), channel_id=1, source_target_pairs={{0,192},{4,196},{8,200},{12,204},{16,208},{20,212},{24,216},{28,22... | collective-permute-start | bytes 393224 | tf_op jit(solution)/shard_map/ppermute | solution.py:358
  39.7 5.5 %collective-permute-start.9 = (bf16[512,128]{1,0:T(8,128)(2,1)S(1)}, bf16[512,128]{1,0:T(8,128)(2,1)S(1)}, u32[]{:S(2)}, u32[]{:S(2)}) collective-permute-start(bf16[512,128]{1,0:T(8,128)(2,1)S(1)} %collective-permute-done.5.refs_5_), channel_id=1, source_target_pairs={{0,64},{4,68},{8,72},{12,76},{16,80},{20,84},{24,88},{28,92},{32,9... | collective-permute-start | bytes 393224 | tf_op jit(solution)/shard_map/ppermute | solution.py:358
  39.7 5.5 %collective-permute-start.10 = (bf16[512,128]{1,0:T(8,128)(2,1)S(1)}, bf16[512,128]{1,0:T(8,128)(2,1)S(1)}, u32[]{:S(2)}, u32[]{:S(2)}) collective-permute-start(bf16[512,128]{1,0:T(8,128)(2,1)S(1)} %collective-permute-done.6.refs_6_), channel_id=1, source_target_pairs={{0,192},{4,196},{8,200},{12,204},{16,208},{20,212},{24,216},{28,22... | collective-permute-start | bytes 393224 | tf_op jit(solution)/shard_map/ppermute | solution.py:358
  46.3 14.9 %all-to-all-start.1 = ((bf16[32,16,128]{2,1,0:T(8,128)(2,1)}), bf16[32,16,128]{2,1,0:T(8,128)(2,1)S(1)}, u32[]{:S(2)}, u32[]{:S(2)}) async-start(bf16[32,16,128]{2,1,0:T(8,128)(2,1)} %get-tuple-element.38.after_ref), calls=%async_computation.1 | async-start | bytes 262144 | tf_op jit(solution)/shard_map/all_to_all | solution.py:445
  52.4 7.7 %collective-permute-start.14 = (bf16[512,128]{1,0:T(8,128)(2,1)S(1)}, bf16[512,128]{1,0:T(8,128)(2,1)S(1)}, u32[]{:S(2)}, u32[]{:S(2)}) collective-permute-start(bf16[512,128]{1,0:T(8,128)(2,1)S(1)} %get-tuple-element.43), channel_id=1, source_target_pairs={{0,64},{4,68},{8,72},{12,76},{16,80},{20,84},{24,88},{28,92},{32,9... | collective-permute-start | bytes 393224 | tf_op jit(solution)/shard_map/ppermute | solution.py:358
  53.8 5.7 %copy-start.1 = (bf16[2,256,256]{2,1,0:T(8,128)(2,1)S(1)}, bf16[2,256,256]{2,1,0:T(8,128)(2,1)}, u32[]{:S(2)}) copy-start(bf16[2,256,256]{2,1,0:T(8,128)(2,1)} %constant.31.second_ref.refs_5_) | copy-start | bytes 786436
  53.8 5.7 %copy-start.4 = (f32[2,72,128]{2,1,0:T(8,128)S(1)}, f32[2,72,128]{2,1,0:T(8,128)}, u32[]{:S(2)}) copy-start(f32[2,72,128]{2,1,0:T(8,128)} %constant.26.clone.twist_ref.refs_4_) | copy-start | bytes 221188
  53.8 5.7 %copy-start.6 = (bf16[144,128]{1,0:T(8,128)(2,1)S(1)}, bf16[144,128]{1,0:T(8,128)(2,1)}, u32[]{:S(2)}) copy-start(bf16[144,128]{1,0:T(8,128)(2,1)} %constant.28.first_ref.refs_3_) | copy-start | bytes 110596
  53.8 6.4 %collective-permute-start.15 = (bf16[512,128]{1,0:T(8,128)(2,1)S(1)}, bf16[512,128]{1,0:T(8,128)(2,1)S(1)}, u32[]{:S(2)}, u32[]{:S(2)}) collective-permute-start(bf16[512,128]{1,0:T(8,128)(2,1)S(1)} %get-tuple-element.44), channel_id=1, source_target_pairs={{0,192},{4,196},{8,200},{12,204},{16,208},{20,212},{24,216},{28,22... | collective-permute-start | bytes 393224 | tf_op jit(solution)/shard_map/ppermute | solution.py:358
  55.4 4.1 %collective-permute-start.12 = (bf16[256,128]{1,0:T(8,128)(2,1)S(1)}, bf16[256,128]{1,0:T(8,128)(2,1)S(1)}, u32[]{:S(2)}, u32[]{:S(2)}) collective-permute-start(bf16[256,128]{1,0:T(8,128)(2,1)S(1)} %get-tuple-element.40), channel_id=1, source_target_pairs={{0,4},{4,0},{8,12},{12,8},{16,20},{20,16},{24,28},{28,24},{32,36},... | collective-permute-start | bytes 196616 | tf_op jit(solution)/shard_map/ppermute | solution.py:358
  58.6 1.5 %collective-permute-start.11 = (bf16[128,256]{1,0:T(8,128)(2,1)S(1)}, bf16[128,256]{1,0:T(8,128)(2,1)S(1)}, u32[]{:S(2)}, u32[]{:S(2)}) collective-permute-start(bf16[128,256]{1,0:T(8,128)(2,1)S(1)} %get-tuple-element.37), channel_id=1, source_target_pairs={{0,4},{4,0},{8,12},{12,8},{16,20},{20,16},{24,28},{28,24},{32,36},... | collective-permute-start | bytes 196616 | tf_op jit(solution)/shard_map/ppermute | solution.py:358
  59.5 1.8 %copy-start.5 = (bf16[2,256,256]{2,1,0:T(8,128)(2,1)S(1)}, bf16[2,256,256]{2,1,0:T(8,128)(2,1)}, u32[]{:S(2)}) copy-start(bf16[2,256,256]{2,1,0:T(8,128)(2,1)} %constant.34.refs_6_) | copy-start | bytes 786436
  59.5 1.8 %copy-start.10 = (bf16[64,432]{1,0:T(8,128)(2,1)S(1)}, bf16[64,432]{1,0:T(8,128)(2,1)}, u32[]{:S(2)}) copy-start(bf16[64,432]{1,0:T(8,128)(2,1)} %constant.35.refs_7_) | copy-start | bytes 165892
  80.1 5.6 %copy-start.2 = (bf16[128,512]{1,0:T(8,128)(2,1)S(1)}, bf16[128,512]{1,0:T(8,128)(2,1)}, u32[]{:S(2)}) copy-start(bf16[128,512]{1,0:T(8,128)(2,1)} %refs_5_.1) | copy-start | bytes 393220
  80.1 5.6 %copy-start.3 = (bf16[128,512]{1,0:T(8,128)(2,1)S(1)}, bf16[128,512]{1,0:T(8,128)(2,1)}, u32[]{:S(2)}) copy-start(bf16[128,512]{1,0:T(8,128)(2,1)} %refs_6_.1) | copy-start | bytes 393220
  80.3 6.5 %collective-permute-start.16 = (bf16[256,128]{1,0:T(8,128)(2,1)S(1)}, bf16[256,128]{1,0:T(8,128)(2,1)S(1)}, u32[]{:S(2)}, u32[]{:S(2)}) collective-permute-start(bf16[256,128]{1,0:T(8,128)(2,1)S(1)} %get-tuple-element.50), channel_id=1, source_target_pairs={{0,4},{4,0},{8,12},{12,8},{16,20},{20,16},{24,28},{28,24},{32,36},... | collective-permute-start | bytes 196616 | tf_op jit(solution)/shard_map/ppermute | solution.py:358
  85.6 1.2 %collective-permute-start.17 = (f32[32,256]{1,0:T(8,128)S(1)}, f32[32,256]{1,0:T(8,128)S(1)}, u32[]{:S(2)}, u32[]{:S(2)}) collective-permute-start(f32[32,256]{1,0:T(8,128)S(1)} %get-tuple-element.52), channel_id=1, source_target_pairs={{0,4},{4,0},{8,12},{12,8},{16,20},{20,16},{24,28},{28,24},{32,36},... | collective-permute-start | bytes 98312 | tf_op jit(solution)/shard_map/ppermute | solution.py:358
